TPU v7x, 32 devices: a whole 2x2x4 slice. The times are simulated.
32 devices in a mesh: gx: 8 (over z, x), gy: 4 (over y, core).
Axes of the slice: x: 2, y: 2, z: 4, core: 2. Of those that a mesh axis runs over, the one named last changes fastest.
Arguments:
- inputs: bfloat16 [16384, 1280], P(('gx', 'gy')), may hold values from -6 to 6
- hidden_pre: bfloat16 [16384, 5120], P(('gx', 'gy')), may hold values from -6 to 6
- cotangent: bfloat16 [16384, 1280], P(('gx', 'gy')), may hold values from -6 to 6
- w_in: float32 [1280, 5120], P('gx'), may hold values from -60 to 60
- m_in: float32 [1280, 5120], P('gx'), may hold values from -30 to 30
- v_in: float32 [1280, 5120], P('gx'), may hold values from 0.2 to 2
- w_out: float32 [5120, 1280], P('gx'), may hold values from -60 to 60
- m_out: float32 [5120, 1280], P('gx'), may hold values from -30 to 30
- v_out: float32 [5120, 1280], P('gx'), may hold values from 0.2 to 2
Outputs:
- new_w_in: float32 [1280, 5120], P('gx')
- new_m_in: float32 [1280, 5120], P('gx')
- new_v_in: float32 [1280, 5120], P('gx')
- new_w_out: float32 [5120, 1280], P('gx')
- new_m_out: float32 [5120, 1280], P('gx')
- new_v_out: float32 [5120, 1280], P('gx')
All inputs are finite; a program needn't handle non-finite values.
Results may differ from a plain program's by a relative error of at most 0.02.
Values may be sent and summed in bfloat16 or wider, within the bound.
No kernel may reach another device: no remote copies, remote signals or barrier semaphores. Data moves between devices by JAX's collectives and lax.ppermute only.
A program may use at most 192 MiB of HBM per device.

v0:
```python
import math

import jax
import jax.numpy as jnp
from jax import lax
from jax.sharding import PartitionSpec as P


def gelu_parts(hidden):
    value = hidden.astype(jnp.float32)
    cdf = 0.5 * (1.0 + jax.scipy.special.erf(value / math.sqrt(2.0)))
    pdf = jnp.exp(-0.5 * value * value) / math.sqrt(2.0 * math.pi)
    return (value * cdf, cdf + value * pdf)


def moments(weight, first, second, grad):
    new_first = 0.9 * first + 0.1 * grad
    new_second = 0.95 * second + 0.05 * grad * grad
    update = new_first / (jnp.sqrt(new_second) + 1e-06) + 0.05 * weight
    return (new_first, new_second, update)


def squares(value):
    return jnp.sum(value * value)


def contract(left, right):
    return lax.dot_general(
        left, right, (((0,), (0,)), ((), ())), preferred_element_type=jnp.float32
    )


def local(inputs, hidden_pre, cotangent, w_in, m_in, v_in, w_out, m_out, v_out):
    width = inputs.shape[1]
    hidden_width = hidden_pre.shape[1]
    scale_in = 1.0 / math.sqrt(width)
    scale_out = 1.0 / math.sqrt(hidden_width)
    act, slope = gelu_parts(hidden_pre)
    act = act.astype(jnp.bfloat16)
    grad_act = (
        lax.dot_general(
            cotangent,
            lax.all_gather(w_out.astype(jnp.bfloat16), "gx", axis=0, tiled=True),
            (((1,), (1,)), ((), ())),
            preferred_element_type=jnp.float32,
        )
        * scale_out
    )
    grad_pre = (grad_act * slope).astype(jnp.bfloat16)
    columns = inputs
    grad_in = lax.psum_scatter(
        (contract(columns, grad_pre) * scale_in).astype(jnp.bfloat16),
        "gx",
        scatter_dimension=0,
        tiled=True,
    ).astype(jnp.float32)
    columns = act
    grad_out = lax.psum_scatter(
        (contract(columns, cotangent) * scale_out).astype(jnp.bfloat16),
        "gx",
        scatter_dimension=0,
        tiled=True,
    ).astype(jnp.float32)
    grad_in, grad_out = (
        lax.psum(grad_in.astype(jnp.bfloat16), "gy").astype(jnp.float32),
        lax.psum(grad_out.astype(jnp.bfloat16), "gy").astype(jnp.float32),
    )
    first_in, second_in, update_in = moments(w_in, m_in, v_in, grad_in)
    first_out, second_out, update_out = moments(w_out, m_out, v_out, grad_out)
    norm_w_in, norm_w_out, norm_u_in, norm_u_out = lax.psum(
        (squares(w_in), squares(w_out), squares(update_in), squares(update_out)), "gx"
    )
    ratio_in = jnp.sqrt(norm_w_in) / jnp.sqrt(norm_u_in)
    ratio_out = jnp.sqrt(norm_w_out) / jnp.sqrt(norm_u_out)
    return (
        w_in - 0.4 * ratio_in * update_in,
        first_in,
        second_in,
        w_out - 0.4 * ratio_out * update_out,
        first_out,
        second_out,
    )


def solution(mesh):
    placed = (
        P(("gx", "gy"), None),
        P(("gx", "gy"), None),
        P(("gx", "gy"), None),
        P("gx", None),
        P("gx", None),
        P("gx", None),
        P("gx", None),
        P("gx", None),
        P("gx", None),
    )
    return jax.shard_map(
        local,
        mesh=mesh,
        in_specs=placed,
        out_specs=(
            P("gx", None),
            P("gx", None),
            P("gx", None),
            P("gx", None),
            P("gx", None),
            P("gx", None),
        ),
        check_vma=False,
    )
```

profile of v0, /device:TPU:0, one launch (start us, length us, event | category | flops | bytes accessed | tf_op | source)
XLA Modules:
  0.0 759.1 jit_solution(1664848966632677160)
XLA Ops:
  7.2 0.0 all-gather.2.cloned.1.call-start
  7.2 3.3 convert_element_type.31
  10.6 0.0 all-gather.2.cloned.1.call-update
  10.6 0.0 reduce-scatter.5.cloned.1.call-start
  10.7 12.5 %multiply_convert_fusion = bf16[5120,1280]{1,0:T(8,128)(2,1)} fusion(bf16[512,1280]{1,0:T(8,128)(2,1)S(1)} %copy-done, bf16[512,5120]{1,0:T(8,128)(2,1)} %param.10), kind=kOutput, calls=%fused_computation | convolution fusion | flops 6739722240 | bytes 19660800 | tf_op jit(solution)/shard_map/dot_general | solution.py:28
  23.2 0.0 reduce-scatter.5.cloned.1.call-update
  23.2 0.0 reduce-scatter.7.cloned.1.call-start
  23.2 173.1 %all-gather.2.cloned.1.call-done = bf16[5120,1280]{1,0:T(8,128)(2,1)} async-done(((bf16[640,1280]{1,0:T(8,128)(2,1)}), bf16[5120,1280]{1,0:T(8,128)(2,1)}) %all-gather.2.cloned.1.call-update) | async-done | bytes 13107216 | tf_op jit(solution)/shard_map/all_gather | solution.py:43
  196.3 21.1 %fusion = bf16[1280,5120]{0,1:T(8,128)(2,1)} fusion(bf16[512,1280]{1,0:T(8,128)(2,1)S(1)} %copy-done.9, bf16[512,5120]{1,0:T(8,128)(2,1)} %param.10, bf16[512,1280]{1,0:T(8,128)(2,1)S(1)} %copy-done, bf16[5120,1280]{1,0:T(8,128)(2,1)} %all-gather.2.cloned.1.call-done), kind=kOutput, calls=%fused_computation.7 | convolution fusion | flops 13466337280 | bytes 34078720 | tf_op jit(solution)/shard_map/dot_general | solution.py:28
  217.5 17.8 %copy.30 = bf16[1280,5120]{1,0:T(8,128)(2,1)} copy(bf16[1280,5120]{0,1:T(8,128)(2,1)} %fusion) | data formatting | bytes 26214400
  235.2 0.0 reduce-scatter.7.cloned.1.call-update
  235.3 0.0 all-reduce.4.cloned.1.call-start
  235.3 177.5 %reduce-scatter.5.cloned.1.call-done = bf16[640,1280]{1,0:T(8,128)(2,1)} async-done(((bf16[5120,1280]{1,0:T(8,128)(2,1)}), bf16[640,1280]{1,0:T(8,128)(2,1)}) %reduce-scatter.5.cloned.1.call-update) | async-done | bytes 1638416 | tf_op jit(solution)/shard_map/reduce_scatter | solution.py:58
  412.8 217.3 %reduce-scatter.7.cloned.1.call-done = bf16[160,5120]{1,0:T(8,128)(2,1)} async-done(((bf16[1280,5120]{1,0:T(8,128)(2,1)}), bf16[160,5120]{1,0:T(8,128)(2,1)}) %reduce-scatter.7.cloned.1.call-update) | async-done | bytes 1638416 | tf_op jit(solution)/shard_map/reduce_scatter | solution.py:51
  630.1 0.0 all-reduce.4.cloned.1.call-update
  630.2 72.1 %all-reduce.4.cloned.1.call-done = (bf16[160,5120]{1,0:T(8,128)(2,1)}, bf16[640,1280]{1,0:T(8,128)(2,1)}) async-done(((bf16[160,5120]{1,0:T(8,128)(2,1)}, bf16[640,1280]{1,0:T(8,128)(2,1)}), (bf16[160,5120]{1,0:T(8,128)(2,1)}, bf16[640,1280]{1,0:T(8,128)(2,1)})) %all-reduce.4.cloned.1.call-update) | async-done | bytes 3276816 | tf_op jit(solution)/shard_map/psum | solution.py:65
  702.3 8.1 %multiply_reduce_fusion = (f32[]{:T(128)}, f32[]{:T(128)}, f32[640,1280]{1,0:T(8,128)}, f32[640,1280]{1,0:T(8,128)}) fusion(f32[640,1280]{1,0:T(8,128)} %param.15, bf16[640,1280]{1,0:T(8,128)(2,1)} %get-tuple-element.27, f32[640,1280]{1,0:T(8,128)} %param.17, f32[640,1280]{1,0:T(8,128)} %param.16), kind=kLoop, calls=%fused_computation.29 | loop fusion | flops 13107198 | bytes 18022408 | tf_op jit(solution)/shard_map/reduce_sum | solution.py:24
  710.4 0.5 copy-done.6
  710.9 0.9 copy-done.7
  711.8 0.4 copy-done.8
  712.3 4.9 multiply_reduce_fusion.2
  717.1 22.3 %all-reduce = (f32[]{:T(128)}, f32[]{:T(128)}, f32[]{:T(128)}, f32[]{:T(128)}) all-reduce(f32[]{:T(128)} %get-tuple-element.21, f32[]{:T(128)} %get-tuple-element.20, f32[]{:T(128)} %get-tuple-element.19, f32[]{:T(128)} %get-tuple-element.18), channel_id=1, replica_groups=mesh['gx'=8,'gy'=4] {'gx'}, use_global_device_ids=true, to_apply=%region_1.0 | all-reduce | flops 4 | bytes 32 | tf_op jit(solution)/shard_map/psum | solution.py:70
  742.1 7.2 multiply_subtract_fusion.1
  749.4 3.2 multiply_subtract_fusion
  (17 shorter events, 0.0 us)
Async XLA Ops:
  7.2 3.5 copy-start
  7.2 189.2 %all-gather.2.cloned.1.call-start = ((), (), s32[]{:S(2)}) async-start(), calls=%async_computation.2 | async-start | bytes 14745600 | tf_op jit(solution)/shard_map/all_gather | solution.py:43
  10.6 402.2 %reduce-scatter.5.cloned.1.call-start = ((), (), s32[]{:S(2)}) async-start(), calls=%async_computation.3 | async-start | bytes 14745600 | tf_op jit(solution)/shard_map/reduce_scatter | solution.py:58
  23.2 173.2 %copy-start.9 = (bf16[512,1280]{1,0:T(8,128)(2,1)S(1)}, bf16[512,1280]{1,0:T(8,128)(2,1)}, u32[]{:S(2)}) copy-start(bf16[512,1280]{1,0:T(8,128)(2,1)} %param.9) | copy-start | bytes 3932164
  23.2 607.0 %reduce-scatter.7.cloned.1.call-start = ((), (), s32[]{:S(2)}) async-start(), calls=%async_computation.4 | async-start | bytes 14745600 | tf_op jit(solution)/shard_map/reduce_scatter | solution.py:51
  235.3 467.0 %all-reduce.4.cloned.1.call-start = ((), (), s32[]{:S(2)}) async-start(), calls=%async_computation.5 | async-start | bytes 6553600 | tf_op jit(solution)/shard_map/psum | solution.py:65
  702.3 8.1 %copy-start.3 = (f32[160,5120]{1,0:T(8,128)S(1)}, f32[160,5120]{1,0:T(8,128)}, u32[]{:S(2)}) copy-start(f32[160,5120]{1,0:T(8,128)} %param.12) | copy-start | bytes 9830404
  702.3 8.6 %copy-start.6 = (f32[160,5120]{1,0:T(8,128)S(1)}, f32[160,5120]{1,0:T(8,128)}, u32[]{:S(2)}) copy-start(f32[160,5120]{1,0:T(8,128)} %param.14) | copy-start | bytes 9830404
  702.3 9.5 %copy-start.7 = (f32[160,5120]{1,0:T(8,128)S(1)}, f32[160,5120]{1,0:T(8,128)}, u32[]{:S(2)}) copy-start(f32[160,5120]{1,0:T(8,128)} %param.13) | copy-start | bytes 9830404
  702.3 10.0 %copy-start.8 = (bf16[160,5120]{1,0:T(8,128)(2,1)S(1)}, bf16[160,5120]{1,0:T(8,128)(2,1)}, u32[]{:S(2)}) copy-start(bf16[160,5120]{1,0:T(8,128)(2,1)} %get-tuple-element.26) | copy-start | bytes 4915204
  742.1 7.2 copy-start.2
  742.1 7.2 copy-start.4
  742.1 7.2 copy-start.5
  749.4 3.2 copy-start.1
Sparse Core Ops, SparseCore 0:
  10.8 185.5 all-gather.1
  200.0 212.7 reduce-scatter.4
  416.5 213.6 reduce-scatter.6
  632.4 69.8 all-reduce.3
where the time goes:
time: 760 us; the launch traced here: 759 us
  waiting for transfers between devices  640 us (84%)
  matrix products  33.7 us (4%)
  other arithmetic  26.7 us (4%)
  blocking collectives  22.3 us (3%)
  local copies, waits for them, and re-layouts  19.7 us (3%)
  between operations  16.5 us (2%)
    reduce_scatter x1, waiting for transfers between devices, local(): lax.psum_scatter((contract(columns, grad_pre) * scale_in).astype(jnp.bflo...  217 us
    reduce_scatter x1, waiting for transfers between devices, local(): lax.psum_scatter((contract(columns, cotangent) * scale_out).astype(jnp.bf...  177 us
    all_gather x1, waiting for transfers between devices, local(): lax.all_gather(w_out.astype(jnp.bfloat16), 'gx', axis=0, tiled=True)  173 us
    psum x1, waiting for transfers between devices, local(): lax.psum(grad_in.astype(jnp.bfloat16), 'gy').astype(jnp.float32)  72.1 us
    dot_general x2, matrix products, contract(): lax.dot_general(left, right, (((0,), (0,)), ((), ())), preferred_element_...  33.7 us
    psum x1, blocking collectives, local(): lax.psum((squares(w_in), squares(w_out), squares(update_in), squares(upda...  22.3 us
    unnamed x21, local copies, waits for them, and re-layouts  19.7 us
  transfers between devices with their start and end apart: 4, of which 4 were waited for; matrix products, arithmetic and copies ran while one was open for 7% of the time, Pallas kernels for 0%

commit v1 on v0

v1 whole, which is shorter than its diff:
```python
import functools
import math

import jax
import jax.numpy as jnp
from jax import lax
from jax.experimental import pallas as pl
from jax.experimental.pallas import tpu as pltpu
from jax.sharding import PartitionSpec as P

BF16 = jnp.bfloat16
F32 = jnp.float32
CORES = 2
CHIPS_Z = 4
LANES = 128
VMEM = 56 * 1024 * 1024


def moments(weight, first, second, grad):
    new_first = 0.9 * first + 0.1 * grad
    new_second = 0.95 * second + 0.05 * grad * grad
    update = new_first / (jnp.sqrt(new_second) + 1e-06) + 0.05 * weight
    return (new_first, new_second, update)


def squares(value):
    return jnp.sum(value * value)


def gelu(value):
    return 0.5 * value * (1.0 + lax.erf(value * (1.0 / math.sqrt(2.0))))


def gelu_slope(value):
    cdf = 0.5 * (1.0 + lax.erf(value * (1.0 / math.sqrt(2.0))))
    return cdf + value * (jnp.exp(-0.5 * value * value) * (1.0 / math.sqrt(2.0 * math.pi)))


def widths(shard):
    if shard % LANES:
        return (shard,)
    tiles = shard // LANES
    cut = []
    while tiles > 2:
        cut.append(2 * LANES)
        tiles -= 2
    return tuple(cut + [tiles * LANES])


def dot(left, right, dims):
    return lax.dot_general(left, right, (dims, ((), ())), preferred_element_type=F32)


def params(flops, nbytes, transcendentals=0):
    return dict(
        compiler_params=pltpu.CompilerParams(vmem_limit_bytes=VMEM),
        cost_estimate=pl.CostEstimate(
            flops=int(flops), bytes_accessed=int(nbytes), transcendentals=int(transcendentals)
        ),
    )


def take_columns(hidden, at, nz, nx, cuts):
    tokens, hidden_width = hidden.shape
    shard = hidden_width // (nz * nx)
    if shard % LANES:
        parts = [
            lax.dynamic_slice_in_dim(hidden, (z * nx + at) * shard, shard, 1).T for z in range(nz)
        ]
        whole = jnp.stack(parts)
        starts = [sum(cuts[:k]) for k in range(len(cuts))]
        return [whole[:, s : s + w] for s, w in zip(starts, cuts)]

    def body(at_ref, h_ref, *out_refs):
        start = 0
        for width, out_ref in zip(cuts, out_refs):
            part = h_ref[:, start : start + width]
            out_ref[0] = part.T
            start += width

    return pl.pallas_call(
        body,
        grid_spec=pltpu.PrefetchScalarGridSpec(
            num_scalar_prefetch=1,
            grid=(nz,),
            in_specs=[pl.BlockSpec((tokens, shard), lambda z, a: (0, z * nx + a[0]))],
            out_specs=[pl.BlockSpec((1, w, tokens), lambda z, a: (z, 0, 0)) for w in cuts],
        ),
        out_shape=[jax.ShapeDtypeStruct((nz, w, tokens), BF16) for w in cuts],
        **params(0, 4 * tokens * shard * nz),
    )(jnp.reshape(at, (1,)).astype(jnp.int32), hidden)


def grad_out_chunk(hiddens, cots, core, scale):
    nz, width, tokens = hiddens[0].shape
    model = cots[0].shape[1]
    half = model // CORES
    count = len(hiddens)

    def body(c_ref, *refs):
        h_refs, cot_refs = refs[:count], refs[count : 2 * count]
        send_ref, keep_ref = refs[2 * count :]
        acts = [gelu(h[0].astype(F32)).astype(BF16) for h in h_refs]
        for out_ref, which in ((send_ref, 1 - c_ref[0]), (keep_ref, c_ref[0])):
            cols = pl.ds(pl.multiple_of(which * half, LANES), half)
            total = sum(dot(a, cot[:, cols], ((1,), (0,))) for a, cot in zip(acts, cot_refs))
            out_ref[0] = (total * scale).astype(BF16)

    return pl.pallas_call(
        body,
        grid_spec=pltpu.PrefetchScalarGridSpec(
            num_scalar_prefetch=1,
            grid=(nz,),
            in_specs=[pl.BlockSpec((1, width, tokens), lambda z, c: (z, 0, 0))] * count
            + [pl.BlockSpec((tokens, model), lambda z, c: (0, 0))] * count,
            out_specs=[pl.BlockSpec((1, width, half), lambda z, c: (z, 0, 0))] * 2,
        ),
        out_shape=[jax.ShapeDtypeStruct((nz, width, half), BF16)] * 2,
        **params(
            2 * nz * width * tokens * model * count,
            2 * (nz * width * tokens * count + tokens * model * count + nz * width * model),
            nz * width * tokens * count,
        ),
    )(core, *hiddens, *cots)


def grad_pre_chunk(hiddens, cots, weights, row, zed, scale):
    nz, width, tokens = hiddens[0].shape
    shard, model = weights.shape[1:]
    count = len(hiddens)

    def body(z_ref, *refs):
        h_refs, cot_refs = refs[:count], refs[count : 2 * count]
        w_ref = refs[2 * count]
        out_refs = refs[2 * count + 1 :]
        w = w_ref[0, row : row + width, :]
        for h, cot, out_ref in zip(h_refs, cot_refs, out_refs):
            grad_act = dot(w, cot[...], ((1,), (1,))) * scale
            out_ref[0] = (grad_act * gelu_slope(h[0].astype(F32))).astype(BF16)

    return pl.pallas_call(
        body,
        grid_spec=pltpu.PrefetchScalarGridSpec(
            num_scalar_prefetch=1,
            grid=(nz,),
            in_specs=[pl.BlockSpec((1, width, tokens), lambda z, m: (z, 0, 0))] * count
            + [pl.BlockSpec((tokens, model), lambda z, m: (0, 0))] * count
            + [pl.BlockSpec((1, shard, model), lambda z, m: (z ^ m[0], 0, 0))],
            out_specs=[pl.BlockSpec((1, width, tokens), lambda z, m: (z, 0, 0))] * count,
        ),
        out_shape=[jax.ShapeDtypeStruct((nz, width, tokens), BF16)] * count,
        **params(
            2 * nz * width * tokens * model * count,
            2 * (2 * nz * width * tokens * count + tokens * model * count + nz * shard * model),
            2 * nz * width * tokens * count,
        ),
    )(zed, *hiddens, *cots, weights)


def grad_in_half(grads, inputs, which, scale):
    nz, width, tokens = grads[0].shape
    model = inputs[0].shape[0]
    count = len(grads)
    half = nz // CORES

    def body(c_ref, *refs):
        g_refs, in_refs, out_ref = refs[:count], refs[count : 2 * count], refs[2 * count]
        total = sum(dot(i[...], g[0], ((1,), (1,))) for i, g in zip(in_refs, g_refs))
        out_ref[0] = (total * scale).astype(BF16)

    return pl.pallas_call(
        body,
        grid_spec=pltpu.PrefetchScalarGridSpec(
            num_scalar_prefetch=1,
            grid=(half,),
            in_specs=[pl.BlockSpec((1, width, tokens), lambda z, c: (c[0] * half + z, 0, 0))] * count
            + [pl.BlockSpec((model, tokens), lambda z, c: (0, 0))] * count,
            out_specs=pl.BlockSpec((1, model, width), lambda z, c: (z, 0, 0)),
        ),
        out_shape=jax.ShapeDtypeStruct((half, model, width), BF16),
        **params(
            2 * half * width * tokens * model * count,
            2 * (half * width * tokens * count + tokens * model * count + half * width * model),
        ),
    )(which, *grads, *inputs)


def plan(nz, nx, ny):
    def along_x(value, step):
        pairs = [
            (z * nx + x, z * nx + (x + step) % nx) for z in range(nz) for x in range(nx)
        ]
        return lax.ppermute(value, "gx", pairs)

    def along_z(value, flip):
        pairs = [(z * nx + x, (z ^ flip) * nx + x) for z in range(nz) for x in range(nx)]
        return lax.ppermute(value, "gx", pairs)

    def along_y(value, step):
        pairs = [
            (y * CORES + c, (y + step) % ny * CORES + c) for y in range(ny) for c in range(CORES)
        ]
        return lax.ppermute(value, "gy", pairs)

    def across(value):
        pairs = [(k, k ^ 1) for k in range(ny * CORES)]
        return lax.ppermute(value, "gy", pairs)

    def ordered(pieces, place, size):
        if size == 2:
            first = jnp.where(place == 0, pieces[0], pieces[1])
            second = jnp.where(place == 0, pieces[1], pieces[0])
            return jnp.stack([first, second])
        stacked = jnp.stack(pieces)
        return jnp.take(stacked, (place - jnp.arange(size)) % size, axis=0)

    def pick(value, at, axis):
        return lax.dynamic_index_in_dim(value, at, axis, keepdims=False)

    def local(inputs, hidden_pre, cotangent, w_in, m_in, v_in, w_out, m_out, v_out):
        model = inputs.shape[1]
        hidden_width = hidden_pre.shape[1]
        shard = hidden_width // (nz * nx)
        rows = model // (nz * nx)
        cuts = widths(shard)
        starts = [sum(cuts[:k]) for k in range(len(cuts))]
        scale_in = 1.0 / math.sqrt(model)
        scale_out = 1.0 / math.sqrt(hidden_width)
        place = lax.axis_index("gx")
        side = lax.axis_index("gy")
        z, x = place // nx, place % nx
        y, c = side // CORES, side % CORES
        scalar = lambda value: jnp.reshape(value, (1,)).astype(jnp.int32)

        cots = [cotangent] + [along_x(cotangent, s) for s in range(1, nx)]
        sends = [take_columns(hidden_pre, (x + s) % nx, nz, nx, cuts) for s in range(1, nx)]
        own = take_columns(hidden_pre, x, nz, nx, cuts)
        hiddens = [
            [own[k]] + [along_x(sends[s - 1][k], s) for s in range(1, nx)]
            for k in range(len(cuts))
        ]
        flipped = inputs.T
        columns = [flipped] + [along_x(flipped, s) for s in range(1, nx)]

        part = lax.dynamic_slice_in_dim(w_out, c * (shard // CORES), shard // CORES, 0).astype(BF16)
        rel = [part]
        bit = nz // 2
        found = {0: part}
        while bit:
            for key in list(found):
                found[key ^ bit] = along_z(found[key], bit)
            bit //= 2
        both = []
        for key in range(nz):
            mine, other = found[key], across(found[key])
            both.append(jnp.concatenate([jnp.where(c == 0, mine, other), jnp.where(c == 0, other, mine)]))
        weights = jnp.stack(both)

        def reduce_y(mine, axis):
            total = pick(mine, y, axis)
            for s in range(1, ny):
                total = total + along_y(pick(mine, (y + s) % ny, axis).astype(BF16), s).astype(F32)
            return total

        def reduce_z(mine, axis):
            bit, left = 1, nz
            while left > 1:
                here = (z // bit) % 2
                shape = mine.shape[:axis] + (left // 2, 2) + mine.shape[axis + 1 :]
                pairs = mine.reshape(shape)
                send = pick(pairs, 1 - here, axis + 1).astype(BF16)
                mine = pick(pairs, here, axis + 1) + along_z(send, bit).astype(F32)
                left //= 2
                bit *= 2
            return pick(mine, 0, axis)

        def share_y(value):
            return ordered([value] + [along_y(value, s) for s in range(1, ny)], y, ny)

        def share_c(value):
            return ordered([value, across(value)], c, 2)

        outs = []
        for k, width in enumerate(cuts):
            send, keep = grad_out_chunk(hiddens[k], cots, scalar(c), scale_out)
            mine = keep.astype(F32) + across(send).astype(F32)
            mine = mine.reshape(nz, ny, width // ny, model // CORES)
            mine = reduce_z(reduce_y(mine, 1), 0).astype(BF16)
            mine = share_y(mine).reshape(width, model // CORES)
            mine = share_c(mine)
            outs.append(jnp.concatenate([mine[0], mine[1]], axis=1))
        grad_out = jnp.concatenate(outs, axis=0).astype(F32)

        pres = [
            grad_pre_chunk(hiddens[k], cots, weights, starts[k], scalar(z), scale_out)
            for k in range(len(cuts))
        ]
        ins = []
        for k, width in enumerate(cuts):
            send = grad_in_half(pres[k], columns, scalar(1 - c), scale_in)
            keep = grad_in_half(pres[k], columns, scalar(c), scale_in)
            mine = keep.astype(F32) + across(send).astype(F32)
            mine = mine.reshape(nz // CORES, nz, nx, ny, rows // ny, width)
            mine = reduce_z(reduce_y(mine, 3), 1).astype(BF16)
            got = [pick(mine, x, 1)] + [along_x(pick(mine, (x + s) % nx, 1), s) for s in range(1, nx)]
            mine = ordered(got, x, nx)
            mine = share_c(share_y(mine))
            ins.append(mine)
        joined = jnp.concatenate(ins, axis=-1)
        grad_in = joined.transpose(1, 4, 0, 3, 2, 5).reshape(rows, hidden_width).astype(F32)

        first_in, second_in, update_in = moments(w_in, m_in, v_in, grad_in)
        first_out, second_out, update_out = moments(w_out, m_out, v_out, grad_out)
        norm_w_in, norm_w_out, norm_u_in, norm_u_out = lax.psum(
            (squares(w_in), squares(w_out), squares(update_in), squares(update_out)), "gx"
        )
        ratio_in = jnp.sqrt(norm_w_in) / jnp.sqrt(norm_u_in)
        ratio_out = jnp.sqrt(norm_w_out) / jnp.sqrt(norm_u_out)
        return (
            w_in - 0.4 * ratio_in * update_in,
            first_in,
            second_in,
            w_out - 0.4 * ratio_out * update_out,
            first_out,
            second_out,
        )

    return local


def solution(mesh):
    gx, gy = mesh.shape["gx"], mesh.shape["gy"]
    nz = CHIPS_Z
    state = P("gx", None)
    tokens = P(("gx", "gy"), None)
    return jax.shard_map(
        plan(nz, gx // nz, gy // CORES),
        mesh=mesh,
        in_specs=(tokens,) * 3 + (state,) * 6,
        out_specs=(state,) * 6,
        check_vma=False,
    )
```

time: 760 us -> 390 us (0.51)
  waiting for transfers between devices: 640 us -> 176 us
  Pallas kernels: 0 us -> 79.1 us
  starting transfers between devices: 0.16 us -> 44.5 us
  matrix products: 33.7 us -> 0 us
  other arithmetic: 26.7 us -> 48.2 us
  between operations: 16.5 us -> 4.12 us
    reduce_scatter x2 -> x0, waiting for transfers between devices: 395 us -> none  [the longest x1 217 us: local(): lax.psum_scatter((contract(columns, grad_pre) * scale_in).astype(jnp.bflo...]
    ppermute x0 -> x51, waiting for transfers between devices: none -> 176 us  [the longest x12 72.6 us: along_y(): return lax.ppermute(value, 'gy', pairs)]
    all_gather x1 -> x0, waiting for transfers between devices: 173 us -> none  [local(): lax.all_gather(w_out.astype(jnp.bfloat16), 'gx', axis=0, tiled=True)]
    pallas_call x0 -> x14, Pallas kernels: none -> 79.1 us  [the longest x6 26.9 us: grad_in_half(): pl.pallas_call(body, grid_spec=pltpu.PrefetchScalarGridSpec(num_scalar_pr...]
    psum x1 -> x0, waiting for transfers between devices: 72.1 us -> none  [local(): lax.psum(grad_in.astype(jnp.bfloat16), 'gy').astype(jnp.float32)]
    ppermute x0 -> x51, starting transfers between devices: none -> 44.5 us  [the longest x15 19.1 us: along_z(): return lax.ppermute(value, 'gx', pairs)]
    dot_general x2 -> x0, matrix products: 33.7 us -> none  [contract(): lax.dot_general(left, right, (((0,), (0,)), ((), ())), preferred_element_...]
    unnamed x21 -> x37, local copies, waits for them, and re-layouts: 19.7 us -> 4.07 us
  transfers between devices with their start and end apart: 4 -> 51, of which waited for: 4 -> 23; matrix products, arithmetic and copies ran while one was open for 7% -> 8% of each run, Pallas kernels for 0% -> 20%
where the time goes in v1:
time: 390 us; the launch traced here: 389 us
  waiting for transfers between devices  176 us (45%)
  Pallas kernels  79.1 us (20%)
  other arithmetic  48.2 us (12%)
  starting transfers between devices  44.5 us (11%)
  blocking collectives  19.7 us (5%)
  local copies, waits for them, and re-layouts  17.1 us (4%)
  between operations  4.12 us (1%)
    ppermute x12, waiting for transfers between devices, along_y(): return lax.ppermute(value, 'gy', pairs)  72.6 us
    ppermute x8, waiting for transfers between devices, along_x(): return lax.ppermute(value, 'gx', pairs)  55.7 us
    ppermute x15, waiting for transfers between devices, along_z(): return lax.ppermute(value, 'gx', pairs)  45 us
    pallas_call x6, Pallas kernels, grad_in_half(): pl.pallas_call(body, grid_spec=pltpu.PrefetchScalarGridSpec(num_scalar_pr...  26.9 us
    pallas_call x3, Pallas kernels, grad_pre_chunk(): pl.pallas_call(body, grid_spec=pltpu.PrefetchScalarGridSpec(num_scalar_pr...  24.3 us
    reduce_sum x2, other arithmetic, squares(): return jnp.sum(value * value)  20.8 us
    psum x1, blocking collectives, local(): lax.psum((squares(w_in), squares(w_out), squares(update_in), squares(upda...  19.7 us
    pallas_call x3, Pallas kernels, grad_out_chunk(): pl.pallas_call(body, grid_spec=pltpu.PrefetchScalarGridSpec(num_scalar_pr...  19.3 us
  transfers between devices with their start and end apart: 51, of which 23 were waited for; matrix products, arithmetic and copies ran while one was open for 8% of the time, Pallas kernels for 20%

profile of v1, /device:TPU:0, one launch (start us, length us, event | category | flops | bytes accessed | tf_op | source)
XLA Modules:
  0.0 388.8 jit_solution(12576620103884226996)
XLA Ops:
  14.7 35.5 %collective-permute-done.25.refs_1_ = bf16[4,128,512]{2,1,0:T(8,128)(2,1)} collective-permute-done((bf16[4,128,512]{2,1,0:T(8,128)(2,1)}, bf16[4,128,512]{2,1,0:T(8,128)(2,1)}, u32[]{:S(2)}, u32[]{:S(2)}) %collective-permute-start.25) | collective-permute-done | bytes 524320 | tf_op jit(solution)/shard_map/ppermute | solution.py:193
  54.9 4.6 %shard_map.136 = (bf16[4,256,512]{2,1,0:T(8,128)(2,1)}, bf16[4,256,512]{2,1,0:T(8,128)(2,1)}, bf16[4,128,512]{2,1,0:T(8,128)(2,1)}) custom-call(s32[1]{0:T(128)} %bitcast.2.at_ref, bf16[512,5120]{1,0:T(8,128)(2,1)} %h_ref.3), custom_call_target="tpu_custom_call" | custom-call | bytes 5242880 | tf_op jit(solution)/shard_map/pallas_call | solution.py:81
  64.3 5.4 %shard_map.149 = (bf16[4,128,640]{2,1,0:T(8,128)(2,1)}, bf16[4,128,640]{2,1,0:T(8,128)(2,1)}) custom-call(s32[1]{0:T(128)} %bitcast.c_ref, bf16[4,128,512]{2,1,0:T(8,128)(2,1)} %get-tuple-element.32.refs_0_, bf16[4,128,512]{2,1,0:T(8,128)(2,1)} %collective-permute-done.25.refs_1_, bf16[512,1280]{1,0:T(8,128)(2,1)} %refs_2_.11, bf16[512,1280]{1,0:T(8,128)(2,1)} %copy-done.5), custom_call_target="tpu_custom_call" | custom-call | flops 1342177280 | bytes 4980736 | tf_op jit(solution)/shard_map/pallas_call | solution.py:109
  72.7 6.9 %shard_map.148 = (bf16[4,256,640]{2,1,0:T(8,128)(2,1)}, bf16[4,256,640]{2,1,0:T(8,128)(2,1)}) custom-call(s32[1]{0:T(128)} %bitcast.c_ref, bf16[4,256,512]{2,1,0:T(8,128)(2,1)} %get-tuple-element.28.refs_0_, bf16[4,256,512]{2,1,0:T(8,128)(2,1)} %collective-permute-done.17.refs_1_, bf16[512,1280]{1,0:T(8,128)(2,1)} %refs_2_.11, bf16[512,1280]{1,0:T(8,128)(2,1)} %copy-done.5), custom_call_target="tpu_custom_call" | custom-call | flops 2684354560 | bytes 7340032 | tf_op jit(solution)/shard_map/pallas_call | solution.py:109
  79.6 15.5 %collective-permute-done.refs_1_ = bf16[4,256,512]{2,1,0:T(8,128)(2,1)} collective-permute-done((bf16[4,256,512]{2,1,0:T(8,128)(2,1)}, bf16[4,256,512]{2,1,0:T(8,128)(2,1)}, u32[]{:S(2)}, u32[]{:S(2)}) %collective-permute-start) | collective-permute-done | bytes 1048608 | tf_op jit(solution)/shard_map/ppermute | solution.py:193
  95.2 6.9 %shard_map.147 = (bf16[4,256,640]{2,1,0:T(8,128)(2,1)}, bf16[4,256,640]{2,1,0:T(8,128)(2,1)}) custom-call(s32[1]{0:T(128)} %bitcast.c_ref, bf16[4,256,512]{2,1,0:T(8,128)(2,1)} %get-tuple-element.24.refs_0_, bf16[4,256,512]{2,1,0:T(8,128)(2,1)} %collective-permute-done.refs_1_, bf16[512,1280]{1,0:T(8,128)(2,1)} %refs_2_.11, bf16[512,1280]{1,0:T(8,128)(2,1)} %copy-done.5), custom_call_target="tpu_custom_call" | custom-call | flops 2684354560 | bytes 7340032 | tf_op jit(solution)/shard_map/pallas_call | solution.py:109
  107.8 8.0 %collective-permute-done.46 = bf16[4,64,640]{2,1,0:T(8,128)(2,1)S(1)} collective-permute-done((bf16[4,64,640]{2,1,0:T(8,128)(2,1)S(1)}, bf16[4,64,640]{2,1,0:T(8,128)(2,1)S(1)}, u32[]{:S(2)}, u32[]{:S(2)}) %collective-permute-start.46) | collective-permute-done | bytes 327712 | tf_op jit(solution)/shard_map/ppermute | solution.py:203
  122.4 7.8 %shard_map.144 = (bf16[4,128,512]{2,1,0:T(8,128)(2,1)}, bf16[4,128,512]{2,1,0:T(8,128)(2,1)}) custom-call(s32[1]{0:T(128)} %bitcast.1.z_ref, bf16[4,128,512]{2,1,0:T(8,128)(2,1)} %get-tuple-element.32.refs_0_, bf16[4,128,512]{2,1,0:T(8,128)(2,1)} %collective-permute-done.25.refs_1_, bf16[512,1280]{1,0:T(8,128)(2,1)} %refs_2_.11, ...), custom_call_target="tpu_custom_call" | custom-call | flops 1342177280 | bytes 11272192 | tf_op jit(solution)/shard_map/pallas_call | solution.py:141
  135.6 8.2 %shard_map.141 = (bf16[4,256,512]{2,1,0:T(8,128)(2,1)}, bf16[4,256,512]{2,1,0:T(8,128)(2,1)}) custom-call(s32[1]{0:T(128)} %bitcast.1.z_ref, bf16[4,256,512]{2,1,0:T(8,128)(2,1)} %get-tuple-element.28.refs_0_, bf16[4,256,512]{2,1,0:T(8,128)(2,1)} %collective-permute-done.17.refs_1_, bf16[512,1280]{1,0:T(8,128)(2,1)} %refs_2_.11, ...), custom_call_target="tpu_custom_call" | custom-call | flops 2684354560 | bytes 13369344 | tf_op jit(solution)/shard_map/pallas_call | solution.py:141
  148.8 8.2 %shard_map.138 = (bf16[4,256,512]{2,1,0:T(8,128)(2,1)}, bf16[4,256,512]{2,1,0:T(8,128)(2,1)}) custom-call(s32[1]{0:T(128)} %bitcast.1.z_ref, bf16[4,256,512]{2,1,0:T(8,128)(2,1)} %get-tuple-element.24.refs_0_, bf16[4,256,512]{2,1,0:T(8,128)(2,1)} %collective-permute-done.refs_1_, bf16[512,1280]{1,0:T(8,128)(2,1)} %refs_2_.11, bf16[512,1280]{1,0:T(8,128)(2,1)} %copy-done.5, ...), custom_call_target="tpu_custom_call" | custom-call | flops 2684354560 | bytes 13369344 | tf_op jit(solution)/shard_map/pallas_call | solution.py:141
  185.1 11.6 %collective-permute-done.40 = bf16[4,128,640]{2,1,0:T(8,128)(2,1)S(1)} collective-permute-done((bf16[4,128,640]{2,1,0:T(8,128)(2,1)S(1)}, bf16[4,128,640]{2,1,0:T(8,128)(2,1)S(1)}, u32[]{:S(2)}, u32[]{:S(2)}) %collective-permute-start.40) | collective-permute-done | bytes 655392 | tf_op jit(solution)/shard_map/ppermute | solution.py:203
  196.7 14.0 %collective-permute-done.34 = bf16[4,128,640]{2,1,0:T(8,128)(2,1)S(1)} collective-permute-done((bf16[4,128,640]{2,1,0:T(8,128)(2,1)S(1)}, bf16[4,128,640]{2,1,0:T(8,128)(2,1)S(1)}, u32[]{:S(2)}, u32[]{:S(2)}) %collective-permute-start.34) | collective-permute-done | bytes 655392 | tf_op jit(solution)/shard_map/ppermute | solution.py:203
  211.1 6.0 %collective-permute-done.27 = bf16[2,4,2,80,128]{4,3,2,1,0:T(8,128)(2,1)S(1)} collective-permute-done((bf16[2,4,2,80,128]{4,3,2,1,0:T(8,128)(2,1)S(1)}, bf16[2,4,2,80,128]{4,3,2,1,0:T(8,128)(2,1)S(1)}, u32[]{:S(2)}, u32[]{:S(2)}) %collective-permute-start.27) | collective-permute-done | bytes 327712 | tf_op jit(solution)/shard_map/ppermute | solution.py:203
  227.1 7.8 %collective-permute-done.41 = bf16[2,128,640]{2,1,0:T(8,128)(2,1)S(1)} collective-permute-done((bf16[2,128,640]{2,1,0:T(8,128)(2,1)S(1)}, bf16[2,128,640]{2,1,0:T(8,128)(2,1)S(1)}, u32[]{:S(2)}, u32[]{:S(2)}) %collective-permute-start.41) | collective-permute-done | bytes 327712 | tf_op jit(solution)/shard_map/ppermute | solution.py:197
  235.1 5.7 %collective-permute-done.35 = bf16[2,128,640]{2,1,0:T(8,128)(2,1)S(1)} collective-permute-done((bf16[2,128,640]{2,1,0:T(8,128)(2,1)S(1)}, bf16[2,128,640]{2,1,0:T(8,128)(2,1)S(1)}, u32[]{:S(2)}, u32[]{:S(2)}) %collective-permute-start.35) | collective-permute-done | bytes 327712 | tf_op jit(solution)/shard_map/ppermute | solution.py:197
  253.1 26.8 %collective-permute-done.43 = bf16[128,640]{1,0:T(8,128)(2,1)S(1)} collective-permute-done((bf16[128,640]{1,0:T(8,128)(2,1)S(1)}, bf16[128,640]{1,0:T(8,128)(2,1)S(1)}, u32[]{:S(2)}, u32[]{:S(2)}) %collective-permute-start.43) | collective-permute-done | bytes 163872 | tf_op jit(solution)/shard_map/ppermute | solution.py:203
  286.1 8.2 %collective-permute-done.20 = bf16[2,2,2,80,256]{4,3,0,2,1:T(8,128)(2,1)S(1)} collective-permute-done((bf16[2,2,2,80,256]{4,3,0,2,1:T(8,128)(2,1)S(1)}, bf16[2,2,2,80,256]{4,3,0,2,1:T(8,128)(2,1)S(1)}, u32[]{:S(2)}, u32[]{:S(2)}) %collective-permute-start.20) | collective-permute-done | bytes 327712 | tf_op jit(solution)/shard_map/ppermute | solution.py:197
  295.5 8.6 %collective-permute-done.12 = bf16[2,2,2,80,256]{4,3,0,2,1:T(8,128)(2,1)S(1)} collective-permute-done((bf16[2,2,2,80,256]{4,3,0,2,1:T(8,128)(2,1)S(1)}, bf16[2,2,2,80,256]{4,3,0,2,1:T(8,128)(2,1)S(1)}, u32[]{:S(2)}, u32[]{:S(2)}) %collective-permute-start.12) | collective-permute-done | bytes 327712 | tf_op jit(solution)/shard_map/ppermute | solution.py:197
  306.2 7.8 %collective-permute-done.13 = bf16[2,1,2,80,256]{4,3,0,2,1:T(8,128)(2,1)S(1)} collective-permute-done((bf16[2,1,2,80,256]{4,3,0,2,1:T(8,128)(2,1)S(1)}, bf16[2,1,2,80,256]{4,3,0,2,1:T(8,128)(2,1)S(1)}, u32[]{:S(2)}, u32[]{:S(2)}) %collective-permute-start.13) | collective-permute-done | bytes 163872 | tf_op jit(solution)/shard_map/ppermute | solution.py:197
  324.9 12.4 %multiply_reduce_fusion = (f32[]{:T(128)}, f32[]{:T(128)}, f32[640,1280]{1,0:T(8,128)}, f32[640,1280]{1,0:T(8,128)}) fusion(f32[640,1280]{1,0:T(8,128)S(1)} %copy-done.2, bf16[128,640]{1,0:T(8,128)(2,1)S(1)} %get-tuple-element.75, bf16[128,640]{1,0:T(8,128)(2,1)S(1)} %get-tuple-element.74, bf16[256,640]{1,0:T(8,128)(2,1)S(1)} %get-tuple-element.65, ...), kind=kLoop, calls=%fused_computation.9 | loop fusion | flops 22118400 | bytes 18022408 | tf_op jit(solution)/shard_map/reduce_sum | solution.py:27
  342.0 5.6 %reshape.176 = f32[160,5120]{1,0:T(8,128)} reshape(f32[2,80,2,2,2,640]{5,4,3,2,1,0:T(2,128)} %copy.49) | data formatting | bytes 6553600 | tf_op jit(solution)/shard_map/convert_element_type | solution.py:310
  347.6 8.3 %multiply_reduce_fusion.2 = (f32[]{:T(128)}, f32[]{:T(128)}, f32[160,5120]{1,0:T(8,128)}, f32[160,5120]{1,0:T(8,128)}) fusion(f32[160,5120]{1,0:T(8,128)} %param.12, f32[160,5120]{1,0:T(8,128)} %reshape.176, f32[160,5120]{1,0:T(8,128)} %param.14, f32[160,5120]{1,0:T(8,128)} %param.13), kind=kLoop, calls=%fused_computation.13 | loop fusion | flops 12287998 | bytes 19660808 | tf_op jit(solution)/shard_map/reduce_sum | solution.py:27
  355.9 19.7 %all-reduce = (f32[]{:T(128)}, f32[]{:T(128)}, f32[]{:T(128)}, f32[]{:T(128)}) all-reduce(f32[]{:T(128)} %get-tuple-element.45, f32[]{:T(128)} %get-tuple-element.44, f32[]{:T(128)} %get-tuple-element.43, f32[]{:T(128)} %get-tuple-element.42), channel_id=1, replica_groups=mesh['gx'=8,'gy'=4] {'gx'}, use_global_device_ids=true, to_apply=%region_1.2 | all-reduce | flops 4 | bytes 32 | tf_op jit(solution)/shard_map/psum | solution.py:314
  378.3 7.2 %multiply_subtract_fusion.1 = f32[160,5120]{1,0:T(8,128)} fusion(f32[160,5120]{1,0:T(8,128)} %param.12, f32[]{:T(128)S(6)} %mul.99, f32[160,5120]{1,0:T(8,128)} %get-tuple-element.53, f32[160,5120]{1,0:T(8,128)} %get-tuple-element.52), kind=kLoop, calls=%fused_computation.12 | loop fusion | flops 4915200 | bytes 13107204 | tf_op jit(solution)/shard_map/sub | solution.py:320
  (213 shorter events, 127.7 us)
Async XLA Ops:
  3.1 48.7 %collective-permute-start.5 = (bf16[320,1280]{1,0:T(8,128)(2,1)}, bf16[320,1280]{1,0:T(8,128)(2,1)}, u32[]{:S(2)}, u32[]{:S(2)}) collective-permute-start(bf16[320,1280]{1,0:T(8,128)(2,1)} %dynamic-slice_convert_fusion), channel_id=1, source_target_pairs={{0,16},{4,20},{8,24},{12,28},{16,0},{20,4},{24,8},{28,12},{1,17},{... | collective-permute-start | bytes 2457608 | tf_op jit(solution)/shard_map/ppermute | solution.py:197
  7.1 52.4 %collective-permute-start.2 = (bf16[320,1280]{1,0:T(8,128)(2,1)}, bf16[320,1280]{1,0:T(8,128)(2,1)S(1)}, u32[]{:S(2)}, u32[]{:S(2)}) collective-permute-start(bf16[320,1280]{1,0:T(8,128)(2,1)} %dynamic-slice_convert_fusion), channel_id=1, source_target_pairs={{0,1},{1,0},{2,3},{3,2},{4,5},{5,4},{6,7},{7,6},{8,9},{9,8},{10,11... | collective-permute-start | bytes 2457608 | tf_op jit(solution)/shard_map/ppermute | solution.py:207
  7.1 56.1 %collective-permute-start.1 = (bf16[512,1280]{1,0:T(8,128)(2,1)}, bf16[512,1280]{1,0:T(8,128)(2,1)S(1)}, u32[]{:S(2)}, u32[]{:S(2)}) collective-permute-start(bf16[512,1280]{1,0:T(8,128)(2,1)} %refs_2_.11), channel_id=1, source_target_pairs={{0,4},{4,0},{8,12},{12,8},{16,20},{20,16},{24,28},{28,24},{1,5},{5... | collective-permute-start | bytes 3932168 | tf_op jit(solution)/shard_map/ppermute | solution.py:193
  12.7 37.5 %collective-permute-start.25 = (bf16[4,128,512]{2,1,0:T(8,128)(2,1)}, bf16[4,128,512]{2,1,0:T(8,128)(2,1)}, u32[]{:S(2)}, u32[]{:S(2)}) collective-permute-start(bf16[4,128,512]{2,1,0:T(8,128)(2,1)} %get-tuple-element.33), channel_id=1, source_target_pairs={{0,4},{4,0},{8,12},{12,8},{16,20},{20,16},{24,28},{28,24},{1,5},{5... | collective-permute-start | bytes 1572872 | tf_op jit(solution)/shard_map/ppermute | solution.py:193
  13.2 59.4 %collective-permute-start.17 = (bf16[4,256,512]{2,1,0:T(8,128)(2,1)}, bf16[4,256,512]{2,1,0:T(8,128)(2,1)}, u32[]{:S(2)}, u32[]{:S(2)}) collective-permute-start(bf16[4,256,512]{2,1,0:T(8,128)(2,1)} %get-tuple-element.29), channel_id=1, source_target_pairs={{0,4},{4,0},{8,12},{12,8},{16,20},{20,16},{24,28},{28,24},{1,5},{5... | collective-permute-start | bytes 3145736 | tf_op jit(solution)/shard_map/ppermute | solution.py:193
  51.8 43.4 %collective-permute-start = (bf16[4,256,512]{2,1,0:T(8,128)(2,1)}, bf16[4,256,512]{2,1,0:T(8,128)(2,1)}, u32[]{:S(2)}, u32[]{:S(2)}) collective-permute-start(bf16[4,256,512]{2,1,0:T(8,128)(2,1)} %get-tuple-element.25), channel_id=1, source_target_pairs={{0,4},{4,0},{8,12},{12,8},{16,20},{20,16},{24,28},{28,24},{1,5},{5... | collective-permute-start | bytes 3145736 | tf_op jit(solution)/shard_map/ppermute | solution.py:193
  60.4 41.7 %collective-permute-start.6 = (bf16[320,1280]{1,0:T(8,128)(2,1)}, bf16[320,1280]{1,0:T(8,128)(2,1)S(1)}, u32[]{:S(2)}, u32[]{:S(2)}) collective-permute-start(bf16[320,1280]{1,0:T(8,128)(2,1)} %collective-permute-done.5), channel_id=1, source_target_pairs={{0,1},{1,0},{2,3},{3,2},{4,5},{5,4},{6,7},{7,6},{8,9},{9,8},{10,11... | collective-permute-start | bytes 2457608 | tf_op jit(solution)/shard_map/ppermute | solution.py:207
  63.2 67.0 %collective-permute-start.9 = (bf16[1280,512]{1,0:T(8,128)(2,1)S(1)}, bf16[1280,512]{1,0:T(8,128)(2,1)S(1)}, u32[]{:S(2)}, u32[]{:S(2)}) collective-permute-start(bf16[1280,512]{1,0:T(8,128)(2,1)S(1)} %bitcast.178), channel_id=1, source_target_pairs={{0,4},{4,0},{8,12},{12,8},{16,20},{20,16},{24,28},{28,24},{1,5},{5... | collective-permute-start | bytes 3932168 | tf_op jit(solution)/shard_map/ppermute | solution.py:193
  70.0 33.9 %collective-permute-start.7 = (bf16[320,1280]{1,0:T(8,128)(2,1)}, bf16[320,1280]{1,0:T(8,128)(2,1)}, u32[]{:S(2)}, u32[]{:S(2)}) collective-permute-start(bf16[320,1280]{1,0:T(8,128)(2,1)} %collective-permute-done.5), channel_id=1, source_target_pairs={{0,8},{4,12},{8,0},{12,4},{16,24},{20,28},{24,16},{28,20},{1,9},{5... | collective-permute-start | bytes 2457608 | tf_op jit(solution)/shard_map/ppermute | solution.py:197
  72.7 31.4 %collective-permute-start.4 = (bf16[320,1280]{1,0:T(8,128)(2,1)}, bf16[320,1280]{1,0:T(8,128)(2,1)S(1)}, u32[]{:S(2)}, u32[]{:S(2)}) collective-permute-start(bf16[320,1280]{1,0:T(8,128)(2,1)} %collective-permute-done.3), channel_id=1, source_target_pairs={{0,1},{1,0},{2,3},{3,2},{4,5},{5,4},{6,7},{7,6},{8,9},{9,8},{10,11... | collective-permute-start | bytes 2457608 | tf_op jit(solution)/shard_map/ppermute | solution.py:207
  102.1 73.6 %collective-permute-start.39 = (bf16[4,256,640]{2,1,0:T(8,128)(2,1)}, bf16[4,256,640]{2,1,0:T(8,128)(2,1)}, u32[]{:S(2)}, u32[]{:S(2)}) collective-permute-start(bf16[4,256,640]{2,1,0:T(8,128)(2,1)} %get-tuple-element.39), channel_id=1, source_target_pairs={{0,1},{1,0},{2,3},{3,2},{4,5},{5,4},{6,7},{7,6},{8,9},{9,8},{10,11... | collective-permute-start | bytes 3932168 | tf_op jit(solution)/shard_map/ppermute | solution.py:207
  103.9 75.1 %collective-permute-start.33 = (bf16[4,256,640]{2,1,0:T(8,128)(2,1)}, bf16[4,256,640]{2,1,0:T(8,128)(2,1)}, u32[]{:S(2)}, u32[]{:S(2)}) collective-permute-start(bf16[4,256,640]{2,1,0:T(8,128)(2,1)} %get-tuple-element.37), channel_id=1, source_target_pairs={{0,1},{1,0},{2,3},{3,2},{4,5},{5,4},{6,7},{7,6},{8,9},{9,8},{10,11... | collective-permute-start | bytes 3932168 | tf_op jit(solution)/shard_map/ppermute | solution.py:207
  115.9 50.2 %collective-permute-start.47 = (bf16[2,64,640]{2,1,0:T(8,128)(2,1)S(1)}, bf16[2,64,640]{2,1,0:T(8,128)(2,1)S(1)}, u32[]{:S(2)}, u32[]{:S(2)}) collective-permute-start(bf16[2,64,640]{2,1,0:T(8,128)(2,1)S(1)} %fusion.16), channel_id=1, source_target_pairs={{0,8},{4,12},{8,0},{12,4},{16,24},{20,28},{24,16},{28,20},{1,9},{5... | collective-permute-start | bytes 491528 | tf_op jit(solution)/shard_map/ppermute | solution.py:197
  135.6 47.5 %collective-permute-start.26 = (bf16[2,1280,128]{2,1,0:T(8,128)(2,1)}, bf16[2,1280,128]{2,1,0:T(8,128)(2,1)S(1)}, u32[]{:S(2)}, u32[]{:S(2)}) collective-permute-start(bf16[2,1280,128]{2,1,0:T(8,128)(2,1)} %shard_map.146), channel_id=1, source_target_pairs={{0,1},{1,0},{2,3},{3,2},{4,5},{5,4},{6,7},{7,6},{8,9},{9,8},{10,11... | collective-permute-start | bytes 1966088 | tf_op jit(solution)/shard_map/ppermute | solution.py:207
  148.3 97.3 %collective-permute-start.18 = (bf16[2,1280,256]{2,1,0:T(8,128)(2,1)}, bf16[2,1280,256]{2,1,0:T(8,128)(2,1)S(1)}, u32[]{:S(2)}, u32[]{:S(2)}) collective-permute-start(bf16[2,1280,256]{2,1,0:T(8,128)(2,1)} %shard_map.143), channel_id=1, source_target_pairs={{0,1},{1,0},{2,3},{3,2},{4,5},{5,4},{6,7},{7,6},{8,9},{9,8},{10,11... | collective-permute-start | bytes 3932168 | tf_op jit(solution)/shard_map/ppermute | solution.py:207
  175.6 72.1 %collective-permute-start.10 = (bf16[2,1280,256]{2,1,0:T(8,128)(2,1)S(1)}, bf16[2,1280,256]{2,1,0:T(8,128)(2,1)S(1)}, u32[]{:S(2)}, u32[]{:S(2)}) collective-permute-start(bf16[2,1280,256]{2,1,0:T(8,128)(2,1)S(1)} %copy-done.14), channel_id=1, source_target_pairs={{0,1},{1,0},{2,3},{3,2},{4,5},{5,4},{6,7},{7,6},{8,9},{9,8},{10,11... | collective-permute-start | bytes 3932168 | tf_op jit(solution)/shard_map/ppermute | solution.py:207
  181.4 29.4 %collective-permute-start.34 = (bf16[4,128,640]{2,1,0:T(8,128)(2,1)S(1)}, bf16[4,128,640]{2,1,0:T(8,128)(2,1)S(1)}, u32[]{:S(2)}, u32[]{:S(2)}) collective-permute-start(bf16[4,128,640]{2,1,0:T(8,128)(2,1)S(1)} %fusion.5), channel_id=1, source_target_pairs={{0,2},{1,3},{2,0},{3,1},{4,6},{5,7},{6,4},{7,5},{8,10},{9,11},{10,... | collective-permute-start | bytes 1966088 | tf_op jit(solution)/shard_map/ppermute | solution.py:203
  184.5 32.5 %collective-permute-start.27 = (bf16[2,4,2,80,128]{4,3,2,1,0:T(8,128)(2,1)S(1)}, bf16[2,4,2,80,128]{4,3,2,1,0:T(8,128)(2,1)S(1)}, u32[]{:S(2)}, u32[]{:S(2)}) collective-permute-start(bf16[2,4,2,80,128]{4,3,2,1,0:T(8,128)(2,1)S(1)} %fusion.7), channel_id=1, source_target_pairs={{0,2},{1,3},{2,0},{3,1},{4,6},{5,7},{6,4},{7,5},{8,10},{9,11},{10,... | collective-permute-start | bytes 983048 | tf_op jit(solution)/shard_map/ppermute | solution.py:203
  219.4 21.4 %collective-permute-start.35 = (bf16[2,128,640]{2,1,0:T(8,128)(2,1)S(1)}, bf16[2,128,640]{2,1,0:T(8,128)(2,1)S(1)}, u32[]{:S(2)}, u32[]{:S(2)}) collective-permute-start(bf16[2,128,640]{2,1,0:T(8,128)(2,1)S(1)} %fusion.11), channel_id=1, source_target_pairs={{0,8},{4,12},{8,0},{12,4},{16,24},{20,28},{24,16},{28,20},{1,9},{5... | collective-permute-start | bytes 983048 | tf_op jit(solution)/shard_map/ppermute | solution.py:197
  246.1 37.5 %collective-permute-start.19 = (bf16[2,4,2,80,256]{4,3,2,1,0:T(8,128)(2,1)S(1)}, bf16[2,4,2,80,256]{4,3,2,1,0:T(8,128)(2,1)S(1)}, u32[]{:S(2)}, u32[]{:S(2)}) collective-permute-start(bf16[2,4,2,80,256]{4,3,2,1,0:T(8,128)(2,1)S(1)} %fusion.4), channel_id=1, source_target_pairs={{0,2},{1,3},{2,0},{3,1},{4,6},{5,7},{6,4},{7,5},{8,10},{9,11},{10,... | collective-permute-start | bytes 1966088 | tf_op jit(solution)/shard_map/ppermute | solution.py:203
  248.1 36.7 %collective-permute-start.11 = (bf16[2,4,2,80,256]{4,3,2,1,0:T(8,128)(2,1)S(1)}, bf16[2,4,2,80,256]{4,3,2,1,0:T(8,128)(2,1)S(1)}, u32[]{:S(2)}, u32[]{:S(2)}) collective-permute-start(bf16[2,4,2,80,256]{4,3,2,1,0:T(8,128)(2,1)S(1)} %fusion.3), channel_id=1, source_target_pairs={{0,2},{1,3},{2,0},{3,1},{4,6},{5,7},{6,4},{7,5},{8,10},{9,11},{10,... | collective-permute-start | bytes 1966088 | tf_op jit(solution)/shard_map/ppermute | solution.py:203
  248.7 31.2 %collective-permute-start.43 = (bf16[128,640]{1,0:T(8,128)(2,1)S(1)}, bf16[128,640]{1,0:T(8,128)(2,1)S(1)}, u32[]{:S(2)}, u32[]{:S(2)}) collective-permute-start(bf16[128,640]{1,0:T(8,128)(2,1)S(1)} %fusion.14), channel_id=1, source_target_pairs={{0,2},{1,3},{2,0},{3,1},{4,6},{5,7},{6,4},{7,5},{8,10},{9,11},{10,... | collective-permute-start | bytes 491528 | tf_op jit(solution)/shard_map/ppermute | solution.py:203
  252.4 29.2 %collective-permute-start.37 = (bf16[128,640]{1,0:T(8,128)(2,1)S(1)}, bf16[128,640]{1,0:T(8,128)(2,1)S(1)}, u32[]{:S(2)}, u32[]{:S(2)}) collective-permute-start(bf16[128,640]{1,0:T(8,128)(2,1)S(1)} %fusion.13), channel_id=1, source_target_pairs={{0,2},{1,3},{2,0},{3,1},{4,6},{5,7},{6,4},{7,5},{8,10},{9,11},{10,... | collective-permute-start | bytes 491528 | tf_op jit(solution)/shard_map/ppermute | solution.py:203
  253.0 28.8 %collective-permute-start.32 = (bf16[2,2,2,80,128]{4,3,2,1,0:T(8,128)(2,1)S(1)}, bf16[2,2,2,80,128]{4,3,2,1,0:T(8,128)(2,1)S(1)}, u32[]{:S(2)}, u32[]{:S(2)}) collective-permute-start(bf16[2,2,2,80,128]{4,3,2,1,0:T(8,128)(2,1)S(1)} %pad_maximum_fusion.7), channel_id=1, source_target_pairs={{0,1},{1,0},{2,3},{3,2},{4,5},{5,4},{6,7},{7,6},{8,9},{9,8},{10,11... | collective-permute-start | bytes 491528 | tf_op jit(solution)/shard_map/ppermute | solution.py:207
  (45 other events, 457.3 us)

commit v2 on v1

v2 whole, which is shorter than its diff:
```python
import functools
import math

import jax
import jax.numpy as jnp
from jax import lax
from jax.experimental import pallas as pl
from jax.experimental.pallas import tpu as pltpu
from jax.sharding import PartitionSpec as P

BF16 = jnp.bfloat16
F32 = jnp.float32
CORES = 2
CHIPS_Z = 4
LANES = 128
VMEM = 32 * 1024 * 1024


def moments(weight, first, second, grad):
    new_first = 0.9 * first + 0.1 * grad
    new_second = 0.95 * second + 0.05 * grad * grad
    update = new_first / (jnp.sqrt(new_second) + 1e-06) + 0.05 * weight
    return (new_first, new_second, update)


def squares(value):
    return jnp.sum(value * value)


def gelu(value):
    return 0.5 * value * (1.0 + lax.erf(value * (1.0 / math.sqrt(2.0))))


def gelu_slope(value):
    cdf = 0.5 * (1.0 + lax.erf(value * (1.0 / math.sqrt(2.0))))
    return cdf + value * (jnp.exp(-0.5 * value * value) * (1.0 / math.sqrt(2.0 * math.pi)))


def widths(shard):
    if shard % LANES:
        return (shard,)
    tiles = shard // LANES
    cut = []
    while tiles > 2:
        cut.append(2 * LANES)
        tiles -= 2
    return tuple(cut + [tiles * LANES])


def dot(left, right, dims):
    return lax.dot_general(left, right, (dims, ((), ())), preferred_element_type=F32)


def params():
    return dict(
        compiler_params=pltpu.CompilerParams(vmem_limit_bytes=VMEM),
        cost_estimate=pl.CostEstimate(flops=1, bytes_accessed=1, transcendentals=0),
    )


def take_columns(hidden, at, nz, nx, cuts):
    tokens, hidden_width = hidden.shape
    shard = hidden_width // (nz * nx)
    if shard % LANES:
        parts = [
            lax.dynamic_slice_in_dim(hidden, (z * nx + at) * shard, shard, 1).T for z in range(nz)
        ]
        whole = jnp.stack(parts)
        starts = [sum(cuts[:k]) for k in range(len(cuts))]
        return [whole[:, s : s + w] for s, w in zip(starts, cuts)]

    def body(at_ref, h_ref, *out_refs):
        start = 0
        for width, out_ref in zip(cuts, out_refs):
            part = h_ref[:, start : start + width]
            out_ref[0] = part.T
            start += width

    return pl.pallas_call(
        body,
        grid_spec=pltpu.PrefetchScalarGridSpec(
            num_scalar_prefetch=1,
            grid=(nz,),
            in_specs=[pl.BlockSpec((tokens, shard), lambda z, a: (0, z * nx + a[0]))],
            out_specs=[pl.BlockSpec((1, w, tokens), lambda z, a: (z, 0, 0)) for w in cuts],
        ),
        out_shape=[jax.ShapeDtypeStruct((nz, w, tokens), BF16) for w in cuts],
        **params(),
    )(jnp.reshape(at, (1,)).astype(jnp.int32), hidden)


def grad_out_chunk(hiddens, cots, core, scale):
    nz, width, tokens = hiddens[0].shape
    model = cots[0].shape[1]
    half = model // CORES
    count = len(hiddens)

    def body(c_ref, *refs):
        h_refs, cot_refs = refs[:count], refs[count : 2 * count]
        send_ref, keep_ref = refs[2 * count :]
        acts = [gelu(h[0].astype(F32)).astype(BF16) for h in h_refs]
        for out_ref, which in ((send_ref, 1 - c_ref[0]), (keep_ref, c_ref[0])):
            cols = pl.ds(pl.multiple_of(which * half, LANES), half)
            total = sum(dot(a, cot[:, cols], ((1,), (0,))) for a, cot in zip(acts, cot_refs))
            out_ref[0] = (total * scale).astype(BF16)

    return pl.pallas_call(
        body,
        grid_spec=pltpu.PrefetchScalarGridSpec(
            num_scalar_prefetch=1,
            grid=(nz,),
            in_specs=[pl.BlockSpec((1, width, tokens), lambda z, c: (z, 0, 0))] * count
            + [pl.BlockSpec((tokens, model), lambda z, c: (0, 0))] * count,
            out_specs=[pl.BlockSpec((1, width, half), lambda z, c: (z, 0, 0))] * 2,
        ),
        out_shape=[jax.ShapeDtypeStruct((nz, width, half), BF16)] * 2,
        **params(),
    )(core, *hiddens, *cots)


def grad_pre_chunk(hiddens, cots, mine, other, row, core, scale):
    nz, width, tokens = hiddens[0].shape
    part, model = mine.shape[1:]
    count = len(hiddens)

    def body(c_ref, *refs):
        h_refs, cot_refs = refs[:count], refs[count : 2 * count]
        mine_ref, other_ref = refs[2 * count : 2 * count + 2]
        out_refs, w_ref = refs[2 * count + 2 : -1], refs[-1]
        for at, ref in ((c_ref[0], mine_ref), (1 - c_ref[0], other_ref)):
            w_ref[pl.ds(pl.multiple_of(at * part, 16), part), :] = ref[0]
        w = w_ref[row : row + width, :]
        for h, cot, out_ref in zip(h_refs, cot_refs, out_refs):
            grad_act = dot(w, cot[...], ((1,), (1,))) * scale
            out_ref[0] = (grad_act * gelu_slope(h[0].astype(F32))).astype(BF16)

    return pl.pallas_call(
        body,
        grid_spec=pltpu.PrefetchScalarGridSpec(
            num_scalar_prefetch=1,
            grid=(nz,),
            in_specs=[pl.BlockSpec((1, width, tokens), lambda z, c: (z, 0, 0))] * count
            + [pl.BlockSpec((tokens, model), lambda z, c: (0, 0))] * count
            + [pl.BlockSpec((1, part, model), lambda z, c: (z, 0, 0))] * CORES,
            out_specs=[pl.BlockSpec((1, width, tokens), lambda z, c: (z, 0, 0))] * count,
            scratch_shapes=[pltpu.VMEM((CORES * part, model), BF16)],
        ),
        out_shape=[jax.ShapeDtypeStruct((nz, width, tokens), BF16)] * count,
        **params(),
    )(core, *hiddens, *cots, mine, other)


def grad_in_chunk(grads, inputs, core, scale):
    nz, width, tokens = grads[0].shape
    model = inputs[0].shape[0]
    count = len(grads)
    half = nz // CORES

    def body(c_ref, *refs):
        g_refs, in_refs = refs[:count], refs[count : 2 * count]
        send_ref, keep_ref = refs[2 * count :]
        left = jnp.concatenate([i[...] for i in in_refs], axis=1)
        right = jnp.concatenate([g[0] for g in g_refs], axis=1)
        total = (dot(left, right, ((1,), (1,))) * scale).astype(BF16)
        step = pl.program_id(0)

        @pl.when(step < half)
        def _():
            send_ref[0] = total

        @pl.when(step >= half)
        def _():
            keep_ref[0] = total

    def shard_at(step, c):
        return ((c[0] + 1 + step // half) % CORES * half + step % half, 0, 0)

    return pl.pallas_call(
        body,
        grid_spec=pltpu.PrefetchScalarGridSpec(
            num_scalar_prefetch=1,
            grid=(nz,),
            in_specs=[pl.BlockSpec((1, width, tokens), shard_at)] * count
            + [pl.BlockSpec((model, tokens), lambda z, c: (0, 0))] * count,
            out_specs=[
                pl.BlockSpec((1, model, width), lambda z, c: (jnp.minimum(z, half - 1), 0, 0)),
                pl.BlockSpec((1, model, width), lambda z, c: (jnp.maximum(z - half, 0), 0, 0)),
            ],
        ),
        out_shape=[jax.ShapeDtypeStruct((half, model, width), BF16)] * 2,
        **params(),
    )(core, *grads, *inputs)


def transposed(value):
    rows, cols = value.shape
    wide = 2 * LANES

    def body(in_ref, out_ref):
        out_ref[...] = in_ref[...].T

    return pl.pallas_call(
        body,
        grid=(cols // wide,),
        in_specs=[pl.BlockSpec((rows, wide), lambda n: (0, n))],
        out_specs=pl.BlockSpec((wide, rows), lambda n: (n, 0)),
        out_shape=jax.ShapeDtypeStruct((cols, rows), value.dtype),
        **params(),
    )(value)


def half_rows(weight, core):
    rows, cols = weight.shape
    part = rows // CORES
    wide = 2 * LANES

    def body(c_ref, in_ref, out_ref):
        out_ref[...] = in_ref[...].astype(BF16)

    return pl.pallas_call(
        body,
        grid_spec=pltpu.PrefetchScalarGridSpec(
            num_scalar_prefetch=1,
            grid=(cols // wide,),
            in_specs=[pl.BlockSpec((part, wide), lambda n, c: (c[0], n))],
            out_specs=pl.BlockSpec((part, wide), lambda n, c: (0, n)),
        ),
        out_shape=jax.ShapeDtypeStruct((part, cols), BF16),
        **params(),
    )(core, weight)


def stack(pieces, places):
    count = len(pieces)
    shape = pieces[0].shape

    def body(at_ref, *refs):
        for n in range(count):
            refs[count][at_ref[n]] = refs[n][...]

    whole = lambda at: (0,) * len(shape)
    return pl.pallas_call(
        body,
        grid_spec=pltpu.PrefetchScalarGridSpec(
            num_scalar_prefetch=1,
            grid=(),
            in_specs=[pl.BlockSpec(shape, whole)] * count,
            out_specs=pl.BlockSpec((count, *shape), lambda at: (0,) * (1 + len(shape))),
        ),
        out_shape=jax.ShapeDtypeStruct((count, *shape), pieces[0].dtype),
        **params(),
    )(places, *pieces)


def add_tiles(tiles):
    def body(*refs):
        refs[-1][...] = sum(ref[...] for ref in refs[:-1])

    return pl.pallas_call(
        body, out_shape=jax.ShapeDtypeStruct(tiles[0].shape, F32), **params()
    )(*tiles)


def reduce_step(place, keep, cross, from_y, from_z, shift, stage, ny, split):
    lead, nz, mid, _, high, wide = keep.shape
    bit = len(from_z)

    def zed(n, at):
        if stage == "y":
            return n
        if stage == "end":
            return at[2]
        low = at[2] % (1 << bit)
        mine = (at[2] // (1 << bit)) % 2
        return n * (2 << bit) + (1 - mine) * (1 << bit) + low

    count = {"y": nz, "z": nz >> (bit + 1), "end": 1}[stage]
    six = (lead, 1, mid, 1, high, wide)
    five = (lead, 1, mid, high, wide)
    specs = [pl.BlockSpec(six, lambda n, at: (0, zed(n, at), 0, (at[1] + shift) % ny, 0, 0))] * 2
    specs += [pl.BlockSpec(five, lambda n, at: (0, zed(n, at), 0, 0, 0))] * len(from_y)
    specs += [
        pl.BlockSpec(five, lambda n, at, j=j: (0, zed(n, at) // (2 << j), 0, 0, 0)) for j in range(bit)
    ]

    def body(at_ref, *refs):
        ins = refs[: len(specs)]
        outs = refs[len(specs) :]
        for p in range(lead):
            for m in range(mid):
                total = ins[0][p, 0, m, 0].astype(F32) + ins[1][p, 0, m, 0].astype(F32)
                for ref in ins[2:]:
                    total = total + ref[p, 0, m].astype(F32)
                total = total.astype(BF16)
                if not split:
                    outs[0][p, 0, m] = total
                    continue
                for s in range(mid):

                    @pl.when((at_ref[0] + s) % mid == m)
                    def _(s=s, total=total):
                        outs[s][p] = total

    if split:
        out_specs = [pl.BlockSpec((lead, high, wide), lambda n, at: (0, 0, 0))] * mid
        out_shape = [jax.ShapeDtypeStruct((lead, high, wide), BF16)] * mid
    else:
        out_specs = [pl.BlockSpec(five, lambda n, at: (0, n, 0, 0, 0))]
        out_shape = [jax.ShapeDtypeStruct((lead, count, mid, high, wide), BF16)]
    out = pl.pallas_call(
        body,
        grid_spec=pltpu.PrefetchScalarGridSpec(
            num_scalar_prefetch=1, grid=(count,), in_specs=specs, out_specs=out_specs
        ),
        out_shape=out_shape,
        **params(),
    )(place, keep, cross, *from_y, *from_z)
    return out if split else out[0]


def moments_kernel(core, weight, first, second, mine, other, grid, state_spec, grad_specs, owner, axis):
    block = state_spec.block_shape
    count = len(mine)

    def body(c_ref, w_ref, m_ref, v_ref, *refs):
        mine_refs, other_refs = refs[:count], refs[count : 2 * count]
        new_m_ref, new_v_ref, u_ref, sum_ref = refs[2 * count :]
        totals = [jnp.zeros((8, LANES), F32)] * 2
        start = 0
        ours = owner(pl.program_id(0)) == c_ref[0]
        for mine_ref, other_ref in zip(mine_refs, other_refs):
            size = mine_ref.size // block[1 - axis]
            shape = (size, block[1]) if axis == 0 else (block[0], size)
            at = (slice(start, start + size), slice(None))
            at = at if axis == 0 else at[::-1]
            grad = jnp.where(ours, mine_ref[...].reshape(shape), other_ref[...].reshape(shape)).astype(F32)
            weight = w_ref[at]
            new_m, new_v, update = moments(weight, m_ref[at], v_ref[at], grad)
            new_m_ref[at] = new_m
            new_v_ref[at] = new_v
            u_ref[at] = update
            for n, value in enumerate((weight, update)):
                square = value * value
                for col in range(0, shape[1], LANES):
                    totals[n] = totals[n] + square[:, col : col + LANES].reshape(-1, 8, LANES).sum(0)
            start += size

        @pl.when(pl.program_id(0) == 0)
        def _():
            sum_ref[...] = jnp.zeros_like(sum_ref)

        sum_ref[:8] += totals[0]
        sum_ref[8:] += totals[1]

    state = jax.ShapeDtypeStruct(weight.shape, F32)
    return pl.pallas_call(
        body,
        grid_spec=pltpu.PrefetchScalarGridSpec(
            num_scalar_prefetch=1,
            grid=grid,
            in_specs=[state_spec] * 3 + grad_specs * 2,
            out_specs=[state_spec] * 3 + [pl.BlockSpec((16, LANES), lambda n, c: (0, 0))],
        ),
        out_shape=[state] * 3 + [jax.ShapeDtypeStruct((16, LANES), F32)],
        **params(),
    )(core, weight, first, second, *mine, *other)


def step_weights(weight, update, tiles):
    rows, cols = weight.shape
    high = rows // 5
    count = len(tiles)

    def body(w_ref, u_ref, *refs):
        sums = sum(ref[...] for ref in refs[:count])
        ratio = jnp.sqrt(jnp.sum(sums[:8], keepdims=True)) / jnp.sqrt(jnp.sum(sums[8:], keepdims=True))
        refs[count][...] = w_ref[...] - 0.4 * ratio * u_ref[...]

    spec = pl.BlockSpec((high, cols), lambda n: (n, 0))
    tile = pl.BlockSpec((16, LANES), lambda n: (0, 0))
    return pl.pallas_call(
        body,
        grid=(rows // high,),
        in_specs=[spec] * 2 + [tile] * count,
        out_specs=spec,
        out_shape=jax.ShapeDtypeStruct(weight.shape, F32),
        **params(),
    )(weight, update, *tiles)


class Order:
    def __init__(self):
        self.last = None

    def after(self, *values):
        if self.last is None:
            return values
        return lax.optimization_barrier((*values, self.last))[:-1]

    def did(self, value):
        self.last = value


def plan(nz, nx, ny):
    def along_x(value, step):
        pairs = [
            (z * nx + x, z * nx + (x + step) % nx) for z in range(nz) for x in range(nx)
        ]
        return lax.ppermute(value, "gx", pairs)

    def along_z(value, flip):
        pairs = [(z * nx + x, (z ^ flip) * nx + x) for z in range(nz) for x in range(nx)]
        return lax.ppermute(value, "gx", pairs)

    def along_y(value, step):
        pairs = [
            (y * CORES + c, (y + step) % ny * CORES + c) for y in range(ny) for c in range(CORES)
        ]
        return lax.ppermute(value, "gy", pairs)

    def across(value):
        pairs = [(k, k ^ 1) for k in range(ny * CORES)]
        return lax.ppermute(value, "gy", pairs)

    class Reduce:
        def __init__(self, order, at, send, keep, shape):
            self.order, self.at, self.place = order, at, jnp.stack(at).astype(jnp.int32)
            self.keep = keep.reshape(shape)
            self.cross = across(send).reshape(shape)
            self.from_y = []
            self.from_z = []

        def step(self, shift, stage, split=False):
            count = len(self.from_y)
            got = self.order.after(self.keep, self.cross, *self.from_y, *self.from_z)
            out = reduce_step(
                self.place, got[0], got[1], got[2 : 2 + count], got[2 + count :], shift, stage, ny, split
            )
            self.order.did(out[0] if split else out)
            return out

        def send_y(self):
            from_y = []
            for s in range(1, ny):
                from_y.append(along_y(self.step(s, "y"), s))
            self.from_y = from_y

        def send_z(self):
            bit = len(self.from_z)
            self.from_z.append(along_z(self.step(0, "z"), 1 << bit))

        def finish(self):
            out = self.step(0, "end", True)
            self.held = [out[0]] + [along_x(out[s], s) for s in range(1, len(out))]
            if len(out) == 1:
                self.share_y(out[0])

        def share_y(self, value):
            self.held = [value] + [along_y(value, s) for s in range(1, ny)]

        def stacked(self, place, size):
            places = jnp.stack([(place - s) % size for s in range(size)]).astype(jnp.int32)
            value = stack(self.order.after(*self.held), places)
            self.order.did(value)
            return value

        def stack_x(self):
            self.share_y(self.stacked(self.at[0], nx))

        def stack_y(self):
            value = self.stacked(self.at[1], ny)
            self.held = [value, across(value)]

    def local(inputs, hidden_pre, cotangent, w_in, m_in, v_in, w_out, m_out, v_out):
        model = inputs.shape[1]
        hidden_width = hidden_pre.shape[1]
        shard = hidden_width // (nz * nx)
        rows = model // (nz * nx)
        cuts = widths(shard)
        chunks = range(len(cuts))
        last = len(cuts) - 1
        starts = [sum(cuts[:k]) for k in chunks]
        scale_in = 1.0 / math.sqrt(model)
        scale_out = 1.0 / math.sqrt(hidden_width)
        place = lax.axis_index("gx")
        side = lax.axis_index("gy")
        z, x = place // nx, place % nx
        y, c = side // CORES, side % CORES
        core = jnp.reshape(c, (1,)).astype(jnp.int32)
        order = Order()
        hops = nz.bit_length() - 1

        cots = [cotangent] + [along_x(cotangent, s) for s in range(1, nx)]
        hiddens = [[] for _ in chunks]
        sends = []
        for s in range(1, nx):
            sends.append(take_columns(*order.after(hidden_pre), (x + s) % nx, nz, nx, cuts))
            order.did(sends[-1][0])
        late = last if last > 1 else last + 1
        for k in range(late):
            hiddens[k] = [along_x(sends[s - 1][k], s) for s in range(1, nx)]

        part = half_rows(*order.after(w_out), core)
        order.did(part)
        found = {0: part}
        bit = nz // 2
        while bit:
            for key in list(found):
                found[key ^ bit] = along_z(found[key], bit)
            bit //= 2

        flipped = transposed(*order.after(inputs))
        order.did(flipped)
        own = take_columns(*order.after(hidden_pre), x, nz, nx, cuts)
        order.did(own[0])
        came = cots[1:] + hiddens[0]
        tied = lax.optimization_barrier((flipped, *[value[k] for value in sends for k in chunks], *came))
        for k in range(late, len(cuts)):
            hiddens[k] = [along_x(tied[1 + (s - 1) * len(cuts) + k], s) for s in range(1, nx)]
        columns = [flipped] + [along_x(tied[0], s) for s in range(1, nx)]
        hiddens = [[own[k]] + hiddens[k] for k in chunks]

        outs = [None for _ in chunks]
        ins = [None for _ in chunks]
        pres = [None for _ in chunks]

        def stack_weights():
            places = jnp.stack([z ^ key for key in range(nz)]).astype(jnp.int32)
            mine = stack(order.after(*[found[key] for key in range(nz)]), places)
            order.did(mine)
            return [mine, across(mine)]

        def start_out(k):
            got = order.after(*hiddens[k], *cots)
            send, keep = grad_out_chunk(got[:nx], got[nx:], core, scale_out)
            order.did(keep)
            outs[k] = Reduce(
                order, (x, y, z), send, keep, (1, nz, 1, ny, cuts[k] // ny, model // CORES)
            )

        def start_pre(k):
            got = order.after(*hiddens[k], *cots, *weights)
            pres[k] = grad_pre_chunk(got[:nx], got[nx : 2 * nx], got[-2], got[-1], starts[k], core, scale_out)
            order.did(pres[k][0])

        def start_in(k):
            got = order.after(*pres[k], *columns)
            send, keep = grad_in_chunk(got[:nx], got[nx:], core, scale_in)
            order.did(keep)
            ins[k] = Reduce(
                order, (x, y, z), send, keep, (nz // CORES, nz, nx, ny, rows // ny, cuts[k])
            )

        def sums(tile):
            tiles = order.after(*([tile] + [along_z(tile, flip) for flip in range(1, nz)]))
            tile = add_tiles(tiles)
            order.did(tile)
            return [tile] + [along_x(tile, s) for s in range(1, nx)]

        def new_weights(weight, update, tiles):
            got = order.after(weight, update, *tiles)
            value = step_weights(got[0], got[1], got[2:])
            order.did(value)
            return value

        for k in chunks:
            start_out(k)
            if k == 0:
                weights = stack_weights()
            if k > 0:
                outs[k - 1].send_z()
            outs[k].send_y()
            start_pre(k)
            if k > 0:
                outs[k - 1].send_z()
        for k in chunks[:-1]:
            outs[k].finish()
        outs[last].send_z()

        for k in chunks:
            start_in(k)
            ins[k].send_y()
            if k == 0:
                outs[last].send_z()
            elif k == 1:
                outs[last].finish()
        if last == 0:
            outs[last].finish()
        for k in chunks:
            outs[k].stack_y()
        ins[0].send_z()

        half = model // CORES
        got = order.after(
            w_out, m_out, v_out, *[outs[k].held[0] for k in chunks], *[outs[k].held[1] for k in chunks]
        )
        first_out, second_out, update_out, tile = moments_kernel(
            core,
            *got[:3],
            got[3 : 4 + last],
            got[4 + last :],
            (CORES,),
            pl.BlockSpec((shard, half), lambda n, c: (0, n)),
            [pl.BlockSpec((ny, 1, w // ny, half), lambda n, c: (0, 0, 0, 0)) for w in cuts],
            lambda n: n,
            0,
        )
        order.did(tile)
        for _ in range(hops - 1):
            ins[0].send_z()
        tiles = sums(tile)
        ins[0].finish()
        for k in range(1, len(cuts)):
            ins[k].send_z()
            ins[k - 1].stack_x()
            for _ in range(hops - 1):
                ins[k].send_z()
            ins[k - 1].stack_y()
            if k == 1:
                new_w_out = new_weights(w_out, update_out, tiles)
            ins[k].finish()
        if last == 0:
            new_w_out = new_weights(w_out, update_out, tiles)
        ins[last].stack_x()
        ins[last].stack_y()

        got = order.after(
            w_in, m_in, v_in, *[ins[k].held[0] for k in chunks], *[ins[k].held[1] for k in chunks]
        )
        mine, other = got[3 : 4 + last], got[4 + last :]
        if shard % LANES:
            joined = [
                jnp.stack([jnp.where(c == 0, a, b), jnp.where(c == 0, b, a)]) for a, b in zip(mine, other)
            ]
            grad = jnp.concatenate(joined, axis=-1).transpose(1, 4, 0, 3, 2, 5)
            grad = grad.reshape(rows, hidden_width).astype(F32)
            first_in, second_in, update_in = moments(*got[:3], grad)
            tile = jnp.concatenate(
                [
                    jnp.sum((value * value).reshape(-1, 8, LANES), axis=0)
                    for value in (w_in, update_in)
                ]
            )
        else:
            zs = nz // CORES
            first_in, second_in, update_in, tile = moments_kernel(
                core,
                *got[:3],
                mine,
                other,
                (nz * nx,),
                pl.BlockSpec((rows, shard), lambda n, c: (0, n)),
                [
                    pl.BlockSpec(
                        (ny, 1, 1, rows // ny, w), lambda n, c: (0, n % nx, n // nx % zs, 0, 0)
                    )
                    for w in cuts
                ],
                lambda n: n // nx // zs,
                1,
            )
        order.did(tile)
        new_w_in = new_weights(w_in, update_in, sums(tile))
        return (new_w_in, first_in, second_in, new_w_out, first_out, second_out)

    return local


def solution(mesh):
    gx, gy = mesh.shape["gx"], mesh.shape["gy"]
    nz = CHIPS_Z
    state = P("gx", None)
    tokens = P(("gx", "gy"), None)
    return jax.shard_map(
        plan(nz, gx // nz, gy // CORES),
        mesh=mesh,
        in_specs=(tokens,) * 3 + (state,) * 6,
        out_specs=(state,) * 6,
        check_vma=False,
    )
```

time: 390 us -> 344 us (0.88)
  other arithmetic: 48.2 us -> 0.3 us
  waiting for transfers between devices: 176 us -> 144 us
  Pallas kernels: 79.1 us -> 111 us
  blocking collectives: 19.7 us -> 0 us
  local copies, waits for them, and re-layouts: 17.1 us -> 30.7 us
  starting transfers between devices: 44.5 us -> 55.1 us
    pallas_call x6 -> x45, Pallas kernels: 26.9 us -> 77.6 us  [the longest x24 37.2 us: reduce_step(): pl.pallas_call(body, grid_spec=pltpu.PrefetchScalarGridSpec(num_scalar_pr...]
    ppermute x8 -> x10, waiting for transfers between devices: 55.7 us -> 27.8 us  [along_x(): return lax.ppermute(value, 'gx', pairs)]
    unnamed x37 -> x106, local copies, waits for them, and re-layouts: 4.07 us -> 30.7 us
    ppermute x12, waiting for transfers between devices: 72.6 us -> 46.5 us  [along_y(): return lax.ppermute(value, 'gy', pairs)]
    reduce_sum x2 -> x0, other arithmetic: 20.8 us -> none  [squares(): return jnp.sum(value * value)]
    psum x1 -> x0, blocking collectives: 19.7 us -> none  [local(): lax.psum((squares(w_in), squares(w_out), squares(update_in), squares(upda...]
    convert_element_type x21 -> x0, local copies, waits for them, and re-layouts: 13 us -> none  [the longest x2 9.79 us: local(): joined.transpose(1, 4, 0, 3, 2, 5).reshape(rows, hidden_width).astype(F32)]
    ppermute x15 -> x21, waiting for transfers between devices: 45 us -> 55.9 us  [along_z(): return lax.ppermute(value, 'gx', pairs)]
  transfers between devices with their start and end apart: 51 -> 56, of which waited for: 23 -> 33; matrix products, arithmetic and copies ran while one was open for 8% -> 0% of each run, Pallas kernels for 20% -> 22%
where the time goes in v2:
time: 344 us; the launch traced here: 343 us
  waiting for transfers between devices  144 us (42%)
  Pallas kernels  111 us (32%)
  starting transfers between devices  55.1 us (16%)
  local copies, waits for them, and re-layouts  30.7 us (9%)
    ppermute x21, waiting for transfers between devices, along_z(): return lax.ppermute(value, 'gx', pairs)  55.9 us
    ppermute x12, waiting for transfers between devices, along_y(): return lax.ppermute(value, 'gy', pairs)  46.5 us
    pallas_call x24, Pallas kernels, reduce_step(): pl.pallas_call(body, grid_spec=pltpu.PrefetchScalarGridSpec(num_scalar_pr...  37.2 us
    unnamed x106, local copies, waits for them, and re-layouts  30.7 us
    ppermute x10, waiting for transfers between devices, along_x(): return lax.ppermute(value, 'gx', pairs)  27.8 us
    ppermute x21, starting transfers between devices, along_z(): return lax.ppermute(value, 'gx', pairs)  25.5 us
    pallas_call x3, Pallas kernels, grad_pre_chunk(): pl.pallas_call(body, grid_spec=pltpu.PrefetchScalarGridSpec(num_scalar_pr...  17.4 us
    ppermute x12, starting transfers between devices, along_y(): return lax.ppermute(value, 'gy', pairs)  16.1 us
  transfers between devices with their start and end apart: 56, of which 33 were waited for; matrix products, arithmetic and copies ran while one was open for 0% of the time, Pallas kernels for 22%

profile of v2, /device:TPU:0, one launch (start us, length us, event | category | flops | bytes accessed | tf_op | source)
XLA Modules:
  0.0 342.6 jit_solution(14183389092397798060)
XLA Ops:
  9.6 4.1 %collective-permute-start.3 = (bf16[320,1280]{1,0:T(8,128)(2,1)S(1)}, bf16[320,1280]{1,0:T(8,128)(2,1)}, u32[]{:S(2)}, u32[]{:S(2)}) collective-permute-start(bf16[320,1280]{1,0:T(8,128)(2,1)S(1)} %shard_map.137.refs_0_), channel_id=1, source_target_pairs={{0,16},{4,20},{8,24},{12,28},{16,0},{20,4},{24,8},{28,12},{1,17},{... | collective-permute-start | bytes 2457608 | tf_op jit(solution)/shard_map/ppermute | solution.py:413
  17.3 32.4 %collective-permute-done.3.refs_2_ = bf16[320,1280]{1,0:T(8,128)(2,1)} collective-permute-done((bf16[320,1280]{1,0:T(8,128)(2,1)S(1)}, bf16[320,1280]{1,0:T(8,128)(2,1)}, u32[]{:S(2)}, u32[]{:S(2)}) %collective-permute-start.3) | collective-permute-done | bytes 819232 | tf_op jit(solution)/shard_map/ppermute | solution.py:413
  57.6 8.9 %collective-permute-done.refs_1_ = bf16[4,256,512]{2,1,0:T(8,128)(2,1)} collective-permute-done((bf16[4,256,512]{2,1,0:T(8,128)(2,1)}, bf16[4,256,512]{2,1,0:T(8,128)(2,1)}, u32[]{:S(2)}, u32[]{:S(2)}) %collective-permute-start) | collective-permute-done | bytes 1048608 | tf_op jit(solution)/shard_map/ppermute | solution.py:409
  68.2 5.4 %shard_map.140 = (bf16[4,256,640]{2,1,0:T(8,128)(2,1)}, bf16[4,256,640]{2,1,0:T(8,128)(2,1)S(1)}) custom-call(s32[1]{0:T(128)} %bitcast.c_ref, bf16[4,256,512]{2,1,0:T(8,128)(2,1)S(1)} %copy-done.35, bf16[4,256,512]{2,1,0:T(8,128)(2,1)} %collective-permute-done.refs_1_, bf16[512,1280]{1,0:T(8,128)(2,1)S(1)} %copy-done, ...), custom_call_target="tpu_custom_call" | custom-call | flops 1 | bytes 1 | tf_op jit(solution)/shard_map/pallas_call | solution.py:107
  79.3 5.6 %collective-permute-done.6 = bf16[4,256,640]{2,1,0:T(8,128)(2,1)} collective-permute-done((bf16[4,256,640]{2,1,0:T(8,128)(2,1)}, bf16[4,256,640]{2,1,0:T(8,128)(2,1)}, u32[]{:S(2)}, u32[]{:S(2)}) %collective-permute-start.6) | collective-permute-done | bytes 1310752 | tf_op jit(solution)/shard_map/ppermute | solution.py:423
  90.2 5.9 %shard_map.143 = (bf16[4,256,512]{2,1,0:T(8,128)(2,1)S(1)}, bf16[4,256,512]{2,1,0:T(8,128)(2,1)S(1)}) custom-call(s32[1]{0:T(128)} %bitcast.c_ref, bf16[4,256,512]{2,1,0:T(8,128)(2,1)S(1)} %copy-done.36, bf16[4,256,512]{2,1,0:T(8,128)(2,1)} %collective-permute-done.refs_1_, bf16[512,1280]{1,0:T(8,128)(2,1)S(1)} %copy-done.1, ...), custom_call_target="tpu_custom_call" | custom-call | flops 1 | bytes 1 | tf_op jit(solution)/shard_map/pallas_call | solution.py:137
  96.1 7.0 %collective-permute-done.10.refs_1_ = bf16[4,256,512]{2,1,0:T(8,128)(2,1)} collective-permute-done((bf16[4,256,512]{2,1,0:T(8,128)(2,1)}, bf16[4,256,512]{2,1,0:T(8,128)(2,1)}, u32[]{:S(2)}, u32[]{:S(2)}) %collective-permute-start.10) | collective-permute-done | bytes 1048608 | tf_op jit(solution)/shard_map/ppermute | solution.py:409
  103.2 5.2 %shard_map.144 = (bf16[4,256,640]{2,1,0:T(8,128)(2,1)S(1)}, bf16[4,256,640]{2,1,0:T(8,128)(2,1)S(1)}) custom-call(s32[1]{0:T(128)} %bitcast.c_ref, bf16[4,256,512]{2,1,0:T(8,128)(2,1)S(1)} %copy-done.33, bf16[4,256,512]{2,1,0:T(8,128)(2,1)} %collective-permute-done.10.refs_1_, bf16[512,1280]{1,0:T(8,128)(2,1)S(1)} %copy-done.1, bf16[512,1280]{1,0:T(8,128)(2,1)S(1)} %copy-done.3), custom_call_target="tpu_custom_call" | custom-call | flops 1 | bytes 1 | tf_op jit(solution)/shard_map/pallas_call | solution.py:107
  111.5 14.1 %collective-permute-done.9.refs_2_ = bf16[1,4,1,128,640]{4,3,2,1,0:T(8,128)(2,1)S(1)} collective-permute-done((bf16[1,4,1,128,640]{4,3,2,1,0:T(8,128)(2,1)S(1)}, bf16[1,4,1,128,640]{4,3,2,1,0:T(8,128)(2,1)S(1)}, u32[]{:S(2)}, u32[]{:S(2)}) %collective-permute-start.9) | collective-permute-done | bytes 655392 | tf_op jit(solution)/shard_map/ppermute | solution.py:419
  132.8 5.9 %shard_map.147 = (bf16[4,256,512]{2,1,0:T(8,128)(2,1)S(1)}, bf16[4,256,512]{2,1,0:T(8,128)(2,1)S(1)}) custom-call(s32[1]{0:T(128)} %bitcast.c_ref, bf16[4,256,512]{2,1,0:T(8,128)(2,1)S(1)} %copy-done.33, bf16[4,256,512]{2,1,0:T(8,128)(2,1)} %collective-permute-done.10.refs_1_, bf16[512,1280]{1,0:T(8,128)(2,1)S(1)} %copy-done.1, ...), custom_call_target="tpu_custom_call" | custom-call | flops 1 | bytes 1 | tf_op jit(solution)/shard_map/pallas_call | solution.py:137
  142.9 4.1 %collective-permute-done.14.refs_2_ = bf16[1,4,1,128,640]{4,3,2,1,0:T(8,128)(2,1)S(1)} collective-permute-done((bf16[1,4,1,128,640]{4,3,2,1,0:T(8,128)(2,1)S(1)}, bf16[1,4,1,128,640]{4,3,2,1,0:T(8,128)(2,1)S(1)}, u32[]{:S(2)}, u32[]{:S(2)}) %collective-permute-start.14) | collective-permute-done | bytes 655392 | tf_op jit(solution)/shard_map/ppermute | solution.py:419
  150.9 5.6 %shard_map.152 = (bf16[4,128,512]{2,1,0:T(8,128)(2,1)S(1)}, bf16[4,128,512]{2,1,0:T(8,128)(2,1)S(1)}) custom-call(s32[1]{0:T(128)} %bitcast.c_ref, bf16[4,128,512]{2,1,0:T(8,128)(2,1)S(1)} %copy-done.46, bf16[4,128,512]{2,1,0:T(8,128)(2,1)S(1)} %collective-permute-done.8.refs_1_, bf16[512,1280]{1,0:T(8,128)(2,1)S(1)} %copy-done.1, ...), custom_call_target="tpu_custom_call" | custom-call | flops 1 | bytes 1 | tf_op jit(solution)/shard_map/pallas_call | solution.py:137
  162.6 4.0 %collective-permute-done.17.refs_4_ = bf16[1,1,1,128,640]{4,3,2,1,0:T(8,128)(2,1)S(1)} collective-permute-done((bf16[1,1,1,128,640]{4,3,2,1,0:T(8,128)(2,1)S(1)}, bf16[1,1,1,128,640]{4,3,2,1,0:T(8,128)(2,1)S(1)}, u32[]{:S(2)}, u32[]{:S(2)}) %collective-permute-start.17) | collective-permute-done | bytes 163872 | tf_op jit(solution)/shard_map/ppermute | solution.py:413
  168.6 4.0 %shard_map.157 = (bf16[2,1280,256]{2,1,0:T(8,128)(2,1)S(1)}, bf16[2,1280,256]{2,1,0:T(8,128)(2,1)S(1)}) custom-call(s32[1]{0:T(128)} %bitcast.c_ref, bf16[4,256,512]{2,1,0:T(8,128)(2,1)S(1)} %get-tuple-element.319.refs_0_, bf16[4,256,512]{2,1,0:T(8,128)(2,1)S(1)} %get-tuple-element.320.refs_1_, bf16[1280,512]{1,0:T(8,128)(2,1)S(1)} %copy-done.16, ...), custom_call_target="tpu_custom_call" | custom-call | flops 1 | bytes 1 | tf_op jit(solution)/shard_map/pallas_call | solution.py:178
  180.0 4.0 %shard_map.160 = (bf16[2,1280,256]{2,1,0:T(8,128)(2,1)S(1)}, bf16[2,1280,256]{2,1,0:T(8,128)(2,1)S(1)}) custom-call(s32[1]{0:T(128)} %bitcast.c_ref, bf16[4,256,512]{2,1,0:T(8,128)(2,1)S(1)} %get-tuple-element.332.refs_0_, bf16[4,256,512]{2,1,0:T(8,128)(2,1)S(1)} %get-tuple-element.333.refs_1_, bf16[1280,512]{1,0:T(8,128)(2,1)S(1)} %copy-done.16, ...), custom_call_target="tpu_custom_call" | custom-call | flops 1 | bytes 1 | tf_op jit(solution)/shard_map/pallas_call | solution.py:178
  192.0 3.9 %shard_map.163 = (bf16[2,1280,128]{2,1,0:T(8,128)(2,1)S(1)}, bf16[2,1280,128]{2,1,0:T(8,128)(2,1)S(1)}) custom-call(s32[1]{0:T(128)} %bitcast.c_ref, bf16[4,128,512]{2,1,0:T(8,128)(2,1)S(1)} %get-tuple-element.346.refs_0_, bf16[4,128,512]{2,1,0:T(8,128)(2,1)S(1)} %get-tuple-element.347.refs_1_, bf16[1280,512]{1,0:T(8,128)(2,1)S(1)} %copy-done.16, ...), custom_call_target="tpu_custom_call" | custom-call | flops 1 | bytes 1 | tf_op jit(solution)/shard_map/pallas_call | solution.py:178
  207.6 10.5 %collective-permute-done.26.refs_1_ = bf16[1,128,640]{2,1,0:T(8,128)(2,1)} collective-permute-done((bf16[1,128,640]{2,1,0:T(8,128)(2,1)S(1)}, bf16[1,128,640]{2,1,0:T(8,128)(2,1)}, u32[]{:S(2)}, u32[]{:S(2)}) %collective-permute-start.26) | collective-permute-done | bytes 163872 | tf_op jit(solution)/shard_map/ppermute | solution.py:419
  223.8 13.1 %collective-permute-done.24.refs_1_ = bf16[1,64,640]{2,1,0:T(8,128)(2,1)S(1)} collective-permute-done((bf16[1,64,640]{2,1,0:T(8,128)(2,1)S(1)}, bf16[1,64,640]{2,1,0:T(8,128)(2,1)S(1)}, u32[]{:S(2)}, u32[]{:S(2)}) %collective-permute-start.24) | collective-permute-done | bytes 81952 | tf_op jit(solution)/shard_map/ppermute | solution.py:419
  245.6 5.3 %shard_map.169 = (f32[640,1280]{1,0:T(8,128)}, f32[640,1280]{1,0:T(8,128)}, f32[640,1280]{1,0:T(8,128)S(1)}, f32[16,128]{1,0:T(8,128)S(1)}) custom-call(s32[1]{0:T(128)} %bitcast.c_ref, f32[640,1280]{1,0:T(8,128)S(1)} %copy-done.5, f32[640,1280]{1,0:T(8,128)S(1)} %copy-done.37, f32[640,1280]{1,0:T(8,128)S(1)} %copy-done.38, ...), custom_call_target="tpu_custom_call" | custom-call | flops 1 | bytes 1 | tf_op jit(solution)/shard_map/pallas_call | solution.py:356
  272.8 3.8 %collective-permute-done.36.refs_1_ = bf16[2,80,256]{2,1,0:T(8,128)(2,1)S(1)} collective-permute-done((bf16[2,80,256]{2,1,0:T(8,128)(2,1)S(1)}, bf16[2,80,256]{2,1,0:T(8,128)(2,1)S(1)}, u32[]{:S(2)}, u32[]{:S(2)}) %collective-permute-start.36) | collective-permute-done | bytes 81952 | tf_op jit(solution)/shard_map/ppermute | solution.py:409
  288.6 3.2 shard_map.177
  306.3 3.7 %collective-permute-done.46.refs_4_ = bf16[2,1,2,80,128]{4,3,2,1,0:T(8,128)(2,1)S(1)} collective-permute-done((bf16[2,1,2,80,128]{4,3,2,1,0:T(8,128)(2,1)S(1)}, bf16[2,1,2,80,128]{4,3,2,1,0:T(8,128)(2,1)S(1)}, u32[]{:S(2)}, u32[]{:S(2)}) %collective-permute-start.46) | collective-permute-done | bytes 81952 | tf_op jit(solution)/shard_map/ppermute | solution.py:413
  322.8 6.2 %shard_map.186 = (f32[160,5120]{1,0:T(8,128)}, f32[160,5120]{1,0:T(8,128)}, f32[160,5120]{1,0:T(8,128)S(1)}, f32[16,128]{1,0:T(8,128)S(1)}) custom-call(s32[1]{0:T(128)} %bitcast.c_ref, f32[160,5120]{1,0:T(8,128)S(1)} %copy-done.25, f32[160,5120]{1,0:T(8,128)S(1)} %copy-done.39, f32[160,5120]{1,0:T(8,128)S(1)} %copy-done.40, ...), custom_call_target="tpu_custom_call" | custom-call | flops 1 | bytes 1 | tf_op jit(solution)/shard_map/pallas_call | solution.py:356
  339.3 3.2 shard_map.188
  (251 shorter events, 171.9 us)
Async XLA Ops:
  9.6 40.1 %collective-permute-start.3 = (bf16[320,1280]{1,0:T(8,128)(2,1)S(1)}, bf16[320,1280]{1,0:T(8,128)(2,1)}, u32[]{:S(2)}, u32[]{:S(2)}) collective-permute-start(bf16[320,1280]{1,0:T(8,128)(2,1)S(1)} %shard_map.137.refs_0_), channel_id=1, source_target_pairs={{0,16},{4,20},{8,24},{12,28},{16,0},{20,4},{24,8},{28,12},{1,17},{... | collective-permute-start | bytes 2457608 | tf_op jit(solution)/shard_map/ppermute | solution.py:413
  13.7 52.8 %collective-permute-start.1 = (bf16[512,1280]{1,0:T(8,128)(2,1)S(1)}, bf16[512,1280]{1,0:T(8,128)(2,1)S(1)}, u32[]{:S(2)}, u32[]{:S(2)}) collective-permute-start(bf16[512,1280]{1,0:T(8,128)(2,1)S(1)} %copy-done), channel_id=1, source_target_pairs={{0,4},{4,0},{8,12},{12,8},{16,20},{20,16},{24,28},{28,24},{1,5},{5... | collective-permute-start | bytes 3932168 | tf_op jit(solution)/shard_map/ppermute | solution.py:409
  15.2 51.3 %collective-permute-start = (bf16[4,256,512]{2,1,0:T(8,128)(2,1)}, bf16[4,256,512]{2,1,0:T(8,128)(2,1)}, u32[]{:S(2)}, u32[]{:S(2)}) collective-permute-start(bf16[4,256,512]{2,1,0:T(8,128)(2,1)} %copy-done.48), channel_id=1, source_target_pairs={{0,4},{4,0},{8,12},{12,8},{16,20},{20,16},{24,28},{28,24},{1,5},{5... | collective-permute-start | bytes 3145736 | tf_op jit(solution)/shard_map/ppermute | solution.py:409
  15.7 59.0 %collective-permute-start.2 = (bf16[320,1280]{1,0:T(8,128)(2,1)S(1)}, bf16[320,1280]{1,0:T(8,128)(2,1)}, u32[]{:S(2)}, u32[]{:S(2)}) collective-permute-start(bf16[320,1280]{1,0:T(8,128)(2,1)S(1)} %shard_map.137.refs_0_), channel_id=1, source_target_pairs={{0,8},{4,12},{8,0},{12,4},{16,24},{20,28},{24,16},{28,20},{1,9},{5... | collective-permute-start | bytes 2457608 | tf_op jit(solution)/shard_map/ppermute | solution.py:413
  49.7 25.0 %collective-permute-start.4 = (bf16[320,1280]{1,0:T(8,128)(2,1)}, bf16[320,1280]{1,0:T(8,128)(2,1)}, u32[]{:S(2)}, u32[]{:S(2)}) collective-permute-start(bf16[320,1280]{1,0:T(8,128)(2,1)} %collective-permute-done.3.refs_2_), channel_id=1, source_target_pairs={{0,8},{4,12},{8,0},{12,4},{16,24},{20,28},{24,16},{28,20},{1,9},{5... | collective-permute-start | bytes 2457608 | tf_op jit(solution)/shard_map/ppermute | solution.py:413
  77.1 11.7 %collective-permute-start.5 = (bf16[4,320,1280]{2,1,0:T(8,128)(2,1)S(1)}, bf16[4,320,1280]{2,1,0:T(8,128)(2,1)}, u32[]{:S(2)}, u32[]{:S(2)}) collective-permute-start(bf16[4,320,1280]{2,1,0:T(8,128)(2,1)S(1)} %shard_map.141.refs_4_), channel_id=1, source_target_pairs={{0,1},{1,0},{2,3},{3,2},{4,5},{5,4},{6,7},{7,6},{8,9},{9,8},{10,11... | collective-permute-start | bytes 9830408 | tf_op jit(solution)/shard_map/ppermute | solution.py:423
  77.7 25.5 %collective-permute-start.10 = (bf16[4,256,512]{2,1,0:T(8,128)(2,1)}, bf16[4,256,512]{2,1,0:T(8,128)(2,1)}, u32[]{:S(2)}, u32[]{:S(2)}) collective-permute-start(bf16[4,256,512]{2,1,0:T(8,128)(2,1)} %get-tuple-element.256), channel_id=1, source_target_pairs={{0,4},{4,0},{8,12},{12,8},{16,20},{20,16},{24,28},{28,24},{1,5},{5... | collective-permute-start | bytes 3145736 | tf_op jit(solution)/shard_map/ppermute | solution.py:409
  108.3 22.0 %collective-permute-start.12 = (bf16[4,256,640]{2,1,0:T(8,128)(2,1)S(1)}, bf16[4,256,640]{2,1,0:T(8,128)(2,1)S(1)}, u32[]{:S(2)}, u32[]{:S(2)}) collective-permute-start(bf16[4,256,640]{2,1,0:T(8,128)(2,1)S(1)} %get-tuple-element.270), channel_id=1, source_target_pairs={{0,1},{1,0},{2,3},{3,2},{4,5},{5,4},{6,7},{7,6},{8,9},{9,8},{10,11... | collective-permute-start | bytes 3932168 | tf_op jit(solution)/shard_map/ppermute | solution.py:423
  108.4 17.1 %collective-permute-start.9 = (bf16[1,4,1,128,640]{4,3,2,1,0:T(8,128)(2,1)S(1)}, bf16[1,4,1,128,640]{4,3,2,1,0:T(8,128)(2,1)S(1)}, u32[]{:S(2)}, u32[]{:S(2)}) collective-permute-start(bf16[1,4,1,128,640]{4,3,2,1,0:T(8,128)(2,1)S(1)} %shard_map.142), channel_id=1, source_target_pairs={{0,2},{1,3},{2,0},{3,1},{4,6},{5,7},{6,4},{7,5},{8,10},{9,11},{10,... | collective-permute-start | bytes 1966088 | tf_op jit(solution)/shard_map/ppermute | solution.py:419
  110.0 30.3 %collective-permute-start.8 = (bf16[4,128,512]{2,1,0:T(8,128)(2,1)S(1)}, bf16[4,128,512]{2,1,0:T(8,128)(2,1)S(1)}, u32[]{:S(2)}, u32[]{:S(2)}) collective-permute-start(bf16[4,128,512]{2,1,0:T(8,128)(2,1)S(1)} %copy-done.50), channel_id=1, source_target_pairs={{0,4},{4,0},{8,12},{12,8},{16,20},{20,16},{24,28},{28,24},{1,5},{5... | collective-permute-start | bytes 1572872 | tf_op jit(solution)/shard_map/ppermute | solution.py:409
  128.9 39.7 %collective-permute-start.7 = (bf16[1280,512]{1,0:T(8,128)(2,1)S(1)}, bf16[1280,512]{1,0:T(8,128)(2,1)S(1)}, u32[]{:S(2)}, u32[]{:S(2)}) collective-permute-start(bf16[1280,512]{1,0:T(8,128)(2,1)S(1)} %copy-done.16), channel_id=1, source_target_pairs={{0,4},{4,0},{8,12},{12,8},{16,20},{20,16},{24,28},{28,24},{1,5},{5... | collective-permute-start | bytes 3932168 | tf_op jit(solution)/shard_map/ppermute | solution.py:409
  131.2 15.8 %collective-permute-start.14 = (bf16[1,4,1,128,640]{4,3,2,1,0:T(8,128)(2,1)S(1)}, bf16[1,4,1,128,640]{4,3,2,1,0:T(8,128)(2,1)S(1)}, u32[]{:S(2)}, u32[]{:S(2)}) collective-permute-start(bf16[1,4,1,128,640]{4,3,2,1,0:T(8,128)(2,1)S(1)} %shard_map.146), channel_id=1, source_target_pairs={{0,2},{1,3},{2,0},{3,1},{4,6},{5,7},{6,4},{7,5},{8,10},{9,11},{10,... | collective-permute-start | bytes 1966088 | tf_op jit(solution)/shard_map/ppermute | solution.py:419
  149.0 18.9 %collective-permute-start.15 = (bf16[1,4,1,64,640]{4,3,2,1,0:T(8,128)(2,1)S(1)}, bf16[1,4,1,64,640]{4,3,2,1,0:T(8,128)(2,1)S(1)}, u32[]{:S(2)}, u32[]{:S(2)}) collective-permute-start(bf16[1,4,1,64,640]{4,3,2,1,0:T(8,128)(2,1)S(1)} %shard_map.151), channel_id=1, source_target_pairs={{0,2},{1,3},{2,0},{3,1},{4,6},{5,7},{6,4},{7,5},{8,10},{9,11},{10,... | collective-permute-start | bytes 983048 | tf_op jit(solution)/shard_map/ppermute | solution.py:419
  196.7 40.7 %collective-permute-start.20 = (bf16[2,4,2,80,256]{4,3,2,1,0:T(8,128)(2,1)}, bf16[2,4,2,80,256]{4,3,2,1,0:T(8,128)(2,1)}, u32[]{:S(2)}, u32[]{:S(2)}) collective-permute-start(bf16[2,4,2,80,256]{4,3,2,1,0:T(8,128)(2,1)} %shard_map.158), channel_id=1, source_target_pairs={{0,2},{1,3},{2,0},{3,1},{4,6},{5,7},{6,4},{7,5},{8,10},{9,11},{10,... | collective-permute-start | bytes 1966088 | tf_op jit(solution)/shard_map/ppermute | solution.py:419
  198.4 19.7 %collective-permute-start.26 = (bf16[1,128,640]{2,1,0:T(8,128)(2,1)S(1)}, bf16[1,128,640]{2,1,0:T(8,128)(2,1)}, u32[]{:S(2)}, u32[]{:S(2)}) collective-permute-start(bf16[1,128,640]{2,1,0:T(8,128)(2,1)S(1)} %shard_map.154.refs_0_), channel_id=1, source_target_pairs={{0,2},{1,3},{2,0},{3,1},{4,6},{5,7},{6,4},{7,5},{8,10},{9,11},{10,... | collective-permute-start | bytes 491528 | tf_op jit(solution)/shard_map/ppermute | solution.py:419
  198.8 22.8 %collective-permute-start.25 = (bf16[1,128,640]{2,1,0:T(8,128)(2,1)}, bf16[1,128,640]{2,1,0:T(8,128)(2,1)}, u32[]{:S(2)}, u32[]{:S(2)}) collective-permute-start(bf16[1,128,640]{2,1,0:T(8,128)(2,1)} %shard_map.155.refs_0_), channel_id=1, source_target_pairs={{0,2},{1,3},{2,0},{3,1},{4,6},{5,7},{6,4},{7,5},{8,10},{9,11},{10,... | collective-permute-start | bytes 491528 | tf_op jit(solution)/shard_map/ppermute | solution.py:419
  200.5 67.2 %collective-permute-start.37 = (bf16[2,4,2,80,256]{4,3,2,1,0:T(8,128)(2,1)}, bf16[2,4,2,80,256]{4,3,2,1,0:T(8,128)(2,1)}, u32[]{:S(2)}, u32[]{:S(2)}) collective-permute-start(bf16[2,4,2,80,256]{4,3,2,1,0:T(8,128)(2,1)} %shard_map.161), channel_id=1, source_target_pairs={{0,2},{1,3},{2,0},{3,1},{4,6},{5,7},{6,4},{7,5},{8,10},{9,11},{10,... | collective-permute-start | bytes 1966088 | tf_op jit(solution)/shard_map/ppermute | solution.py:419
  201.6 35.2 %collective-permute-start.24 = (bf16[1,64,640]{2,1,0:T(8,128)(2,1)S(1)}, bf16[1,64,640]{2,1,0:T(8,128)(2,1)S(1)}, u32[]{:S(2)}, u32[]{:S(2)}) collective-permute-start(bf16[1,64,640]{2,1,0:T(8,128)(2,1)S(1)} %shard_map.162.refs_0_), channel_id=1, source_target_pairs={{0,2},{1,3},{2,0},{3,1},{4,6},{5,7},{6,4},{7,5},{8,10},{9,11},{10,... | collective-permute-start | bytes 245768 | tf_op jit(solution)/shard_map/ppermute | solution.py:419
  223.2 20.5 %collective-permute-start.30 = (bf16[2,1,128,640]{3,2,1,0:T(8,128)(2,1)S(1)}, bf16[2,1,128,640]{3,2,1,0:T(8,128)(2,1)S(1)}, u32[]{:S(2)}, u32[]{:S(2)}) collective-permute-start(bf16[2,1,128,640]{3,2,1,0:T(8,128)(2,1)S(1)} %shard_map.166.refs_1_), channel_id=1, source_target_pairs={{0,1},{1,0},{2,3},{3,2},{4,5},{5,4},{6,7},{7,6},{8,9},{9,8},{10,11... | collective-permute-start | bytes 983048 | tf_op jit(solution)/shard_map/ppermute | solution.py:423
  223.3 20.4 %collective-permute-start.29 = (bf16[2,1,128,640]{3,2,1,0:T(8,128)(2,1)S(1)}, bf16[2,1,128,640]{3,2,1,0:T(8,128)(2,1)S(1)}, u32[]{:S(2)}, u32[]{:S(2)}) collective-permute-start(bf16[2,1,128,640]{3,2,1,0:T(8,128)(2,1)S(1)} %shard_map.165.refs_0_), channel_id=1, source_target_pairs={{0,1},{1,0},{2,3},{3,2},{4,5},{5,4},{6,7},{7,6},{8,9},{9,8},{10,11... | collective-permute-start | bytes 983048 | tf_op jit(solution)/shard_map/ppermute | solution.py:423
  253.9 11.5 %collective-permute-start.32 = (bf16[2,1,2,80,256]{4,3,2,1,0:T(8,128)(2,1)S(1)}, bf16[2,1,2,80,256]{4,3,2,1,0:T(8,128)(2,1)S(1)}, u32[]{:S(2)}, u32[]{:S(2)}) collective-permute-start(bf16[2,1,2,80,256]{4,3,2,1,0:T(8,128)(2,1)S(1)} %shard_map.170), channel_id=1, source_target_pairs={{0,16},{4,20},{8,24},{12,28},{16,0},{20,4},{24,8},{28,12},{1,17},{... | collective-permute-start | bytes 491528 | tf_op jit(solution)/shard_map/ppermute | solution.py:413
  270.5 24.3 %collective-permute-start.43 = (bf16[2,4,2,80,128]{4,3,2,1,0:T(8,128)(2,1)}, bf16[2,4,2,80,128]{4,3,2,1,0:T(8,128)(2,1)}, u32[]{:S(2)}, u32[]{:S(2)}) collective-permute-start(bf16[2,4,2,80,128]{4,3,2,1,0:T(8,128)(2,1)} %shard_map.164), channel_id=1, source_target_pairs={{0,2},{1,3},{2,0},{3,1},{4,6},{5,7},{6,4},{7,5},{8,10},{9,11},{10,... | collective-permute-start | bytes 983048 | tf_op jit(solution)/shard_map/ppermute | solution.py:419
  305.2 16.2 %collective-permute-start.49 = (bf16[2,2,2,80,256]{4,3,2,1,0:T(8,128)(2,1)S(1)}, bf16[2,2,2,80,256]{4,3,2,1,0:T(8,128)(2,1)S(1)}, u32[]{:S(2)}, u32[]{:S(2)}) collective-permute-start(bf16[2,2,2,80,256]{4,3,2,1,0:T(8,128)(2,1)S(1)} %shard_map.176.refs_0_), channel_id=1, source_target_pairs={{0,1},{1,0},{2,3},{3,2},{4,5},{5,4},{6,7},{7,6},{8,9},{9,8},{10,11... | collective-permute-start | bytes 983048 | tf_op jit(solution)/shard_map/ppermute | solution.py:423
  305.8 17.0 %collective-permute-start.50 = (bf16[2,2,2,80,256]{4,3,2,1,0:T(8,128)(2,1)S(1)}, bf16[2,2,2,80,256]{4,3,2,1,0:T(8,128)(2,1)S(1)}, u32[]{:S(2)}, u32[]{:S(2)}) collective-permute-start(bf16[2,2,2,80,256]{4,3,2,1,0:T(8,128)(2,1)S(1)} %shard_map.182.refs_1_), channel_id=1, source_target_pairs={{0,1},{1,0},{2,3},{3,2},{4,5},{5,4},{6,7},{7,6},{8,9},{9,8},{10,11... | collective-permute-start | bytes 983048 | tf_op jit(solution)/shard_map/ppermute | solution.py:423
  (85 other events, 668.6 us)

commit v3 on v2

--- a/solution.py
+++ b/solution.py
@@ -13,7 +13,8 @@
 CORES = 2
 CHIPS_Z = 4
 LANES = 128
-VMEM = 32 * 1024 * 1024
+PARTS = 2
+VMEM = 56 * 1024 * 1024
 
 
 def moments(weight, first, second, grad):
@@ -39,12 +40,8 @@
 def widths(shard):
     if shard % LANES:
         return (shard,)
-    tiles = shard // LANES
-    cut = []
-    while tiles > 2:
-        cut.append(2 * LANES)
-        tiles -= 2
-    return tuple(cut + [tiles * LANES])
+    first = shard // LANES * 2 // 5 * LANES
+    return (first, shard - first)
 
 
 def dot(left, right, dims):
@@ -58,138 +55,179 @@
     )
 
 
-def take_columns(hidden, at, nz, nx, cuts):
+def pack(hidden, cotangent, at, nz, nx, cuts):
     tokens, hidden_width = hidden.shape
+    model = cotangent.shape[1]
     shard = hidden_width // (nz * nx)
+    first = cuts[0]
     if shard % LANES:
         parts = [
             lax.dynamic_slice_in_dim(hidden, (z * nx + at) * shard, shard, 1).T for z in range(nz)
         ]
-        whole = jnp.stack(parts)
-        starts = [sum(cuts[:k]) for k in range(len(cuts))]
-        return [whole[:, s : s + w] for s, w in zip(starts, cuts)]
-
-    def body(at_ref, h_ref, *out_refs):
-        start = 0
-        for width, out_ref in zip(cuts, out_refs):
-            part = h_ref[:, start : start + width]
-            out_ref[0] = part.T
+        return [jnp.concatenate([cotangent.T, *parts])]
+
+    def body(at_ref, h_ref, cot_ref, out_ref, *later_refs):
+        z = pl.program_id(0)
+
+        @pl.when(z == 0)
+        def _():
+            out_ref[:model] = cot_ref[...].T
+
+        out_ref[pl.ds(pl.multiple_of(model + z * first, LANES), first)] = h_ref[:, :first].T
+        start = first
+        for width, later_ref in zip(cuts[1:], later_refs):
+            later_ref[0] = h_ref[:, start : start + width].T
             start += width
 
+    total = model + nz * first
     return pl.pallas_call(
         body,
         grid_spec=pltpu.PrefetchScalarGridSpec(
             num_scalar_prefetch=1,
             grid=(nz,),
-            in_specs=[pl.BlockSpec((tokens, shard), lambda z, a: (0, z * nx + a[0]))],
-            out_specs=[pl.BlockSpec((1, w, tokens), lambda z, a: (z, 0, 0)) for w in cuts],
-        ),
-        out_shape=[jax.ShapeDtypeStruct((nz, w, tokens), BF16) for w in cuts],
-        **params(),
-    )(jnp.reshape(at, (1,)).astype(jnp.int32), hidden)
-
-
-def grad_out_chunk(hiddens, cots, core, scale):
-    nz, width, tokens = hiddens[0].shape
-    model = cots[0].shape[1]
+            in_specs=[
+                pl.BlockSpec((tokens, shard), lambda z, a: (0, z * nx + a[0])),
+                pl.BlockSpec((tokens, model), lambda z, a: (0, 0)),
+            ],
+            out_specs=[pl.BlockSpec((total, tokens), lambda z, a: (0, 0))]
+            + [pl.BlockSpec((1, w, tokens), lambda z, a: (z, 0, 0)) for w in cuts[1:]],
+        ),
+        out_shape=[jax.ShapeDtypeStruct((total, tokens), BF16)]
+        + [jax.ShapeDtypeStruct((nz, w, tokens), BF16) for w in cuts[1:]],
+        **params(),
+    )(jnp.reshape(at, (1,)).astype(jnp.int32), hidden, cotangent)
+
+
+class Tokens:
+    def __init__(self, packs, hiddens, model, nz, width):
+        tokens = packs[0].shape[1]
+        self.model, self.width, self.count = model, width, len(packs)
+        if hiddens is None:
+            self.arrays = list(packs)
+            self.specs = [pl.BlockSpec(packs[0].shape, lambda z, c: (0, 0))] * len(packs)
+        else:
+            self.arrays = [*packs, *hiddens]
+            self.specs = [pl.BlockSpec((model, tokens), lambda z, c: (0, 0))] * len(packs)
+            self.specs += [pl.BlockSpec((1, width, tokens), lambda z, c: (z, 0, 0))] * len(packs)
+
+    def cot(self, refs, n):
+        return refs[n].at[: self.model]
+
+    def hidden(self, refs, n):
+        if len(refs) == self.count:
+            row = self.model + pl.program_id(0) * self.width
+            return refs[n][pl.ds(pl.multiple_of(row, 16), self.width)].astype(F32)
+        return refs[self.count + n][0].astype(F32)
+
+
+def grad_out_chunk(tokens, core, nz, scale):
+    width, model = tokens.width, tokens.model
     half = model // CORES
-    count = len(hiddens)
+    high = width // PARTS
+    count = len(tokens.arrays)
 
     def body(c_ref, *refs):
-        h_refs, cot_refs = refs[:count], refs[count : 2 * count]
-        send_ref, keep_ref = refs[2 * count :]
-        acts = [gelu(h[0].astype(F32)).astype(BF16) for h in h_refs]
-        for out_ref, which in ((send_ref, 1 - c_ref[0]), (keep_ref, c_ref[0])):
-            cols = pl.ds(pl.multiple_of(which * half, LANES), half)
-            total = sum(dot(a, cot[:, cols], ((1,), (0,))) for a, cot in zip(acts, cot_refs))
-            out_ref[0] = (total * scale).astype(BF16)
+        ins, outs = refs[:count], refs[count:]
+        acts = jnp.concatenate(
+            [gelu(tokens.hidden(ins, n)).astype(BF16) for n in range(tokens.count)], axis=1
+        )
+        for which in range(2):
+            cols = pl.ds(pl.multiple_of((c_ref[0] + 1 + which) % CORES * half, 16), half)
+            right = jnp.concatenate([tokens.cot(ins, n)[cols, :] for n in range(tokens.count)], axis=1)
+            total = (dot(acts, right, ((1,), (1,))) * scale).astype(BF16)
+            for p in range(PARTS):
+                value = total[p * high : (p + 1) * high]
+                if which:
+                    outs[PARTS][p, 0] = value
+                else:
+                    outs[p][0] = value
 
     return pl.pallas_call(
         body,
         grid_spec=pltpu.PrefetchScalarGridSpec(
             num_scalar_prefetch=1,
             grid=(nz,),
-            in_specs=[pl.BlockSpec((1, width, tokens), lambda z, c: (z, 0, 0))] * count
-            + [pl.BlockSpec((tokens, model), lambda z, c: (0, 0))] * count,
-            out_specs=[pl.BlockSpec((1, width, half), lambda z, c: (z, 0, 0))] * 2,
-        ),
-        out_shape=[jax.ShapeDtypeStruct((nz, width, half), BF16)] * 2,
-        **params(),
-    )(core, *hiddens, *cots)
-
-
-def grad_pre_chunk(hiddens, cots, mine, other, row, core, scale):
-    nz, width, tokens = hiddens[0].shape
-    part, model = mine.shape[1:]
-    count = len(hiddens)
+            in_specs=tokens.specs,
+            out_specs=[pl.BlockSpec((1, high, half), lambda z, c: (z, 0, 0))] * PARTS
+            + [pl.BlockSpec((PARTS, 1, high, half), lambda z, c: (0, z, 0, 0))],
+        ),
+        out_shape=[jax.ShapeDtypeStruct((nz, high, half), BF16)] * PARTS
+        + [jax.ShapeDtypeStruct((PARTS, nz, high, half), BF16)],
+        **params(),
+    )(core, *tokens.arrays)
+
+
+def grad_pre_chunk(tokens, weights, row, scale):
+    nz, shard, model = weights.shape
+    width = tokens.width
+    count = len(tokens.arrays)
+    long = tokens.arrays[0].shape[1]
 
     def body(c_ref, *refs):
-        h_refs, cot_refs = refs[:count], refs[count : 2 * count]
-        mine_ref, other_ref = refs[2 * count : 2 * count + 2]
-        out_refs, w_ref = refs[2 * count + 2 : -1], refs[-1]
-        for at, ref in ((c_ref[0], mine_ref), (1 - c_ref[0], other_ref)):
-            w_ref[pl.ds(pl.multiple_of(at * part, 16), part), :] = ref[0]
-        w = w_ref[row : row + width, :]
-        for h, cot, out_ref in zip(h_refs, cot_refs, out_refs):
-            grad_act = dot(w, cot[...], ((1,), (1,))) * scale
-            out_ref[0] = (grad_act * gelu_slope(h[0].astype(F32))).astype(BF16)
+        ins = refs[:count]
+        w_ref, out_ref = refs[count:]
+        w = w_ref[0, row : row + width, :]
+        for n in range(tokens.count):
+            grad_act = dot(w, tokens.cot(ins, n)[...], ((1,), (0,))) * scale
+            out_ref[0, :, n * long : (n + 1) * long] = (
+                grad_act * gelu_slope(tokens.hidden(ins, n))
+            ).astype(BF16)
 
     return pl.pallas_call(
         body,
         grid_spec=pltpu.PrefetchScalarGridSpec(
             num_scalar_prefetch=1,
             grid=(nz,),
-            in_specs=[pl.BlockSpec((1, width, tokens), lambda z, c: (z, 0, 0))] * count
-            + [pl.BlockSpec((tokens, model), lambda z, c: (0, 0))] * count
-            + [pl.BlockSpec((1, part, model), lambda z, c: (z, 0, 0))] * CORES,
-            out_specs=[pl.BlockSpec((1, width, tokens), lambda z, c: (z, 0, 0))] * count,
-            scratch_shapes=[pltpu.VMEM((CORES * part, model), BF16)],
-        ),
-        out_shape=[jax.ShapeDtypeStruct((nz, width, tokens), BF16)] * count,
-        **params(),
-    )(core, *hiddens, *cots, mine, other)
-
-
-def grad_in_chunk(grads, inputs, core, scale):
-    nz, width, tokens = grads[0].shape
-    model = inputs[0].shape[0]
-    count = len(grads)
+            in_specs=tokens.specs + [pl.BlockSpec((1, shard, model), lambda z, c: (z, 0, 0))],
+            out_specs=pl.BlockSpec((1, width, tokens.count * long), lambda z, c: (z, 0, 0)),
+        ),
+        out_shape=jax.ShapeDtypeStruct((nz, width, tokens.count * long), BF16),
+        **params(),
+    )(jnp.zeros((1,), jnp.int32), *tokens.arrays, weights)
+
+
+def grad_in_chunk(grads, inputs, core, scale, cut):
+    nz, width, long = grads.shape
+    model, tokens = inputs[0].shape
+    count = len(inputs)
     half = nz // CORES
-
-    def body(c_ref, *refs):
-        g_refs, in_refs = refs[:count], refs[count : 2 * count]
-        send_ref, keep_ref = refs[2 * count :]
+    high = model // cut
+
+    def body(c_ref, g_ref, *refs):
+        in_refs, outs = refs[:count], refs[count:]
         left = jnp.concatenate([i[...] for i in in_refs], axis=1)
-        right = jnp.concatenate([g[0] for g in g_refs], axis=1)
-        total = (dot(left, right, ((1,), (1,))) * scale).astype(BF16)
+        total = (dot(left, g_ref[0], ((1,), (1,))) * scale).astype(BF16)
         step = pl.program_id(0)
-
-        @pl.when(step < half)
-        def _():
-            send_ref[0] = total
+        for n in range(half):
+
+            @pl.when(step == n)
+            def _(n=n):
+                for h in range(cut):
+                    outs[n * cut + h][...] = total[h * high : (h + 1) * high]
 
         @pl.when(step >= half)
         def _():
-            keep_ref[0] = total
-
-    def shard_at(step, c):
-        return ((c[0] + 1 + step // half) % CORES * half + step % half, 0, 0)
+            outs[-1][0] = total
 
     return pl.pallas_call(
         body,
         grid_spec=pltpu.PrefetchScalarGridSpec(
             num_scalar_prefetch=1,
             grid=(nz,),
-            in_specs=[pl.BlockSpec((1, width, tokens), shard_at)] * count
+            in_specs=[
+                pl.BlockSpec(
+                    (1, width, long),
+                    lambda z, c: ((c[0] + 1 + z // half) % CORES * half + z % half, 0, 0),
+                )
+            ]
             + [pl.BlockSpec((model, tokens), lambda z, c: (0, 0))] * count,
-            out_specs=[
-                pl.BlockSpec((1, model, width), lambda z, c: (jnp.minimum(z, half - 1), 0, 0)),
-                pl.BlockSpec((1, model, width), lambda z, c: (jnp.maximum(z - half, 0), 0, 0)),
-            ],
-        ),
-        out_shape=[jax.ShapeDtypeStruct((half, model, width), BF16)] * 2,
-        **params(),
-    )(core, *grads, *inputs)
+            out_specs=[pl.BlockSpec((high, width), lambda z, c: (0, 0))] * (half * cut)
+            + [pl.BlockSpec((1, model, width), lambda z, c: (jnp.maximum(z - half, 0), 0, 0))],
+        ),
+        out_shape=[jax.ShapeDtypeStruct((high, width), BF16)] * (half * cut)
+        + [jax.ShapeDtypeStruct((half, model, width), BF16)],
+        **params(),
+    )(core, grads, *inputs)
 
 
 def transposed(value):
@@ -230,24 +268,52 @@
     )(core, weight)
 
 
-def stack(pieces, places):
+def stack(pieces, places, inner=False):
     count = len(pieces)
     shape = pieces[0].shape
+    out = (shape[0], count, *shape[1:]) if inner else (count, *shape)
 
     def body(at_ref, *refs):
         for n in range(count):
-            refs[count][at_ref[n]] = refs[n][...]
-
-    whole = lambda at: (0,) * len(shape)
+            if inner:
+                for p in range(shape[0]):
+                    refs[count][p, at_ref[n]] = refs[n][p]
+            else:
+                refs[count][at_ref[n]] = refs[n][...]
+
     return pl.pallas_call(
         body,
         grid_spec=pltpu.PrefetchScalarGridSpec(
             num_scalar_prefetch=1,
             grid=(),
-            in_specs=[pl.BlockSpec(shape, whole)] * count,
-            out_specs=pl.BlockSpec((count, *shape), lambda at: (0,) * (1 + len(shape))),
-        ),
-        out_shape=jax.ShapeDtypeStruct((count, *shape), pieces[0].dtype),
+            in_specs=[pl.BlockSpec(shape, lambda at: (0,) * len(shape))] * count,
+            out_specs=pl.BlockSpec(out, lambda at: (0,) * len(out)),
+        ),
+        out_shape=jax.ShapeDtypeStruct(out, pieces[0].dtype),
+        **params(),
+    )(places, *pieces)
+
+
+def stack_rows(pieces, places):
+    count = len(pieces)
+    high, cols = pieces[0].shape
+    wide = 2 * LANES
+    parts = CORES
+
+    def body(at_ref, *refs):
+        for n in range(count):
+            row = pl.multiple_of(at_ref[1, n] * high, 16)
+            refs[count][at_ref[0, n], pl.ds(row, high)] = refs[n][...]
+
+    return pl.pallas_call(
+        body,
+        grid_spec=pltpu.PrefetchScalarGridSpec(
+            num_scalar_prefetch=1,
+            grid=(cols // wide,),
+            in_specs=[pl.BlockSpec((high, wide), lambda n, at: (0, n))] * count,
+            out_specs=pl.BlockSpec((count // parts, parts * high, wide), lambda n, at: (0, 0, n)),
+        ),
+        out_shape=jax.ShapeDtypeStruct((count // parts, parts * high, cols), pieces[0].dtype),
         **params(),
     )(places, *pieces)
 
@@ -261,7 +327,7 @@
     )(*tiles)
 
 
-def reduce_step(place, keep, cross, from_y, from_z, shift, stage, ny, split):
+def reduce_step(place, keep, crosses, from_y, from_z, shift, stage, ny, split):
     lead, nz, mid, _, high, wide = keep.shape
     bit = len(from_z)
 
@@ -277,7 +343,22 @@
     count = {"y": nz, "z": nz >> (bit + 1), "end": 1}[stage]
     six = (lead, 1, mid, 1, high, wide)
     five = (lead, 1, mid, high, wide)
-    specs = [pl.BlockSpec(six, lambda n, at: (0, zed(n, at), 0, (at[1] + shift) % ny, 0, 0))] * 2
+    specs = [pl.BlockSpec(six, lambda n, at: (0, zed(n, at), 0, (at[1] + shift) % ny, 0, 0))]
+    each = len(crosses) // lead
+    long = nz // each
+    for h in range(len(crosses)):
+        specs.append(
+            pl.BlockSpec(
+                six[1:],
+                lambda n, at, h=h % each: (
+                    jnp.clip(zed(n, at) - h * long, 0, long - 1),
+                    0,
+                    (at[1] + shift) % ny,
+                    0,
+                    0,
+                ),
+            )
+        )
     specs += [pl.BlockSpec(five, lambda n, at: (0, zed(n, at), 0, 0, 0))] * len(from_y)
     specs += [
         pl.BlockSpec(five, lambda n, at, j=j: (0, zed(n, at) // (2 << j), 0, 0, 0)) for j in range(bit)
@@ -288,8 +369,13 @@
         outs = refs[len(specs) :]
         for p in range(lead):
             for m in range(mid):
-                total = ins[0][p, 0, m, 0].astype(F32) + ins[1][p, 0, m, 0].astype(F32)
-                for ref in ins[2:]:
+                total = ins[1 + p * each][0, m, 0]
+                for h in range(1, each):
+                    total = jnp.where(
+                        zed(pl.program_id(0), at_ref) >= h * long, ins[1 + p * each + h][0, m, 0], total
+                    )
+                total = total.astype(F32) + ins[0][p, 0, m, 0].astype(F32)
+                for ref in ins[1 + len(crosses) :]:
                     total = total + ref[p, 0, m].astype(F32)
                 total = total.astype(BF16)
                 if not split:
@@ -314,7 +400,7 @@
         ),
         out_shape=out_shape,
         **params(),
-    )(place, keep, cross, *from_y, *from_z)
+    )(place, keep, *crosses, *from_y, *from_z)
     return out if split else out[0]
 
 
@@ -423,18 +509,22 @@
         return lax.ppermute(value, "gy", pairs)
 
     class Reduce:
-        def __init__(self, order, at, send, keep, shape):
+        def __init__(self, order, at, sends, keep, shape):
             self.order, self.at, self.place = order, at, jnp.stack(at).astype(jnp.int32)
             self.keep = keep.reshape(shape)
-            self.cross = across(send).reshape(shape)
+            each = len(sends) // shape[0]
+            self.crosses = [
+                across(send).reshape(shape[1] // each, *shape[2:]) for send in sends
+            ]
             self.from_y = []
             self.from_z = []
 
         def step(self, shift, stage, split=False):
-            count = len(self.from_y)
-            got = self.order.after(self.keep, self.cross, *self.from_y, *self.from_z)
+            got = self.order.after(self.keep, *self.crosses, *self.from_y, *self.from_z)
+            lead = 1 + len(self.crosses)
+            count = lead + len(self.from_y)
             out = reduce_step(
-                self.place, got[0], got[1], got[2 : 2 + count], got[2 + count :], shift, stage, ny, split
+                self.place, got[0], got[1:lead], got[lead:count], got[count:], shift, stage, ny, split
             )
             self.order.did(out[0] if split else out)
             return out
@@ -458,17 +548,17 @@
         def share_y(self, value):
             self.held = [value] + [along_y(value, s) for s in range(1, ny)]
 
-        def stacked(self, place, size):
+        def stacked(self, place, size, inner=False):
             places = jnp.stack([(place - s) % size for s in range(size)]).astype(jnp.int32)
-            value = stack(self.order.after(*self.held), places)
+            value = stack(self.order.after(*self.held), places, inner)
             self.order.did(value)
             return value
 
         def stack_x(self):
             self.share_y(self.stacked(self.at[0], nx))
 
-        def stack_y(self):
-            value = self.stacked(self.at[1], ny)
+        def stack_y(self, inner=False):
+            value = self.stacked(self.at[1], ny, inner)
             self.held = [value, across(value)]
 
     def local(inputs, hidden_pre, cotangent, w_in, m_in, v_in, w_out, m_out, v_out):
@@ -488,71 +578,74 @@
         y, c = side // CORES, side % CORES
         core = jnp.reshape(c, (1,)).astype(jnp.int32)
         order = Order()
-        hops = nz.bit_length() - 1
-
-        cots = [cotangent] + [along_x(cotangent, s) for s in range(1, nx)]
-        hiddens = [[] for _ in chunks]
-        sends = []
-        for s in range(1, nx):
-            sends.append(take_columns(*order.after(hidden_pre), (x + s) % nx, nz, nx, cuts))
-            order.did(sends[-1][0])
-        late = last if last > 1 else last + 1
-        for k in range(late):
-            hiddens[k] = [along_x(sends[s - 1][k], s) for s in range(1, nx)]
+
+        packs, hiddens = [], []
+        for t in range(1, nx):
+            sent = pack(*order.after(hidden_pre, cotangent), (x + t) % nx, nz, nx, cuts)
+            order.did(sent[0])
+            packs.append(along_x(sent[0], t))
+            hiddens.append([along_x(value, t) for value in sent[1:]])
 
         part = half_rows(*order.after(w_out), core)
         order.did(part)
-        found = {0: part}
-        bit = nz // 2
+        flipped = transposed(*order.after(inputs))
+        order.did(flipped)
+        columns = [flipped] + [along_x(flipped, t) for t in range(1, nx)]
+        own = pack(*order.after(hidden_pre, cotangent), x, nz, nx, cuts)
+        order.did(own[0])
+        found = {0: part, nz // 2: along_z(part, nz // 2)}
+        bit = nz // 4
         while bit:
             for key in list(found):
-                found[key ^ bit] = along_z(found[key], bit)
+                value = found[key]
+                if key:
+                    (value,) = order.after(value)
+                found[key ^ bit] = along_z(value, bit)
             bit //= 2
-
-        flipped = transposed(*order.after(inputs))
-        order.did(flipped)
-        own = take_columns(*order.after(hidden_pre), x, nz, nx, cuts)
-        order.did(own[0])
-        came = cots[1:] + hiddens[0]
-        tied = lax.optimization_barrier((flipped, *[value[k] for value in sends for k in chunks], *came))
-        for k in range(late, len(cuts)):
-            hiddens[k] = [along_x(tied[1 + (s - 1) * len(cuts) + k], s) for s in range(1, nx)]
-        columns = [flipped] + [along_x(tied[0], s) for s in range(1, nx)]
-        hiddens = [[own[k]] + hiddens[k] for k in chunks]
+        crossed = [across(found[key]) for key in range(nz)]
+        packs = [own[0]] + packs
+        hiddens = [own[1:]] + hiddens
 
         outs = [None for _ in chunks]
         ins = [None for _ in chunks]
         pres = [None for _ in chunks]
 
         def stack_weights():
-            places = jnp.stack([z ^ key for key in range(nz)]).astype(jnp.int32)
-            mine = stack(order.after(*[found[key] for key in range(nz)]), places)
-            order.did(mine)
-            return [mine, across(mine)]
+            pieces = order.after(*[found[key] for key in range(nz)], *crossed)
+            blocks = jnp.stack([z ^ key for key in range(nz)] * CORES)
+            halves = jnp.stack([c] * nz + [1 - c] * nz)
+            value = stack_rows(pieces, jnp.stack([blocks, halves]).astype(jnp.int32))
+            order.did(value)
+            return value
+
+        def tokens(k, *more):
+            later = [] if k == 0 else [value[k - 1] for value in hiddens]
+            got = order.after(*packs, *later, *more)
+            count = nx + len(later)
+            blocks = Tokens(got[:nx], got[nx:count] if later else None, model, nz, cuts[k])
+            return blocks, got[count:]
 
         def start_out(k):
-            got = order.after(*hiddens[k], *cots)
-            send, keep = grad_out_chunk(got[:nx], got[nx:], core, scale_out)
+            *sends, keep = grad_out_chunk(tokens(k)[0], core, nz, scale_out)
             order.did(keep)
-            outs[k] = Reduce(
-                order, (x, y, z), send, keep, (1, nz, 1, ny, cuts[k] // ny, model // CORES)
-            )
+            shape = (PARTS, nz, 1, ny, cuts[k] // PARTS // ny, model // CORES)
+            outs[k] = Reduce(order, (x, y, z), sends, keep, shape)
 
         def start_pre(k):
-            got = order.after(*hiddens[k], *cots, *weights)
-            pres[k] = grad_pre_chunk(got[:nx], got[nx : 2 * nx], got[-2], got[-1], starts[k], core, scale_out)
-            order.did(pres[k][0])
+            blocks, got = tokens(k, weights)
+            pres[k] = grad_pre_chunk(blocks, got[0], starts[k], scale_out)
+            order.did(pres[k])
 
         def start_in(k):
-            got = order.after(*pres[k], *columns)
-            send, keep = grad_in_chunk(got[:nx], got[nx:], core, scale_in)
+            got = order.after(pres[k], *columns)
+            *sends, keep = grad_in_chunk(got[0], got[1:], core, scale_in, PARTS if k else 1)
             order.did(keep)
-            ins[k] = Reduce(
-                order, (x, y, z), send, keep, (nz // CORES, nz, nx, ny, rows // ny, cuts[k])
-            )
-
-        def sums(tile):
-            tiles = order.after(*([tile] + [along_z(tile, flip) for flip in range(1, nz)]))
+            shape = (nz // CORES, nz, nx, ny, rows // ny, cuts[k])
+            ins[k] = Reduce(order, (x, y, z), sends, keep, shape)
+
+        def sums(tile, zs=None):
+            zs = zs or [along_z(tile, flip) for flip in range(1, nz)]
+            tiles = order.after(tile, *zs)
             tile = add_tiles(tiles)
             order.did(tile)
             return [tile] + [along_x(tile, s) for s in range(1, nx)]
@@ -563,32 +656,38 @@
             order.did(value)
             return value
 
-        for k in chunks:
-            start_out(k)
-            if k == 0:
-                weights = stack_weights()
-            if k > 0:
-                outs[k - 1].send_z()
-            outs[k].send_y()
-            start_pre(k)
-            if k > 0:
-                outs[k - 1].send_z()
-        for k in chunks[:-1]:
-            outs[k].finish()
-        outs[last].send_z()
-
-        for k in chunks:
-            start_in(k)
-            ins[k].send_y()
-            if k == 0:
-                outs[last].send_z()
-            elif k == 1:
-                outs[last].finish()
-        if last == 0:
-            outs[last].finish()
-        for k in chunks:
-            outs[k].stack_y()
-        ins[0].send_z()
+        start_out(0)
+        outs[0].send_y()
+        weights = stack_weights()
+        start_pre(0)
+        outs[0].send_z()
+        start_in(0)
+        ins[0].send_y()
+        outs[0].send_z()
+        if last:
+            ins[0].send_z()
+            start_out(1)
+            outs[1].send_y()
+            outs[0].finish()
+            start_pre(1)
+            ins[0].send_z()
+            start_in(1)
+            ins[1].send_y()
+            ins[0].finish()
+            outs[1].send_z()
+            ins[0].stack_x()
+            outs[0].stack_y(True)
+            outs[1].send_z()
+            ins[0].stack_y()
+            outs[1].finish()
+            ins[1].send_z()
+            outs[1].stack_y(True)
+            ins[1].send_z()
+        else:
+            outs[0].finish()
+            ins[0].send_z()
+            ins[0].send_z()
+            outs[0].stack_y(True)
 
         half = model // CORES
         got = order.after(
@@ -601,26 +700,15 @@
             got[4 + last :],
             (CORES,),
             pl.BlockSpec((shard, half), lambda n, c: (0, n)),
-            [pl.BlockSpec((ny, 1, w // ny, half), lambda n, c: (0, 0, 0, 0)) for w in cuts],
+            [
+                pl.BlockSpec((PARTS, ny, w // PARTS // ny, half), lambda n, c: (0, 0, 0, 0)) for w in cuts
+            ],
             lambda n: n,
             0,
         )
         order.did(tile)
-        for _ in range(hops - 1):
-            ins[0].send_z()
+        ins[last].finish()
         tiles = sums(tile)
-        ins[0].finish()
-        for k in range(1, len(cuts)):
-            ins[k].send_z()
-            ins[k - 1].stack_x()
-            for _ in range(hops - 1):
-                ins[k].send_z()
-            ins[k - 1].stack_y()
-            if k == 1:
-                new_w_out = new_weights(w_out, update_out, tiles)
-            ins[k].finish()
-        if last == 0:
-            new_w_out = new_weights(w_out, update_out, tiles)
         ins[last].stack_x()
         ins[last].stack_y()
 
@@ -660,7 +748,9 @@
                 1,
             )
         order.did(tile)
-        new_w_in = new_weights(w_in, update_in, sums(tile))
+        zs = [along_z(tile, flip) for flip in range(1, nz)]
+        new_w_out = new_weights(w_out, update_out, tiles)
+        new_w_in = new_weights(w_in, update_in, sums(tile, zs))
         return (new_w_in, first_in, second_in, new_w_out, first_out, second_out)
 
     return local

time: 344 us -> 363 us (1.055)
  Pallas kernels: 111 us -> 182 us
  waiting for transfers between devices: 144 us -> 106 us
  starting transfers between devices: 55.1 us -> 44.7 us
  local copies, waits for them, and re-layouts: 30.7 us -> 25.5 us
    ppermute x12 -> x8, waiting for transfers between devices: 46.5 us -> 15.2 us  [along_y(): return lax.ppermute(value, 'gy', pairs)]
    pallas_call x2 -> x3, Pallas kernels: 3.49 us -> 19.6 us  [the longest x2 11.4 us: pack(): pl.pallas_call(body, grid_spec=pltpu.PrefetchScalarGridSpec(num_scalar_pr...]
    pallas_call x24 -> x16, Pallas kernels: 37.2 us -> 51.6 us  [reduce_step(): pl.pallas_call(body, grid_spec=pltpu.PrefetchScalarGridSpec(num_scalar_pr...]
    ppermute x10 -> x7, waiting for transfers between devices: 27.8 us -> 14.1 us  [along_x(): return lax.ppermute(value, 'gx', pairs)]
    ppermute x21 -> x17, waiting for transfers between devices: 55.9 us -> 65.4 us  [along_z(): return lax.ppermute(value, 'gx', pairs)]
    pallas_call x2, Pallas kernels: 11.5 us -> 20.1 us  [moments_kernel(): pl.pallas_call(body, grid_spec=pltpu.PrefetchScalarGridSpec(num_scalar_pr...]
    ppermute x12 -> x8, starting transfers between devices: 16.1 us -> 8.31 us  [along_y(): return lax.ppermute(value, 'gy', pairs)]
    pallas_call x2, Pallas kernels: 6.45 us -> 12.9 us  [step_weights(): pl.pallas_call(body, grid=(rows // high,), in_specs=[spec] * 2 + [tile] *...]
  transfers between devices with their start and end apart: 56 -> 50, of which waited for: 33 -> 28; matrix products, arithmetic and copies ran while one was open for 0% -> 1% of each run, Pallas kernels for 22% -> 42%
where the time goes in v3:
time: 363 us; the launch traced here: 361 us
  Pallas kernels  182 us (50%)
  waiting for transfers between devices  106 us (29%)
  starting transfers between devices  44.7 us (12%)
  local copies, waits for them, and re-layouts  25.5 us (7%)
    ppermute x17, waiting for transfers between devices, along_z(): return lax.ppermute(value, 'gx', pairs)  65.4 us
    pallas_call x16, Pallas kernels, reduce_step(): pl.pallas_call(body, grid_spec=pltpu.PrefetchScalarGridSpec(num_scalar_pr...  51.6 us
    unnamed x106, local copies, waits for them, and re-layouts  25.4 us
    ppermute x17, starting transfers between devices, along_z(): return lax.ppermute(value, 'gx', pairs)  22 us
    pallas_call x2, Pallas kernels, moments_kernel(): pl.pallas_call(body, grid_spec=pltpu.PrefetchScalarGridSpec(num_scalar_pr...  20.1 us
    pallas_call x2, Pallas kernels, grad_pre_chunk(): pl.pallas_call(body, grid_spec=pltpu.PrefetchScalarGridSpec(num_scalar_pr...  18.6 us
    pallas_call x2, Pallas kernels, grad_in_chunk(): pl.pallas_call(body, grid_spec=pltpu.PrefetchScalarGridSpec(num_scalar_pr...  17.9 us
    pallas_call x2, Pallas kernels, grad_out_chunk(): pl.pallas_call(body, grid_spec=pltpu.PrefetchScalarGridSpec(num_scalar_pr...  15.9 us
  transfers between devices with their start and end apart: 50, of which 28 were waited for; matrix products, arithmetic and copies ran while one was open for 1% of the time, Pallas kernels for 42%

profile of v3, /device:TPU:0, one launch (start us, length us, event | category | flops | bytes accessed | tf_op | source)
XLA Modules:
  0.0 361.0 jit_solution(1324321593782318448)
XLA Ops:
  0.7 5.7 %shard_map.136 = (bf16[2304,512]{1,0:T(8,128)(2,1)}, bf16[4,384,512]{2,1,0:T(8,128)(2,1)}) custom-call(s32[1]{0:T(128)} %bitcast.8.at_ref, bf16[512,5120]{1,0:T(8,128)(2,1)} %h_ref.2, bf16[512,1280]{1,0:T(8,128)(2,1)} %cot_ref.2), custom_call_target="tpu_custom_call" | custom-call | flops 1 | bytes 1 | tf_op jit(solution)/shard_map/pallas_call | solution.py:83
  17.3 4.2 %shard_map.138.refs_0_ = bf16[1280,512]{1,0:T(8,128)(2,1)} custom-call(bf16[512,1280]{1,0:T(8,128)(2,1)} %in_ref.1), custom_call_target="tpu_custom_call" | custom-call | flops 1 | bytes 1 | tf_op jit(solution)/shard_map/pallas_call | solution.py:240
  21.6 5.7 %shard_map.139 = (bf16[2304,512]{1,0:T(8,128)(2,1)}, bf16[4,384,512]{2,1,0:T(8,128)(2,1)}) custom-call(s32[1]{0:T(128)} %bitcast.5.at_ref, bf16[512,5120]{1,0:T(8,128)(2,1)} %h_ref.2, bf16[512,1280]{1,0:T(8,128)(2,1)} %cot_ref.2), custom_call_target="tpu_custom_call" | custom-call | flops 1 | bytes 1 | tf_op jit(solution)/shard_map/pallas_call | solution.py:83
  27.2 24.5 %collective-permute-done.2.refs_2_ = bf16[320,1280]{1,0:T(8,128)(2,1)} collective-permute-done((bf16[320,1280]{1,0:T(8,128)(2,1)}, bf16[320,1280]{1,0:T(8,128)(2,1)}, u32[]{:S(2)}, u32[]{:S(2)}) %collective-permute-start.2) | collective-permute-done | bytes 819232 | tf_op jit(solution)/shard_map/ppermute | solution.py:499
  52.3 8.4 %collective-permute-done.refs_1_ = bf16[2304,512]{1,0:T(8,128)(2,1)S(1)} collective-permute-done((bf16[2304,512]{1,0:T(8,128)(2,1)}, bf16[2304,512]{1,0:T(8,128)(2,1)S(1)}, u32[]{:S(2)}, u32[]{:S(2)}) %collective-permute-start) | collective-permute-done | bytes 2359328 | tf_op jit(solution)/shard_map/ppermute | solution.py:495
  62.1 7.3 %shard_map.140 = (bf16[4,128,640]{2,1,0:T(8,128)(2,1)}, bf16[4,128,640]{2,1,0:T(8,128)(2,1)}, bf16[2,4,128,640]{3,2,1,0:T(8,128)(2,1)}) custom-call(s32[1]{0:T(128)} %bitcast.c_ref, bf16[2304,512]{1,0:T(8,128)(2,1)} %get-tuple-element.257.refs_0_, bf16[2304,512]{1,0:T(8,128)(2,1)} %copy-done), custom_call_target="tpu_custom_call" | custom-call | flops 1 | bytes 1 | tf_op jit(solution)/shard_map/pallas_call | solution.py:145
  82.7 8.2 %shard_map.142.refs_2_.refs_4_ = bf16[4,640,1280]{2,1,0:T(8,128)(2,1)} custom-call(s32[2,8]{1,0:T(2,128)} %pad_add_fusion.at_ref, bf16[320,1280]{1,0:T(8,128)(2,1)} %shard_map.137.refs_0_, bf16[320,1280]{1,0:T(8,128)(2,1)} %collective-permute-done.1.refs_1_, bf16[320,1280]{1,0:T(8,128)(2,1)} %collective-permute-done.2.refs_2_, ...), custom_call_target="tpu_custom_call" | custom-call | flops 1 | bytes 1 | tf_op jit(solution)/shard_map/pallas_call | solution.py:308
  90.9 8.5 %shard_map.143.g_ref = bf16[4,256,1024]{2,1,0:T(8,128)(2,1)} custom-call(s32[1]{0:T(128)} %constant.85.clone.1.c_ref, bf16[2304,512]{1,0:T(8,128)(2,1)} %get-tuple-element.257.refs_0_, bf16[2304,512]{1,0:T(8,128)(2,1)} %copy-done, bf16[4,640,1280]{2,1,0:T(8,128)(2,1)} %shard_map.142.refs_2_.refs_4_), custom_call_target="tpu_custom_call" | custom-call | flops 1 | bytes 1 | tf_op jit(solution)/shard_map/pallas_call | solution.py:176
  104.2 7.3 %shard_map.145 = (bf16[1280,256]{1,0:T(8,128)(2,1)}, bf16[1280,256]{1,0:T(8,128)(2,1)}, bf16[2,1280,256]{2,1,0:T(8,128)(2,1)}) custom-call(s32[1]{0:T(128)} %bitcast.c_ref, bf16[4,256,1024]{2,1,0:T(8,128)(2,1)} %shard_map.143.g_ref, bf16[1280,512]{1,0:T(8,128)(2,1)} %shard_map.138.refs_0_, bf16[1280,512]{1,0:T(8,128)(2,1)} %copy-done.16), custom_call_target="tpu_custom_call" | custom-call | flops 1 | bytes 1 | tf_op jit(solution)/shard_map/pallas_call | solution.py:212
  115.6 4.2 %shard_map.146 = bf16[2,4,2,80,256]{4,3,2,1,0:T(8,128)(2,1)} custom-call(s32[3]{0:T(128)} %pad_add_fusion.3.at_ref, bf16[2,4,2,2,80,256]{5,4,3,2,1,0:T(8,128)(2,1)} %bitcast.41, bf16[4,2,2,80,256]{4,3,2,1,0:T(8,128)(2,1)} %bitcast.61, bf16[4,2,2,80,256]{4,3,2,1,0:T(8,128)(2,1)} %bitcast.65), custom_call_target="tpu_custom_call" | custom-call | flops 1 | bytes 1 | tf_op jit(solution)/shard_map/pallas_call | solution.py:396
  121.8 7.9 %collective-permute-done.15.refs_4_ = bf16[2,2,1,64,640]{4,3,2,1,0:T(8,128)(2,1)S(1)} collective-permute-done((bf16[2,2,1,64,640]{4,3,2,1,0:T(8,128)(2,1)S(1)}, bf16[2,2,1,64,640]{4,3,2,1,0:T(8,128)(2,1)S(1)}, u32[]{:S(2)}, u32[]{:S(2)}) %collective-permute-start.15) | collective-permute-done | bytes 327712 | tf_op jit(solution)/shard_map/ppermute | solution.py:499
  141.5 8.6 %shard_map.149 = (bf16[4,192,640]{2,1,0:T(8,128)(2,1)}, bf16[4,192,640]{2,1,0:T(8,128)(2,1)}, bf16[2,4,192,640]{3,2,1,0:T(8,128)(2,1)}) custom-call(s32[1]{0:T(128)} %bitcast.c_ref, bf16[2304,512]{1,0:T(8,128)(2,1)} %get-tuple-element.257.refs_0_, bf16[2304,512]{1,0:T(8,128)(2,1)} %copy-done, bf16[4,384,512]{2,1,0:T(8,128)(2,1)} %get-tuple-element.259.refs_2_, ...), custom_call_target="tpu_custom_call" | custom-call | flops 1 | bytes 1 | tf_op jit(solution)/shard_map/pallas_call | solution.py:145
  155.2 4.4 %shard_map.150 = bf16[2,4,1,96,640]{4,3,2,1,0:T(8,128)(2,1)} custom-call(s32[3]{0:T(128)} %pad_add_fusion.3.at_ref, bf16[2,4,1,2,96,640]{5,4,3,2,1,0:T(8,128)(2,1)} %bitcast.33, bf16[4,1,2,96,640]{4,3,2,1,0:T(8,128)(2,1)} %bitcast.45, bf16[4,1,2,96,640]{4,3,2,1,0:T(8,128)(2,1)} %bitcast.49), custom_call_target="tpu_custom_call" | custom-call | flops 1 | bytes 1 | tf_op jit(solution)/shard_map/pallas_call | solution.py:396
  162.7 7.8 %collective-permute-done.18.refs_5_ = bf16[2,1,1,64,640]{4,3,2,1,0:T(8,128)(2,1)S(1)} collective-permute-done((bf16[2,1,1,64,640]{4,3,2,1,0:T(8,128)(2,1)S(1)}, bf16[2,1,1,64,640]{4,3,2,1,0:T(8,128)(2,1)S(1)}, u32[]{:S(2)}, u32[]{:S(2)}) %collective-permute-start.18) | collective-permute-done | bytes 163872 | tf_op jit(solution)/shard_map/ppermute | solution.py:499
  173.9 10.1 %shard_map.152.g_ref = bf16[4,384,1024]{2,1,0:T(8,128)(2,1)} custom-call(s32[1]{0:T(128)} %constant.85.clone.1.c_ref, bf16[2304,512]{1,0:T(8,128)(2,1)} %get-tuple-element.257.refs_0_, bf16[2304,512]{1,0:T(8,128)(2,1)} %copy-done, bf16[4,384,512]{2,1,0:T(8,128)(2,1)} %get-tuple-element.259.refs_2_, bf16[4,384,512]{2,1,0:T(8,128)(2,1)} %copy-done.13, ...), custom_call_target="tpu_custom_call" | custom-call | flops 1 | bytes 1 | tf_op jit(solution)/shard_map/pallas_call | solution.py:176
  187.3 10.6 %shard_map.154 = (bf16[640,384]{1,0:T(8,128)(2,1)}, bf16[640,384]{1,0:T(8,128)(2,1)}, bf16[640,384]{1,0:T(8,128)(2,1)}, bf16[640,384]{1,0:T(8,128)(2,1)}, bf16[2,1280,384]{2,1,0:T(8,128)(2,1)}) custom-call(s32[1]{0:T(128)} %bitcast.c_ref, bf16[4,384,1024]{2,1,0:T(8,128)(2,1)} %shard_map.152.g_ref, bf16[1280,512]{1,0:T(8,128)(2,1)} %shard_map.138.refs_0_, ...), custom_call_target="tpu_custom_call" | custom-call | flops 1 | bytes 1 | tf_op jit(solution)/shard_map/pallas_call | solution.py:212
  202.9 4.8 %shard_map.155 = bf16[2,4,2,80,384]{4,3,2,1,0:T(8,128)(2,1)} custom-call(s32[3]{0:T(128)} %pad_add_fusion.3.at_ref, bf16[2,4,2,2,80,384]{5,4,3,2,1,0:T(8,128)(2,1)} %bitcast.29, bf16[2,2,2,80,384]{4,3,2,1,0:T(8,128)(2,1)} %bitcast.69, bf16[2,2,2,80,384]{4,3,2,1,0:T(8,128)(2,1)} %bitcast.73, bf16[2,2,2,80,384]{4,3,2,1,0:T(8,128)(2,1)} %bitcast.77, ...), custom_call_target="tpu_custom_call" | custom-call | flops 1 | bytes 1 | tf_op jit(solution)/shard_map/pallas_call | solution.py:396
  209.2 10.4 %collective-permute-done.21.refs_5_ = bf16[2,1,2,80,256]{4,3,2,1,0:T(8,128)(2,1)S(1)} collective-permute-done((bf16[2,1,2,80,256]{4,3,2,1,0:T(8,128)(2,1)S(1)}, bf16[2,1,2,80,256]{4,3,2,1,0:T(8,128)(2,1)S(1)}, u32[]{:S(2)}, u32[]{:S(2)}) %collective-permute-start.21) | collective-permute-done | bytes 163872 | tf_op jit(solution)/shard_map/ppermute | solution.py:499
  270.2 6.6 %collective-permute-done.33.refs_6_ = bf16[2,2,2,80,384]{4,3,2,1,0:T(8,128)(2,1)S(1)} collective-permute-done((bf16[2,2,2,80,384]{4,3,2,1,0:T(8,128)(2,1)}, bf16[2,2,2,80,384]{4,3,2,1,0:T(8,128)(2,1)S(1)}, u32[]{:S(2)}, u32[]{:S(2)}) %collective-permute-start.33) | collective-permute-done | bytes 491552 | tf_op jit(solution)/shard_map/ppermute | solution.py:499
  283.8 8.9 %shard_map.166 = (f32[640,1280]{1,0:T(8,128)}, f32[640,1280]{1,0:T(8,128)}, f32[640,1280]{1,0:T(8,128)}, f32[16,128]{1,0:T(8,128)}) custom-call(s32[1]{0:T(128)} %bitcast.c_ref, f32[640,1280]{1,0:T(8,128)} %w_ref.2, f32[640,1280]{1,0:T(8,128)} %m_ref, f32[640,1280]{1,0:T(8,128)} %v_ref, bf16[2,2,64,640]{3,2,1,0:T(8,128)(2,1)} %shard_map.159.refs_0_, ...), custom_call_target="tpu_custom_call" | custom-call | flops 1 | bytes 1 | tf_op jit(solution)/shard_map/pallas_call | solution.py:442
  312.1 5.8 %collective-permute-done.42.refs_1_ = bf16[2,2,80,384]{3,2,1,0:T(8,128)(2,1)S(1)} collective-permute-done((bf16[2,2,80,384]{3,2,1,0:T(8,128)(2,1)}, bf16[2,2,80,384]{3,2,1,0:T(8,128)(2,1)S(1)}, u32[]{:S(2)}, u32[]{:S(2)}) %collective-permute-start.42) | collective-permute-done | bytes 245792 | tf_op jit(solution)/shard_map/ppermute | solution.py:505
  324.8 11.3 %shard_map.171 = (f32[160,5120]{1,0:T(8,128)}, f32[160,5120]{1,0:T(8,128)}, f32[160,5120]{1,0:T(8,128)}, f32[16,128]{1,0:T(8,128)}) custom-call(s32[1]{0:T(128)} %bitcast.c_ref, f32[160,5120]{1,0:T(8,128)} %w_ref.3, f32[160,5120]{1,0:T(8,128)} %m_ref.1, f32[160,5120]{1,0:T(8,128)} %v_ref.1, bf16[2,2,2,80,256]{4,3,2,1,0:T(8,128)(2,1)} %shard_map.161.refs_0_, ...), custom_call_target="tpu_custom_call" | custom-call | flops 1 | bytes 1 | tf_op jit(solution)/shard_map/pallas_call | solution.py:442
  341.0 6.5 %shard_map.172 = f32[640,1280]{1,0:T(8,128)} custom-call(f32[640,1280]{1,0:T(8,128)} %w_ref.2, f32[640,1280]{1,0:T(8,128)} %get-tuple-element.361.u_ref, f32[16,128]{1,0:T(8,128)} %shard_map.168.refs_0_, f32[16,128]{1,0:T(8,128)} %copy-done.43), custom_call_target="tpu_custom_call" | custom-call | flops 1 | bytes 1 | tf_op jit(solution)/shard_map/pallas_call | solution.py:467
  354.5 6.5 %shard_map.174 = f32[160,5120]{1,0:T(8,128)} custom-call(f32[160,5120]{1,0:T(8,128)} %w_ref.3, f32[160,5120]{1,0:T(8,128)} %get-tuple-element.369.u_ref, f32[16,128]{1,0:T(8,128)} %shard_map.173.refs_0_, f32[16,128]{1,0:T(8,128)} %copy-done.44), custom_call_target="tpu_custom_call" | custom-call | flops 1 | bytes 1 | tf_op jit(solution)/shard_map/pallas_call | solution.py:467
  (227 shorter events, 166.1 us)
Async XLA Ops:
  6.3 54.4 %collective-permute-start = (bf16[2304,512]{1,0:T(8,128)(2,1)}, bf16[2304,512]{1,0:T(8,128)(2,1)S(1)}, u32[]{:S(2)}, u32[]{:S(2)}) collective-permute-start(bf16[2304,512]{1,0:T(8,128)(2,1)} %get-tuple-element.191), channel_id=1, source_target_pairs={{0,4},{4,0},{8,12},{12,8},{16,20},{20,16},{24,28},{28,24},{1,5},{5... | collective-permute-start | bytes 7077896 | tf_op jit(solution)/shard_map/ppermute | solution.py:495
  13.2 38.6 %collective-permute-start.2 = (bf16[320,1280]{1,0:T(8,128)(2,1)}, bf16[320,1280]{1,0:T(8,128)(2,1)}, u32[]{:S(2)}, u32[]{:S(2)}) collective-permute-start(bf16[320,1280]{1,0:T(8,128)(2,1)} %shard_map.137.refs_0_), channel_id=1, source_target_pairs={{0,16},{4,20},{8,24},{12,28},{16,0},{20,4},{24,8},{28,12},{1,17},{... | collective-permute-start | bytes 2457608 | tf_op jit(solution)/shard_map/ppermute | solution.py:499
  15.8 54.2 %collective-permute-start.1 = (bf16[320,1280]{1,0:T(8,128)(2,1)}, bf16[320,1280]{1,0:T(8,128)(2,1)}, u32[]{:S(2)}, u32[]{:S(2)}) collective-permute-start(bf16[320,1280]{1,0:T(8,128)(2,1)} %shard_map.137.refs_0_), channel_id=1, source_target_pairs={{0,8},{4,12},{8,0},{12,4},{16,24},{20,28},{24,16},{28,20},{1,9},{5... | collective-permute-start | bytes 2457608 | tf_op jit(solution)/shard_map/ppermute | solution.py:499
  51.8 20.0 %collective-permute-start.3 = (bf16[320,1280]{1,0:T(8,128)(2,1)}, bf16[320,1280]{1,0:T(8,128)(2,1)}, u32[]{:S(2)}, u32[]{:S(2)}) collective-permute-start(bf16[320,1280]{1,0:T(8,128)(2,1)} %collective-permute-done.2.refs_2_), channel_id=1, source_target_pairs={{0,8},{4,12},{8,0},{12,4},{16,24},{20,28},{24,16},{28,20},{1,9},{5... | collective-permute-start | bytes 2457608 | tf_op jit(solution)/shard_map/ppermute | solution.py:499
  70.0 33.1 %collective-permute-start.10 = (bf16[1280,512]{1,0:T(8,128)(2,1)}, bf16[1280,512]{1,0:T(8,128)(2,1)S(1)}, u32[]{:S(2)}, u32[]{:S(2)}) collective-permute-start(bf16[1280,512]{1,0:T(8,128)(2,1)} %shard_map.138.refs_0_), channel_id=1, source_target_pairs={{0,4},{4,0},{8,12},{12,8},{16,20},{20,16},{24,28},{28,24},{1,5},{5... | collective-permute-start | bytes 3932168 | tf_op jit(solution)/shard_map/ppermute | solution.py:495
  72.0 10.7 %collective-permute-start.5 = (bf16[320,1280]{1,0:T(8,128)(2,1)}, bf16[320,1280]{1,0:T(8,128)(2,1)}, u32[]{:S(2)}, u32[]{:S(2)}) collective-permute-start(bf16[320,1280]{1,0:T(8,128)(2,1)} %collective-permute-done.1.refs_1_), channel_id=1, source_target_pairs={{0,1},{1,0},{2,3},{3,2},{4,5},{5,4},{6,7},{7,6},{8,9},{9,8},{10,11... | collective-permute-start | bytes 2457608 | tf_op jit(solution)/shard_map/ppermute | solution.py:509
  78.6 20.8 %collective-permute-start.11 = (bf16[2,4,1,64,640]{4,3,2,1,0:T(8,128)(2,1)}, bf16[2,4,1,64,640]{4,3,2,1,0:T(8,128)(2,1)S(1)}, u32[]{:S(2)}, u32[]{:S(2)}) collective-permute-start(bf16[2,4,1,64,640]{4,3,2,1,0:T(8,128)(2,1)} %shard_map.141), channel_id=1, source_target_pairs={{0,2},{1,3},{2,0},{3,1},{4,6},{5,7},{6,4},{7,5},{8,10},{9,11},{10,... | collective-permute-start | bytes 1966088 | tf_op jit(solution)/shard_map/ppermute | solution.py:505
  80.4 59.9 %collective-permute-start.17 = (bf16[4,384,512]{2,1,0:T(8,128)(2,1)}, bf16[4,384,512]{2,1,0:T(8,128)(2,1)S(1)}, u32[]{:S(2)}, u32[]{:S(2)}) collective-permute-start(bf16[4,384,512]{2,1,0:T(8,128)(2,1)} %get-tuple-element.240), channel_id=1, source_target_pairs={{0,4},{4,0},{8,12},{12,8},{16,20},{20,16},{24,28},{28,24},{1,5},{5... | collective-permute-start | bytes 4718600 | tf_op jit(solution)/shard_map/ppermute | solution.py:495
  119.7 17.0 %collective-permute-start.14 = (bf16[2,4,2,80,256]{4,3,2,1,0:T(8,128)(2,1)}, bf16[2,4,2,80,256]{4,3,2,1,0:T(8,128)(2,1)S(1)}, u32[]{:S(2)}, u32[]{:S(2)}) collective-permute-start(bf16[2,4,2,80,256]{4,3,2,1,0:T(8,128)(2,1)} %shard_map.146), channel_id=1, source_target_pairs={{0,2},{1,3},{2,0},{3,1},{4,6},{5,7},{6,4},{7,5},{8,10},{9,11},{10,... | collective-permute-start | bytes 1966088 | tf_op jit(solution)/shard_map/ppermute | solution.py:505
  150.6 33.3 %collective-permute-start.16 = (bf16[2,2,2,80,256]{4,3,2,1,0:T(8,128)(2,1)S(1)}, bf16[2,2,2,80,256]{4,3,2,1,0:T(8,128)(2,1)S(1)}, u32[]{:S(2)}, u32[]{:S(2)}) collective-permute-start(bf16[2,2,2,80,256]{4,3,2,1,0:T(8,128)(2,1)S(1)} %copy-done.29), channel_id=1, source_target_pairs={{0,8},{4,12},{8,0},{12,4},{16,24},{20,28},{24,16},{28,20},{1,9},{5... | collective-permute-start | bytes 983048 | tf_op jit(solution)/shard_map/ppermute | solution.py:499
  159.6 63.4 %collective-permute-start.27 = (bf16[2,4,1,96,640]{4,3,2,1,0:T(8,128)(2,1)}, bf16[2,4,1,96,640]{4,3,2,1,0:T(8,128)(2,1)S(1)}, u32[]{:S(2)}, u32[]{:S(2)}) collective-permute-start(bf16[2,4,1,96,640]{4,3,2,1,0:T(8,128)(2,1)} %shard_map.150), channel_id=1, source_target_pairs={{0,2},{1,3},{2,0},{3,1},{4,6},{5,7},{6,4},{7,5},{8,10},{9,11},{10,... | collective-permute-start | bytes 2949128 | tf_op jit(solution)/shard_map/ppermute | solution.py:505
  160.2 10.4 %collective-permute-start.18 = (bf16[2,1,1,64,640]{4,3,2,1,0:T(8,128)(2,1)S(1)}, bf16[2,1,1,64,640]{4,3,2,1,0:T(8,128)(2,1)S(1)}, u32[]{:S(2)}, u32[]{:S(2)}) collective-permute-start(bf16[2,1,1,64,640]{4,3,2,1,0:T(8,128)(2,1)S(1)} %copy-done.36), channel_id=1, source_target_pairs={{0,16},{4,20},{8,24},{12,28},{16,0},{20,4},{24,8},{28,12},{1,17},{... | collective-permute-start | bytes 491528 | tf_op jit(solution)/shard_map/ppermute | solution.py:499
  207.7 52.9 %collective-permute-start.31 = (bf16[2,4,2,80,384]{4,3,2,1,0:T(8,128)(2,1)}, bf16[2,4,2,80,384]{4,3,2,1,0:T(8,128)(2,1)S(1)}, u32[]{:S(2)}, u32[]{:S(2)}) collective-permute-start(bf16[2,4,2,80,384]{4,3,2,1,0:T(8,128)(2,1)} %shard_map.155), channel_id=1, source_target_pairs={{0,2},{1,3},{2,0},{3,1},{4,6},{5,7},{6,4},{7,5},{8,10},{9,11},{10,... | collective-permute-start | bytes 2949128 | tf_op jit(solution)/shard_map/ppermute | solution.py:505
  209.2 10.4 %collective-permute-start.21 = (bf16[2,1,2,80,256]{4,3,2,1,0:T(8,128)(2,1)S(1)}, bf16[2,1,2,80,256]{4,3,2,1,0:T(8,128)(2,1)S(1)}, u32[]{:S(2)}, u32[]{:S(2)}) collective-permute-start(bf16[2,1,2,80,256]{4,3,2,1,0:T(8,128)(2,1)S(1)} %copy-done.35), channel_id=1, source_target_pairs={{0,16},{4,20},{8,24},{12,28},{16,0},{20,4},{24,8},{28,12},{1,17},{... | collective-permute-start | bytes 491528 | tf_op jit(solution)/shard_map/ppermute | solution.py:499
  226.9 12.5 %collective-permute-start.29 = (bf16[2,2,1,96,640]{4,3,2,1,0:T(8,128)(2,1)}, bf16[2,2,1,96,640]{4,3,2,1,0:T(8,128)(2,1)S(1)}, u32[]{:S(2)}, u32[]{:S(2)}) collective-permute-start(bf16[2,2,1,96,640]{4,3,2,1,0:T(8,128)(2,1)} %shard_map.157), channel_id=1, source_target_pairs={{0,8},{4,12},{8,0},{12,4},{16,24},{20,28},{24,16},{28,20},{1,9},{5... | collective-permute-start | bytes 1474568 | tf_op jit(solution)/shard_map/ppermute | solution.py:499
  243.0 12.5 %collective-permute-start.32 = (bf16[2,1,1,96,640]{4,3,2,1,0:T(8,128)(2,1)}, bf16[2,1,1,96,640]{4,3,2,1,0:T(8,128)(2,1)S(1)}, u32[]{:S(2)}, u32[]{:S(2)}) collective-permute-start(bf16[2,1,1,96,640]{4,3,2,1,0:T(8,128)(2,1)} %shard_map.160), channel_id=1, source_target_pairs={{0,16},{4,20},{8,24},{12,28},{16,0},{20,4},{24,8},{28,12},{1,17},{... | collective-permute-start | bytes 737288 | tf_op jit(solution)/shard_map/ppermute | solution.py:499
  264.6 12.2 %collective-permute-start.33 = (bf16[2,2,2,80,384]{4,3,2,1,0:T(8,128)(2,1)}, bf16[2,2,2,80,384]{4,3,2,1,0:T(8,128)(2,1)S(1)}, u32[]{:S(2)}, u32[]{:S(2)}) collective-permute-start(bf16[2,2,2,80,384]{4,3,2,1,0:T(8,128)(2,1)} %shard_map.163), channel_id=1, source_target_pairs={{0,8},{4,12},{8,0},{12,4},{16,24},{20,28},{24,16},{28,20},{1,9},{5... | collective-permute-start | bytes 1474568 | tf_op jit(solution)/shard_map/ppermute | solution.py:499
  269.7 12.7 %collective-permute-start.37 = (bf16[2,2,96,640]{3,2,1,0:T(8,128)(2,1)}, bf16[2,2,96,640]{3,2,1,0:T(8,128)(2,1)S(1)}, u32[]{:S(2)}, u32[]{:S(2)}) collective-permute-start(bf16[2,2,96,640]{3,2,1,0:T(8,128)(2,1)} %shard_map.164.refs_1_), channel_id=1, source_target_pairs={{0,1},{1,0},{2,3},{3,2},{4,5},{5,4},{6,7},{7,6},{8,9},{9,8},{10,11... | collective-permute-start | bytes 1474568 | tf_op jit(solution)/shard_map/ppermute | solution.py:509
  269.7 12.7 %collective-permute-start.36 = (bf16[2,2,64,640]{3,2,1,0:T(8,128)(2,1)S(1)}, bf16[2,2,64,640]{3,2,1,0:T(8,128)(2,1)S(1)}, u32[]{:S(2)}, u32[]{:S(2)}) collective-permute-start(bf16[2,2,64,640]{3,2,1,0:T(8,128)(2,1)S(1)} %copy-done.20), channel_id=1, source_target_pairs={{0,1},{1,0},{2,3},{3,2},{4,5},{5,4},{6,7},{7,6},{8,9},{9,8},{10,11... | collective-permute-start | bytes 983048 | tf_op jit(solution)/shard_map/ppermute | solution.py:509
  280.5 12.6 %collective-permute-start.35 = (bf16[2,1,2,80,384]{4,3,2,1,0:T(8,128)(2,1)}, bf16[2,1,2,80,384]{4,3,2,1,0:T(8,128)(2,1)S(1)}, u32[]{:S(2)}, u32[]{:S(2)}) collective-permute-start(bf16[2,1,2,80,384]{4,3,2,1,0:T(8,128)(2,1)} %shard_map.165), channel_id=1, source_target_pairs={{0,16},{4,20},{8,24},{12,28},{16,0},{20,4},{24,8},{28,12},{1,17},{... | collective-permute-start | bytes 737288 | tf_op jit(solution)/shard_map/ppermute | solution.py:499
  297.0 11.4 %collective-permute-start.38 = (bf16[2,80,384]{2,1,0:T(8,128)(2,1)}, bf16[2,80,384]{2,1,0:T(8,128)(2,1)S(1)}, u32[]{:S(2)}, u32[]{:S(2)}) collective-permute-start(bf16[2,80,384]{2,1,0:T(8,128)(2,1)} %get-tuple-element.341), channel_id=1, source_target_pairs={{0,4},{4,0},{8,12},{12,8},{16,20},{20,16},{24,28},{28,24},{1,5},{5... | collective-permute-start | bytes 368648 | tf_op jit(solution)/shard_map/ppermute | solution.py:495
  321.6 18.8 %collective-permute-start.48 = (f32[16,128]{1,0:T(8,128)}, f32[16,128]{1,0:T(8,128)S(1)}, u32[]{:S(2)}, u32[]{:S(2)}) collective-permute-start(f32[16,128]{1,0:T(8,128)} %shard_map.168.refs_0_), channel_id=1, source_target_pairs={{0,4},{4,0},{8,12},{12,8},{16,20},{20,16},{24,28},{28,24},{1,5},{5... | collective-permute-start | bytes 24584 | tf_op jit(solution)/shard_map/ppermute | solution.py:495
  336.0 11.5 %collective-permute-start.47 = (f32[16,128]{1,0:T(8,128)}, f32[16,128]{1,0:T(8,128)S(1)}, u32[]{:S(2)}, u32[]{:S(2)}) collective-permute-start(f32[16,128]{1,0:T(8,128)} %get-tuple-element.364.refs_0_), channel_id=1, source_target_pairs={{0,24},{4,28},{8,16},{12,20},{16,8},{20,12},{24,0},{28,4},{1,25},{... | collective-permute-start | bytes 24584 | tf_op jit(solution)/shard_map/ppermute | solution.py:499
  337.7 9.8 %collective-permute-start.46 = (f32[16,128]{1,0:T(8,128)}, f32[16,128]{1,0:T(8,128)S(1)}, u32[]{:S(2)}, u32[]{:S(2)}) collective-permute-start(f32[16,128]{1,0:T(8,128)} %get-tuple-element.364.refs_0_), channel_id=1, source_target_pairs={{0,16},{4,20},{8,24},{12,28},{16,0},{20,4},{24,8},{28,12},{1,17},{... | collective-permute-start | bytes 24584 | tf_op jit(solution)/shard_map/ppermute | solution.py:499
  (79 other events, 278.9 us)

commit v4 on v3

--- a/solution.py
+++ b/solution.py
@@ -14,7 +14,7 @@
 CHIPS_Z = 4
 LANES = 128
 PARTS = 2
-VMEM = 56 * 1024 * 1024
+VMEM = 24 * 1024 * 1024
 
 
 def moments(weight, first, second, grad):

time: 363 us -> 305 us (0.84)
  Pallas kernels: 182 us -> 99.4 us
  waiting for transfers between devices: 106 us -> 140 us
  local copies, waits for them, and re-layouts: 25.5 us -> 17 us
    pallas_call x16, Pallas kernels: 51.6 us -> 25.6 us  [reduce_step(): pl.pallas_call(body, grid_spec=pltpu.PrefetchScalarGridSpec(num_scalar_pr...]
    ppermute x8, waiting for transfers between devices: 15.2 us -> 29.5 us  [along_y(): return lax.ppermute(value, 'gy', pairs)]
    ppermute x17, waiting for transfers between devices: 65.4 us -> 79.1 us  [along_z(): return lax.ppermute(value, 'gx', pairs)]
    pallas_call x6, Pallas kernels: 14.6 us -> 3.42 us  [stack(): pl.pallas_call(body, grid_spec=pltpu.PrefetchScalarGridSpec(num_scalar_pr...]
    ppermute x7, waiting for transfers between devices: 14.1 us -> 23.1 us  [along_x(): return lax.ppermute(value, 'gx', pairs)]
    pallas_call x2, Pallas kernels: 20.1 us -> 11.6 us  [moments_kernel(): pl.pallas_call(body, grid_spec=pltpu.PrefetchScalarGridSpec(num_scalar_pr...]
    unnamed x106 -> x78, local copies, waits for them, and re-layouts: 25.4 us -> 16.8 us
    pallas_call x2, Pallas kernels: 18.6 us -> 11.3 us  [grad_pre_chunk(): pl.pallas_call(body, grid_spec=pltpu.PrefetchScalarGridSpec(num_scalar_pr...]
  transfers between devices with their start and end apart: 50 -> 50, of which waited for: 28 -> 30; matrix products, arithmetic and copies ran while one was open for 1% -> 0% of each run, Pallas kernels for 42% -> 27%
where the time goes in v4:
time: 305 us; the launch traced here: 304 us
  waiting for transfers between devices  140 us (46%)
  Pallas kernels  99.4 us (33%)
  starting transfers between devices  45.9 us (15%)
  local copies, waits for them, and re-layouts  17 us (6%)
    ppermute x17, waiting for transfers between devices, along_z(): return lax.ppermute(value, 'gx', pairs)  79.1 us
    ppermute x8, waiting for transfers between devices, along_y(): return lax.ppermute(value, 'gy', pairs)  29.5 us
    pallas_call x16, Pallas kernels, reduce_step(): pl.pallas_call(body, grid_spec=pltpu.PrefetchScalarGridSpec(num_scalar_pr...  25.6 us
    ppermute x7, waiting for transfers between devices, along_x(): return lax.ppermute(value, 'gx', pairs)  23.1 us
    ppermute x17, starting transfers between devices, along_z(): return lax.ppermute(value, 'gx', pairs)  20.9 us
    unnamed x78, local copies, waits for them, and re-layouts  16.8 us
    pallas_call x2, Pallas kernels, grad_in_chunk(): pl.pallas_call(body, grid_spec=pltpu.PrefetchScalarGridSpec(num_scalar_pr...  14.5 us
    pallas_call x2, Pallas kernels, moments_kernel(): pl.pallas_call(body, grid_spec=pltpu.PrefetchScalarGridSpec(num_scalar_pr...  11.6 us
  transfers between devices with their start and end apart: 50, of which 30 were waited for; matrix products, arithmetic and copies ran while one was open for 0% of the time, Pallas kernels for 27%

profile of v4, /device:TPU:0, one launch (start us, length us, event | category | flops | bytes accessed | tf_op | source)
XLA Modules:
  0.0 303.9 jit_solution(12355106786304417653)
XLA Ops:
  24.7 28.9 %collective-permute-done.2.refs_2_ = bf16[320,1280]{1,0:T(8,128)(2,1)} collective-permute-done((bf16[320,1280]{1,0:T(8,128)(2,1)}, bf16[320,1280]{1,0:T(8,128)(2,1)}, u32[]{:S(2)}, u32[]{:S(2)}) %collective-permute-start.2) | collective-permute-done | bytes 819232 | tf_op jit(solution)/shard_map/ppermute | solution.py:499
  54.1 8.2 %collective-permute-done.refs_1_ = bf16[2304,512]{1,0:T(8,128)(2,1)S(1)} collective-permute-done((bf16[2304,512]{1,0:T(8,128)(2,1)}, bf16[2304,512]{1,0:T(8,128)(2,1)S(1)}, u32[]{:S(2)}, u32[]{:S(2)}) %collective-permute-start) | collective-permute-done | bytes 2359328 | tf_op jit(solution)/shard_map/ppermute | solution.py:495
  62.3 4.3 %shard_map.140 = (bf16[4,128,640]{2,1,0:T(8,128)(2,1)S(1)}, bf16[4,128,640]{2,1,0:T(8,128)(2,1)S(1)}, bf16[2,4,128,640]{3,2,1,0:T(8,128)(2,1)S(1)}) custom-call(s32[1]{0:T(128)} %bitcast.c_ref, bf16[2304,512]{1,0:T(8,128)(2,1)S(1)} %get-tuple-element.257.refs_0_, bf16[2304,512]{1,0:T(8,128)(2,1)S(1)} %collective-permute-done.refs_1_), custom_call_target="tpu_custom_call" | custom-call | flops 1 | bytes 1 | tf_op jit(solution)/shard_map/pallas_call | solution.py:145
  82.2 5.3 %shard_map.142.refs_2_.refs_4_ = bf16[4,640,1280]{2,1,0:T(8,128)(2,1)S(1)} custom-call(s32[2,8]{1,0:T(2,128)S(1)} %pad_add_fusion.at_ref, bf16[320,1280]{1,0:T(8,128)(2,1)} %shard_map.137.refs_0_, bf16[320,1280]{1,0:T(8,128)(2,1)} %collective-permute-done.1.refs_1_, bf16[320,1280]{1,0:T(8,128)(2,1)} %collective-permute-done.2.refs_2_, ...), custom_call_target="tpu_custom_call" | custom-call | flops 1 | bytes 1 | tf_op jit(solution)/shard_map/pallas_call | solution.py:308
  87.6 4.2 %shard_map.143.g_ref = bf16[4,256,1024]{2,1,0:T(8,128)(2,1)S(1)} custom-call(s32[1]{0:T(128)} %constant.85.clone.1.c_ref, bf16[2304,512]{1,0:T(8,128)(2,1)S(1)} %copy-done.1, bf16[2304,512]{1,0:T(8,128)(2,1)S(1)} %collective-permute-done.refs_1_, bf16[4,640,1280]{2,1,0:T(8,128)(2,1)S(1)} %shard_map.142.refs_2_.refs_4_), custom_call_target="tpu_custom_call" | custom-call | flops 1 | bytes 1 | tf_op jit(solution)/shard_map/pallas_call | solution.py:176
  91.8 4.6 %collective-permute-done.11.refs_3_ = bf16[2,4,1,64,640]{4,3,2,1,0:T(8,128)(2,1)} collective-permute-done((bf16[2,4,1,64,640]{4,3,2,1,0:T(8,128)(2,1)}, bf16[2,4,1,64,640]{4,3,2,1,0:T(8,128)(2,1)}, u32[]{:S(2)}, u32[]{:S(2)}) %collective-permute-start.11) | collective-permute-done | bytes 655392 | tf_op jit(solution)/shard_map/ppermute | solution.py:505
  101.5 5.8 %shard_map.145 = (bf16[1280,256]{1,0:T(8,128)(2,1)S(1)}, bf16[1280,256]{1,0:T(8,128)(2,1)S(1)}, bf16[2,1280,256]{2,1,0:T(8,128)(2,1)S(1)}) custom-call(s32[1]{0:T(128)} %bitcast.c_ref, bf16[4,256,1024]{2,1,0:T(8,128)(2,1)S(1)} %shard_map.143.g_ref, bf16[1280,512]{1,0:T(8,128)(2,1)} %shard_map.138.refs_0_, bf16[1280,512]{1,0:T(8,128)(2,1)} %collective-permute-done.10.refs_1_), custom_call_target="tpu_custom_call" | custom-call | flops 1 | bytes 1 | tf_op jit(solution)/shard_map/pallas_call | solution.py:212
  114.9 7.9 %collective-permute-done.15.refs_4_ = bf16[2,2,1,64,640]{4,3,2,1,0:T(8,128)(2,1)S(1)} collective-permute-done((bf16[2,2,1,64,640]{4,3,2,1,0:T(8,128)(2,1)S(1)}, bf16[2,2,1,64,640]{4,3,2,1,0:T(8,128)(2,1)S(1)}, u32[]{:S(2)}, u32[]{:S(2)}) %collective-permute-start.15) | collective-permute-done | bytes 327712 | tf_op jit(solution)/shard_map/ppermute | solution.py:499
  124.4 3.9 %collective-permute-done.14.refs_3_ = bf16[2,4,2,80,256]{4,3,2,1,0:T(8,128)(2,1)S(1)} collective-permute-done((bf16[2,4,2,80,256]{4,3,2,1,0:T(8,128)(2,1)S(1)}, bf16[2,4,2,80,256]{4,3,2,1,0:T(8,128)(2,1)S(1)}, u32[]{:S(2)}, u32[]{:S(2)}) %collective-permute-start.14) | collective-permute-done | bytes 655392 | tf_op jit(solution)/shard_map/ppermute | solution.py:505
  129.4 5.5 %collective-permute-done.17.refs_3_ = bf16[4,384,512]{2,1,0:T(8,128)(2,1)} collective-permute-done((bf16[4,384,512]{2,1,0:T(8,128)(2,1)}, bf16[4,384,512]{2,1,0:T(8,128)(2,1)}, u32[]{:S(2)}, u32[]{:S(2)}) %collective-permute-start.17) | collective-permute-done | bytes 1572896 | tf_op jit(solution)/shard_map/ppermute | solution.py:495
  134.8 7.0 %shard_map.149 = (bf16[4,192,640]{2,1,0:T(8,128)(2,1)S(1)}, bf16[4,192,640]{2,1,0:T(8,128)(2,1)S(1)}, bf16[2,4,192,640]{3,2,1,0:T(8,128)(2,1)S(1)}) custom-call(s32[1]{0:T(128)} %bitcast.c_ref, bf16[2304,512]{1,0:T(8,128)(2,1)S(1)} %copy-done.1, bf16[2304,512]{1,0:T(8,128)(2,1)S(1)} %collective-permute-done.refs_1_, bf16[4,384,512]{2,1,0:T(8,128)(2,1)S(1)} %copy-done.31, ...), custom_call_target="tpu_custom_call" | custom-call | flops 1 | bytes 1 | tf_op jit(solution)/shard_map/pallas_call | solution.py:145
  151.4 7.8 %collective-permute-done.18.refs_5_ = bf16[2,1,1,64,640]{4,3,2,1,0:T(8,128)(2,1)S(1)} collective-permute-done((bf16[2,1,1,64,640]{4,3,2,1,0:T(8,128)(2,1)S(1)}, bf16[2,1,1,64,640]{4,3,2,1,0:T(8,128)(2,1)S(1)}, u32[]{:S(2)}, u32[]{:S(2)}) %collective-permute-start.18) | collective-permute-done | bytes 163872 | tf_op jit(solution)/shard_map/ppermute | solution.py:499
  160.8 7.1 %shard_map.152.g_ref = bf16[4,384,1024]{2,1,0:T(8,128)(2,1)S(1)} custom-call(s32[1]{0:T(128)} %constant.85.clone.1.c_ref, bf16[2304,512]{1,0:T(8,128)(2,1)S(1)} %copy-done.1, bf16[2304,512]{1,0:T(8,128)(2,1)S(1)} %collective-permute-done.refs_1_, bf16[4,384,512]{2,1,0:T(8,128)(2,1)S(1)} %copy-done.31, bf16[4,384,512]{2,1,0:T(8,128)(2,1)} %collective-permute-done.17.refs_3_, ...), custom_call_target="tpu_custom_call" | custom-call | flops 1 | bytes 1 | tf_op jit(solution)/shard_map/pallas_call | solution.py:176
  168.6 8.7 %shard_map.154 = (bf16[640,384]{1,0:T(8,128)(2,1)S(1)}, bf16[640,384]{1,0:T(8,128)(2,1)S(1)}, bf16[640,384]{1,0:T(8,128)(2,1)S(1)}, bf16[640,384]{1,0:T(8,128)(2,1)S(1)}, bf16[2,1280,384]{2,1,0:T(8,128)(2,1)S(1)}) custom-call(s32[1]{0:T(128)} %bitcast.c_ref, bf16[4,384,1024]{2,1,0:T(8,128)(2,1)S(1)} %shard_map.152.g_ref, ...), custom_call_target="tpu_custom_call" | custom-call | flops 1 | bytes 1 | tf_op jit(solution)/shard_map/pallas_call | solution.py:212
  184.9 10.1 %collective-permute-done.21.refs_5_ = bf16[2,1,2,80,256]{4,3,2,1,0:T(8,128)(2,1)S(1)} collective-permute-done((bf16[2,1,2,80,256]{4,3,2,1,0:T(8,128)(2,1)S(1)}, bf16[2,1,2,80,256]{4,3,2,1,0:T(8,128)(2,1)S(1)}, u32[]{:S(2)}, u32[]{:S(2)}) %collective-permute-start.21) | collective-permute-done | bytes 163872 | tf_op jit(solution)/shard_map/ppermute | solution.py:499
  204.1 7.6 %collective-permute-done.30.refs_1_ = bf16[2,64,640]{2,1,0:T(8,128)(2,1)S(1)} collective-permute-done((bf16[2,64,640]{2,1,0:T(8,128)(2,1)S(1)}, bf16[2,64,640]{2,1,0:T(8,128)(2,1)S(1)}, u32[]{:S(2)}, u32[]{:S(2)}) %collective-permute-start.30) | collective-permute-done | bytes 163872 | tf_op jit(solution)/shard_map/ppermute | solution.py:505
  218.8 4.7 %collective-permute-done.28.refs_1_ = bf16[2,2,80,256]{3,2,1,0:T(8,128)(2,1)S(1)} collective-permute-done((bf16[2,2,80,256]{3,2,1,0:T(8,128)(2,1)S(1)}, bf16[2,2,80,256]{3,2,1,0:T(8,128)(2,1)S(1)}, u32[]{:S(2)}, u32[]{:S(2)}) %collective-permute-start.28) | collective-permute-done | bytes 163872 | tf_op jit(solution)/shard_map/ppermute | solution.py:505
  224.1 7.3 %collective-permute-done.32.refs_5_ = bf16[2,1,1,96,640]{4,3,2,1,0:T(8,128)(2,1)S(1)} collective-permute-done((bf16[2,1,1,96,640]{4,3,2,1,0:T(8,128)(2,1)S(1)}, bf16[2,1,1,96,640]{4,3,2,1,0:T(8,128)(2,1)S(1)}, u32[]{:S(2)}, u32[]{:S(2)}) %collective-permute-start.32) | collective-permute-done | bytes 245792 | tf_op jit(solution)/shard_map/ppermute | solution.py:499
  236.2 3.9 %collective-permute-done.34.refs_1_ = bf16[2,96,640]{2,1,0:T(8,128)(2,1)S(1)} collective-permute-done((bf16[2,96,640]{2,1,0:T(8,128)(2,1)S(1)}, bf16[2,96,640]{2,1,0:T(8,128)(2,1)S(1)}, u32[]{:S(2)}, u32[]{:S(2)}) %collective-permute-start.34) | collective-permute-done | bytes 245792 | tf_op jit(solution)/shard_map/ppermute | solution.py:505
  241.2 6.9 %collective-permute-done.33.refs_6_ = bf16[2,2,2,80,384]{4,3,2,1,0:T(8,128)(2,1)S(1)} collective-permute-done((bf16[2,2,2,80,384]{4,3,2,1,0:T(8,128)(2,1)S(1)}, bf16[2,2,2,80,384]{4,3,2,1,0:T(8,128)(2,1)S(1)}, u32[]{:S(2)}, u32[]{:S(2)}) %collective-permute-start.33) | collective-permute-done | bytes 491552 | tf_op jit(solution)/shard_map/ppermute | solution.py:499
  250.9 5.4 %shard_map.166 = (f32[640,1280]{1,0:T(8,128)}, f32[640,1280]{1,0:T(8,128)}, f32[640,1280]{1,0:T(8,128)S(1)}, f32[16,128]{1,0:T(8,128)S(1)}) custom-call(s32[1]{0:T(128)} %bitcast.c_ref, f32[640,1280]{1,0:T(8,128)S(1)} %copy-done.6, f32[640,1280]{1,0:T(8,128)S(1)} %copy-done.34, f32[640,1280]{1,0:T(8,128)S(1)} %copy-done.35, ...), custom_call_target="tpu_custom_call" | custom-call | flops 1 | bytes 1 | tf_op jit(solution)/shard_map/pallas_call | solution.py:442
  256.3 5.6 %collective-permute-done.35.refs_7_ = bf16[2,1,2,80,384]{4,3,2,1,0:T(8,128)(2,1)S(1)} collective-permute-done((bf16[2,1,2,80,384]{4,3,2,1,0:T(8,128)(2,1)S(1)}, bf16[2,1,2,80,384]{4,3,2,1,0:T(8,128)(2,1)S(1)}, u32[]{:S(2)}, u32[]{:S(2)}) %collective-permute-start.35) | collective-permute-done | bytes 245792 | tf_op jit(solution)/shard_map/ppermute | solution.py:499
  275.3 4.8 %collective-permute-done.42.refs_1_ = bf16[2,2,80,384]{3,2,1,0:T(8,128)(2,1)S(1)} collective-permute-done((bf16[2,2,80,384]{3,2,1,0:T(8,128)(2,1)S(1)}, bf16[2,2,80,384]{3,2,1,0:T(8,128)(2,1)S(1)}, u32[]{:S(2)}, u32[]{:S(2)}) %collective-permute-start.42) | collective-permute-done | bytes 245792 | tf_op jit(solution)/shard_map/ppermute | solution.py:505
  283.1 6.2 %shard_map.171 = (f32[160,5120]{1,0:T(8,128)}, f32[160,5120]{1,0:T(8,128)}, f32[160,5120]{1,0:T(8,128)S(1)}, f32[16,128]{1,0:T(8,128)S(1)}) custom-call(s32[1]{0:T(128)} %bitcast.c_ref, f32[160,5120]{1,0:T(8,128)S(1)} %copy-done.14, f32[160,5120]{1,0:T(8,128)S(1)} %copy-done.36, f32[160,5120]{1,0:T(8,128)S(1)} %copy-done.37, ...), custom_call_target="tpu_custom_call" | custom-call | flops 1 | bytes 1 | tf_op jit(solution)/shard_map/pallas_call | solution.py:442
  (199 shorter events, 131.0 us)
Async XLA Ops:
  7.9 54.4 %collective-permute-start = (bf16[2304,512]{1,0:T(8,128)(2,1)}, bf16[2304,512]{1,0:T(8,128)(2,1)S(1)}, u32[]{:S(2)}, u32[]{:S(2)}) collective-permute-start(bf16[2304,512]{1,0:T(8,128)(2,1)} %get-tuple-element.191), channel_id=1, source_target_pairs={{0,4},{4,0},{8,12},{12,8},{16,20},{20,16},{24,28},{28,24},{1,5},{5... | collective-permute-start | bytes 7077896 | tf_op jit(solution)/shard_map/ppermute | solution.py:495
  15.0 38.6 %collective-permute-start.2 = (bf16[320,1280]{1,0:T(8,128)(2,1)}, bf16[320,1280]{1,0:T(8,128)(2,1)}, u32[]{:S(2)}, u32[]{:S(2)}) collective-permute-start(bf16[320,1280]{1,0:T(8,128)(2,1)} %shard_map.137.refs_0_), channel_id=1, source_target_pairs={{0,16},{4,20},{8,24},{12,28},{16,0},{20,4},{24,8},{28,12},{1,17},{... | collective-permute-start | bytes 2457608 | tf_op jit(solution)/shard_map/ppermute | solution.py:499
  17.5 52.1 %collective-permute-start.1 = (bf16[320,1280]{1,0:T(8,128)(2,1)}, bf16[320,1280]{1,0:T(8,128)(2,1)}, u32[]{:S(2)}, u32[]{:S(2)}) collective-permute-start(bf16[320,1280]{1,0:T(8,128)(2,1)} %shard_map.137.refs_0_), channel_id=1, source_target_pairs={{0,8},{4,12},{8,0},{12,4},{16,24},{20,28},{24,16},{28,20},{1,9},{5... | collective-permute-start | bytes 2457608 | tf_op jit(solution)/shard_map/ppermute | solution.py:499
  53.5 19.4 %collective-permute-start.3 = (bf16[320,1280]{1,0:T(8,128)(2,1)}, bf16[320,1280]{1,0:T(8,128)(2,1)}, u32[]{:S(2)}, u32[]{:S(2)}) collective-permute-start(bf16[320,1280]{1,0:T(8,128)(2,1)} %collective-permute-done.2.refs_2_), channel_id=1, source_target_pairs={{0,8},{4,12},{8,0},{12,4},{16,24},{20,28},{24,16},{28,20},{1,9},{5... | collective-permute-start | bytes 2457608 | tf_op jit(solution)/shard_map/ppermute | solution.py:499
  69.6 9.4 %collective-permute-start.4 = (bf16[320,1280]{1,0:T(8,128)(2,1)}, bf16[320,1280]{1,0:T(8,128)(2,1)}, u32[]{:S(2)}, u32[]{:S(2)}) collective-permute-start(bf16[320,1280]{1,0:T(8,128)(2,1)} %shard_map.137.refs_0_), channel_id=1, source_target_pairs={{0,1},{1,0},{2,3},{3,2},{4,5},{5,4},{6,7},{7,6},{8,9},{9,8},{10,11... | collective-permute-start | bytes 2457608 | tf_op jit(solution)/shard_map/ppermute | solution.py:509
  69.6 31.9 %collective-permute-start.10 = (bf16[1280,512]{1,0:T(8,128)(2,1)}, bf16[1280,512]{1,0:T(8,128)(2,1)}, u32[]{:S(2)}, u32[]{:S(2)}) collective-permute-start(bf16[1280,512]{1,0:T(8,128)(2,1)} %shard_map.138.refs_0_), channel_id=1, source_target_pairs={{0,4},{4,0},{8,12},{12,8},{16,20},{20,16},{24,28},{28,24},{1,5},{5... | collective-permute-start | bytes 3932168 | tf_op jit(solution)/shard_map/ppermute | solution.py:495
  72.9 9.3 %collective-permute-start.5 = (bf16[320,1280]{1,0:T(8,128)(2,1)}, bf16[320,1280]{1,0:T(8,128)(2,1)}, u32[]{:S(2)}, u32[]{:S(2)}) collective-permute-start(bf16[320,1280]{1,0:T(8,128)(2,1)} %collective-permute-done.1.refs_1_), channel_id=1, source_target_pairs={{0,1},{1,0},{2,3},{3,2},{4,5},{5,4},{6,7},{7,6},{8,9},{9,8},{10,11... | collective-permute-start | bytes 2457608 | tf_op jit(solution)/shard_map/ppermute | solution.py:509
  79.0 17.3 %collective-permute-start.11 = (bf16[2,4,1,64,640]{4,3,2,1,0:T(8,128)(2,1)}, bf16[2,4,1,64,640]{4,3,2,1,0:T(8,128)(2,1)}, u32[]{:S(2)}, u32[]{:S(2)}) collective-permute-start(bf16[2,4,1,64,640]{4,3,2,1,0:T(8,128)(2,1)} %shard_map.141), channel_id=1, source_target_pairs={{0,2},{1,3},{2,0},{3,1},{4,6},{5,7},{6,4},{7,5},{8,10},{9,11},{10,... | collective-permute-start | bytes 1966088 | tf_op jit(solution)/shard_map/ppermute | solution.py:505
  80.6 54.3 %collective-permute-start.17 = (bf16[4,384,512]{2,1,0:T(8,128)(2,1)}, bf16[4,384,512]{2,1,0:T(8,128)(2,1)}, u32[]{:S(2)}, u32[]{:S(2)}) collective-permute-start(bf16[4,384,512]{2,1,0:T(8,128)(2,1)} %get-tuple-element.240), channel_id=1, source_target_pairs={{0,4},{4,0},{8,12},{12,8},{16,20},{20,16},{24,28},{28,24},{1,5},{5... | collective-permute-start | bytes 4718600 | tf_op jit(solution)/shard_map/ppermute | solution.py:495
  111.5 16.9 %collective-permute-start.14 = (bf16[2,4,2,80,256]{4,3,2,1,0:T(8,128)(2,1)S(1)}, bf16[2,4,2,80,256]{4,3,2,1,0:T(8,128)(2,1)S(1)}, u32[]{:S(2)}, u32[]{:S(2)}) collective-permute-start(bf16[2,4,2,80,256]{4,3,2,1,0:T(8,128)(2,1)S(1)} %shard_map.146), channel_id=1, source_target_pairs={{0,2},{1,3},{2,0},{3,1},{4,6},{5,7},{6,4},{7,5},{8,10},{9,11},{10,... | collective-permute-start | bytes 1966088 | tf_op jit(solution)/shard_map/ppermute | solution.py:505
  113.3 9.5 %collective-permute-start.15 = (bf16[2,2,1,64,640]{4,3,2,1,0:T(8,128)(2,1)S(1)}, bf16[2,2,1,64,640]{4,3,2,1,0:T(8,128)(2,1)S(1)}, u32[]{:S(2)}, u32[]{:S(2)}) collective-permute-start(bf16[2,2,1,64,640]{4,3,2,1,0:T(8,128)(2,1)S(1)} %shard_map.144), channel_id=1, source_target_pairs={{0,8},{4,12},{8,0},{12,4},{16,24},{20,28},{24,16},{28,20},{1,9},{5... | collective-permute-start | bytes 983048 | tf_op jit(solution)/shard_map/ppermute | solution.py:499
  142.4 25.5 %collective-permute-start.16 = (bf16[2,2,2,80,256]{4,3,2,1,0:T(8,128)(2,1)S(1)}, bf16[2,2,2,80,256]{4,3,2,1,0:T(8,128)(2,1)S(1)}, u32[]{:S(2)}, u32[]{:S(2)}) collective-permute-start(bf16[2,2,2,80,256]{4,3,2,1,0:T(8,128)(2,1)S(1)} %shard_map.148), channel_id=1, source_target_pairs={{0,8},{4,12},{8,0},{12,4},{16,24},{20,28},{24,16},{28,20},{1,9},{5... | collective-permute-start | bytes 983048 | tf_op jit(solution)/shard_map/ppermute | solution.py:499
  147.0 48.8 %collective-permute-start.27 = (bf16[2,4,1,96,640]{4,3,2,1,0:T(8,128)(2,1)S(1)}, bf16[2,4,1,96,640]{4,3,2,1,0:T(8,128)(2,1)S(1)}, u32[]{:S(2)}, u32[]{:S(2)}) collective-permute-start(bf16[2,4,1,96,640]{4,3,2,1,0:T(8,128)(2,1)S(1)} %shard_map.150), channel_id=1, source_target_pairs={{0,2},{1,3},{2,0},{3,1},{4,6},{5,7},{6,4},{7,5},{8,10},{9,11},{10,... | collective-permute-start | bytes 2949128 | tf_op jit(solution)/shard_map/ppermute | solution.py:505
  148.9 10.4 %collective-permute-start.18 = (bf16[2,1,1,64,640]{4,3,2,1,0:T(8,128)(2,1)S(1)}, bf16[2,1,1,64,640]{4,3,2,1,0:T(8,128)(2,1)S(1)}, u32[]{:S(2)}, u32[]{:S(2)}) collective-permute-start(bf16[2,1,1,64,640]{4,3,2,1,0:T(8,128)(2,1)S(1)} %shard_map.147), channel_id=1, source_target_pairs={{0,16},{4,20},{8,24},{12,28},{16,0},{20,4},{24,8},{28,12},{1,17},{... | collective-permute-start | bytes 491528 | tf_op jit(solution)/shard_map/ppermute | solution.py:499
  184.2 49.6 %collective-permute-start.31 = (bf16[2,4,2,80,384]{4,3,2,1,0:T(8,128)(2,1)}, bf16[2,4,2,80,384]{4,3,2,1,0:T(8,128)(2,1)}, u32[]{:S(2)}, u32[]{:S(2)}) collective-permute-start(bf16[2,4,2,80,384]{4,3,2,1,0:T(8,128)(2,1)} %shard_map.155), channel_id=1, source_target_pairs={{0,2},{1,3},{2,0},{3,1},{4,6},{5,7},{6,4},{7,5},{8,10},{9,11},{10,... | collective-permute-start | bytes 2949128 | tf_op jit(solution)/shard_map/ppermute | solution.py:505
  184.7 10.4 %collective-permute-start.21 = (bf16[2,1,2,80,256]{4,3,2,1,0:T(8,128)(2,1)S(1)}, bf16[2,1,2,80,256]{4,3,2,1,0:T(8,128)(2,1)S(1)}, u32[]{:S(2)}, u32[]{:S(2)}) collective-permute-start(bf16[2,1,2,80,256]{4,3,2,1,0:T(8,128)(2,1)S(1)} %shard_map.153), channel_id=1, source_target_pairs={{0,16},{4,20},{8,24},{12,28},{16,0},{20,4},{24,8},{28,12},{1,17},{... | collective-permute-start | bytes 491528 | tf_op jit(solution)/shard_map/ppermute | solution.py:499
  197.5 14.7 %collective-permute-start.29 = (bf16[2,2,1,96,640]{4,3,2,1,0:T(8,128)(2,1)}, bf16[2,2,1,96,640]{4,3,2,1,0:T(8,128)(2,1)}, u32[]{:S(2)}, u32[]{:S(2)}) collective-permute-start(bf16[2,2,1,96,640]{4,3,2,1,0:T(8,128)(2,1)} %shard_map.157), channel_id=1, source_target_pairs={{0,8},{4,12},{8,0},{12,4},{16,24},{20,28},{24,16},{28,20},{1,9},{5... | collective-permute-start | bytes 1474568 | tf_op jit(solution)/shard_map/ppermute | solution.py:499
  197.5 14.2 %collective-permute-start.30 = (bf16[2,64,640]{2,1,0:T(8,128)(2,1)S(1)}, bf16[2,64,640]{2,1,0:T(8,128)(2,1)S(1)}, u32[]{:S(2)}, u32[]{:S(2)}) collective-permute-start(bf16[2,64,640]{2,1,0:T(8,128)(2,1)S(1)} %shard_map.151.refs_0_), channel_id=1, source_target_pairs={{0,2},{1,3},{2,0},{3,1},{4,6},{5,7},{6,4},{7,5},{8,10},{9,11},{10,... | collective-permute-start | bytes 491528 | tf_op jit(solution)/shard_map/ppermute | solution.py:505
  218.0 13.4 %collective-permute-start.32 = (bf16[2,1,1,96,640]{4,3,2,1,0:T(8,128)(2,1)S(1)}, bf16[2,1,1,96,640]{4,3,2,1,0:T(8,128)(2,1)S(1)}, u32[]{:S(2)}, u32[]{:S(2)}) collective-permute-start(bf16[2,1,1,96,640]{4,3,2,1,0:T(8,128)(2,1)S(1)} %shard_map.160), channel_id=1, source_target_pairs={{0,16},{4,20},{8,24},{12,28},{16,0},{20,4},{24,8},{28,12},{1,17},{... | collective-permute-start | bytes 737288 | tf_op jit(solution)/shard_map/ppermute | solution.py:499
  236.2 12.0 %collective-permute-start.33 = (bf16[2,2,2,80,384]{4,3,2,1,0:T(8,128)(2,1)S(1)}, bf16[2,2,2,80,384]{4,3,2,1,0:T(8,128)(2,1)S(1)}, u32[]{:S(2)}, u32[]{:S(2)}) collective-permute-start(bf16[2,2,2,80,384]{4,3,2,1,0:T(8,128)(2,1)S(1)} %shard_map.163), channel_id=1, source_target_pairs={{0,8},{4,12},{8,0},{12,4},{16,24},{20,28},{24,16},{28,20},{1,9},{5... | collective-permute-start | bytes 1474568 | tf_op jit(solution)/shard_map/ppermute | solution.py:499
  240.7 10.2 %collective-permute-start.37 = (bf16[2,2,96,640]{3,2,1,0:T(8,128)(2,1)S(1)}, bf16[2,2,96,640]{3,2,1,0:T(8,128)(2,1)S(1)}, u32[]{:S(2)}, u32[]{:S(2)}) collective-permute-start(bf16[2,2,96,640]{3,2,1,0:T(8,128)(2,1)S(1)} %shard_map.164.refs_1_), channel_id=1, source_target_pairs={{0,1},{1,0},{2,3},{3,2},{4,5},{5,4},{6,7},{7,6},{8,9},{9,8},{10,11... | collective-permute-start | bytes 1474568 | tf_op jit(solution)/shard_map/ppermute | solution.py:509
  240.8 10.2 %collective-permute-start.36 = (bf16[2,2,64,640]{3,2,1,0:T(8,128)(2,1)S(1)}, bf16[2,2,64,640]{3,2,1,0:T(8,128)(2,1)S(1)}, u32[]{:S(2)}, u32[]{:S(2)}) collective-permute-start(bf16[2,2,64,640]{3,2,1,0:T(8,128)(2,1)S(1)} %shard_map.159.refs_0_), channel_id=1, source_target_pairs={{0,1},{1,0},{2,3},{3,2},{4,5},{5,4},{6,7},{7,6},{8,9},{9,8},{10,11... | collective-permute-start | bytes 983048 | tf_op jit(solution)/shard_map/ppermute | solution.py:509
  249.9 12.0 %collective-permute-start.35 = (bf16[2,1,2,80,384]{4,3,2,1,0:T(8,128)(2,1)S(1)}, bf16[2,1,2,80,384]{4,3,2,1,0:T(8,128)(2,1)S(1)}, u32[]{:S(2)}, u32[]{:S(2)}) collective-permute-start(bf16[2,1,2,80,384]{4,3,2,1,0:T(8,128)(2,1)S(1)} %shard_map.165), channel_id=1, source_target_pairs={{0,16},{4,20},{8,24},{12,28},{16,0},{20,4},{24,8},{28,12},{1,17},{... | collective-permute-start | bytes 737288 | tf_op jit(solution)/shard_map/ppermute | solution.py:499
  281.3 12.4 %collective-permute-start.48 = (f32[16,128]{1,0:T(8,128)S(1)}, f32[16,128]{1,0:T(8,128)S(1)}, u32[]{:S(2)}, u32[]{:S(2)}) collective-permute-start(f32[16,128]{1,0:T(8,128)S(1)} %shard_map.168.refs_0_), channel_id=1, source_target_pairs={{0,4},{4,0},{8,12},{12,8},{16,20},{20,16},{24,28},{28,24},{1,5},{5... | collective-permute-start | bytes 24584 | tf_op jit(solution)/shard_map/ppermute | solution.py:495
  (65 other events, 687.6 us)

commit v5 on v4

--- a/solution.py
+++ b/solution.py
@@ -15,6 +15,7 @@
 LANES = 128
 PARTS = 2
 VMEM = 24 * 1024 * 1024
+WIDE = 56 * 1024 * 1024
 
 
 def moments(weight, first, second, grad):
@@ -48,9 +49,9 @@
     return lax.dot_general(left, right, (dims, ((), ())), preferred_element_type=F32)
 
 
-def params():
+def params(grant=VMEM):
     return dict(
-        compiler_params=pltpu.CompilerParams(vmem_limit_bytes=VMEM),
+        compiler_params=pltpu.CompilerParams(vmem_limit_bytes=grant),
         cost_estimate=pl.CostEstimate(flops=1, bytes_accessed=1, transcendentals=0),
     )
 
@@ -120,10 +121,10 @@
         return refs[self.count + n][0].astype(F32)
 
 
-def grad_out_chunk(tokens, core, nz, scale):
+def grad_out_chunk(tokens, core, nz, scale, parts):
     width, model = tokens.width, tokens.model
     half = model // CORES
-    high = width // PARTS
+    high = width // parts
     count = len(tokens.arrays)
 
     def body(c_ref, *refs):
@@ -135,10 +136,10 @@
             cols = pl.ds(pl.multiple_of((c_ref[0] + 1 + which) % CORES * half, 16), half)
             right = jnp.concatenate([tokens.cot(ins, n)[cols, :] for n in range(tokens.count)], axis=1)
             total = (dot(acts, right, ((1,), (1,))) * scale).astype(BF16)
-            for p in range(PARTS):
+            for p in range(parts):
                 value = total[p * high : (p + 1) * high]
                 if which:
-                    outs[PARTS][p, 0] = value
+                    outs[parts][p, 0] = value
                 else:
                     outs[p][0] = value
 
@@ -148,46 +149,55 @@
             num_scalar_prefetch=1,
             grid=(nz,),
             in_specs=tokens.specs,
-            out_specs=[pl.BlockSpec((1, high, half), lambda z, c: (z, 0, 0))] * PARTS
-            + [pl.BlockSpec((PARTS, 1, high, half), lambda z, c: (0, z, 0, 0))],
+            out_specs=[pl.BlockSpec((1, high, half), lambda z, c: (z, 0, 0))] * parts
+            + [pl.BlockSpec((parts, 1, high, half), lambda z, c: (0, z, 0, 0))],
         ),
-        out_shape=[jax.ShapeDtypeStruct((nz, high, half), BF16)] * PARTS
-        + [jax.ShapeDtypeStruct((PARTS, nz, high, half), BF16)],
+        out_shape=[jax.ShapeDtypeStruct((nz, high, half), BF16)] * parts
+        + [jax.ShapeDtypeStruct((parts, nz, high, half), BF16)],
         **params(),
     )(core, *tokens.arrays)
 
 
-def grad_pre_chunk(tokens, weights, row, scale):
-    nz, shard, model = weights.shape
+def grad_pre_chunk(tokens, mine, other, nz, row, core, scale):
+    part, model = mine[0].shape
     width = tokens.width
     count = len(tokens.arrays)
     long = tokens.arrays[0].shape[1]
 
     def body(c_ref, *refs):
         ins = refs[:count]
-        w_ref, out_ref = refs[count:]
-        w = w_ref[0, row : row + width, :]
+        out_ref, w_ref = refs[count + 2 * nz :]
+        for h in range(nz):
+
+            @pl.when((pl.program_id(0) ^ c_ref[1]) == h)
+            def _(h=h):
+                for at, ref in ((c_ref[0], refs[count + h]), (1 - c_ref[0], refs[count + nz + h])):
+                    w_ref[pl.ds(pl.multiple_of(at * part, 16), part), :] = ref[...]
+
+        w = w_ref[row : row + width, :]
         for n in range(tokens.count):
             grad_act = dot(w, tokens.cot(ins, n)[...], ((1,), (0,))) * scale
             out_ref[0, :, n * long : (n + 1) * long] = (
                 grad_act * gelu_slope(tokens.hidden(ins, n))
             ).astype(BF16)
 
+    w_specs = [pl.BlockSpec((part, model), lambda z, c: (0, 0))] * nz
     return pl.pallas_call(
         body,
         grid_spec=pltpu.PrefetchScalarGridSpec(
             num_scalar_prefetch=1,
             grid=(nz,),
-            in_specs=tokens.specs + [pl.BlockSpec((1, shard, model), lambda z, c: (z, 0, 0))],
+            in_specs=tokens.specs + w_specs * 2,
             out_specs=pl.BlockSpec((1, width, tokens.count * long), lambda z, c: (z, 0, 0)),
+            scratch_shapes=[pltpu.VMEM((CORES * part, model), BF16)],
         ),
         out_shape=jax.ShapeDtypeStruct((nz, width, tokens.count * long), BF16),
         **params(),
-    )(jnp.zeros((1,), jnp.int32), *tokens.arrays, weights)
-
-
-def grad_in_chunk(grads, inputs, core, scale, cut):
-    nz, width, long = grads.shape
+    )(core, *tokens.arrays, *mine, *other)
+
+
+def grad_in_chunk(grads, inputs, core, scale, cut, block, width):
+    nz, _, long = grads.shape
     model, tokens = inputs[0].shape
     count = len(inputs)
     half = nz // CORES
@@ -217,7 +227,7 @@
             in_specs=[
                 pl.BlockSpec(
                     (1, width, long),
-                    lambda z, c: ((c[0] + 1 + z // half) % CORES * half + z % half, 0, 0),
+                    lambda z, c: ((c[0] + 1 + z // half) % CORES * half + z % half, block, 0),
                 )
             ]
             + [pl.BlockSpec((model, tokens), lambda z, c: (0, 0))] * count,
@@ -249,8 +259,7 @@
 
 def half_rows(weight, core):
     rows, cols = weight.shape
-    part = rows // CORES
-    wide = 2 * LANES
+    high = rows // CORES // 2
 
     def body(c_ref, in_ref, out_ref):
         out_ref[...] = in_ref[...].astype(BF16)
@@ -259,12 +268,12 @@
         body,
         grid_spec=pltpu.PrefetchScalarGridSpec(
             num_scalar_prefetch=1,
-            grid=(cols // wide,),
-            in_specs=[pl.BlockSpec((part, wide), lambda n, c: (c[0], n))],
-            out_specs=pl.BlockSpec((part, wide), lambda n, c: (0, n)),
+            grid=(2,),
+            in_specs=[pl.BlockSpec((high, cols), lambda n, c: (c[0] * 2 + n, 0))],
+            out_specs=pl.BlockSpec((high, cols), lambda n, c: (n, 0)),
         ),
-        out_shape=jax.ShapeDtypeStruct((part, cols), BF16),
-        **params(),
+        out_shape=jax.ShapeDtypeStruct((2 * high, cols), BF16),
+        **params(WIDE),
     )(core, weight)
 
 
@@ -290,30 +299,6 @@
             out_specs=pl.BlockSpec(out, lambda at: (0,) * len(out)),
         ),
         out_shape=jax.ShapeDtypeStruct(out, pieces[0].dtype),
-        **params(),
-    )(places, *pieces)
-
-
-def stack_rows(pieces, places):
-    count = len(pieces)
-    high, cols = pieces[0].shape
-    wide = 2 * LANES
-    parts = CORES
-
-    def body(at_ref, *refs):
-        for n in range(count):
-            row = pl.multiple_of(at_ref[1, n] * high, 16)
-            refs[count][at_ref[0, n], pl.ds(row, high)] = refs[n][...]
-
-    return pl.pallas_call(
-        body,
-        grid_spec=pltpu.PrefetchScalarGridSpec(
-            num_scalar_prefetch=1,
-            grid=(cols // wide,),
-            in_specs=[pl.BlockSpec((high, wide), lambda n, at: (0, n))] * count,
-            out_specs=pl.BlockSpec((count // parts, parts * high, wide), lambda n, at: (0, 0, n)),
-        ),
-        out_shape=jax.ShapeDtypeStruct((count // parts, parts * high, cols), pieces[0].dtype),
         **params(),
     )(places, *pieces)
 
@@ -404,13 +389,15 @@
     return out if split else out[0]
 
 
-def moments_kernel(core, weight, first, second, mine, other, grid, state_spec, grad_specs, owner, axis):
+def moments_kernel(core, weight, first, second, mine, other, grid, state_spec, grad_specs, owner, axis, tiles):
     block = state_spec.block_shape
     count = len(mine)
+    long = 16 * (1 + len(tiles))
 
     def body(c_ref, w_ref, m_ref, v_ref, *refs):
         mine_refs, other_refs = refs[:count], refs[count : 2 * count]
-        new_m_ref, new_v_ref, u_ref, sum_ref = refs[2 * count :]
+        tile_refs = refs[2 * count : 2 * count + len(tiles)]
+        new_m_ref, new_v_ref, u_ref, sum_ref = refs[2 * count + len(tiles) :]
         totals = [jnp.zeros((8, LANES), F32)] * 2
         start = 0
         ours = owner(pl.program_id(0)) == c_ref[0]
@@ -433,10 +420,12 @@
 
         @pl.when(pl.program_id(0) == 0)
         def _():
-            sum_ref[...] = jnp.zeros_like(sum_ref)
+            sum_ref[:16] = jnp.zeros((16, LANES), F32)
+            for n, tile_ref in enumerate(tile_refs):
+                sum_ref[16 * (n + 1) : 16 * (n + 2)] = tile_ref[...]
 
         sum_ref[:8] += totals[0]
-        sum_ref[8:] += totals[1]
+        sum_ref[8:16] += totals[1]
 
     state = jax.ShapeDtypeStruct(weight.shape, F32)
     return pl.pallas_call(
@@ -444,26 +433,28 @@
         grid_spec=pltpu.PrefetchScalarGridSpec(
             num_scalar_prefetch=1,
             grid=grid,
-            in_specs=[state_spec] * 3 + grad_specs * 2,
-            out_specs=[state_spec] * 3 + [pl.BlockSpec((16, LANES), lambda n, c: (0, 0))],
+            in_specs=[state_spec] * 3
+            + grad_specs * 2
+            + [pl.BlockSpec((16, LANES), lambda n, c: (0, 0))] * len(tiles),
+            out_specs=[state_spec] * 3 + [pl.BlockSpec((long, LANES), lambda n, c: (0, 0))],
         ),
-        out_shape=[state] * 3 + [jax.ShapeDtypeStruct((16, LANES), F32)],
-        **params(),
-    )(core, weight, first, second, *mine, *other)
-
-
-def step_weights(weight, update, tiles):
+        out_shape=[state] * 3 + [jax.ShapeDtypeStruct((long, LANES), F32)],
+        **params(),
+    )(core, weight, first, second, *mine, *other, *tiles)
+
+
+def step_weights(weight, update, tiles, at):
     rows, cols = weight.shape
     high = rows // 5
     count = len(tiles)
 
     def body(w_ref, u_ref, *refs):
-        sums = sum(ref[...] for ref in refs[:count])
+        sums = sum(ref[at : at + 16] for ref in refs[:count])
         ratio = jnp.sqrt(jnp.sum(sums[:8], keepdims=True)) / jnp.sqrt(jnp.sum(sums[8:], keepdims=True))
         refs[count][...] = w_ref[...] - 0.4 * ratio * u_ref[...]
 
     spec = pl.BlockSpec((high, cols), lambda n: (n, 0))
-    tile = pl.BlockSpec((16, LANES), lambda n: (0, 0))
+    tile = pl.BlockSpec(tiles[0].shape, lambda n: (0, 0))
     return pl.pallas_call(
         body,
         grid=(rows // high,),
@@ -577,6 +568,7 @@
         z, x = place // nx, place % nx
         y, c = side // CORES, side % CORES
         core = jnp.reshape(c, (1,)).astype(jnp.int32)
+        at_core = jnp.stack([c, z]).astype(jnp.int32)
         order = Order()
 
         packs, hiddens = [], []
@@ -602,21 +594,19 @@
                     (value,) = order.after(value)
                 found[key ^ bit] = along_z(value, bit)
             bit //= 2
-        crossed = [across(found[key]) for key in range(nz)]
+        found = [found[key] for key in range(nz)]
+        crossed = [across(value) for value in [*order.after(*found[: nz // 2]), *found[nz // 2 :]]]
         packs = [own[0]] + packs
         hiddens = [own[1:]] + hiddens
 
+        parts = [1] + [PARTS] * last
         outs = [None for _ in chunks]
-        ins = [None for _ in chunks]
+        pieces_in = [(0, 0, cuts[0])]
+        if last:
+            small = cuts[1] // 3
+            pieces_in += [(1, 0, 2 * small), (1, 2, small)]
+        ins = [None for _ in pieces_in]
         pres = [None for _ in chunks]
-
-        def stack_weights():
-            pieces = order.after(*[found[key] for key in range(nz)], *crossed)
-            blocks = jnp.stack([z ^ key for key in range(nz)] * CORES)
-            halves = jnp.stack([c] * nz + [1 - c] * nz)
-            value = stack_rows(pieces, jnp.stack([blocks, halves]).astype(jnp.int32))
-            order.did(value)
-            return value
 
         def tokens(k, *more):
             later = [] if k == 0 else [value[k - 1] for value in hiddens]
@@ -626,96 +616,110 @@
             return blocks, got[count:]
 
         def start_out(k):
-            *sends, keep = grad_out_chunk(tokens(k)[0], core, nz, scale_out)
+            blocks, _ = tokens(k, *([*crossed[: nz // 2], found[nz // 2]] if k == 0 else []))
+            *sends, keep = grad_out_chunk(blocks, core, nz, scale_out, parts[k])
             order.did(keep)
-            shape = (PARTS, nz, 1, ny, cuts[k] // PARTS // ny, model // CORES)
+            shape = (parts[k], nz, 1, ny, cuts[k] // parts[k] // ny, model // CORES)
             outs[k] = Reduce(order, (x, y, z), sends, keep, shape)
 
         def start_pre(k):
-            blocks, got = tokens(k, weights)
-            pres[k] = grad_pre_chunk(blocks, got[0], starts[k], scale_out)
+            blocks, got = tokens(k, *found, *crossed)
+            pres[k] = grad_pre_chunk(blocks, got[:nz], got[nz:], nz, starts[k], at_core, scale_out)
             order.did(pres[k])
 
         def start_in(k):
-            got = order.after(pres[k], *columns)
-            *sends, keep = grad_in_chunk(got[0], got[1:], core, scale_in, PARTS if k else 1)
+            chunk, block, width = pieces_in[k]
+            got = order.after(pres[chunk], *columns)
+            *sends, keep = grad_in_chunk(
+                got[0], got[1:], core, scale_in, PARTS if width > LANES else 1, block, width
+            )
             order.did(keep)
-            shape = (nz // CORES, nz, nx, ny, rows // ny, cuts[k])
+            shape = (nz // CORES, nz, nx, ny, rows // ny, width)
             ins[k] = Reduce(order, (x, y, z), sends, keep, shape)
 
-        def sums(tile, zs=None):
-            zs = zs or [along_z(tile, flip) for flip in range(1, nz)]
-            tiles = order.after(tile, *zs)
+        def sums(tile):
+            tiles = order.after(tile, *[along_z(tile, flip) for flip in range(1, nz)])
             tile = add_tiles(tiles)
             order.did(tile)
-            return [tile] + [along_x(tile, s) for s in range(1, nx)]
-
-        def new_weights(weight, update, tiles):
+            return [tile] + [along_x(tile, t) for t in range(1, nx)]
+
+        def new_weights(weight, update, tiles, at):
             got = order.after(weight, update, *tiles)
-            value = step_weights(got[0], got[1], got[2:])
+            value = step_weights(got[0], got[1], got[2:], at)
             order.did(value)
             return value
 
+        def moments_out():
+            half = model // CORES
+            got = order.after(
+                w_out, m_out, v_out, *[outs[k].held[0] for k in chunks], *[outs[k].held[1] for k in chunks]
+            )
+            new = moments_kernel(
+                core,
+                *got[:3],
+                got[3 : 4 + last],
+                got[4 + last :],
+                (CORES,),
+                pl.BlockSpec((shard, half), lambda n, c: (0, n)),
+                [
+                    pl.BlockSpec((p, ny, w // p // ny, half), lambda n, c: (0, 0, 0, 0))
+                    for w, p in zip(cuts, parts)
+                ],
+                lambda n: n,
+                0,
+                [],
+            )
+            order.did(new[3])
+            return new
+
         start_out(0)
         outs[0].send_y()
-        weights = stack_weights()
         start_pre(0)
+        start_in(0)
         outs[0].send_z()
-        start_in(0)
         ins[0].send_y()
         outs[0].send_z()
+        ins[0].send_z()
+        outs[0].finish()
         if last:
-            ins[0].send_z()
             start_out(1)
             outs[1].send_y()
-            outs[0].finish()
             start_pre(1)
             ins[0].send_z()
             start_in(1)
+            start_in(2)
             ins[1].send_y()
+            ins[2].send_y()
             ins[0].finish()
             outs[1].send_z()
             ins[0].stack_x()
             outs[0].stack_y(True)
+            ins[1].send_z()
             outs[1].send_z()
             ins[0].stack_y()
+            ins[2].send_z()
+            ins[1].send_z()
             outs[1].finish()
-            ins[1].send_z()
+            ins[2].send_z()
             outs[1].stack_y(True)
-            ins[1].send_z()
+            ins[1].finish()
+            first_out, second_out, update_out, tile = moments_out()
+            ins[2].finish()
+            for n in (1, 2):
+                ins[n].stack_x()
+            for n in (1, 2):
+                ins[n].stack_y()
         else:
-            outs[0].finish()
-            ins[0].send_z()
             ins[0].send_z()
             outs[0].stack_y(True)
-
-        half = model // CORES
-        got = order.after(
-            w_out, m_out, v_out, *[outs[k].held[0] for k in chunks], *[outs[k].held[1] for k in chunks]
-        )
-        first_out, second_out, update_out, tile = moments_kernel(
-            core,
-            *got[:3],
-            got[3 : 4 + last],
-            got[4 + last :],
-            (CORES,),
-            pl.BlockSpec((shard, half), lambda n, c: (0, n)),
-            [
-                pl.BlockSpec((PARTS, ny, w // PARTS // ny, half), lambda n, c: (0, 0, 0, 0)) for w in cuts
-            ],
-            lambda n: n,
-            0,
-        )
-        order.did(tile)
-        ins[last].finish()
-        tiles = sums(tile)
-        ins[last].stack_x()
-        ins[last].stack_y()
-
-        got = order.after(
-            w_in, m_in, v_in, *[ins[k].held[0] for k in chunks], *[ins[k].held[1] for k in chunks]
-        )
-        mine, other = got[3 : 4 + last], got[4 + last :]
+            ins[0].finish()
+            first_out, second_out, update_out, tile = moments_out()
+            ins[0].stack_x()
+            ins[0].stack_y()
+
+        held = [value.held for value in ins]
+        got = order.after(w_in, m_in, v_in, tile, *[pair[0] for pair in held], *[pair[1] for pair in held])
+        mine, other = got[4 : 4 + len(ins)], got[4 + len(ins) :]
         if shard % LANES:
             joined = [
                 jnp.stack([jnp.where(c == 0, a, b), jnp.where(c == 0, b, a)]) for a, b in zip(mine, other)
@@ -728,6 +732,7 @@
                     jnp.sum((value * value).reshape(-1, 8, LANES), axis=0)
                     for value in (w_in, update_in)
                 ]
+                + [got[3]]
             )
         else:
             zs = nz // CORES
@@ -742,15 +747,16 @@
                     pl.BlockSpec(
                         (ny, 1, 1, rows // ny, w), lambda n, c: (0, n % nx, n // nx % zs, 0, 0)
                     )
-                    for w in cuts
+                    for _, _, w in pieces_in
                 ],
                 lambda n: n // nx // zs,
                 1,
+                [got[3]],
             )
         order.did(tile)
-        zs = [along_z(tile, flip) for flip in range(1, nz)]
-        new_w_out = new_weights(w_out, update_out, tiles)
-        new_w_in = new_weights(w_in, update_in, sums(tile, zs))
+        tiles = sums(tile)
+        new_w_in = new_weights(w_in, update_in, tiles, 0)
+        new_w_out = new_weights(w_out, update_out, tiles, 16)
         return (new_w_in, first_in, second_in, new_w_out, first_out, second_out)
 
     return local

time: 305 us -> 293 us (0.961)
  waiting for transfers between devices: 140 us -> 116 us
  Pallas kernels: 99.4 us -> 105 us
  local copies, waits for them, and re-layouts: 17 us -> 21 us
    ppermute x8 -> x10, waiting for transfers between devices: 29.5 us -> 12 us  [along_y(): return lax.ppermute(value, 'gy', pairs)]
    ppermute x7, waiting for transfers between devices: 23.1 us -> 15.6 us  [along_x(): return lax.ppermute(value, 'gx', pairs)]
    pallas_call x1 -> x0, Pallas kernels: 5.33 us -> none  [stack_rows(): pl.pallas_call(body, grid_spec=pltpu.PrefetchScalarGridSpec(num_scalar_pr...]
    pallas_call x2, Pallas kernels: 11.3 us -> 16.3 us  [grad_pre_chunk(): pl.pallas_call(body, grid_spec=pltpu.PrefetchScalarGridSpec(num_scalar_pr...]
    ppermute x17 -> x16, waiting for transfers between devices: 79.1 us -> 83.5 us  [along_z(): return lax.ppermute(value, 'gx', pairs)]
    unnamed x78 -> x114, local copies, waits for them, and re-layouts: 16.8 us -> 21 us
    ppermute x18 -> x22, waiting for transfers between devices: 8.47 us -> 4.62 us  [across(): return lax.ppermute(value, 'gy', pairs)]
    pallas_call x16 -> x20, Pallas kernels: 25.6 us -> 28.4 us  [reduce_step(): pl.pallas_call(body, grid_spec=pltpu.PrefetchScalarGridSpec(num_scalar_pr...]
  transfers between devices with their start and end apart: 50 -> 55, of which waited for: 30 -> 24; matrix products, arithmetic and copies ran while one was open for 0% -> 0% of each run, Pallas kernels for 27% -> 26%
where the time goes in v5:
time: 293 us; the launch traced here: 292 us
  waiting for transfers between devices  116 us (40%)
  Pallas kernels  105 us (36%)
  starting transfers between devices  48.4 us (17%)
  local copies, waits for them, and re-layouts  21 us (7%)
    ppermute x16, waiting for transfers between devices, along_z(): return lax.ppermute(value, 'gx', pairs)  83.5 us
    pallas_call x20, Pallas kernels, reduce_step(): pl.pallas_call(body, grid_spec=pltpu.PrefetchScalarGridSpec(num_scalar_pr...  28.4 us
    ppermute x16, starting transfers between devices, along_z(): return lax.ppermute(value, 'gx', pairs)  23.3 us
    unnamed x114, local copies, waits for them, and re-layouts  21 us
    pallas_call x3, Pallas kernels, grad_in_chunk(): pl.pallas_call(body, grid_spec=pltpu.PrefetchScalarGridSpec(num_scalar_pr...  17.1 us
    pallas_call x2, Pallas kernels, grad_pre_chunk(): pl.pallas_call(body, grid_spec=pltpu.PrefetchScalarGridSpec(num_scalar_pr...  16.3 us
    ppermute x7, waiting for transfers between devices, along_x(): return lax.ppermute(value, 'gx', pairs)  15.6 us
    ppermute x10, waiting for transfers between devices, along_y(): return lax.ppermute(value, 'gy', pairs)  12 us
  transfers between devices with their start and end apart: 55, of which 24 were waited for; matrix products, arithmetic and copies ran while one was open for 0% of the time, Pallas kernels for 26%

profile of v5, /device:TPU:0, one launch (start us, length us, event | category | flops | bytes accessed | tf_op | source)
XLA Modules:
  0.0 292.1 jit_solution(14812912298897792629)
XLA Ops:
  4.5 2.9 %shard_map.136 = (bf16[2304,512]{1,0:T(8,128)(2,1)}, bf16[4,384,512]{2,1,0:T(8,128)(2,1)S(1)}) custom-call(s32[1]{0:T(128)} %bitcast.6.at_ref, bf16[512,5120]{1,0:T(8,128)(2,1)S(1)} %copy-done.8, bf16[512,1280]{1,0:T(8,128)(2,1)S(1)} %copy-done.23), custom_call_target="tpu_custom_call" | custom-call | flops 1 | bytes 1 | tf_op jit(solution)/shard_map/pallas_call | solution.py:84
  24.7 26.5 %collective-permute-done.1.refs_3_.refs_5_ = bf16[320,1280]{1,0:T(8,128)(2,1)S(1)} collective-permute-done((bf16[320,1280]{1,0:T(8,128)(2,1)}, bf16[320,1280]{1,0:T(8,128)(2,1)S(1)}, u32[]{:S(2)}, u32[]{:S(2)}) %collective-permute-start.1) | collective-permute-done | bytes 819232 | tf_op jit(solution)/shard_map/ppermute | solution.py:490
  55.6 7.4 %collective-permute-done.refs_1_ = bf16[2304,512]{1,0:T(8,128)(2,1)S(1)} collective-permute-done((bf16[2304,512]{1,0:T(8,128)(2,1)}, bf16[2304,512]{1,0:T(8,128)(2,1)S(1)}, u32[]{:S(2)}, u32[]{:S(2)}) %collective-permute-start) | collective-permute-done | bytes 2359328 | tf_op jit(solution)/shard_map/ppermute | solution.py:486
  62.9 4.6 %shard_map.140 = (bf16[4,256,640]{2,1,0:T(8,128)(2,1)}, bf16[1,4,256,640]{3,2,1,0:T(8,128)(2,1)S(1)}) custom-call(s32[1]{0:T(128)} %bitcast.c_ref, bf16[2304,512]{1,0:T(8,128)(2,1)S(1)} %get-tuple-element.301.refs_0_, bf16[2304,512]{1,0:T(8,128)(2,1)S(1)} %collective-permute-done.refs_1_), custom_call_target="tpu_custom_call" | custom-call | flops 1 | bytes 1 | tf_op jit(solution)/shard_map/pallas_call | solution.py:146
  71.9 17.7 %collective-permute-done.7.refs_5_.refs_7_ = bf16[320,1280]{1,0:T(8,128)(2,1)} collective-permute-done((bf16[320,1280]{1,0:T(8,128)(2,1)}, bf16[320,1280]{1,0:T(8,128)(2,1)}, u32[]{:S(2)}, u32[]{:S(2)}) %collective-permute-start.7) | collective-permute-done | bytes 819232 | tf_op jit(solution)/shard_map/ppermute | solution.py:490
  99.5 7.2 %shard_map.142.g_ref = bf16[4,256,1024]{2,1,0:T(8,128)(2,1)S(1)} custom-call(s32[2]{0:T(128)S(1)} %pad_add_fusion.2.c_ref, bf16[2304,512]{1,0:T(8,128)(2,1)S(1)} %copy-done.1, bf16[2304,512]{1,0:T(8,128)(2,1)S(1)} %collective-permute-done.refs_1_, bf16[320,1280]{1,0:T(8,128)(2,1)S(1)} %copy-done.20, bf16[320,1280]{1,0:T(8,128)(2,1)S(1)} %copy-done.46, ...), custom_call_target="tpu_custom_call" | custom-call | flops 1 | bytes 1 | tf_op jit(solution)/shard_map/pallas_call | solution.py:185
  106.7 5.9 %shard_map.143 = (bf16[640,256]{1,0:T(8,128)(2,1)S(1)}, bf16[640,256]{1,0:T(8,128)(2,1)S(1)}, bf16[640,256]{1,0:T(8,128)(2,1)S(1)}, bf16[640,256]{1,0:T(8,128)(2,1)S(1)}, bf16[2,1280,256]{2,1,0:T(8,128)(2,1)S(1)}) custom-call(s32[1]{0:T(128)} %bitcast.c_ref, bf16[4,256,1024]{2,1,0:T(8,128)(2,1)S(1)} %shard_map.142.g_ref, ...), custom_call_target="tpu_custom_call" | custom-call | flops 1 | bytes 1 | tf_op jit(solution)/shard_map/pallas_call | solution.py:222
  119.0 7.9 %collective-permute-done.11.refs_3_ = bf16[1,2,1,128,640]{4,3,2,1,0:T(8,128)(2,1)S(1)} collective-permute-done((bf16[1,2,1,128,640]{4,3,2,1,0:T(8,128)(2,1)S(1)}, bf16[1,2,1,128,640]{4,3,2,1,0:T(8,128)(2,1)S(1)}, u32[]{:S(2)}, u32[]{:S(2)}) %collective-permute-start.11) | collective-permute-done | bytes 327712 | tf_op jit(solution)/shard_map/ppermute | solution.py:490
  134.8 3.2 %collective-permute-done.16.refs_4_ = bf16[1,1,1,128,640]{4,3,2,1,0:T(8,128)(2,1)S(1)} collective-permute-done((bf16[1,1,1,128,640]{4,3,2,1,0:T(8,128)(2,1)S(1)}, bf16[1,1,1,128,640]{4,3,2,1,0:T(8,128)(2,1)S(1)}, u32[]{:S(2)}, u32[]{:S(2)}) %collective-permute-start.16) | collective-permute-done | bytes 163872 | tf_op jit(solution)/shard_map/ppermute | solution.py:490
  139.7 6.0 %shard_map.149 = (bf16[4,192,640]{2,1,0:T(8,128)(2,1)S(1)}, bf16[4,192,640]{2,1,0:T(8,128)(2,1)S(1)}, bf16[2,4,192,640]{3,2,1,0:T(8,128)(2,1)S(1)}) custom-call(s32[1]{0:T(128)} %bitcast.c_ref, bf16[2304,512]{1,0:T(8,128)(2,1)S(1)} %copy-done.1, bf16[2304,512]{1,0:T(8,128)(2,1)S(1)} %collective-permute-done.refs_1_, bf16[4,384,512]{2,1,0:T(8,128)(2,1)S(1)} %copy-done.22, ...), custom_call_target="tpu_custom_call" | custom-call | flops 1 | bytes 1 | tf_op jit(solution)/shard_map/pallas_call | solution.py:146
  152.5 9.1 %shard_map.151.g_ref = bf16[4,384,1024]{2,1,0:T(8,128)(2,1)S(1)} custom-call(s32[2]{0:T(128)S(1)} %pad_add_fusion.2.c_ref, bf16[2304,512]{1,0:T(8,128)(2,1)S(1)} %copy-done.1, bf16[2304,512]{1,0:T(8,128)(2,1)S(1)} %collective-permute-done.refs_1_, bf16[4,384,512]{2,1,0:T(8,128)(2,1)S(1)} %copy-done.22, ...), custom_call_target="tpu_custom_call" | custom-call | flops 1 | bytes 1 | tf_op jit(solution)/shard_map/pallas_call | solution.py:185
  162.3 5.8 %shard_map.153 = (bf16[640,256]{1,0:T(8,128)(2,1)S(1)}, bf16[640,256]{1,0:T(8,128)(2,1)S(1)}, bf16[640,256]{1,0:T(8,128)(2,1)S(1)}, bf16[640,256]{1,0:T(8,128)(2,1)S(1)}, bf16[2,1280,256]{2,1,0:T(8,128)(2,1)S(1)}) custom-call(s32[1]{0:T(128)} %bitcast.c_ref, bf16[4,384,1024]{2,1,0:T(8,128)(2,1)S(1)} %shard_map.151.g_ref, ...), custom_call_target="tpu_custom_call" | custom-call | flops 1 | bytes 1 | tf_op jit(solution)/shard_map/pallas_call | solution.py:222
  169.2 5.4 %shard_map.154 = (bf16[1280,128]{1,0:T(8,128)(2,1)S(1)}, bf16[1280,128]{1,0:T(8,128)(2,1)S(1)}, bf16[2,1280,128]{2,1,0:T(8,128)(2,1)S(1)}) custom-call(s32[1]{0:T(128)} %bitcast.c_ref, bf16[4,384,1024]{2,1,0:T(8,128)(2,1)S(1)} %shard_map.151.g_ref, bf16[1280,512]{1,0:T(8,128)(2,1)} %shard_map.138.refs_0_, bf16[1280,512]{1,0:T(8,128)(2,1)} %collective-permute-done.10.refs_1_), custom_call_target="tpu_custom_call" | custom-call | flops 1 | bytes 1 | tf_op jit(solution)/shard_map/pallas_call | solution.py:222
  180.8 7.7 %collective-permute-done.23.refs_7_ = bf16[2,1,2,80,256]{4,3,2,1,0:T(8,128)(2,1)S(1)} collective-permute-done((bf16[2,1,2,80,256]{4,3,2,1,0:T(8,128)(2,1)S(1)}, bf16[2,1,2,80,256]{4,3,2,1,0:T(8,128)(2,1)S(1)}, u32[]{:S(2)}, u32[]{:S(2)}) %collective-permute-start.23) | collective-permute-done | bytes 163872 | tf_op jit(solution)/shard_map/ppermute | solution.py:490
  193.9 3.5 %collective-permute-done.30.refs_1_ = bf16[2,80,256]{2,1,0:T(8,128)(2,1)S(1)} collective-permute-done((bf16[2,80,256]{2,1,0:T(8,128)(2,1)}, bf16[2,80,256]{2,1,0:T(8,128)(2,1)S(1)}, u32[]{:S(2)}, u32[]{:S(2)}) %collective-permute-start.30) | collective-permute-done | bytes 81952 | tf_op jit(solution)/shard_map/ppermute | solution.py:486
  213.9 4.8 %collective-permute-done.37.refs_1_ = bf16[2,2,80,256]{3,2,1,0:T(8,128)(2,1)S(1)} collective-permute-done((bf16[2,2,80,256]{3,2,1,0:T(8,128)(2,1)S(1)}, bf16[2,2,80,256]{3,2,1,0:T(8,128)(2,1)S(1)}, u32[]{:S(2)}, u32[]{:S(2)}) %collective-permute-start.37) | collective-permute-done | bytes 163872 | tf_op jit(solution)/shard_map/ppermute | solution.py:496
  225.6 5.3 %collective-permute-done.39.refs_4_ = bf16[2,2,2,80,128]{4,3,2,1,0:T(8,128)(2,1)S(1)} collective-permute-done((bf16[2,2,2,80,128]{4,3,2,1,0:T(8,128)(2,1)S(1)}, bf16[2,2,2,80,128]{4,3,2,1,0:T(8,128)(2,1)S(1)}, u32[]{:S(2)}, u32[]{:S(2)}) %collective-permute-start.39) | collective-permute-done | bytes 163872 | tf_op jit(solution)/shard_map/ppermute | solution.py:490
  235.7 9.3 %collective-permute-done.42.refs_7_ = bf16[2,1,2,80,256]{4,3,2,1,0:T(8,128)(2,1)S(1)} collective-permute-done((bf16[2,1,2,80,256]{4,3,2,1,0:T(8,128)(2,1)S(1)}, bf16[2,1,2,80,256]{4,3,2,1,0:T(8,128)(2,1)S(1)}, u32[]{:S(2)}, u32[]{:S(2)}) %collective-permute-start.42) | collective-permute-done | bytes 163872 | tf_op jit(solution)/shard_map/ppermute | solution.py:490
  247.4 5.3 %shard_map.170 = (f32[640,1280]{1,0:T(8,128)}, f32[640,1280]{1,0:T(8,128)}, f32[640,1280]{1,0:T(8,128)S(1)}, f32[16,128]{1,0:T(8,128)S(1)}) custom-call(s32[1]{0:T(128)} %bitcast.c_ref, f32[640,1280]{1,0:T(8,128)S(1)} %copy-done.4, f32[640,1280]{1,0:T(8,128)S(1)} %copy-done.41, f32[640,1280]{1,0:T(8,128)S(1)} %copy-done.42, ...), custom_call_target="tpu_custom_call" | custom-call | flops 1 | bytes 1 | tf_op jit(solution)/shard_map/pallas_call | solution.py:431
  261.9 3.6 %collective-permute-done.47.refs_1_ = bf16[2,2,80,128]{3,2,1,0:T(8,128)(2,1)S(1)} collective-permute-done((bf16[2,2,80,128]{3,2,1,0:T(8,128)(2,1)S(1)}, bf16[2,2,80,128]{3,2,1,0:T(8,128)(2,1)S(1)}, u32[]{:S(2)}, u32[]{:S(2)}) %collective-permute-start.47) | collective-permute-done | bytes 81952 | tf_op jit(solution)/shard_map/ppermute | solution.py:496
  267.5 6.2 %shard_map.176 = (f32[160,5120]{1,0:T(8,128)}, f32[160,5120]{1,0:T(8,128)}, f32[160,5120]{1,0:T(8,128)S(1)}, f32[32,128]{1,0:T(8,128)S(1)}) custom-call(s32[1]{0:T(128)} %bitcast.c_ref, f32[160,5120]{1,0:T(8,128)S(1)} %copy-done.14, f32[160,5120]{1,0:T(8,128)S(1)} %copy-done.43, f32[160,5120]{1,0:T(8,128)S(1)} %copy-done.44, ...), custom_call_target="tpu_custom_call" | custom-call | flops 1 | bytes 1 | tf_op jit(solution)/shard_map/pallas_call | solution.py:431
  278.5 3.4 %collective-permute-done.53.refs_3_ = f32[32,128]{1,0:T(8,128)S(1)} collective-permute-done((f32[32,128]{1,0:T(8,128)S(1)}, f32[32,128]{1,0:T(8,128)S(1)}, u32[]{:S(2)}, u32[]{:S(2)}) %collective-permute-start.53) | collective-permute-done | bytes 16416 | tf_op jit(solution)/shard_map/ppermute | solution.py:490
  285.7 3.2 %shard_map.178 = f32[160,5120]{1,0:T(8,128)} custom-call(f32[160,5120]{1,0:T(8,128)S(1)} %copy-done.14, f32[160,5120]{1,0:T(8,128)S(1)} %get-tuple-element.448.u_ref, f32[32,128]{1,0:T(8,128)S(1)} %shard_map.177.refs_0_, f32[32,128]{1,0:T(8,128)S(1)} %collective-permute-done.54.refs_1_), custom_call_target="tpu_custom_call" | custom-call | flops 1 | bytes 1 | tf_op jit(solution)/shard_map/pallas_call | solution.py:458
  288.9 3.2 %shard_map.179 = f32[640,1280]{1,0:T(8,128)} custom-call(f32[640,1280]{1,0:T(8,128)S(1)} %copy-done.4, f32[640,1280]{1,0:T(8,128)S(1)} %get-tuple-element.455.u_ref, f32[32,128]{1,0:T(8,128)S(1)} %shard_map.177.refs_0_, f32[32,128]{1,0:T(8,128)S(1)} %collective-permute-done.54.refs_1_), custom_call_target="tpu_custom_call" | custom-call | flops 1 | bytes 1 | tf_op jit(solution)/shard_map/pallas_call | solution.py:458
  (248 shorter events, 125.4 us)
Async XLA Ops:
  8.5 54.4 %collective-permute-start = (bf16[2304,512]{1,0:T(8,128)(2,1)}, bf16[2304,512]{1,0:T(8,128)(2,1)S(1)}, u32[]{:S(2)}, u32[]{:S(2)}) collective-permute-start(bf16[2304,512]{1,0:T(8,128)(2,1)} %get-tuple-element.233), channel_id=1, source_target_pairs={{0,4},{4,0},{8,12},{12,8},{16,20},{20,16},{24,28},{28,24},{1,5},{5... | collective-permute-start | bytes 7077896 | tf_op jit(solution)/shard_map/ppermute | solution.py:486
  13.8 37.3 %collective-permute-start.1 = (bf16[320,1280]{1,0:T(8,128)(2,1)}, bf16[320,1280]{1,0:T(8,128)(2,1)S(1)}, u32[]{:S(2)}, u32[]{:S(2)}) collective-permute-start(bf16[320,1280]{1,0:T(8,128)(2,1)} %shard_map.137.refs_2_.refs_4_), channel_id=1, source_target_pairs={{0,8},{4,12},{8,0},{12,4},{16,24},{20,28},{24,16},{28,20},{1,9},{5... | collective-permute-start | bytes 2457608 | tf_op jit(solution)/shard_map/ppermute | solution.py:490
  15.4 38.3 %collective-permute-start.4 = (bf16[320,1280]{1,0:T(8,128)(2,1)}, bf16[320,1280]{1,0:T(8,128)(2,1)}, u32[]{:S(2)}, u32[]{:S(2)}) collective-permute-start(bf16[320,1280]{1,0:T(8,128)(2,1)} %shard_map.137.refs_2_.refs_4_), channel_id=1, source_target_pairs={{0,16},{4,20},{8,24},{12,28},{16,0},{20,4},{24,8},{28,12},{1,17},{... | collective-permute-start | bytes 2457608 | tf_op jit(solution)/shard_map/ppermute | solution.py:490
  68.6 21.1 %collective-permute-start.5 = (bf16[4,256,640]{2,1,0:T(8,128)(2,1)}, bf16[4,256,640]{2,1,0:T(8,128)(2,1)}, u32[]{:S(2)}, u32[]{:S(2)}) collective-permute-start(bf16[4,256,640]{2,1,0:T(8,128)(2,1)} %get-tuple-element.244), channel_id=1, source_target_pairs={{0,1},{1,0},{2,3},{3,2},{4,5},{5,4},{6,7},{7,6},{8,9},{9,8},{10,11... | collective-permute-start | bytes 3932168 | tf_op jit(solution)/shard_map/ppermute | solution.py:500
  68.6 21.1 %collective-permute-start.7 = (bf16[320,1280]{1,0:T(8,128)(2,1)}, bf16[320,1280]{1,0:T(8,128)(2,1)}, u32[]{:S(2)}, u32[]{:S(2)}) collective-permute-start(bf16[320,1280]{1,0:T(8,128)(2,1)} %collective-permute-done.4.refs_4_.refs_6_), channel_id=1, source_target_pairs={{0,8},{4,12},{8,0},{12,4},{16,24},{20,28},{24,16},{28,20},{1,9},{5... | collective-permute-start | bytes 2457608 | tf_op jit(solution)/shard_map/ppermute | solution.py:490
  70.4 36.2 %collective-permute-start.10 = (bf16[1280,512]{1,0:T(8,128)(2,1)}, bf16[1280,512]{1,0:T(8,128)(2,1)}, u32[]{:S(2)}, u32[]{:S(2)}) collective-permute-start(bf16[1280,512]{1,0:T(8,128)(2,1)} %shard_map.138.refs_0_), channel_id=1, source_target_pairs={{0,4},{4,0},{8,12},{12,8},{16,20},{20,16},{24,28},{28,24},{1,5},{5... | collective-permute-start | bytes 3932168 | tf_op jit(solution)/shard_map/ppermute | solution.py:486
  71.9 25.2 %collective-permute-start.8 = (bf16[320,1280]{1,0:T(8,128)(2,1)}, bf16[320,1280]{1,0:T(8,128)(2,1)}, u32[]{:S(2)}, u32[]{:S(2)}) collective-permute-start(bf16[320,1280]{1,0:T(8,128)(2,1)} %collective-permute-done.4.refs_4_.refs_6_), channel_id=1, source_target_pairs={{0,1},{1,0},{2,3},{3,2},{4,5},{5,4},{6,7},{7,6},{8,9},{9,8},{10,11... | collective-permute-start | bytes 2457608 | tf_op jit(solution)/shard_map/ppermute | solution.py:500
  93.8 19.4 %collective-permute-start.6 = (bf16[1,4,1,128,640]{4,3,2,1,0:T(8,128)(2,1)S(1)}, bf16[1,4,1,128,640]{4,3,2,1,0:T(8,128)(2,1)S(1)}, u32[]{:S(2)}, u32[]{:S(2)}) collective-permute-start(bf16[1,4,1,128,640]{4,3,2,1,0:T(8,128)(2,1)S(1)} %shard_map.141), channel_id=1, source_target_pairs={{0,2},{1,3},{2,0},{3,1},{4,6},{5,7},{6,4},{7,5},{8,10},{9,11},{10,... | collective-permute-start | bytes 1966088 | tf_op jit(solution)/shard_map/ppermute | solution.py:496
  95.6 44.0 %collective-permute-start.20 = (bf16[4,384,512]{2,1,0:T(8,128)(2,1)}, bf16[4,384,512]{2,1,0:T(8,128)(2,1)S(1)}, u32[]{:S(2)}, u32[]{:S(2)}) collective-permute-start(bf16[4,384,512]{2,1,0:T(8,128)(2,1)} %copy-done.55), channel_id=1, source_target_pairs={{0,4},{4,0},{8,12},{12,8},{16,20},{20,16},{24,28},{28,24},{1,5},{5... | collective-permute-start | bytes 4718600 | tf_op jit(solution)/shard_map/ppermute | solution.py:486
  116.9 16.8 %collective-permute-start.17 = (bf16[2,4,2,80,256]{4,3,2,1,0:T(8,128)(2,1)S(1)}, bf16[2,4,2,80,256]{4,3,2,1,0:T(8,128)(2,1)S(1)}, u32[]{:S(2)}, u32[]{:S(2)}) collective-permute-start(bf16[2,4,2,80,256]{4,3,2,1,0:T(8,128)(2,1)S(1)} %shard_map.145), channel_id=1, source_target_pairs={{0,2},{1,3},{2,0},{3,1},{4,6},{5,7},{6,4},{7,5},{8,10},{9,11},{10,... | collective-permute-start | bytes 1966088 | tf_op jit(solution)/shard_map/ppermute | solution.py:496
  117.4 9.5 %collective-permute-start.11 = (bf16[1,2,1,128,640]{4,3,2,1,0:T(8,128)(2,1)S(1)}, bf16[1,2,1,128,640]{4,3,2,1,0:T(8,128)(2,1)S(1)}, u32[]{:S(2)}, u32[]{:S(2)}) collective-permute-start(bf16[1,2,1,128,640]{4,3,2,1,0:T(8,128)(2,1)S(1)} %shard_map.144), channel_id=1, source_target_pairs={{0,8},{4,12},{8,0},{12,4},{16,24},{20,28},{24,16},{28,20},{1,9},{5... | collective-permute-start | bytes 983048 | tf_op jit(solution)/shard_map/ppermute | solution.py:490
  128.5 9.6 %collective-permute-start.16 = (bf16[1,1,1,128,640]{4,3,2,1,0:T(8,128)(2,1)S(1)}, bf16[1,1,1,128,640]{4,3,2,1,0:T(8,128)(2,1)S(1)}, u32[]{:S(2)}, u32[]{:S(2)}) collective-permute-start(bf16[1,1,1,128,640]{4,3,2,1,0:T(8,128)(2,1)S(1)} %shard_map.146), channel_id=1, source_target_pairs={{0,16},{4,20},{8,24},{12,28},{16,0},{20,4},{24,8},{28,12},{1,17},{... | collective-permute-start | bytes 491528 | tf_op jit(solution)/shard_map/ppermute | solution.py:490
  146.3 15.3 %collective-permute-start.19 = (bf16[2,2,2,80,256]{4,3,2,1,0:T(8,128)(2,1)S(1)}, bf16[2,2,2,80,256]{4,3,2,1,0:T(8,128)(2,1)S(1)}, u32[]{:S(2)}, u32[]{:S(2)}) collective-permute-start(bf16[2,2,2,80,256]{4,3,2,1,0:T(8,128)(2,1)S(1)} %shard_map.147), channel_id=1, source_target_pairs={{0,8},{4,12},{8,0},{12,4},{16,24},{20,28},{24,16},{28,20},{1,9},{5... | collective-permute-start | bytes 983048 | tf_op jit(solution)/shard_map/ppermute | solution.py:490
  150.9 38.4 %collective-permute-start.31 = (bf16[2,4,1,96,640]{4,3,2,1,0:T(8,128)(2,1)S(1)}, bf16[2,4,1,96,640]{4,3,2,1,0:T(8,128)(2,1)S(1)}, u32[]{:S(2)}, u32[]{:S(2)}) collective-permute-start(bf16[2,4,1,96,640]{4,3,2,1,0:T(8,128)(2,1)S(1)} %shard_map.150), channel_id=1, source_target_pairs={{0,2},{1,3},{2,0},{3,1},{4,6},{5,7},{6,4},{7,5},{8,10},{9,11},{10,... | collective-permute-start | bytes 2949128 | tf_op jit(solution)/shard_map/ppermute | solution.py:496
  177.6 22.9 %collective-permute-start.33 = (bf16[2,4,2,80,256]{4,3,2,1,0:T(8,128)(2,1)}, bf16[2,4,2,80,256]{4,3,2,1,0:T(8,128)(2,1)}, u32[]{:S(2)}, u32[]{:S(2)}) collective-permute-start(bf16[2,4,2,80,256]{4,3,2,1,0:T(8,128)(2,1)} %shard_map.155), channel_id=1, source_target_pairs={{0,2},{1,3},{2,0},{3,1},{4,6},{5,7},{6,4},{7,5},{8,10},{9,11},{10,... | collective-permute-start | bytes 1966088 | tf_op jit(solution)/shard_map/ppermute | solution.py:496
  178.1 10.4 %collective-permute-start.23 = (bf16[2,1,2,80,256]{4,3,2,1,0:T(8,128)(2,1)S(1)}, bf16[2,1,2,80,256]{4,3,2,1,0:T(8,128)(2,1)S(1)}, u32[]{:S(2)}, u32[]{:S(2)}) collective-permute-start(bf16[2,1,2,80,256]{4,3,2,1,0:T(8,128)(2,1)S(1)} %shard_map.152), channel_id=1, source_target_pairs={{0,16},{4,20},{8,24},{12,28},{16,0},{20,4},{24,8},{28,12},{1,17},{... | collective-permute-start | bytes 491528 | tf_op jit(solution)/shard_map/ppermute | solution.py:490
  191.0 16.7 %collective-permute-start.32 = (bf16[2,2,1,96,640]{4,3,2,1,0:T(8,128)(2,1)}, bf16[2,2,1,96,640]{4,3,2,1,0:T(8,128)(2,1)}, u32[]{:S(2)}, u32[]{:S(2)}) collective-permute-start(bf16[2,2,1,96,640]{4,3,2,1,0:T(8,128)(2,1)} %shard_map.158), channel_id=1, source_target_pairs={{0,8},{4,12},{8,0},{12,4},{16,24},{20,28},{24,16},{28,20},{1,9},{5... | collective-permute-start | bytes 1474568 | tf_op jit(solution)/shard_map/ppermute | solution.py:490
  193.3 25.9 %collective-permute-start.36 = (bf16[2,4,2,80,128]{4,3,2,1,0:T(8,128)(2,1)}, bf16[2,4,2,80,128]{4,3,2,1,0:T(8,128)(2,1)S(1)}, u32[]{:S(2)}, u32[]{:S(2)}) collective-permute-start(bf16[2,4,2,80,128]{4,3,2,1,0:T(8,128)(2,1)} %copy-done.54), channel_id=1, source_target_pairs={{0,2},{1,3},{2,0},{3,1},{4,6},{5,7},{6,4},{7,5},{8,10},{9,11},{10,... | collective-permute-start | bytes 983048 | tf_op jit(solution)/shard_map/ppermute | solution.py:496
  206.3 13.9 %collective-permute-start.35 = (bf16[2,2,2,80,256]{4,3,2,1,0:T(8,128)(2,1)S(1)}, bf16[2,2,2,80,256]{4,3,2,1,0:T(8,128)(2,1)S(1)}, u32[]{:S(2)}, u32[]{:S(2)}) collective-permute-start(bf16[2,2,2,80,256]{4,3,2,1,0:T(8,128)(2,1)S(1)} %shard_map.161), channel_id=1, source_target_pairs={{0,8},{4,12},{8,0},{12,4},{16,24},{20,28},{24,16},{28,20},{1,9},{5... | collective-permute-start | bytes 983048 | tf_op jit(solution)/shard_map/ppermute | solution.py:490
  210.7 12.3 %collective-permute-start.34 = (bf16[2,1,1,96,640]{4,3,2,1,0:T(8,128)(2,1)S(1)}, bf16[2,1,1,96,640]{4,3,2,1,0:T(8,128)(2,1)S(1)}, u32[]{:S(2)}, u32[]{:S(2)}) collective-permute-start(bf16[2,1,1,96,640]{4,3,2,1,0:T(8,128)(2,1)S(1)} %shard_map.162), channel_id=1, source_target_pairs={{0,16},{4,20},{8,24},{12,28},{16,0},{20,4},{24,8},{28,12},{1,17},{... | collective-permute-start | bytes 737288 | tf_op jit(solution)/shard_map/ppermute | solution.py:490
  232.2 15.1 %collective-permute-start.41 = (bf16[2,2,96,640]{3,2,1,0:T(8,128)(2,1)S(1)}, bf16[2,2,96,640]{3,2,1,0:T(8,128)(2,1)S(1)}, u32[]{:S(2)}, u32[]{:S(2)}) collective-permute-start(bf16[2,2,96,640]{3,2,1,0:T(8,128)(2,1)S(1)} %shard_map.168.refs_1_), channel_id=1, source_target_pairs={{0,1},{1,0},{2,3},{3,2},{4,5},{5,4},{6,7},{7,6},{8,9},{9,8},{10,11... | collective-permute-start | bytes 1474568 | tf_op jit(solution)/shard_map/ppermute | solution.py:500
  232.3 15.0 %collective-permute-start.40 = (bf16[1,2,128,640]{3,2,1,0:T(8,128)(2,1)S(1)}, bf16[1,2,128,640]{3,2,1,0:T(8,128)(2,1)S(1)}, u32[]{:S(2)}, u32[]{:S(2)}) collective-permute-start(bf16[1,2,128,640]{3,2,1,0:T(8,128)(2,1)S(1)} %shard_map.160.refs_0_), channel_id=1, source_target_pairs={{0,1},{1,0},{2,3},{3,2},{4,5},{5,4},{6,7},{7,6},{8,9},{9,8},{10,11... | collective-permute-start | bytes 983048 | tf_op jit(solution)/shard_map/ppermute | solution.py:500
  232.8 12.2 %collective-permute-start.42 = (bf16[2,1,2,80,256]{4,3,2,1,0:T(8,128)(2,1)S(1)}, bf16[2,1,2,80,256]{4,3,2,1,0:T(8,128)(2,1)S(1)}, u32[]{:S(2)}, u32[]{:S(2)}) collective-permute-start(bf16[2,1,2,80,256]{4,3,2,1,0:T(8,128)(2,1)S(1)} %shard_map.165), channel_id=1, source_target_pairs={{0,16},{4,20},{8,24},{12,28},{16,0},{20,4},{24,8},{28,12},{1,17},{... | collective-permute-start | bytes 491528 | tf_op jit(solution)/shard_map/ppermute | solution.py:490
  233.8 18.9 %collective-permute-start.44 = (bf16[2,1,2,80,128]{4,3,2,1,0:T(8,128)(2,1)S(1)}, bf16[2,1,2,80,128]{4,3,2,1,0:T(8,128)(2,1)S(1)}, u32[]{:S(2)}, u32[]{:S(2)}) collective-permute-start(bf16[2,1,2,80,128]{4,3,2,1,0:T(8,128)(2,1)S(1)} %shard_map.167), channel_id=1, source_target_pairs={{0,16},{4,20},{8,24},{12,28},{16,0},{20,4},{24,8},{28,12},{1,17},{... | collective-permute-start | bytes 245768 | tf_op jit(solution)/shard_map/ppermute | solution.py:490
  (88 other events, 750.8 us)

commit v6 on v5

--- a/solution.py
+++ b/solution.py
@@ -41,7 +41,7 @@
 def widths(shard):
     if shard % LANES:
         return (shard,)
-    first = shard // LANES * 2 // 5 * LANES
+    first = shard // LANES * 3 // 5 * LANES
     return (first, shard - first)
 
 
@@ -65,9 +65,9 @@
         parts = [
             lax.dynamic_slice_in_dim(hidden, (z * nx + at) * shard, shard, 1).T for z in range(nz)
         ]
-        return [jnp.concatenate([cotangent.T, *parts])]
-
-    def body(at_ref, h_ref, cot_ref, out_ref, *later_refs):
+        return jnp.concatenate([cotangent.T, *parts])
+
+    def body(at_ref, h_ref, cot_ref, out_ref):
         z = pl.program_id(0)
 
         @pl.when(z == 0)
@@ -75,10 +75,6 @@
             out_ref[:model] = cot_ref[...].T
 
         out_ref[pl.ds(pl.multiple_of(model + z * first, LANES), first)] = h_ref[:, :first].T
-        start = first
-        for width, later_ref in zip(cuts[1:], later_refs):
-            later_ref[0] = h_ref[:, start : start + width].T
-            start += width
 
     total = model + nz * first
     return pl.pallas_call(
@@ -90,13 +86,36 @@
                 pl.BlockSpec((tokens, shard), lambda z, a: (0, z * nx + a[0])),
                 pl.BlockSpec((tokens, model), lambda z, a: (0, 0)),
             ],
-            out_specs=[pl.BlockSpec((total, tokens), lambda z, a: (0, 0))]
-            + [pl.BlockSpec((1, w, tokens), lambda z, a: (z, 0, 0)) for w in cuts[1:]],
-        ),
-        out_shape=[jax.ShapeDtypeStruct((total, tokens), BF16)]
-        + [jax.ShapeDtypeStruct((nz, w, tokens), BF16) for w in cuts[1:]],
-        **params(),
+            out_specs=pl.BlockSpec((total, tokens), lambda z, a: (0, 0)),
+        ),
+        out_shape=jax.ShapeDtypeStruct((total, tokens), BF16),
+        **params(WIDE),
     )(jnp.reshape(at, (1,)).astype(jnp.int32), hidden, cotangent)
+
+
+def pack_later(hidden, at, nz, nx, cuts):
+    tokens, hidden_width = hidden.shape
+    shard = hidden_width // (nz * nx)
+    if len(cuts) == 1:
+        return []
+
+    def body(at_ref, h_ref, *out_refs):
+        start = cuts[0]
+        for width, out_ref in zip(cuts[1:], out_refs):
+            out_ref[0] = h_ref[:, start : start + width].T
+            start += width
+
+    return pl.pallas_call(
+        body,
+        grid_spec=pltpu.PrefetchScalarGridSpec(
+            num_scalar_prefetch=1,
+            grid=(nz,),
+            in_specs=[pl.BlockSpec((tokens, shard), lambda z, a: (0, z * nx + a[0]))],
+            out_specs=[pl.BlockSpec((1, w, tokens), lambda z, a: (z, 0, 0)) for w in cuts[1:]],
+        ),
+        out_shape=[jax.ShapeDtypeStruct((nz, w, tokens), BF16) for w in cuts[1:]],
+        **params(WIDE),
+    )(jnp.reshape(at, (1,)).astype(jnp.int32), hidden)
 
 
 class Tokens:
@@ -574,9 +593,8 @@
         packs, hiddens = [], []
         for t in range(1, nx):
             sent = pack(*order.after(hidden_pre, cotangent), (x + t) % nx, nz, nx, cuts)
-            order.did(sent[0])
-            packs.append(along_x(sent[0], t))
-            hiddens.append([along_x(value, t) for value in sent[1:]])
+            order.did(sent)
+            packs.append(along_x(sent, t))
 
         part = half_rows(*order.after(w_out), core)
         order.did(part)
@@ -584,7 +602,12 @@
         order.did(flipped)
         columns = [flipped] + [along_x(flipped, t) for t in range(1, nx)]
         own = pack(*order.after(hidden_pre, cotangent), x, nz, nx, cuts)
-        order.did(own[0])
+        order.did(own)
+        for t in range(nx):
+            value = pack_later(*order.after(hidden_pre), (x + t) % nx, nz, nx, cuts)
+            if value:
+                order.did(value[0])
+            hiddens.append([along_x(h, t) for h in value] if t else value)
         found = {0: part, nz // 2: along_z(part, nz // 2)}
         bit = nz // 4
         while bit:
@@ -596,15 +619,13 @@
             bit //= 2
         found = [found[key] for key in range(nz)]
         crossed = [across(value) for value in [*order.after(*found[: nz // 2]), *found[nz // 2 :]]]
-        packs = [own[0]] + packs
-        hiddens = [own[1:]] + hiddens
-
-        parts = [1] + [PARTS] * last
+        packs = [own] + packs
+
+        parts = [PARTS for _ in chunks]
         outs = [None for _ in chunks]
         pieces_in = [(0, 0, cuts[0])]
         if last:
-            small = cuts[1] // 3
-            pieces_in += [(1, 0, 2 * small), (1, 2, small)]
+            pieces_in.append((1, 0, cuts[1]))
         ins = [None for _ in pieces_in]
         pres = [None for _ in chunks]
 
@@ -678,38 +699,34 @@
         start_in(0)
         outs[0].send_z()
         ins[0].send_y()
-        outs[0].send_z()
-        ins[0].send_z()
-        outs[0].finish()
         if last:
             start_out(1)
             outs[1].send_y()
             start_pre(1)
+            outs[0].send_z()
             ins[0].send_z()
             start_in(1)
-            start_in(2)
             ins[1].send_y()
-            ins[2].send_y()
+            outs[1].send_z()
+            ins[0].send_z()
+            outs[0].finish()
+            outs[1].send_z()
+            ins[1].send_z()
             ins[0].finish()
-            outs[1].send_z()
-            ins[0].stack_x()
             outs[0].stack_y(True)
             ins[1].send_z()
-            outs[1].send_z()
+            ins[0].stack_x()
+            outs[1].finish()
             ins[0].stack_y()
-            ins[2].send_z()
-            ins[1].send_z()
-            outs[1].finish()
-            ins[2].send_z()
+            ins[1].finish()
             outs[1].stack_y(True)
-            ins[1].finish()
+            ins[1].stack_x()
             first_out, second_out, update_out, tile = moments_out()
-            ins[2].finish()
-            for n in (1, 2):
-                ins[n].stack_x()
-            for n in (1, 2):
-                ins[n].stack_y()
+            ins[1].stack_y()
         else:
+            outs[0].send_z()
+            ins[0].send_z()
+            outs[0].finish()
             ins[0].send_z()
             outs[0].stack_y(True)
             ins[0].finish()

time: 293 us -> 282 us (0.962)
  waiting for transfers between devices: 116 us -> 96.7 us
  Pallas kernels: 105 us -> 117 us
  local copies, waits for them, and re-layouts: 21 us -> 17.8 us
    ppermute x16 -> x14, waiting for transfers between devices: 83.5 us -> 53.3 us  [along_z(): return lax.ppermute(value, 'gx', pairs)]
    ppermute x7 -> x6, waiting for transfers between devices: 15.6 us -> 33.1 us  [along_x(): return lax.ppermute(value, 'gx', pairs)]
    ppermute x10 -> x8, waiting for transfers between devices: 12 us -> 1.27 us  [along_y(): return lax.ppermute(value, 'gy', pairs)]
    pallas_call x0 -> x2, Pallas kernels: none -> 7.9 us  [pack_later(): pl.pallas_call(body, grid_spec=pltpu.PrefetchScalarGridSpec(num_scalar_pr...]
    pallas_call x2, Pallas kernels: 4.59 us -> 10.3 us  [pack(): pl.pallas_call(body, grid_spec=pltpu.PrefetchScalarGridSpec(num_scalar_pr...]
    ppermute x22 -> x20, waiting for transfers between devices: 4.62 us -> 9.05 us  [across(): return lax.ppermute(value, 'gy', pairs)]
    unnamed x114 -> x120, local copies, waits for them, and re-layouts: 21 us -> 17.8 us
    pallas_call x20 -> x16, Pallas kernels: 28.4 us -> 25.2 us  [reduce_step(): pl.pallas_call(body, grid_spec=pltpu.PrefetchScalarGridSpec(num_scalar_pr...]
  transfers between devices with their start and end apart: 55 -> 48, of which waited for: 24 -> 30; matrix products, arithmetic and copies ran while one was open for 0% -> 0% of each run, Pallas kernels for 26% -> 32%
where the time goes in v6:
time: 282 us; the launch traced here: 280 us
  Pallas kernels  117 us (41%)
  waiting for transfers between devices  96.7 us (34%)
  starting transfers between devices  47.5 us (17%)
  local copies, waits for them, and re-layouts  17.8 us (6%)
    ppermute x14, waiting for transfers between devices, along_z(): return lax.ppermute(value, 'gx', pairs)  53.3 us
    ppermute x6, waiting for transfers between devices, along_x(): return lax.ppermute(value, 'gx', pairs)  33.1 us
    pallas_call x16, Pallas kernels, reduce_step(): pl.pallas_call(body, grid_spec=pltpu.PrefetchScalarGridSpec(num_scalar_pr...  25.2 us
    ppermute x14, starting transfers between devices, along_z(): return lax.ppermute(value, 'gx', pairs)  23.5 us
    unnamed x120, local copies, waits for them, and re-layouts  17.8 us
    pallas_call x2, Pallas kernels, grad_pre_chunk(): pl.pallas_call(body, grid_spec=pltpu.PrefetchScalarGridSpec(num_scalar_pr...  17.1 us
    pallas_call x2, Pallas kernels, grad_in_chunk(): pl.pallas_call(body, grid_spec=pltpu.PrefetchScalarGridSpec(num_scalar_pr...  14.7 us
    pallas_call x2, Pallas kernels, grad_out_chunk(): pl.pallas_call(body, grid_spec=pltpu.PrefetchScalarGridSpec(num_scalar_pr...  13.7 us
  transfers between devices with their start and end apart: 48, of which 30 were waited for; matrix products, arithmetic and copies ran while one was open for 0% of the time, Pallas kernels for 32%

profile of v6, /device:TPU:0, one launch (start us, length us, event | category | flops | bytes accessed | tf_op | source)
XLA Modules:
  0.0 280.5 jit_solution(1732108914095751425)
XLA Ops:
  0.7 5.2 %shard_map.136 = bf16[2816,512]{1,0:T(8,128)(2,1)} custom-call(s32[1]{0:T(128)} %bitcast.6.at_ref, bf16[512,5120]{1,0:T(8,128)(2,1)} %h_ref.4, bf16[512,1280]{1,0:T(8,128)(2,1)} %cot_ref.2), custom_call_target="tpu_custom_call" | custom-call | flops 1 | bytes 1 | tf_op jit(solution)/shard_map/pallas_call | solution.py:80
  17.7 5.1 %shard_map.139.refs_0_ = bf16[2816,512]{1,0:T(8,128)(2,1)} custom-call(s32[1]{0:T(128)} %bitcast.3.at_ref, bf16[512,5120]{1,0:T(8,128)(2,1)} %h_ref.4, bf16[512,1280]{1,0:T(8,128)(2,1)} %cot_ref.2), custom_call_target="tpu_custom_call" | custom-call | flops 1 | bytes 1 | tf_op jit(solution)/shard_map/pallas_call | solution.py:80
  22.8 3.9 %shard_map.140.refs_2_ = bf16[4,256,512]{2,1,0:T(8,128)(2,1)} custom-call(s32[1]{0:T(128)} %bitcast.7.at_ref, bf16[512,5120]{1,0:T(8,128)(2,1)} %h_ref.4), custom_call_target="tpu_custom_call" | custom-call | flops 1 | bytes 1 | tf_op jit(solution)/shard_map/pallas_call | solution.py:108
  26.7 4.0 %shard_map.141 = bf16[4,256,512]{2,1,0:T(8,128)(2,1)} custom-call(s32[1]{0:T(128)} %bitcast.6.at_ref, bf16[512,5120]{1,0:T(8,128)(2,1)} %h_ref.4), custom_call_target="tpu_custom_call" | custom-call | flops 1 | bytes 1 | tf_op jit(solution)/shard_map/pallas_call | solution.py:108
  30.7 17.7 %collective-permute-done.1.refs_3_.refs_5_ = bf16[320,1280]{1,0:T(8,128)(2,1)} collective-permute-done((bf16[320,1280]{1,0:T(8,128)(2,1)}, bf16[320,1280]{1,0:T(8,128)(2,1)}, u32[]{:S(2)}, u32[]{:S(2)}) %collective-permute-start.1) | collective-permute-done | bytes 819232 | tf_op jit(solution)/shard_map/ppermute | solution.py:509
  52.1 19.4 %collective-permute-done.refs_1_ = bf16[2816,512]{1,0:T(8,128)(2,1)} collective-permute-done((bf16[2816,512]{1,0:T(8,128)(2,1)}, bf16[2816,512]{1,0:T(8,128)(2,1)}, u32[]{:S(2)}, u32[]{:S(2)}) %collective-permute-start) | collective-permute-done | bytes 2883616 | tf_op jit(solution)/shard_map/ppermute | solution.py:505
  71.6 8.1 %shard_map.142 = (bf16[4,192,640]{2,1,0:T(8,128)(2,1)}, bf16[4,192,640]{2,1,0:T(8,128)(2,1)}, bf16[2,4,192,640]{3,2,1,0:T(8,128)(2,1)S(1)}) custom-call(s32[1]{0:T(128)} %bitcast.c_ref, bf16[2816,512]{1,0:T(8,128)(2,1)S(1)} %copy-done, bf16[2816,512]{1,0:T(8,128)(2,1)} %collective-permute-done.refs_1_), custom_call_target="tpu_custom_call" | custom-call | flops 1 | bytes 1 | tf_op jit(solution)/shard_map/pallas_call | solution.py:165
  86.8 3.2 %shard_map.143 = bf16[2,4,1,96,640]{4,3,2,1,0:T(8,128)(2,1)S(1)} custom-call(s32[3]{0:T(128)S(1)} %pad_add_fusion.1.at_ref, bf16[2,4,1,2,96,640]{5,4,3,2,1,0:T(8,128)(2,1)S(1)} %bitcast.25, bf16[4,1,2,96,640]{4,3,2,1,0:T(8,128)(2,1)} %bitcast.9.refs_1_, bf16[4,1,2,96,640]{4,3,2,1,0:T(8,128)(2,1)} %bitcast.10.refs_2_), custom_call_target="tpu_custom_call" | custom-call | flops 1 | bytes 1 | tf_op jit(solution)/shard_map/pallas_call | solution.py:400
  91.9 10.1 %collective-permute-done.8.refs_5_.refs_7_ = bf16[320,1280]{1,0:T(8,128)(2,1)} collective-permute-done((bf16[320,1280]{1,0:T(8,128)(2,1)}, bf16[320,1280]{1,0:T(8,128)(2,1)}, u32[]{:S(2)}, u32[]{:S(2)}) %collective-permute-start.8) | collective-permute-done | bytes 819232 | tf_op jit(solution)/shard_map/ppermute | solution.py:509
  104.6 9.8 %shard_map.144.g_ref = bf16[4,384,1024]{2,1,0:T(8,128)(2,1)S(1)} custom-call(s32[2]{0:T(128)S(1)} %pad_add_fusion.2.c_ref, bf16[2816,512]{1,0:T(8,128)(2,1)S(1)} %copy-done, bf16[2816,512]{1,0:T(8,128)(2,1)} %collective-permute-done.refs_1_, bf16[320,1280]{1,0:T(8,128)(2,1)S(1)} %copy-done.26, bf16[320,1280]{1,0:T(8,128)(2,1)} %collective-permute-done.1.refs_3_.refs_5_, ...), custom_call_target="tpu_custom_call" | custom-call | flops 1 | bytes 1 | tf_op jit(solution)/shard_map/pallas_call | solution.py:204
  115.3 8.7 %shard_map.145 = (bf16[640,384]{1,0:T(8,128)(2,1)S(1)}, bf16[640,384]{1,0:T(8,128)(2,1)S(1)}, bf16[640,384]{1,0:T(8,128)(2,1)S(1)}, bf16[640,384]{1,0:T(8,128)(2,1)S(1)}, bf16[2,1280,384]{2,1,0:T(8,128)(2,1)S(1)}) custom-call(s32[1]{0:T(128)} %bitcast.c_ref, bf16[4,384,1024]{2,1,0:T(8,128)(2,1)S(1)} %shard_map.144.g_ref, ...), custom_call_target="tpu_custom_call" | custom-call | flops 1 | bytes 1 | tf_op jit(solution)/shard_map/pallas_call | solution.py:241
  131.1 5.2 %collective-permute-done.13.refs_3_ = bf16[4,256,512]{2,1,0:T(8,128)(2,1)S(1)} collective-permute-done((bf16[4,256,512]{2,1,0:T(8,128)(2,1)S(1)}, bf16[4,256,512]{2,1,0:T(8,128)(2,1)S(1)}, u32[]{:S(2)}, u32[]{:S(2)}) %collective-permute-start.13) | collective-permute-done | bytes 1048608 | tf_op jit(solution)/shard_map/ppermute | solution.py:505
  136.4 5.6 %shard_map.148 = (bf16[4,128,640]{2,1,0:T(8,128)(2,1)S(1)}, bf16[4,128,640]{2,1,0:T(8,128)(2,1)S(1)}, bf16[2,4,128,640]{3,2,1,0:T(8,128)(2,1)S(1)}) custom-call(s32[1]{0:T(128)} %bitcast.c_ref, bf16[2816,512]{1,0:T(8,128)(2,1)S(1)} %copy-done, bf16[2816,512]{1,0:T(8,128)(2,1)} %collective-permute-done.refs_1_, bf16[4,256,512]{2,1,0:T(8,128)(2,1)S(1)} %copy-done.14, ...), custom_call_target="tpu_custom_call" | custom-call | flops 1 | bytes 1 | tf_op jit(solution)/shard_map/pallas_call | solution.py:165
  147.7 7.4 %shard_map.150.g_ref = bf16[4,256,1024]{2,1,0:T(8,128)(2,1)S(1)} custom-call(s32[2]{0:T(128)S(1)} %pad_add_fusion.2.c_ref, bf16[2816,512]{1,0:T(8,128)(2,1)S(1)} %copy-done, bf16[2816,512]{1,0:T(8,128)(2,1)} %collective-permute-done.refs_1_, bf16[4,256,512]{2,1,0:T(8,128)(2,1)S(1)} %copy-done.14, bf16[4,256,512]{2,1,0:T(8,128)(2,1)S(1)} %collective-permute-done.13.refs_3_, ...), custom_call_target="tpu_custom_call" | custom-call | flops 1 | bytes 1 | tf_op jit(solution)/shard_map/pallas_call | solution.py:204
  158.8 6.0 %shard_map.153 = (bf16[640,256]{1,0:T(8,128)(2,1)S(1)}, bf16[640,256]{1,0:T(8,128)(2,1)S(1)}, bf16[640,256]{1,0:T(8,128)(2,1)S(1)}, bf16[640,256]{1,0:T(8,128)(2,1)S(1)}, bf16[2,1280,256]{2,1,0:T(8,128)(2,1)S(1)}) custom-call(s32[1]{0:T(128)} %bitcast.c_ref, bf16[4,256,1024]{2,1,0:T(8,128)(2,1)S(1)} %shard_map.150.g_ref, ...), custom_call_target="tpu_custom_call" | custom-call | flops 1 | bytes 1 | tf_op jit(solution)/shard_map/pallas_call | solution.py:241
  176.3 13.8 %collective-permute-done.22.refs_6_ = bf16[2,2,2,80,384]{4,3,2,1,0:T(8,128)(2,1)S(1)} collective-permute-done((bf16[2,2,2,80,384]{4,3,2,1,0:T(8,128)(2,1)S(1)}, bf16[2,2,2,80,384]{4,3,2,1,0:T(8,128)(2,1)S(1)}, u32[]{:S(2)}, u32[]{:S(2)}) %collective-permute-start.22) | collective-permute-done | bytes 491552 | tf_op jit(solution)/shard_map/ppermute | solution.py:509
  200.2 4.7 %collective-permute-start.34 = (bf16[2,2,2,80,256]{4,3,2,1,0:T(8,128)(2,1)}, bf16[2,2,2,80,256]{4,3,2,1,0:T(8,128)(2,1)}, u32[]{:S(2)}, u32[]{:S(2)}) collective-permute-start(bf16[2,2,2,80,256]{4,3,2,1,0:T(8,128)(2,1)} %shard_map.159), channel_id=1, source_target_pairs={{0,8},{4,12},{8,0},{12,4},{16,24},{20,28},{24,16},{28,20},{1,9},{5... | collective-permute-start | bytes 983048 | tf_op jit(solution)/shard_map/ppermute | solution.py:509
  243.7 4.3 %collective-permute-done.40.refs_1_ = bf16[2,80,256]{2,1,0:T(8,128)(2,1)S(1)} collective-permute-done((bf16[2,80,256]{2,1,0:T(8,128)(2,1)S(1)}, bf16[2,80,256]{2,1,0:T(8,128)(2,1)S(1)}, u32[]{:S(2)}, u32[]{:S(2)}) %collective-permute-start.40) | collective-permute-done | bytes 81952 | tf_op jit(solution)/shard_map/ppermute | solution.py:505
  250.2 5.4 %shard_map.169 = (f32[640,1280]{1,0:T(8,128)}, f32[640,1280]{1,0:T(8,128)}, f32[640,1280]{1,0:T(8,128)S(1)}, f32[16,128]{1,0:T(8,128)S(1)}) custom-call(s32[1]{0:T(128)} %bitcast.c_ref, f32[640,1280]{1,0:T(8,128)S(1)} %copy-done.6, f32[640,1280]{1,0:T(8,128)S(1)} %copy-done.43, f32[640,1280]{1,0:T(8,128)S(1)} %copy-done.44, ...), custom_call_target="tpu_custom_call" | custom-call | flops 1 | bytes 1 | tf_op jit(solution)/shard_map/pallas_call | solution.py:450
  257.9 6.2 %shard_map.171 = (f32[160,5120]{1,0:T(8,128)}, f32[160,5120]{1,0:T(8,128)}, f32[160,5120]{1,0:T(8,128)S(1)}, f32[32,128]{1,0:T(8,128)S(1)}) custom-call(s32[1]{0:T(128)} %bitcast.c_ref, f32[160,5120]{1,0:T(8,128)S(1)} %copy-done.9, f32[160,5120]{1,0:T(8,128)S(1)} %copy-done.45, f32[160,5120]{1,0:T(8,128)S(1)} %copy-done.46, ...), custom_call_target="tpu_custom_call" | custom-call | flops 1 | bytes 1 | tf_op jit(solution)/shard_map/pallas_call | solution.py:450
  265.3 3.3 %collective-permute-start.44 = (f32[32,128]{1,0:T(8,128)S(1)}, f32[32,128]{1,0:T(8,128)S(1)}, u32[]{:S(2)}, u32[]{:S(2)}) collective-permute-start(f32[32,128]{1,0:T(8,128)S(1)} %get-tuple-element.385.refs_0_), channel_id=1, source_target_pairs={{0,8},{4,12},{8,0},{12,4},{16,24},{20,28},{24,16},{28,20},{1,9},{5... | collective-permute-start | bytes 49160 | tf_op jit(solution)/shard_map/ppermute | solution.py:509
  270.8 3.2 %collective-permute-done.47.refs_1_ = f32[32,128]{1,0:T(8,128)S(1)} collective-permute-done((f32[32,128]{1,0:T(8,128)S(1)}, f32[32,128]{1,0:T(8,128)S(1)}, u32[]{:S(2)}, u32[]{:S(2)}) %collective-permute-start.47) | collective-permute-done | bytes 16416 | tf_op jit(solution)/shard_map/ppermute | solution.py:505
  274.0 3.2 %shard_map.173 = f32[160,5120]{1,0:T(8,128)} custom-call(f32[160,5120]{1,0:T(8,128)S(1)} %copy-done.9, f32[160,5120]{1,0:T(8,128)S(1)} %get-tuple-element.390.u_ref, f32[32,128]{1,0:T(8,128)S(1)} %shard_map.172.refs_0_, f32[32,128]{1,0:T(8,128)S(1)} %collective-permute-done.47.refs_1_), custom_call_target="tpu_custom_call" | custom-call | flops 1 | bytes 1 | tf_op jit(solution)/shard_map/pallas_call | solution.py:477
  277.3 3.2 %shard_map.174 = f32[640,1280]{1,0:T(8,128)} custom-call(f32[640,1280]{1,0:T(8,128)S(1)} %copy-done.6, f32[640,1280]{1,0:T(8,128)S(1)} %get-tuple-element.397.u_ref, f32[32,128]{1,0:T(8,128)S(1)} %shard_map.172.refs_0_, f32[32,128]{1,0:T(8,128)S(1)} %collective-permute-done.47.refs_1_), custom_call_target="tpu_custom_call" | custom-call | flops 1 | bytes 1 | tf_op jit(solution)/shard_map/pallas_call | solution.py:477
  (235 shorter events, 112.5 us)
Async XLA Ops:
  5.8 65.7 %collective-permute-start = (bf16[2816,512]{1,0:T(8,128)(2,1)}, bf16[2816,512]{1,0:T(8,128)(2,1)}, u32[]{:S(2)}, u32[]{:S(2)}) collective-permute-start(bf16[2816,512]{1,0:T(8,128)(2,1)} %shard_map.136), channel_id=1, source_target_pairs={{0,4},{4,0},{8,12},{12,8},{16,20},{20,16},{24,28},{28,24},{1,5},{5... | collective-permute-start | bytes 8650760 | tf_op jit(solution)/shard_map/ppermute | solution.py:505
  11.0 37.4 %collective-permute-start.1 = (bf16[320,1280]{1,0:T(8,128)(2,1)}, bf16[320,1280]{1,0:T(8,128)(2,1)}, u32[]{:S(2)}, u32[]{:S(2)}) collective-permute-start(bf16[320,1280]{1,0:T(8,128)(2,1)} %shard_map.137.refs_2_.refs_4_), channel_id=1, source_target_pairs={{0,8},{4,12},{8,0},{12,4},{16,24},{20,28},{24,16},{28,20},{1,9},{5... | collective-permute-start | bytes 2457608 | tf_op jit(solution)/shard_map/ppermute | solution.py:509
  12.5 38.3 %collective-permute-start.4 = (bf16[320,1280]{1,0:T(8,128)(2,1)}, bf16[320,1280]{1,0:T(8,128)(2,1)}, u32[]{:S(2)}, u32[]{:S(2)}) collective-permute-start(bf16[320,1280]{1,0:T(8,128)(2,1)} %shard_map.137.refs_2_.refs_4_), channel_id=1, source_target_pairs={{0,16},{4,20},{8,24},{12,28},{16,0},{20,4},{24,8},{28,12},{1,17},{... | collective-permute-start | bytes 2457608 | tf_op jit(solution)/shard_map/ppermute | solution.py:509
  81.4 20.6 %collective-permute-start.8 = (bf16[320,1280]{1,0:T(8,128)(2,1)}, bf16[320,1280]{1,0:T(8,128)(2,1)}, u32[]{:S(2)}, u32[]{:S(2)}) collective-permute-start(bf16[320,1280]{1,0:T(8,128)(2,1)} %collective-permute-done.4.refs_4_.refs_6_), channel_id=1, source_target_pairs={{0,8},{4,12},{8,0},{12,4},{16,24},{20,28},{24,16},{28,20},{1,9},{5... | collective-permute-start | bytes 2457608 | tf_op jit(solution)/shard_map/ppermute | solution.py:509
  83.3 32.0 %collective-permute-start.11 = (bf16[1280,512]{1,0:T(8,128)(2,1)}, bf16[1280,512]{1,0:T(8,128)(2,1)}, u32[]{:S(2)}, u32[]{:S(2)}) collective-permute-start(bf16[1280,512]{1,0:T(8,128)(2,1)} %shard_map.138.refs_0_), channel_id=1, source_target_pairs={{0,4},{4,0},{8,12},{12,8},{16,20},{20,16},{24,28},{28,24},{1,5},{5... | collective-permute-start | bytes 3932168 | tf_op jit(solution)/shard_map/ppermute | solution.py:505
  90.1 34.6 %collective-permute-start.7 = (bf16[2,4,1,96,640]{4,3,2,1,0:T(8,128)(2,1)S(1)}, bf16[2,4,1,96,640]{4,3,2,1,0:T(8,128)(2,1)S(1)}, u32[]{:S(2)}, u32[]{:S(2)}) collective-permute-start(bf16[2,4,1,96,640]{4,3,2,1,0:T(8,128)(2,1)S(1)} %shard_map.143), channel_id=1, source_target_pairs={{0,2},{1,3},{2,0},{3,1},{4,6},{5,7},{6,4},{7,5},{8,10},{9,11},{10,... | collective-permute-start | bytes 2949128 | tf_op jit(solution)/shard_map/ppermute | solution.py:515
  91.9 11.8 %collective-permute-start.9 = (bf16[320,1280]{1,0:T(8,128)(2,1)}, bf16[320,1280]{1,0:T(8,128)(2,1)S(1)}, u32[]{:S(2)}, u32[]{:S(2)}) collective-permute-start(bf16[320,1280]{1,0:T(8,128)(2,1)} %collective-permute-done.4.refs_4_.refs_6_), channel_id=1, source_target_pairs={{0,1},{1,0},{2,3},{3,2},{4,5},{5,4},{6,7},{7,6},{8,9},{9,8},{10,11... | collective-permute-start | bytes 2457608 | tf_op jit(solution)/shard_map/ppermute | solution.py:519
  102.0 34.4 %collective-permute-start.13 = (bf16[4,256,512]{2,1,0:T(8,128)(2,1)S(1)}, bf16[4,256,512]{2,1,0:T(8,128)(2,1)S(1)}, u32[]{:S(2)}, u32[]{:S(2)}) collective-permute-start(bf16[4,256,512]{2,1,0:T(8,128)(2,1)S(1)} %copy-done.59), channel_id=1, source_target_pairs={{0,4},{4,0},{8,12},{12,8},{16,20},{20,16},{24,28},{28,24},{1,5},{5... | collective-permute-start | bytes 3145736 | tf_op jit(solution)/shard_map/ppermute | solution.py:505
  129.5 27.9 %collective-permute-start.21 = (bf16[2,4,2,80,384]{4,3,2,1,0:T(8,128)(2,1)S(1)}, bf16[2,4,2,80,384]{4,3,2,1,0:T(8,128)(2,1)S(1)}, u32[]{:S(2)}, u32[]{:S(2)}) collective-permute-start(bf16[2,4,2,80,384]{4,3,2,1,0:T(8,128)(2,1)S(1)} %shard_map.147), channel_id=1, source_target_pairs={{0,2},{1,3},{2,0},{3,1},{4,6},{5,7},{6,4},{7,5},{8,10},{9,11},{10,... | collective-permute-start | bytes 2949128 | tf_op jit(solution)/shard_map/ppermute | solution.py:515
  142.6 13.2 %collective-permute-start.12 = (bf16[2,2,1,96,640]{4,3,2,1,0:T(8,128)(2,1)S(1)}, bf16[2,2,1,96,640]{4,3,2,1,0:T(8,128)(2,1)S(1)}, u32[]{:S(2)}, u32[]{:S(2)}) collective-permute-start(bf16[2,2,1,96,640]{4,3,2,1,0:T(8,128)(2,1)S(1)} %shard_map.146), channel_id=1, source_target_pairs={{0,8},{4,12},{8,0},{12,4},{16,24},{20,28},{24,16},{28,20},{1,9},{5... | collective-permute-start | bytes 1474568 | tf_op jit(solution)/shard_map/ppermute | solution.py:509
  146.1 25.0 %collective-permute-start.23 = (bf16[2,4,1,64,640]{4,3,2,1,0:T(8,128)(2,1)S(1)}, bf16[2,4,1,64,640]{4,3,2,1,0:T(8,128)(2,1)S(1)}, u32[]{:S(2)}, u32[]{:S(2)}) collective-permute-start(bf16[2,4,1,64,640]{4,3,2,1,0:T(8,128)(2,1)S(1)} %shard_map.149), channel_id=1, source_target_pairs={{0,2},{1,3},{2,0},{3,1},{4,6},{5,7},{6,4},{7,5},{8,10},{9,11},{10,... | collective-permute-start | bytes 1966088 | tf_op jit(solution)/shard_map/ppermute | solution.py:515
  169.1 28.5 %collective-permute-start.30 = (bf16[2,4,2,80,256]{4,3,2,1,0:T(8,128)(2,1)S(1)}, bf16[2,4,2,80,256]{4,3,2,1,0:T(8,128)(2,1)S(1)}, u32[]{:S(2)}, u32[]{:S(2)}) collective-permute-start(bf16[2,4,2,80,256]{4,3,2,1,0:T(8,128)(2,1)S(1)} %shard_map.154), channel_id=1, source_target_pairs={{0,2},{1,3},{2,0},{3,1},{4,6},{5,7},{6,4},{7,5},{8,10},{9,11},{10,... | collective-permute-start | bytes 1966088 | tf_op jit(solution)/shard_map/ppermute | solution.py:515
  170.7 19.4 %collective-permute-start.22 = (bf16[2,2,2,80,384]{4,3,2,1,0:T(8,128)(2,1)S(1)}, bf16[2,2,2,80,384]{4,3,2,1,0:T(8,128)(2,1)S(1)}, u32[]{:S(2)}, u32[]{:S(2)}) collective-permute-start(bf16[2,2,2,80,384]{4,3,2,1,0:T(8,128)(2,1)S(1)} %shard_map.152), channel_id=1, source_target_pairs={{0,8},{4,12},{8,0},{12,4},{16,24},{20,28},{24,16},{28,20},{1,9},{5... | collective-permute-start | bytes 1474568 | tf_op jit(solution)/shard_map/ppermute | solution.py:509
  172.0 24.7 %collective-permute-start.31 = (bf16[2,2,1,64,640]{4,3,2,1,0:T(8,128)(2,1)S(1)}, bf16[2,2,1,64,640]{4,3,2,1,0:T(8,128)(2,1)S(1)}, u32[]{:S(2)}, u32[]{:S(2)}) collective-permute-start(bf16[2,2,1,64,640]{4,3,2,1,0:T(8,128)(2,1)S(1)} %shard_map.155), channel_id=1, source_target_pairs={{0,8},{4,12},{8,0},{12,4},{16,24},{20,28},{24,16},{28,20},{1,9},{5... | collective-permute-start | bytes 983048 | tf_op jit(solution)/shard_map/ppermute | solution.py:509
  173.7 21.4 %collective-permute-start.20 = (bf16[2,1,1,96,640]{4,3,2,1,0:T(8,128)(2,1)S(1)}, bf16[2,1,1,96,640]{4,3,2,1,0:T(8,128)(2,1)S(1)}, u32[]{:S(2)}, u32[]{:S(2)}) collective-permute-start(bf16[2,1,1,96,640]{4,3,2,1,0:T(8,128)(2,1)S(1)} %shard_map.151), channel_id=1, source_target_pairs={{0,16},{4,20},{8,24},{12,28},{16,0},{20,4},{24,8},{28,12},{1,17},{... | collective-permute-start | bytes 737288 | tf_op jit(solution)/shard_map/ppermute | solution.py:509
  191.6 16.8 %collective-permute-start.29 = (bf16[2,1,2,80,384]{4,3,2,1,0:T(8,128)(2,1)}, bf16[2,1,2,80,384]{4,3,2,1,0:T(8,128)(2,1)}, u32[]{:S(2)}, u32[]{:S(2)}) collective-permute-start(bf16[2,1,2,80,384]{4,3,2,1,0:T(8,128)(2,1)} %shard_map.156), channel_id=1, source_target_pairs={{0,16},{4,20},{8,24},{12,28},{16,0},{20,4},{24,8},{28,12},{1,17},{... | collective-permute-start | bytes 737288 | tf_op jit(solution)/shard_map/ppermute | solution.py:509
  200.2 21.0 %collective-permute-start.34 = (bf16[2,2,2,80,256]{4,3,2,1,0:T(8,128)(2,1)}, bf16[2,2,2,80,256]{4,3,2,1,0:T(8,128)(2,1)}, u32[]{:S(2)}, u32[]{:S(2)}) collective-permute-start(bf16[2,2,2,80,256]{4,3,2,1,0:T(8,128)(2,1)} %shard_map.159), channel_id=1, source_target_pairs={{0,8},{4,12},{8,0},{12,4},{16,24},{20,28},{24,16},{28,20},{1,9},{5... | collective-permute-start | bytes 983048 | tf_op jit(solution)/shard_map/ppermute | solution.py:509
  204.9 14.7 %collective-permute-start.28 = (bf16[2,96,640]{2,1,0:T(8,128)(2,1)S(1)}, bf16[2,96,640]{2,1,0:T(8,128)(2,1)}, u32[]{:S(2)}, u32[]{:S(2)}) collective-permute-start(bf16[2,96,640]{2,1,0:T(8,128)(2,1)S(1)} %shard_map.157.refs_0_), channel_id=1, source_target_pairs={{0,2},{1,3},{2,0},{3,1},{4,6},{5,7},{6,4},{7,5},{8,10},{9,11},{10,... | collective-permute-start | bytes 737288 | tf_op jit(solution)/shard_map/ppermute | solution.py:515
  217.9 10.2 %collective-permute-start.33 = (bf16[2,80,384]{2,1,0:T(8,128)(2,1)}, bf16[2,80,384]{2,1,0:T(8,128)(2,1)}, u32[]{:S(2)}, u32[]{:S(2)}) collective-permute-start(bf16[2,80,384]{2,1,0:T(8,128)(2,1)} %get-tuple-element.333), channel_id=1, source_target_pairs={{0,4},{4,0},{8,12},{12,8},{16,20},{20,16},{24,28},{28,24},{1,5},{5... | collective-permute-start | bytes 368648 | tf_op jit(solution)/shard_map/ppermute | solution.py:505
  219.5 14.6 %collective-permute-start.32 = (bf16[2,1,1,64,640]{4,3,2,1,0:T(8,128)(2,1)}, bf16[2,1,1,64,640]{4,3,2,1,0:T(8,128)(2,1)S(1)}, u32[]{:S(2)}, u32[]{:S(2)}) collective-permute-start(bf16[2,1,1,64,640]{4,3,2,1,0:T(8,128)(2,1)} %copy-done.56), channel_id=1, source_target_pairs={{0,16},{4,20},{8,24},{12,28},{16,0},{20,4},{24,8},{28,12},{1,17},{... | collective-permute-start | bytes 491528 | tf_op jit(solution)/shard_map/ppermute | solution.py:509
  230.6 8.0 %collective-permute-start.37 = (bf16[2,2,80,384]{3,2,1,0:T(8,128)(2,1)S(1)}, bf16[2,2,80,384]{3,2,1,0:T(8,128)(2,1)S(1)}, u32[]{:S(2)}, u32[]{:S(2)}) collective-permute-start(bf16[2,2,80,384]{3,2,1,0:T(8,128)(2,1)S(1)} %shard_map.163.refs_0_), channel_id=1, source_target_pairs={{0,2},{1,3},{2,0},{3,1},{4,6},{5,7},{6,4},{7,5},{8,10},{9,11},{10,... | collective-permute-start | bytes 737288 | tf_op jit(solution)/shard_map/ppermute | solution.py:515
  231.2 9.5 %collective-permute-start.36 = (bf16[2,1,2,80,256]{4,3,2,1,0:T(8,128)(2,1)S(1)}, bf16[2,1,2,80,256]{4,3,2,1,0:T(8,128)(2,1)S(1)}, u32[]{:S(2)}, u32[]{:S(2)}) collective-permute-start(bf16[2,1,2,80,256]{4,3,2,1,0:T(8,128)(2,1)S(1)} %shard_map.162), channel_id=1, source_target_pairs={{0,16},{4,20},{8,24},{12,28},{16,0},{20,4},{24,8},{28,12},{1,17},{... | collective-permute-start | bytes 491528 | tf_op jit(solution)/shard_map/ppermute | solution.py:509
  237.4 12.7 %collective-permute-start.38 = (bf16[2,2,96,640]{3,2,1,0:T(8,128)(2,1)S(1)}, bf16[2,2,96,640]{3,2,1,0:T(8,128)(2,1)S(1)}, u32[]{:S(2)}, u32[]{:S(2)}) collective-permute-start(bf16[2,2,96,640]{3,2,1,0:T(8,128)(2,1)S(1)} %shard_map.161.refs_0_), channel_id=1, source_target_pairs={{0,1},{1,0},{2,3},{3,2},{4,5},{5,4},{6,7},{7,6},{8,9},{9,8},{10,11... | collective-permute-start | bytes 1474568 | tf_op jit(solution)/shard_map/ppermute | solution.py:519
  243.0 7.1 %collective-permute-start.39 = (bf16[2,2,64,640]{3,2,1,0:T(8,128)(2,1)S(1)}, bf16[2,2,64,640]{3,2,1,0:T(8,128)(2,1)S(1)}, u32[]{:S(2)}, u32[]{:S(2)}) collective-permute-start(bf16[2,2,64,640]{3,2,1,0:T(8,128)(2,1)S(1)} %shard_map.167.refs_1_), channel_id=1, source_target_pairs={{0,1},{1,0},{2,3},{3,2},{4,5},{5,4},{6,7},{7,6},{8,9},{9,8},{10,11... | collective-permute-start | bytes 983048 | tf_op jit(solution)/shard_map/ppermute | solution.py:519
  (84 other events, 1201.1 us)

commit v7 on v6

--- a/solution.py
+++ b/solution.py
@@ -16,6 +16,7 @@
 PARTS = 2
 VMEM = 24 * 1024 * 1024
 WIDE = 56 * 1024 * 1024
+SMALL = 8 * 1024 * 1024
 
 
 def moments(weight, first, second, grad):
@@ -318,7 +319,7 @@
             out_specs=pl.BlockSpec(out, lambda at: (0,) * len(out)),
         ),
         out_shape=jax.ShapeDtypeStruct(out, pieces[0].dtype),
-        **params(),
+        **params(SMALL),
     )(places, *pieces)
 
 
@@ -327,7 +328,7 @@
         refs[-1][...] = sum(ref[...] for ref in refs[:-1])
 
     return pl.pallas_call(
-        body, out_shape=jax.ShapeDtypeStruct(tiles[0].shape, F32), **params()
+        body, out_shape=jax.ShapeDtypeStruct(tiles[0].shape, F32), **params(SMALL)
     )(*tiles)
 
 
@@ -403,7 +404,7 @@
             num_scalar_prefetch=1, grid=(count,), in_specs=specs, out_specs=out_specs
         ),
         out_shape=out_shape,
-        **params(),
+        **params(SMALL),
     )(place, keep, *crosses, *from_y, *from_z)
     return out if split else out[0]
 
@@ -652,7 +653,7 @@
             chunk, block, width = pieces_in[k]
             got = order.after(pres[chunk], *columns)
             *sends, keep = grad_in_chunk(
-                got[0], got[1:], core, scale_in, PARTS if width > LANES else 1, block, width
+                got[0], got[1:], core, scale_in, 1, block, width
             )
             order.did(keep)
             shape = (nz // CORES, nz, nx, ny, rows // ny, width)
@@ -670,16 +671,21 @@
             order.did(value)
             return value
 
-        def moments_out():
+        def moments_out(tile):
             half = model // CORES
             got = order.after(
-                w_out, m_out, v_out, *[outs[k].held[0] for k in chunks], *[outs[k].held[1] for k in chunks]
+                w_out,
+                m_out,
+                v_out,
+                tile,
+                *[outs[k].held[0] for k in chunks],
+                *[outs[k].held[1] for k in chunks],
             )
             new = moments_kernel(
                 core,
                 *got[:3],
-                got[3 : 4 + last],
-                got[4 + last :],
+                got[4 : 5 + last],
+                got[5 + last :],
                 (CORES,),
                 pl.BlockSpec((shard, half), lambda n, c: (0, n)),
                 [
@@ -688,7 +694,7 @@
                 ],
                 lambda n: n,
                 0,
-                [],
+                [got[3]],
             )
             order.did(new[3])
             return new
@@ -700,43 +706,39 @@
         outs[0].send_z()
         ins[0].send_y()
         if last:
+            start_pre(1)
+            start_in(1)
             start_out(1)
+            ins[1].send_y()
+            ins[0].send_z()
+            outs[0].send_z()
             outs[1].send_y()
-            start_pre(1)
-            outs[0].send_z()
-            ins[0].send_z()
-            start_in(1)
-            ins[1].send_y()
-            outs[1].send_z()
             ins[0].send_z()
             outs[0].finish()
-            outs[1].send_z()
             ins[1].send_z()
             ins[0].finish()
+            ins[1].send_z()
+            outs[1].send_z()
             outs[0].stack_y(True)
-            ins[1].send_z()
             ins[0].stack_x()
+            ins[1].finish()
+            outs[1].send_z()
+            ins[0].stack_y()
+            ins[1].stack_x()
             outs[1].finish()
-            ins[0].stack_y()
-            ins[1].finish()
-            outs[1].stack_y(True)
-            ins[1].stack_x()
-            first_out, second_out, update_out, tile = moments_out()
             ins[1].stack_y()
         else:
             outs[0].send_z()
             ins[0].send_z()
             outs[0].finish()
             ins[0].send_z()
-            outs[0].stack_y(True)
             ins[0].finish()
-            first_out, second_out, update_out, tile = moments_out()
             ins[0].stack_x()
             ins[0].stack_y()
 
         held = [value.held for value in ins]
-        got = order.after(w_in, m_in, v_in, tile, *[pair[0] for pair in held], *[pair[1] for pair in held])
-        mine, other = got[4 : 4 + len(ins)], got[4 + len(ins) :]
+        got = order.after(w_in, m_in, v_in, *[pair[0] for pair in held], *[pair[1] for pair in held])
+        mine, other = got[3 : 3 + len(ins)], got[3 + len(ins) :]
         if shard % LANES:
             joined = [
                 jnp.stack([jnp.where(c == 0, a, b), jnp.where(c == 0, b, a)]) for a, b in zip(mine, other)
@@ -749,7 +751,6 @@
                     jnp.sum((value * value).reshape(-1, 8, LANES), axis=0)
                     for value in (w_in, update_in)
                 ]
-                + [got[3]]
             )
         else:
             zs = nz // CORES
@@ -768,12 +769,15 @@
                 ],
                 lambda n: n // nx // zs,
                 1,
-                [got[3]],
+                [],
             )
         order.did(tile)
+
+        outs[last].stack_y(True)
+        first_out, second_out, update_out, tile = moments_out(tile)
         tiles = sums(tile)
-        new_w_in = new_weights(w_in, update_in, tiles, 0)
-        new_w_out = new_weights(w_out, update_out, tiles, 16)
+        new_w_in = new_weights(w_in, update_in, tiles, 16)
+        new_w_out = new_weights(w_out, update_out, tiles, 0)
         return (new_w_in, first_in, second_in, new_w_out, first_out, second_out)
 
     return local

time: 282 us -> 263 us (0.933)
  waiting for transfers between devices: 96.7 us -> 74.1 us
  starting transfers between devices: 47.5 us -> 53.9 us
  local copies, waits for them, and re-layouts: 17.8 us -> 11.6 us
  Pallas kernels: 117 us -> 121 us
    ppermute x14, waiting for transfers between devices: 53.3 us -> 43.8 us  [along_z(): return lax.ppermute(value, 'gx', pairs)]
    ppermute x6, waiting for transfers between devices: 33.1 us -> 24.7 us  [along_x(): return lax.ppermute(value, 'gx', pairs)]
    unnamed x120 -> x94, local copies, waits for them, and re-layouts: 17.8 us -> 11.6 us
    ppermute x20 -> x16, waiting for transfers between devices: 9.05 us -> 3.35 us  [across(): return lax.ppermute(value, 'gy', pairs)]
    ppermute x14, starting transfers between devices: 23.5 us -> 28.3 us  [along_z(): return lax.ppermute(value, 'gx', pairs)]
    pallas_call x16, Pallas kernels: 25.2 us -> 28.6 us  [reduce_step(): pl.pallas_call(body, grid_spec=pltpu.PrefetchScalarGridSpec(num_scalar_pr...]
  transfers between devices with their start and end apart: 48 -> 44, of which waited for: 30 -> 17; matrix products, arithmetic and copies ran while one was open for 0% -> 0% of each run, Pallas kernels for 32% -> 40%
where the time goes in v7:
time: 263 us; the launch traced here: 262 us
  Pallas kernels  121 us (46%)
  waiting for transfers between devices  74.1 us (28%)
  starting transfers between devices  53.9 us (20%)
  local copies, waits for them, and re-layouts  11.6 us (4%)
    ppermute x14, waiting for transfers between devices, along_z(): return lax.ppermute(value, 'gx', pairs)  43.8 us
    pallas_call x16, Pallas kernels, reduce_step(): pl.pallas_call(body, grid_spec=pltpu.PrefetchScalarGridSpec(num_scalar_pr...  28.6 us
    ppermute x14, starting transfers between devices, along_z(): return lax.ppermute(value, 'gx', pairs)  28.3 us
    ppermute x6, waiting for transfers between devices, along_x(): return lax.ppermute(value, 'gx', pairs)  24.7 us
    pallas_call x2, Pallas kernels, grad_pre_chunk(): pl.pallas_call(body, grid_spec=pltpu.PrefetchScalarGridSpec(num_scalar_pr...  18.1 us
    pallas_call x2, Pallas kernels, grad_in_chunk(): pl.pallas_call(body, grid_spec=pltpu.PrefetchScalarGridSpec(num_scalar_pr...  14.6 us
    pallas_call x2, Pallas kernels, grad_out_chunk(): pl.pallas_call(body, grid_spec=pltpu.PrefetchScalarGridSpec(num_scalar_pr...  13.7 us
    ppermute x8, starting transfers between devices, along_y(): return lax.ppermute(value, 'gy', pairs)  12.5 us
  transfers between devices with their start and end apart: 44, of which 17 were waited for; matrix products, arithmetic and copies ran while one was open for 0% of the time, Pallas kernels for 40%

profile of v7, /device:TPU:0, one launch (start us, length us, event | category | flops | bytes accessed | tf_op | source)
XLA Modules:
  0.0 262.2 jit_solution(17590252900546163162)
XLA Ops:
  0.7 5.2 %shard_map.136 = bf16[2816,512]{1,0:T(8,128)(2,1)} custom-call(s32[1]{0:T(128)} %bitcast.8.at_ref, bf16[512,5120]{1,0:T(8,128)(2,1)} %h_ref.4, bf16[512,1280]{1,0:T(8,128)(2,1)} %cot_ref.2), custom_call_target="tpu_custom_call" | custom-call | flops 1 | bytes 1 | tf_op jit(solution)/shard_map/pallas_call | solution.py:81
  5.8 2.9 %collective-permute-start = (bf16[2816,512]{1,0:T(8,128)(2,1)}, bf16[2816,512]{1,0:T(8,128)(2,1)}, u32[]{:S(2)}, u32[]{:S(2)}) collective-permute-start(bf16[2816,512]{1,0:T(8,128)(2,1)} %shard_map.136), channel_id=1, source_target_pairs={{0,4},{4,0},{8,12},{12,8},{16,20},{20,16},{24,28},{28,24},{1,5},{5... | collective-permute-start | bytes 8650760 | tf_op jit(solution)/shard_map/ppermute | solution.py:506
  17.7 5.1 %shard_map.139.refs_0_ = bf16[2816,512]{1,0:T(8,128)(2,1)} custom-call(s32[1]{0:T(128)} %bitcast.5.at_ref, bf16[512,5120]{1,0:T(8,128)(2,1)} %h_ref.4, bf16[512,1280]{1,0:T(8,128)(2,1)} %cot_ref.2), custom_call_target="tpu_custom_call" | custom-call | flops 1 | bytes 1 | tf_op jit(solution)/shard_map/pallas_call | solution.py:81
  22.9 3.9 %shard_map.140.refs_2_ = bf16[4,256,512]{2,1,0:T(8,128)(2,1)} custom-call(s32[1]{0:T(128)} %bitcast.3.at_ref, bf16[512,5120]{1,0:T(8,128)(2,1)} %h_ref.4), custom_call_target="tpu_custom_call" | custom-call | flops 1 | bytes 1 | tf_op jit(solution)/shard_map/pallas_call | solution.py:109
  26.7 4.0 %shard_map.141 = bf16[4,256,512]{2,1,0:T(8,128)(2,1)} custom-call(s32[1]{0:T(128)} %bitcast.8.at_ref, bf16[512,5120]{1,0:T(8,128)(2,1)} %h_ref.4), custom_call_target="tpu_custom_call" | custom-call | flops 1 | bytes 1 | tf_op jit(solution)/shard_map/pallas_call | solution.py:109
  30.8 17.7 %collective-permute-done.1.refs_3_.refs_5_ = bf16[320,1280]{1,0:T(8,128)(2,1)} collective-permute-done((bf16[320,1280]{1,0:T(8,128)(2,1)}, bf16[320,1280]{1,0:T(8,128)(2,1)}, u32[]{:S(2)}, u32[]{:S(2)}) %collective-permute-start.1) | collective-permute-done | bytes 819232 | tf_op jit(solution)/shard_map/ppermute | solution.py:510
  52.2 20.2 %collective-permute-done.refs_1_ = bf16[2816,512]{1,0:T(8,128)(2,1)} collective-permute-done((bf16[2816,512]{1,0:T(8,128)(2,1)}, bf16[2816,512]{1,0:T(8,128)(2,1)}, u32[]{:S(2)}, u32[]{:S(2)}) %collective-permute-start) | collective-permute-done | bytes 2883616 | tf_op jit(solution)/shard_map/ppermute | solution.py:506
  72.4 8.1 %shard_map.142 = (bf16[4,192,640]{2,1,0:T(8,128)(2,1)}, bf16[4,192,640]{2,1,0:T(8,128)(2,1)}, bf16[2,4,192,640]{3,2,1,0:T(8,128)(2,1)S(1)}) custom-call(s32[1]{0:T(128)} %bitcast.c_ref, bf16[2816,512]{1,0:T(8,128)(2,1)S(1)} %copy-done, bf16[2816,512]{1,0:T(8,128)(2,1)} %collective-permute-done.refs_1_), custom_call_target="tpu_custom_call" | custom-call | flops 1 | bytes 1 | tf_op jit(solution)/shard_map/pallas_call | solution.py:166
  88.4 3.1 %shard_map.143 = bf16[2,4,1,96,640]{4,3,2,1,0:T(8,128)(2,1)S(1)} custom-call(s32[3]{0:T(128)S(1)} %pad_add_fusion.2.at_ref, bf16[2,4,1,2,96,640]{5,4,3,2,1,0:T(8,128)(2,1)S(1)} %bitcast.21, bf16[4,1,2,96,640]{4,3,2,1,0:T(8,128)(2,1)} %bitcast.10.refs_1_, bf16[4,1,2,96,640]{4,3,2,1,0:T(8,128)(2,1)} %bitcast.11.refs_2_), custom_call_target="tpu_custom_call" | custom-call | flops 1 | bytes 1 | tf_op jit(solution)/shard_map/pallas_call | solution.py:401
  93.1 10.3 %shard_map.144.g_ref = bf16[4,384,1024]{2,1,0:T(8,128)(2,1)S(1)} custom-call(s32[2]{0:T(128)S(1)} %pad_add_fusion.3.c_ref, bf16[2816,512]{1,0:T(8,128)(2,1)S(1)} %copy-done, bf16[2816,512]{1,0:T(8,128)(2,1)} %collective-permute-done.refs_1_, bf16[320,1280]{1,0:T(8,128)(2,1)S(1)} %copy-done.30, bf16[320,1280]{1,0:T(8,128)(2,1)} %collective-permute-done.1.refs_3_.refs_5_, ...), custom_call_target="tpu_custom_call" | custom-call | flops 1 | bytes 1 | tf_op jit(solution)/shard_map/pallas_call | solution.py:205
  103.4 8.8 %shard_map.145 = (bf16[1280,384]{1,0:T(8,128)(2,1)S(1)}, bf16[1280,384]{1,0:T(8,128)(2,1)S(1)}, bf16[2,1280,384]{2,1,0:T(8,128)(2,1)S(1)}) custom-call(s32[1]{0:T(128)} %bitcast.c_ref, bf16[4,384,1024]{2,1,0:T(8,128)(2,1)S(1)} %shard_map.144.g_ref, bf16[1280,512]{1,0:T(8,128)(2,1)} %shard_map.138.refs_0_, bf16[1280,512]{1,0:T(8,128)(2,1)} %collective-permute-done.10.refs_1_), custom_call_target="tpu_custom_call" | custom-call | flops 1 | bytes 1 | tf_op jit(solution)/shard_map/pallas_call | solution.py:242
  122.0 7.8 %shard_map.148.g_ref = bf16[4,256,1024]{2,1,0:T(8,128)(2,1)S(1)} custom-call(s32[2]{0:T(128)S(1)} %pad_add_fusion.3.c_ref, bf16[2816,512]{1,0:T(8,128)(2,1)S(1)} %copy-done, bf16[2816,512]{1,0:T(8,128)(2,1)} %collective-permute-done.refs_1_, bf16[4,256,512]{2,1,0:T(8,128)(2,1)S(1)} %copy-done.26, bf16[4,256,512]{2,1,0:T(8,128)(2,1)S(1)} %collective-permute-done.15.refs_3_, ...), custom_call_target="tpu_custom_call" | custom-call | flops 1 | bytes 1 | tf_op jit(solution)/shard_map/pallas_call | solution.py:205
  129.9 5.8 %shard_map.149 = (bf16[1280,256]{1,0:T(8,128)(2,1)S(1)}, bf16[1280,256]{1,0:T(8,128)(2,1)S(1)}, bf16[2,1280,256]{2,1,0:T(8,128)(2,1)S(1)}) custom-call(s32[1]{0:T(128)} %bitcast.c_ref, bf16[4,256,1024]{2,1,0:T(8,128)(2,1)S(1)} %shard_map.148.g_ref, bf16[1280,512]{1,0:T(8,128)(2,1)} %shard_map.138.refs_0_, bf16[1280,512]{1,0:T(8,128)(2,1)} %collective-permute-done.10.refs_1_), custom_call_target="tpu_custom_call" | custom-call | flops 1 | bytes 1 | tf_op jit(solution)/shard_map/pallas_call | solution.py:242
  136.2 5.6 %shard_map.150 = (bf16[4,128,640]{2,1,0:T(8,128)(2,1)S(1)}, bf16[4,128,640]{2,1,0:T(8,128)(2,1)S(1)}, bf16[2,4,128,640]{3,2,1,0:T(8,128)(2,1)S(1)}) custom-call(s32[1]{0:T(128)} %bitcast.c_ref, bf16[2816,512]{1,0:T(8,128)(2,1)S(1)} %copy-done, bf16[2816,512]{1,0:T(8,128)(2,1)} %collective-permute-done.refs_1_, bf16[4,256,512]{2,1,0:T(8,128)(2,1)S(1)} %copy-done.26, ...), custom_call_target="tpu_custom_call" | custom-call | flops 1 | bytes 1 | tf_op jit(solution)/shard_map/pallas_call | solution.py:166
  148.8 7.7 %collective-permute-done.21.refs_4_ = bf16[2,2,1,96,640]{4,3,2,1,0:T(8,128)(2,1)S(1)} collective-permute-done((bf16[2,2,1,96,640]{4,3,2,1,0:T(8,128)(2,1)S(1)}, bf16[2,2,1,96,640]{4,3,2,1,0:T(8,128)(2,1)S(1)}, u32[]{:S(2)}, u32[]{:S(2)}) %collective-permute-start.21) | collective-permute-done | bytes 491552 | tf_op jit(solution)/shard_map/ppermute | solution.py:510
  164.7 6.1 %collective-permute-done.18.refs_4_ = bf16[2,2,2,80,384]{4,3,2,1,0:T(8,128)(2,1)S(1)} collective-permute-done((bf16[2,2,2,80,384]{4,3,2,1,0:T(8,128)(2,1)S(1)}, bf16[2,2,2,80,384]{4,3,2,1,0:T(8,128)(2,1)S(1)}, u32[]{:S(2)}, u32[]{:S(2)}) %collective-permute-start.18) | collective-permute-done | bytes 491552 | tf_op jit(solution)/shard_map/ppermute | solution.py:510
  177.9 6.9 %collective-permute-start.28 = (bf16[2,2,2,80,256]{4,3,2,1,0:T(8,128)(2,1)}, bf16[2,2,2,80,256]{4,3,2,1,0:T(8,128)(2,1)}, u32[]{:S(2)}, u32[]{:S(2)}) collective-permute-start(bf16[2,2,2,80,256]{4,3,2,1,0:T(8,128)(2,1)} %shard_map.157), channel_id=1, source_target_pairs={{0,8},{4,12},{8,0},{12,4},{16,24},{20,28},{24,16},{28,20},{1,9},{5... | collective-permute-start | bytes 983048 | tf_op jit(solution)/shard_map/ppermute | solution.py:510
  202.0 3.4 %collective-permute-start.31 = (bf16[2,1,2,80,256]{4,3,2,1,0:T(8,128)(2,1)S(1)}, bf16[2,1,2,80,256]{4,3,2,1,0:T(8,128)(2,1)S(1)}, u32[]{:S(2)}, u32[]{:S(2)}) collective-permute-start(bf16[2,1,2,80,256]{4,3,2,1,0:T(8,128)(2,1)S(1)} %shard_map.159), channel_id=1, source_target_pairs={{0,16},{4,20},{8,24},{12,28},{16,0},{20,4},{24,8},{28,12},{1,17},{... | collective-permute-start | bytes 491528 | tf_op jit(solution)/shard_map/ppermute | solution.py:510
  216.6 3.4 %collective-permute-start.34 = (bf16[2,1,1,64,640]{4,3,2,1,0:T(8,128)(2,1)S(1)}, bf16[2,1,1,64,640]{4,3,2,1,0:T(8,128)(2,1)S(1)}, u32[]{:S(2)}, u32[]{:S(2)}) collective-permute-start(bf16[2,1,1,64,640]{4,3,2,1,0:T(8,128)(2,1)S(1)} %shard_map.164), channel_id=1, source_target_pairs={{0,16},{4,20},{8,24},{12,28},{16,0},{20,4},{24,8},{28,12},{1,17},{... | collective-permute-start | bytes 491528 | tf_op jit(solution)/shard_map/ppermute | solution.py:510
  223.7 2.7 %collective-permute-done.34.refs_5_ = bf16[2,1,1,64,640]{4,3,2,1,0:T(8,128)(2,1)S(1)} collective-permute-done((bf16[2,1,1,64,640]{4,3,2,1,0:T(8,128)(2,1)S(1)}, bf16[2,1,1,64,640]{4,3,2,1,0:T(8,128)(2,1)S(1)}, u32[]{:S(2)}, u32[]{:S(2)}) %collective-permute-start.34) | collective-permute-done | bytes 163872 | tf_op jit(solution)/shard_map/ppermute | solution.py:510
  231.1 6.2 %shard_map.169 = (f32[160,5120]{1,0:T(8,128)}, f32[160,5120]{1,0:T(8,128)}, f32[160,5120]{1,0:T(8,128)S(1)}, f32[16,128]{1,0:T(8,128)S(1)}) custom-call(s32[1]{0:T(128)} %bitcast.c_ref, f32[160,5120]{1,0:T(8,128)S(1)} %copy-done.15, f32[160,5120]{1,0:T(8,128)S(1)} %copy-done.34, f32[160,5120]{1,0:T(8,128)S(1)} %copy-done.35, ...), custom_call_target="tpu_custom_call" | custom-call | flops 1 | bytes 1 | tf_op jit(solution)/shard_map/pallas_call | solution.py:451
  239.6 5.3 %shard_map.171 = (f32[640,1280]{1,0:T(8,128)}, f32[640,1280]{1,0:T(8,128)}, f32[640,1280]{1,0:T(8,128)S(1)}, f32[32,128]{1,0:T(8,128)S(1)}) custom-call(s32[1]{0:T(128)} %bitcast.c_ref, f32[640,1280]{1,0:T(8,128)S(1)} %copy-done.6, f32[640,1280]{1,0:T(8,128)S(1)} %copy-done.36, f32[640,1280]{1,0:T(8,128)S(1)} %copy-done.37, ...), custom_call_target="tpu_custom_call" | custom-call | flops 1 | bytes 1 | tf_op jit(solution)/shard_map/pallas_call | solution.py:451
  255.8 3.2 %shard_map.173 = f32[160,5120]{1,0:T(8,128)} custom-call(f32[160,5120]{1,0:T(8,128)S(1)} %copy-done.15, f32[160,5120]{1,0:T(8,128)S(1)} %get-tuple-element.350.u_ref, f32[32,128]{1,0:T(8,128)S(1)} %shard_map.172.refs_0_, f32[32,128]{1,0:T(8,128)S(1)} %collective-permute-done.43.refs_1_), custom_call_target="tpu_custom_call" | custom-call | flops 1 | bytes 1 | tf_op jit(solution)/shard_map/pallas_call | solution.py:478
  259.0 3.2 %shard_map.174 = f32[640,1280]{1,0:T(8,128)} custom-call(f32[640,1280]{1,0:T(8,128)S(1)} %copy-done.6, f32[640,1280]{1,0:T(8,128)S(1)} %get-tuple-element.357.u_ref, f32[32,128]{1,0:T(8,128)S(1)} %shard_map.172.refs_0_, f32[32,128]{1,0:T(8,128)S(1)} %collective-permute-done.43.refs_1_), custom_call_target="tpu_custom_call" | custom-call | flops 1 | bytes 1 | tf_op jit(solution)/shard_map/pallas_call | solution.py:478
  (201 shorter events, 104.3 us)
Async XLA Ops:
  5.8 66.6 %collective-permute-start = (bf16[2816,512]{1,0:T(8,128)(2,1)}, bf16[2816,512]{1,0:T(8,128)(2,1)}, u32[]{:S(2)}, u32[]{:S(2)}) collective-permute-start(bf16[2816,512]{1,0:T(8,128)(2,1)} %shard_map.136), channel_id=1, source_target_pairs={{0,4},{4,0},{8,12},{12,8},{16,20},{20,16},{24,28},{28,24},{1,5},{5... | collective-permute-start | bytes 8650760 | tf_op jit(solution)/shard_map/ppermute | solution.py:506
  11.0 37.4 %collective-permute-start.1 = (bf16[320,1280]{1,0:T(8,128)(2,1)}, bf16[320,1280]{1,0:T(8,128)(2,1)}, u32[]{:S(2)}, u32[]{:S(2)}) collective-permute-start(bf16[320,1280]{1,0:T(8,128)(2,1)} %shard_map.137.refs_2_.refs_4_), channel_id=1, source_target_pairs={{0,8},{4,12},{8,0},{12,4},{16,24},{20,28},{24,16},{28,20},{1,9},{5... | collective-permute-start | bytes 2457608 | tf_op jit(solution)/shard_map/ppermute | solution.py:510
  12.6 38.3 %collective-permute-start.2 = (bf16[320,1280]{1,0:T(8,128)(2,1)}, bf16[320,1280]{1,0:T(8,128)(2,1)}, u32[]{:S(2)}, u32[]{:S(2)}) collective-permute-start(bf16[320,1280]{1,0:T(8,128)(2,1)} %shard_map.137.refs_2_.refs_4_), channel_id=1, source_target_pairs={{0,16},{4,20},{8,24},{12,28},{16,0},{20,4},{24,8},{28,12},{1,17},{... | collective-permute-start | bytes 2457608 | tf_op jit(solution)/shard_map/ppermute | solution.py:510
  50.8 31.4 %collective-permute-start.3 = (bf16[320,1280]{1,0:T(8,128)(2,1)}, bf16[320,1280]{1,0:T(8,128)(2,1)}, u32[]{:S(2)}, u32[]{:S(2)}) collective-permute-start(bf16[320,1280]{1,0:T(8,128)(2,1)} %collective-permute-done.2.refs_4_.refs_6_), channel_id=1, source_target_pairs={{0,8},{4,12},{8,0},{12,4},{16,24},{20,28},{24,16},{28,20},{1,9},{5... | collective-permute-start | bytes 2457608 | tf_op jit(solution)/shard_map/ppermute | solution.py:510
  51.3 52.1 %collective-permute-start.10 = (bf16[1280,512]{1,0:T(8,128)(2,1)}, bf16[1280,512]{1,0:T(8,128)(2,1)}, u32[]{:S(2)}, u32[]{:S(2)}) collective-permute-start(bf16[1280,512]{1,0:T(8,128)(2,1)} %shard_map.138.refs_0_), channel_id=1, source_target_pairs={{0,4},{4,0},{8,12},{12,8},{16,20},{20,16},{24,28},{28,24},{1,5},{5... | collective-permute-start | bytes 3932168 | tf_op jit(solution)/shard_map/ppermute | solution.py:506
  82.3 10.8 %collective-permute-start.6 = (bf16[320,1280]{1,0:T(8,128)(2,1)}, bf16[320,1280]{1,0:T(8,128)(2,1)}, u32[]{:S(2)}, u32[]{:S(2)}) collective-permute-start(bf16[320,1280]{1,0:T(8,128)(2,1)} %collective-permute-done.2.refs_4_.refs_6_), channel_id=1, source_target_pairs={{0,1},{1,0},{2,3},{3,2},{4,5},{5,4},{6,7},{7,6},{8,9},{9,8},{10,11... | collective-permute-start | bytes 2457608 | tf_op jit(solution)/shard_map/ppermute | solution.py:520
  82.3 10.8 %collective-permute-start.7 = (bf16[320,1280]{1,0:T(8,128)(2,1)}, bf16[320,1280]{1,0:T(8,128)(2,1)}, u32[]{:S(2)}, u32[]{:S(2)}) collective-permute-start(bf16[320,1280]{1,0:T(8,128)(2,1)} %collective-permute-done.3.refs_5_.refs_7_), channel_id=1, source_target_pairs={{0,1},{1,0},{2,3},{3,2},{4,5},{5,4},{6,7},{7,6},{8,9},{9,8},{10,11... | collective-permute-start | bytes 2457608 | tf_op jit(solution)/shard_map/ppermute | solution.py:520
  84.7 37.3 %collective-permute-start.15 = (bf16[4,256,512]{2,1,0:T(8,128)(2,1)}, bf16[4,256,512]{2,1,0:T(8,128)(2,1)S(1)}, u32[]{:S(2)}, u32[]{:S(2)}) collective-permute-start(bf16[4,256,512]{2,1,0:T(8,128)(2,1)} %shard_map.141), channel_id=1, source_target_pairs={{0,4},{4,0},{8,12},{12,8},{16,20},{20,16},{24,28},{28,24},{1,5},{5... | collective-permute-start | bytes 3145736 | tf_op jit(solution)/shard_map/ppermute | solution.py:506
  91.5 23.6 %collective-permute-start.13 = (bf16[2,4,1,96,640]{4,3,2,1,0:T(8,128)(2,1)S(1)}, bf16[2,4,1,96,640]{4,3,2,1,0:T(8,128)(2,1)S(1)}, u32[]{:S(2)}, u32[]{:S(2)}) collective-permute-start(bf16[2,4,1,96,640]{4,3,2,1,0:T(8,128)(2,1)S(1)} %shard_map.143), channel_id=1, source_target_pairs={{0,2},{1,3},{2,0},{3,1},{4,6},{5,7},{6,4},{7,5},{8,10},{9,11},{10,... | collective-permute-start | bytes 2949128 | tf_op jit(solution)/shard_map/ppermute | solution.py:516
  118.3 28.6 %collective-permute-start.14 = (bf16[2,4,2,80,384]{4,3,2,1,0:T(8,128)(2,1)S(1)}, bf16[2,4,2,80,384]{4,3,2,1,0:T(8,128)(2,1)S(1)}, u32[]{:S(2)}, u32[]{:S(2)}) collective-permute-start(bf16[2,4,2,80,384]{4,3,2,1,0:T(8,128)(2,1)S(1)} %shard_map.147), channel_id=1, source_target_pairs={{0,2},{1,3},{2,0},{3,1},{4,6},{5,7},{6,4},{7,5},{8,10},{9,11},{10,... | collective-permute-start | bytes 2949128 | tf_op jit(solution)/shard_map/ppermute | solution.py:516
  141.8 16.3 %collective-permute-start.19 = (bf16[4,128,640]{2,1,0:T(8,128)(2,1)S(1)}, bf16[4,128,640]{2,1,0:T(8,128)(2,1)S(1)}, u32[]{:S(2)}, u32[]{:S(2)}) collective-permute-start(bf16[4,128,640]{2,1,0:T(8,128)(2,1)S(1)} %get-tuple-element.254), channel_id=1, source_target_pairs={{0,1},{1,0},{2,3},{3,2},{4,5},{5,4},{6,7},{7,6},{8,9},{9,8},{10,11... | collective-permute-start | bytes 1966088 | tf_op jit(solution)/shard_map/ppermute | solution.py:520
  142.0 16.2 %collective-permute-start.20 = (bf16[4,128,640]{2,1,0:T(8,128)(2,1)S(1)}, bf16[4,128,640]{2,1,0:T(8,128)(2,1)S(1)}, u32[]{:S(2)}, u32[]{:S(2)}) collective-permute-start(bf16[4,128,640]{2,1,0:T(8,128)(2,1)S(1)} %get-tuple-element.255), channel_id=1, source_target_pairs={{0,1},{1,0},{2,3},{3,2},{4,5},{5,4},{6,7},{7,6},{8,9},{9,8},{10,11... | collective-permute-start | bytes 1966088 | tf_op jit(solution)/shard_map/ppermute | solution.py:520
  142.4 14.1 %collective-permute-start.21 = (bf16[2,2,1,96,640]{4,3,2,1,0:T(8,128)(2,1)S(1)}, bf16[2,2,1,96,640]{4,3,2,1,0:T(8,128)(2,1)S(1)}, u32[]{:S(2)}, u32[]{:S(2)}) collective-permute-start(bf16[2,2,1,96,640]{4,3,2,1,0:T(8,128)(2,1)S(1)} %shard_map.146), channel_id=1, source_target_pairs={{0,8},{4,12},{8,0},{12,4},{16,24},{20,28},{24,16},{28,20},{1,9},{5... | collective-permute-start | bytes 1474568 | tf_op jit(solution)/shard_map/ppermute | solution.py:510
  145.3 30.9 %collective-permute-start.23 = (bf16[2,4,2,80,256]{4,3,2,1,0:T(8,128)(2,1)S(1)}, bf16[2,4,2,80,256]{4,3,2,1,0:T(8,128)(2,1)S(1)}, u32[]{:S(2)}, u32[]{:S(2)}) collective-permute-start(bf16[2,4,2,80,256]{4,3,2,1,0:T(8,128)(2,1)S(1)} %shard_map.151), channel_id=1, source_target_pairs={{0,2},{1,3},{2,0},{3,1},{4,6},{5,7},{6,4},{7,5},{8,10},{9,11},{10,... | collective-permute-start | bytes 1966088 | tf_op jit(solution)/shard_map/ppermute | solution.py:516
  148.3 22.5 %collective-permute-start.18 = (bf16[2,2,2,80,384]{4,3,2,1,0:T(8,128)(2,1)S(1)}, bf16[2,2,2,80,384]{4,3,2,1,0:T(8,128)(2,1)S(1)}, u32[]{:S(2)}, u32[]{:S(2)}) collective-permute-start(bf16[2,2,2,80,384]{4,3,2,1,0:T(8,128)(2,1)S(1)} %shard_map.152), channel_id=1, source_target_pairs={{0,8},{4,12},{8,0},{12,4},{16,24},{20,28},{24,16},{28,20},{1,9},{5... | collective-permute-start | bytes 1474568 | tf_op jit(solution)/shard_map/ppermute | solution.py:510
  160.3 39.2 %collective-permute-start.27 = (bf16[2,4,1,64,640]{4,3,2,1,0:T(8,128)(2,1)}, bf16[2,4,1,64,640]{4,3,2,1,0:T(8,128)(2,1)}, u32[]{:S(2)}, u32[]{:S(2)}) collective-permute-start(bf16[2,4,1,64,640]{4,3,2,1,0:T(8,128)(2,1)} %shard_map.154), channel_id=1, source_target_pairs={{0,2},{1,3},{2,0},{3,1},{4,6},{5,7},{6,4},{7,5},{8,10},{9,11},{10,... | collective-permute-start | bytes 1966088 | tf_op jit(solution)/shard_map/ppermute | solution.py:516
  162.1 12.4 %collective-permute-start.24 = (bf16[2,1,1,96,640]{4,3,2,1,0:T(8,128)(2,1)S(1)}, bf16[2,1,1,96,640]{4,3,2,1,0:T(8,128)(2,1)S(1)}, u32[]{:S(2)}, u32[]{:S(2)}) collective-permute-start(bf16[2,1,1,96,640]{4,3,2,1,0:T(8,128)(2,1)S(1)} %shard_map.153), channel_id=1, source_target_pairs={{0,16},{4,20},{8,24},{12,28},{16,0},{20,4},{24,8},{28,12},{1,17},{... | collective-permute-start | bytes 737288 | tf_op jit(solution)/shard_map/ppermute | solution.py:510
  172.3 12.9 %collective-permute-start.22 = (bf16[2,1,2,80,384]{4,3,2,1,0:T(8,128)(2,1)}, bf16[2,1,2,80,384]{4,3,2,1,0:T(8,128)(2,1)}, u32[]{:S(2)}, u32[]{:S(2)}) collective-permute-start(bf16[2,1,2,80,384]{4,3,2,1,0:T(8,128)(2,1)} %shard_map.155), channel_id=1, source_target_pairs={{0,16},{4,20},{8,24},{12,28},{16,0},{20,4},{24,8},{28,12},{1,17},{... | collective-permute-start | bytes 737288 | tf_op jit(solution)/shard_map/ppermute | solution.py:510
  177.9 16.7 %collective-permute-start.28 = (bf16[2,2,2,80,256]{4,3,2,1,0:T(8,128)(2,1)}, bf16[2,2,2,80,256]{4,3,2,1,0:T(8,128)(2,1)}, u32[]{:S(2)}, u32[]{:S(2)}) collective-permute-start(bf16[2,2,2,80,256]{4,3,2,1,0:T(8,128)(2,1)} %shard_map.157), channel_id=1, source_target_pairs={{0,8},{4,12},{8,0},{12,4},{16,24},{20,28},{24,16},{28,20},{1,9},{5... | collective-permute-start | bytes 983048 | tf_op jit(solution)/shard_map/ppermute | solution.py:510
  184.8 20.6 %collective-permute-start.26 = (bf16[2,96,640]{2,1,0:T(8,128)(2,1)S(1)}, bf16[2,96,640]{2,1,0:T(8,128)(2,1)}, u32[]{:S(2)}, u32[]{:S(2)}) collective-permute-start(bf16[2,96,640]{2,1,0:T(8,128)(2,1)S(1)} %shard_map.156.refs_0_), channel_id=1, source_target_pairs={{0,2},{1,3},{2,0},{3,1},{4,6},{5,7},{6,4},{7,5},{8,10},{9,11},{10,... | collective-permute-start | bytes 737288 | tf_op jit(solution)/shard_map/ppermute | solution.py:516
  193.0 14.0 %collective-permute-start.25 = (bf16[2,80,384]{2,1,0:T(8,128)(2,1)}, bf16[2,80,384]{2,1,0:T(8,128)(2,1)}, u32[]{:S(2)}, u32[]{:S(2)}) collective-permute-start(bf16[2,80,384]{2,1,0:T(8,128)(2,1)} %get-tuple-element.286), channel_id=1, source_target_pairs={{0,4},{4,0},{8,12},{12,8},{16,20},{20,16},{24,28},{28,24},{1,5},{5... | collective-permute-start | bytes 368648 | tf_op jit(solution)/shard_map/ppermute | solution.py:506
  201.3 13.4 %collective-permute-start.30 = (bf16[2,2,1,64,640]{4,3,2,1,0:T(8,128)(2,1)S(1)}, bf16[2,2,1,64,640]{4,3,2,1,0:T(8,128)(2,1)S(1)}, u32[]{:S(2)}, u32[]{:S(2)}) collective-permute-start(bf16[2,2,1,64,640]{4,3,2,1,0:T(8,128)(2,1)S(1)} %shard_map.160), channel_id=1, source_target_pairs={{0,8},{4,12},{8,0},{12,4},{16,24},{20,28},{24,16},{28,20},{1,9},{5... | collective-permute-start | bytes 983048 | tf_op jit(solution)/shard_map/ppermute | solution.py:510
  202.0 10.1 %collective-permute-start.31 = (bf16[2,1,2,80,256]{4,3,2,1,0:T(8,128)(2,1)S(1)}, bf16[2,1,2,80,256]{4,3,2,1,0:T(8,128)(2,1)S(1)}, u32[]{:S(2)}, u32[]{:S(2)}) collective-permute-start(bf16[2,1,2,80,256]{4,3,2,1,0:T(8,128)(2,1)S(1)} %shard_map.159), channel_id=1, source_target_pairs={{0,16},{4,20},{8,24},{12,28},{16,0},{20,4},{24,8},{28,12},{1,17},{... | collective-permute-start | bytes 491528 | tf_op jit(solution)/shard_map/ppermute | solution.py:510
  208.4 11.7 %collective-permute-start.29 = (bf16[2,2,80,384]{3,2,1,0:T(8,128)(2,1)S(1)}, bf16[2,2,80,384]{3,2,1,0:T(8,128)(2,1)S(1)}, u32[]{:S(2)}, u32[]{:S(2)}) collective-permute-start(bf16[2,2,80,384]{3,2,1,0:T(8,128)(2,1)S(1)} %shard_map.162.refs_0_), channel_id=1, source_target_pairs={{0,2},{1,3},{2,0},{3,1},{4,6},{5,7},{6,4},{7,5},{8,10},{9,11},{10,... | collective-permute-start | bytes 737288 | tf_op jit(solution)/shard_map/ppermute | solution.py:516
  (67 other events, 807.9 us)

commit v8 on v7

--- a/solution.py
+++ b/solution.py
@@ -178,42 +178,33 @@
     )(core, *tokens.arrays)
 
 
-def grad_pre_chunk(tokens, mine, other, nz, row, core, scale):
-    part, model = mine[0].shape
+def grad_pre_chunk(tokens, weights, row, core, scale):
+    nz, shard, model = weights.shape
     width = tokens.width
     count = len(tokens.arrays)
     long = tokens.arrays[0].shape[1]
 
     def body(c_ref, *refs):
         ins = refs[:count]
-        out_ref, w_ref = refs[count + 2 * nz :]
-        for h in range(nz):
-
-            @pl.when((pl.program_id(0) ^ c_ref[1]) == h)
-            def _(h=h):
-                for at, ref in ((c_ref[0], refs[count + h]), (1 - c_ref[0], refs[count + nz + h])):
-                    w_ref[pl.ds(pl.multiple_of(at * part, 16), part), :] = ref[...]
-
-        w = w_ref[row : row + width, :]
+        w_ref, out_ref = refs[count:]
+        w = w_ref[0, row : row + width, :]
         for n in range(tokens.count):
             grad_act = dot(w, tokens.cot(ins, n)[...], ((1,), (0,))) * scale
             out_ref[0, :, n * long : (n + 1) * long] = (
                 grad_act * gelu_slope(tokens.hidden(ins, n))
             ).astype(BF16)
 
-    w_specs = [pl.BlockSpec((part, model), lambda z, c: (0, 0))] * nz
     return pl.pallas_call(
         body,
         grid_spec=pltpu.PrefetchScalarGridSpec(
             num_scalar_prefetch=1,
             grid=(nz,),
-            in_specs=tokens.specs + w_specs * 2,
+            in_specs=tokens.specs + [pl.BlockSpec((1, shard, model), lambda z, c: (z, 0, 0))],
             out_specs=pl.BlockSpec((1, width, tokens.count * long), lambda z, c: (z, 0, 0)),
-            scratch_shapes=[pltpu.VMEM((CORES * part, model), BF16)],
         ),
         out_shape=jax.ShapeDtypeStruct((nz, width, tokens.count * long), BF16),
         **params(),
-    )(core, *tokens.arrays, *mine, *other)
+    )(core, *tokens.arrays, weights)
 
 
 def grad_in_chunk(grads, inputs, core, scale, cut, block, width):
@@ -332,31 +323,20 @@
     )(*tiles)
 
 
-def reduce_step(place, keep, crosses, from_y, from_z, shift, stage, ny, split):
+def reduce_step(place, keep, crosses, from_y, shift, ny):
     lead, nz, mid, _, high, wide = keep.shape
-    bit = len(from_z)
-
-    def zed(n, at):
-        if stage == "y":
-            return n
-        if stage == "end":
-            return at[2]
-        low = at[2] % (1 << bit)
-        mine = (at[2] // (1 << bit)) % 2
-        return n * (2 << bit) + (1 - mine) * (1 << bit) + low
-
-    count = {"y": nz, "z": nz >> (bit + 1), "end": 1}[stage]
     six = (lead, 1, mid, 1, high, wide)
     five = (lead, 1, mid, high, wide)
-    specs = [pl.BlockSpec(six, lambda n, at: (0, zed(n, at), 0, (at[1] + shift) % ny, 0, 0))]
     each = len(crosses) // lead
     long = nz // each
+    ends = len(from_y) > 0
+    specs = [pl.BlockSpec(six, lambda n, at: (0, n, 0, (at[1] + shift) % ny, 0, 0))]
     for h in range(len(crosses)):
         specs.append(
             pl.BlockSpec(
                 six[1:],
                 lambda n, at, h=h % each: (
-                    jnp.clip(zed(n, at) - h * long, 0, long - 1),
+                    jnp.clip(n - h * long, 0, long - 1),
                     0,
                     (at[1] + shift) % ny,
                     0,
@@ -364,49 +344,57 @@
                 ),
             )
         )
-    specs += [pl.BlockSpec(five, lambda n, at: (0, zed(n, at), 0, 0, 0))] * len(from_y)
-    specs += [
-        pl.BlockSpec(five, lambda n, at, j=j: (0, zed(n, at) // (2 << j), 0, 0, 0)) for j in range(bit)
-    ]
+    specs += [pl.BlockSpec(five, lambda n, at: (0, n, 0, 0, 0))] * len(from_y)
 
     def body(at_ref, *refs):
-        ins = refs[: len(specs)]
-        outs = refs[len(specs) :]
+        ins, out_ref = refs[:-1], refs[-1]
         for p in range(lead):
             for m in range(mid):
                 total = ins[1 + p * each][0, m, 0]
                 for h in range(1, each):
-                    total = jnp.where(
-                        zed(pl.program_id(0), at_ref) >= h * long, ins[1 + p * each + h][0, m, 0], total
-                    )
+                    total = jnp.where(pl.program_id(0) >= h * long, ins[1 + p * each + h][0, m, 0], total)
                 total = total.astype(F32) + ins[0][p, 0, m, 0].astype(F32)
                 for ref in ins[1 + len(crosses) :]:
                     total = total + ref[p, 0, m].astype(F32)
-                total = total.astype(BF16)
-                if not split:
-                    outs[0][p, 0, m] = total
-                    continue
-                for s in range(mid):
-
-                    @pl.when((at_ref[0] + s) % mid == m)
-                    def _(s=s, total=total):
-                        outs[s][p] = total
-
-    if split:
-        out_specs = [pl.BlockSpec((lead, high, wide), lambda n, at: (0, 0, 0))] * mid
-        out_shape = [jax.ShapeDtypeStruct((lead, high, wide), BF16)] * mid
+                if ends:
+                    out_ref[0, p, m] = total.astype(BF16)
+                else:
+                    out_ref[p, 0, m] = total.astype(BF16)
+
+    if ends:
+        out_spec = pl.BlockSpec((1, lead, mid, high, wide), lambda n, at: (n, 0, 0, 0, 0))
+        shape = (nz, lead, mid, high, wide)
     else:
-        out_specs = [pl.BlockSpec(five, lambda n, at: (0, n, 0, 0, 0))]
-        out_shape = [jax.ShapeDtypeStruct((lead, count, mid, high, wide), BF16)]
-    out = pl.pallas_call(
-        body,
-        grid_spec=pltpu.PrefetchScalarGridSpec(
-            num_scalar_prefetch=1, grid=(count,), in_specs=specs, out_specs=out_specs
-        ),
-        out_shape=out_shape,
+        out_spec = pl.BlockSpec(five, lambda n, at: (0, n, 0, 0, 0))
+        shape = (lead, nz, mid, high, wide)
+    return pl.pallas_call(
+        body,
+        grid_spec=pltpu.PrefetchScalarGridSpec(
+            num_scalar_prefetch=1, grid=(nz,), in_specs=specs, out_specs=out_spec
+        ),
+        out_shape=jax.ShapeDtypeStruct(shape, BF16),
         **params(SMALL),
-    )(place, keep, *crosses, *from_y, *from_z)
-    return out if split else out[0]
+    )(place, keep, *crosses, *from_y)
+
+
+def by_x(place, value):
+    lead, mid, high, wide = value.shape
+
+    def body(at_ref, in_ref, *outs):
+        for s in range(mid):
+            outs[s][...] = in_ref[:, (at_ref[0] + s) % mid]
+
+    return pl.pallas_call(
+        body,
+        grid_spec=pltpu.PrefetchScalarGridSpec(
+            num_scalar_prefetch=1,
+            grid=(),
+            in_specs=[pl.BlockSpec(value.shape, lambda at: (0, 0, 0, 0))],
+            out_specs=[pl.BlockSpec((lead, high, wide), lambda at: (0, 0, 0))] * mid,
+        ),
+        out_shape=[jax.ShapeDtypeStruct((lead, high, wide), BF16)] * mid,
+        **params(SMALL),
+    )(place, value)
 
 
 def moments_kernel(core, weight, first, second, mine, other, grid, state_spec, grad_specs, owner, axis, tiles):
@@ -528,33 +516,28 @@
                 across(send).reshape(shape[1] // each, *shape[2:]) for send in sends
             ]
             self.from_y = []
-            self.from_z = []
-
-        def step(self, shift, stage, split=False):
-            got = self.order.after(self.keep, *self.crosses, *self.from_y, *self.from_z)
+
+        def step(self, shift):
+            got = self.order.after(self.keep, *self.crosses, *self.from_y)
             lead = 1 + len(self.crosses)
-            count = lead + len(self.from_y)
-            out = reduce_step(
-                self.place, got[0], got[1:lead], got[lead:count], got[count:], shift, stage, ny, split
-            )
-            self.order.did(out[0] if split else out)
+            out = reduce_step(self.place, got[0], got[1:lead], got[lead:], shift, ny)
+            self.order.did(out)
             return out
 
         def send_y(self):
-            from_y = []
-            for s in range(1, ny):
-                from_y.append(along_y(self.step(s, "y"), s))
-            self.from_y = from_y
-
-        def send_z(self):
-            bit = len(self.from_z)
-            self.from_z.append(along_z(self.step(0, "z"), 1 << bit))
+            self.from_y = [along_y(self.step(s), s) for s in range(1, ny)]
+
+        def sum_z(self):
+            groups = [[z * nx + x for z in range(nz)] for x in range(nx)]
+            self.total = lax.psum_scatter(self.step(0), "gx", axis_index_groups=groups)
 
         def finish(self):
-            out = self.step(0, "end", True)
+            if self.total.shape[1] == 1:
+                self.share_y(self.total[:, 0])
+                return
+            out = by_x(self.place, *self.order.after(self.total))
+            self.order.did(out[0])
             self.held = [out[0]] + [along_x(out[s], s) for s in range(1, len(out))]
-            if len(out) == 1:
-                self.share_y(out[0])
 
         def share_y(self, value):
             self.held = [value] + [along_y(value, s) for s in range(1, ny)]
@@ -588,7 +571,6 @@
         z, x = place // nx, place % nx
         y, c = side // CORES, side % CORES
         core = jnp.reshape(c, (1,)).astype(jnp.int32)
-        at_core = jnp.stack([c, z]).astype(jnp.int32)
         order = Order()
 
         packs, hiddens = [], []
@@ -599,6 +581,13 @@
 
         part = half_rows(*order.after(w_out), core)
         order.did(part)
+        groups = [
+            [((z * nx + x) * ny + y) * CORES + c for z in range(nz) for c in range(CORES)]
+            for x in range(nx)
+            for y in range(ny)
+        ]
+        weights = lax.all_gather(part, ("gx", "gy"), axis_index_groups=groups)
+        weights = weights.reshape(nz, shard, model)
         flipped = transposed(*order.after(inputs))
         order.did(flipped)
         columns = [flipped] + [along_x(flipped, t) for t in range(1, nx)]
@@ -609,17 +598,6 @@
             if value:
                 order.did(value[0])
             hiddens.append([along_x(h, t) for h in value] if t else value)
-        found = {0: part, nz // 2: along_z(part, nz // 2)}
-        bit = nz // 4
-        while bit:
-            for key in list(found):
-                value = found[key]
-                if key:
-                    (value,) = order.after(value)
-                found[key ^ bit] = along_z(value, bit)
-            bit //= 2
-        found = [found[key] for key in range(nz)]
-        crossed = [across(value) for value in [*order.after(*found[: nz // 2]), *found[nz // 2 :]]]
         packs = [own] + packs
 
         parts = [PARTS for _ in chunks]
@@ -638,15 +616,15 @@
             return blocks, got[count:]
 
         def start_out(k):
-            blocks, _ = tokens(k, *([*crossed[: nz // 2], found[nz // 2]] if k == 0 else []))
+            blocks, _ = tokens(k)
             *sends, keep = grad_out_chunk(blocks, core, nz, scale_out, parts[k])
             order.did(keep)
             shape = (parts[k], nz, 1, ny, cuts[k] // parts[k] // ny, model // CORES)
             outs[k] = Reduce(order, (x, y, z), sends, keep, shape)
 
         def start_pre(k):
-            blocks, got = tokens(k, *found, *crossed)
-            pres[k] = grad_pre_chunk(blocks, got[:nz], got[nz:], nz, starts[k], at_core, scale_out)
+            blocks, got = tokens(k, weights)
+            pres[k] = grad_pre_chunk(blocks, got[0], starts[k], core, scale_out)
             order.did(pres[k])
 
         def start_in(k):
@@ -703,35 +681,29 @@
         outs[0].send_y()
         start_pre(0)
         start_in(0)
-        outs[0].send_z()
+        outs[0].sum_z()
         ins[0].send_y()
         if last:
             start_pre(1)
             start_in(1)
             start_out(1)
             ins[1].send_y()
-            ins[0].send_z()
-            outs[0].send_z()
+            ins[0].sum_z()
             outs[1].send_y()
-            ins[0].send_z()
+            ins[1].sum_z()
             outs[0].finish()
-            ins[1].send_z()
+            outs[0].stack_y(True)
             ins[0].finish()
-            ins[1].send_z()
-            outs[1].send_z()
-            outs[0].stack_y(True)
             ins[0].stack_x()
+            outs[1].sum_z()
+            ins[0].stack_y()
             ins[1].finish()
-            outs[1].send_z()
-            ins[0].stack_y()
             ins[1].stack_x()
+            ins[1].stack_y()
             outs[1].finish()
-            ins[1].stack_y()
         else:
-            outs[0].send_z()
-            ins[0].send_z()
+            ins[0].sum_z()
             outs[0].finish()
-            ins[0].send_z()
             ins[0].finish()
             ins[0].stack_x()
             ins[0].stack_y()

time: 263 us -> 319 us (1.21)
  waiting for transfers between devices: 74.1 us -> 131 us
  starting transfers between devices: 53.9 us -> 31.3 us
  local copies, waits for them, and re-layouts: 11.6 us -> 28.2 us
  between operations: 1.27 us -> 14.2 us
  Pallas kernels: 121 us -> 113 us
    ppermute x6, waiting for transfers between devices: 24.7 us -> 81.8 us  [along_x(): return lax.ppermute(value, 'gx', pairs)]
    ppermute x14 -> x3, waiting for transfers between devices: 43.8 us -> 1.76 us  [along_z(): return lax.ppermute(value, 'gx', pairs)]
    ppermute x8, waiting for transfers between devices: 2.24 us -> 40.7 us  [along_y(): return lax.ppermute(value, 'gy', pairs)]
    ppermute x14 -> x3, starting transfers between devices: 28.3 us -> 4.41 us  [along_z(): return lax.ppermute(value, 'gx', pairs)]
    unnamed x94 -> x86, local copies, waits for them, and re-layouts: 11.6 us -> 28.2 us
    pallas_call x16 -> x8, Pallas kernels: 28.6 us -> 20.6 us  [reduce_step(): pl.pallas_call(body, grid_spec=pltpu.PrefetchScalarGridSpec(num_scalar_pr...]
    pallas_call x2, Pallas kernels: 18.1 us -> 13.3 us  [grad_pre_chunk(): pl.pallas_call(body, grid_spec=pltpu.PrefetchScalarGridSpec(num_scalar_pr...]
  transfers between devices with their start and end apart: 44 -> 34, of which waited for: 17 -> 18; matrix products, arithmetic and copies ran while one was open for 0% -> 0% of each run, Pallas kernels for 40% -> 29%
where the time goes in v8:
time: 319 us; the launch traced here: 318 us
  waiting for transfers between devices  131 us (41%)
  Pallas kernels  113 us (35%)
  starting transfers between devices  31.3 us (10%)
  local copies, waits for them, and re-layouts  28.2 us (9%)
  between operations  14.2 us (4%)
    ppermute x6, waiting for transfers between devices, along_x(): return lax.ppermute(value, 'gx', pairs)  81.8 us
    ppermute x8, waiting for transfers between devices, along_y(): return lax.ppermute(value, 'gy', pairs)  40.7 us
    unnamed x86, local copies, waits for them, and re-layouts  28.2 us
    pallas_call x8, Pallas kernels, reduce_step(): pl.pallas_call(body, grid_spec=pltpu.PrefetchScalarGridSpec(num_scalar_pr...  20.6 us
    pallas_call x2, Pallas kernels, grad_in_chunk(): pl.pallas_call(body, grid_spec=pltpu.PrefetchScalarGridSpec(num_scalar_pr...  15.8 us
    pallas_call x2, Pallas kernels, moments_kernel(): pl.pallas_call(body, grid_spec=pltpu.PrefetchScalarGridSpec(num_scalar_pr...  14.6 us
    pallas_call x2, Pallas kernels, grad_out_chunk(): pl.pallas_call(body, grid_spec=pltpu.PrefetchScalarGridSpec(num_scalar_pr...  13.7 us
    pallas_call x2, Pallas kernels, grad_pre_chunk(): pl.pallas_call(body, grid_spec=pltpu.PrefetchScalarGridSpec(num_scalar_pr...  13.3 us
  transfers between devices with their start and end apart: 34, of which 18 were waited for; matrix products, arithmetic and copies ran while one was open for 0% of the time, Pallas kernels for 29%

profile of v8, /device:TPU:0, one launch (start us, length us, event | category | flops | bytes accessed | tf_op | source)
XLA Modules:
  0.0 318.0 jit_solution(11118942320944590970)
XLA Ops:
  7.2 5.2 %shard_map.136 = bf16[2816,512]{1,0:T(8,128)(2,1)} custom-call(s32[1]{0:T(128)} %bitcast.8.at_ref, bf16[512,5120]{1,0:T(8,128)(2,1)} %h_ref.4, bf16[512,1280]{1,0:T(8,128)(2,1)} %cot_ref.2), custom_call_target="tpu_custom_call" | custom-call | flops 1 | bytes 1 | tf_op jit(solution)/shard_map/pallas_call | solution.py:81
  20.3 5.1 %shard_map.139.refs_0_ = bf16[2816,512]{1,0:T(8,128)(2,1)} custom-call(s32[1]{0:T(128)} %bitcast.5.at_ref, bf16[512,5120]{1,0:T(8,128)(2,1)} %h_ref.4, bf16[512,1280]{1,0:T(8,128)(2,1)} %cot_ref.2), custom_call_target="tpu_custom_call" | custom-call | flops 1 | bytes 1 | tf_op jit(solution)/shard_map/pallas_call | solution.py:81
  25.5 3.9 %shard_map.140.refs_2_ = bf16[4,256,512]{2,1,0:T(8,128)(2,1)} custom-call(s32[1]{0:T(128)} %bitcast.3.at_ref, bf16[512,5120]{1,0:T(8,128)(2,1)} %h_ref.4), custom_call_target="tpu_custom_call" | custom-call | flops 1 | bytes 1 | tf_op jit(solution)/shard_map/pallas_call | solution.py:109
  29.4 4.0 %shard_map.141 = bf16[4,256,512]{2,1,0:T(8,128)(2,1)} custom-call(s32[1]{0:T(128)} %bitcast.8.at_ref, bf16[512,5120]{1,0:T(8,128)(2,1)} %h_ref.4), custom_call_target="tpu_custom_call" | custom-call | flops 1 | bytes 1 | tf_op jit(solution)/shard_map/pallas_call | solution.py:109
  33.4 47.2 %collective-permute-done.refs_1_ = bf16[2816,512]{1,0:T(8,128)(2,1)} collective-permute-done((bf16[2816,512]{1,0:T(8,128)(2,1)}, bf16[2816,512]{1,0:T(8,128)(2,1)}, u32[]{:S(2)}, u32[]{:S(2)}) %collective-permute-start) | collective-permute-done | bytes 2883616 | tf_op jit(solution)/shard_map/ppermute | solution.py:494
  80.6 8.1 %shard_map.142 = (bf16[4,192,640]{2,1,0:T(8,128)(2,1)}, bf16[4,192,640]{2,1,0:T(8,128)(2,1)}, bf16[2,4,192,640]{3,2,1,0:T(8,128)(2,1)S(1)}) custom-call(s32[1]{0:T(128)} %bitcast.c_ref, bf16[2816,512]{1,0:T(8,128)(2,1)S(1)} %copy-done, bf16[2816,512]{1,0:T(8,128)(2,1)} %collective-permute-done.refs_1_), custom_call_target="tpu_custom_call" | custom-call | flops 1 | bytes 1 | tf_op jit(solution)/shard_map/pallas_call | solution.py:166
  95.8 4.1 %shard_map.143 = bf16[2,4,1,96,640]{4,3,2,1,0:T(8,128)(2,1)} custom-call(s32[3]{0:T(128)S(1)} %pad_add_fusion.2.at_ref, bf16[2,4,1,2,96,640]{5,4,3,2,1,0:T(8,128)(2,1)S(1)} %bitcast.30, bf16[4,1,2,96,640]{4,3,2,1,0:T(8,128)(2,1)} %bitcast.11.refs_1_, bf16[4,1,2,96,640]{4,3,2,1,0:T(8,128)(2,1)} %bitcast.12.refs_2_), custom_call_target="tpu_custom_call" | custom-call | flops 1 | bytes 1 | tf_op jit(solution)/shard_map/pallas_call | solution.py:370
  104.5 7.9 %shard_map.144.g_ref = bf16[4,384,1024]{2,1,0:T(8,128)(2,1)S(1)} custom-call(s32[1]{0:T(128)} %bitcast.c_ref, bf16[2816,512]{1,0:T(8,128)(2,1)S(1)} %copy-done, bf16[2816,512]{1,0:T(8,128)(2,1)} %collective-permute-done.refs_1_, bf16[4,640,1280]{2,1,0:T(8,128)(2,1)S(1)} %bitcast.28), custom_call_target="tpu_custom_call" | custom-call | flops 1 | bytes 1 | tf_op jit(solution)/shard_map/pallas_call | solution.py:197
  112.4 9.0 %collective-permute-done.3.refs_1_ = bf16[1280,512]{1,0:T(8,128)(2,1)} collective-permute-done((bf16[1280,512]{1,0:T(8,128)(2,1)}, bf16[1280,512]{1,0:T(8,128)(2,1)}, u32[]{:S(2)}, u32[]{:S(2)}) %collective-permute-start.3) | collective-permute-done | bytes 1310752 | tf_op jit(solution)/shard_map/ppermute | solution.py:494
  121.5 10.0 %shard_map.145 = (bf16[1280,384]{1,0:T(8,128)(2,1)}, bf16[1280,384]{1,0:T(8,128)(2,1)}, bf16[2,1280,384]{2,1,0:T(8,128)(2,1)S(1)}) custom-call(s32[1]{0:T(128)} %bitcast.c_ref, bf16[4,384,1024]{2,1,0:T(8,128)(2,1)S(1)} %shard_map.144.g_ref, bf16[1280,512]{1,0:T(8,128)(2,1)} %shard_map.138.refs_0_, bf16[1280,512]{1,0:T(8,128)(2,1)} %collective-permute-done.3.refs_1_), custom_call_target="tpu_custom_call" | custom-call | flops 1 | bytes 1 | tf_op jit(solution)/shard_map/pallas_call | solution.py:233
  132.0 3.3 %shard_map.146 = bf16[4,2,1,96,640]{4,3,2,1,0:T(8,128)(2,1)S(1)} custom-call(s32[3]{0:T(128)S(1)} %pad_add_fusion.2.at_ref, bf16[2,4,1,2,96,640]{5,4,3,2,1,0:T(8,128)(2,1)S(1)} %bitcast.31, bf16[4,1,2,96,640]{4,3,2,1,0:T(8,128)(2,1)} %bitcast.11.refs_1_, bf16[4,1,2,96,640]{4,3,2,1,0:T(8,128)(2,1)} %bitcast.12.refs_2_, ...), custom_call_target="tpu_custom_call" | custom-call | flops 1 | bytes 1 | tf_op jit(solution)/shard_map/pallas_call | solution.py:370
  144.3 17.4 %collective-permute-done.8.refs_3_ = bf16[4,256,512]{2,1,0:T(8,128)(2,1)S(1)} collective-permute-done((bf16[4,256,512]{2,1,0:T(8,128)(2,1)}, bf16[4,256,512]{2,1,0:T(8,128)(2,1)S(1)}, u32[]{:S(2)}, u32[]{:S(2)}) %collective-permute-start.8) | collective-permute-done | bytes 1048608 | tf_op jit(solution)/shard_map/ppermute | solution.py:494
  164.6 5.5 %shard_map.148.g_ref = bf16[4,256,1024]{2,1,0:T(8,128)(2,1)S(1)} custom-call(s32[1]{0:T(128)} %bitcast.c_ref, bf16[2816,512]{1,0:T(8,128)(2,1)S(1)} %copy-done, bf16[2816,512]{1,0:T(8,128)(2,1)} %collective-permute-done.refs_1_, bf16[4,256,512]{2,1,0:T(8,128)(2,1)S(1)} %copy-done.5, bf16[4,256,512]{2,1,0:T(8,128)(2,1)S(1)} %collective-permute-done.8.refs_3_, ...), custom_call_target="tpu_custom_call" | custom-call | flops 1 | bytes 1 | tf_op jit(solution)/shard_map/pallas_call | solution.py:197
  170.0 5.8 %shard_map.149 = (bf16[1280,256]{1,0:T(8,128)(2,1)S(1)}, bf16[1280,256]{1,0:T(8,128)(2,1)S(1)}, bf16[2,1280,256]{2,1,0:T(8,128)(2,1)S(1)}) custom-call(s32[1]{0:T(128)} %bitcast.c_ref, bf16[4,256,1024]{2,1,0:T(8,128)(2,1)S(1)} %shard_map.148.g_ref, bf16[1280,512]{1,0:T(8,128)(2,1)} %shard_map.138.refs_0_, bf16[1280,512]{1,0:T(8,128)(2,1)} %collective-permute-done.3.refs_1_), custom_call_target="tpu_custom_call" | custom-call | flops 1 | bytes 1 | tf_op jit(solution)/shard_map/pallas_call | solution.py:233
  176.4 5.6 %shard_map.150 = (bf16[4,128,640]{2,1,0:T(8,128)(2,1)S(1)}, bf16[4,128,640]{2,1,0:T(8,128)(2,1)S(1)}, bf16[2,4,128,640]{3,2,1,0:T(8,128)(2,1)S(1)}) custom-call(s32[1]{0:T(128)} %bitcast.c_ref, bf16[2816,512]{1,0:T(8,128)(2,1)S(1)} %copy-done, bf16[2816,512]{1,0:T(8,128)(2,1)} %collective-permute-done.refs_1_, bf16[4,256,512]{2,1,0:T(8,128)(2,1)S(1)} %copy-done.5, ...), custom_call_target="tpu_custom_call" | custom-call | flops 1 | bytes 1 | tf_op jit(solution)/shard_map/pallas_call | solution.py:166
  194.0 13.2 %collective-permute-done.12.refs_3_ = bf16[2,4,2,80,256]{4,3,2,1,0:T(8,128)(2,1)S(1)} collective-permute-done((bf16[2,4,2,80,256]{4,3,2,1,0:T(8,128)(2,1)}, bf16[2,4,2,80,256]{4,3,2,1,0:T(8,128)(2,1)S(1)}, u32[]{:S(2)}, u32[]{:S(2)}) %collective-permute-start.12) | collective-permute-done | bytes 655392 | tf_op jit(solution)/shard_map/ppermute | solution.py:504
  212.0 19.4 %collective-permute-done.11.refs_1_ = bf16[2,96,640]{2,1,0:T(8,128)(2,1)S(1)} collective-permute-done((bf16[2,96,640]{2,1,0:T(8,128)(2,1)}, bf16[2,96,640]{2,1,0:T(8,128)(2,1)S(1)}, u32[]{:S(2)}, u32[]{:S(2)}) %collective-permute-start.11) | collective-permute-done | bytes 245792 | tf_op jit(solution)/shard_map/ppermute | solution.py:504
  237.0 3.1 collective-permute-done.15.refs_1_
  249.8 4.5 %collective-permute-done.16.refs_1_ = bf16[2,2,80,384]{3,2,1,0:T(8,128)(2,1)S(1)} collective-permute-done((bf16[2,2,80,384]{3,2,1,0:T(8,128)(2,1)S(1)}, bf16[2,2,80,384]{3,2,1,0:T(8,128)(2,1)S(1)}, u32[]{:S(2)}, u32[]{:S(2)}) %collective-permute-start.16) | collective-permute-done | bytes 245792 | tf_op jit(solution)/shard_map/ppermute | solution.py:504
  264.0 3.6 %collective-permute-done.19.refs_1_ = bf16[2,2,80,256]{3,2,1,0:T(8,128)(2,1)S(1)} collective-permute-done((bf16[2,2,80,256]{3,2,1,0:T(8,128)(2,1)S(1)}, bf16[2,2,80,256]{3,2,1,0:T(8,128)(2,1)S(1)}, u32[]{:S(2)}, u32[]{:S(2)}) %collective-permute-start.19) | collective-permute-done | bytes 163872 | tf_op jit(solution)/shard_map/ppermute | solution.py:504
  278.1 9.3 %shard_map.163 = (f32[160,5120]{1,0:T(8,128)}, f32[160,5120]{1,0:T(8,128)}, f32[160,5120]{1,0:T(8,128)S(1)}, f32[16,128]{1,0:T(8,128)S(1)}) custom-call(s32[1]{0:T(128)} %bitcast.c_ref, f32[160,5120]{1,0:T(8,128)S(1)} %copy-done.4, f32[160,5120]{1,0:T(8,128)S(1)} %copy-done.19, f32[160,5120]{1,0:T(8,128)S(1)} %copy-done.20, ...), custom_call_target="tpu_custom_call" | custom-call | flops 1 | bytes 1 | tf_op jit(solution)/shard_map/pallas_call | solution.py:439
  289.8 5.3 %shard_map.165 = (f32[640,1280]{1,0:T(8,128)}, f32[640,1280]{1,0:T(8,128)}, f32[640,1280]{1,0:T(8,128)S(1)}, f32[32,128]{1,0:T(8,128)S(1)}) custom-call(s32[1]{0:T(128)} %bitcast.c_ref, f32[640,1280]{1,0:T(8,128)S(1)} %copy-done.1, f32[640,1280]{1,0:T(8,128)S(1)} %copy-done.21, f32[640,1280]{1,0:T(8,128)S(1)} %copy-done.22, ...), custom_call_target="tpu_custom_call" | custom-call | flops 1 | bytes 1 | tf_op jit(solution)/shard_map/pallas_call | solution.py:439
  305.0 3.2 %shard_map.167 = f32[160,5120]{1,0:T(8,128)} custom-call(f32[160,5120]{1,0:T(8,128)S(1)} %copy-done.4, f32[160,5120]{1,0:T(8,128)S(1)} %get-tuple-element.232.u_ref, f32[32,128]{1,0:T(8,128)S(1)} %shard_map.166.refs_0_, f32[32,128]{1,0:T(8,128)S(1)} %collective-permute-done.28.refs_1_), custom_call_target="tpu_custom_call" | custom-call | flops 1 | bytes 1 | tf_op jit(solution)/shard_map/pallas_call | solution.py:466
  308.2 3.2 %shard_map.168 = f32[640,1280]{1,0:T(8,128)} custom-call(f32[640,1280]{1,0:T(8,128)S(1)} %copy-done.1, f32[640,1280]{1,0:T(8,128)S(1)} %get-tuple-element.239.u_ref, f32[32,128]{1,0:T(8,128)S(1)} %shard_map.166.refs_0_, f32[32,128]{1,0:T(8,128)S(1)} %collective-permute-done.28.refs_1_), custom_call_target="tpu_custom_call" | custom-call | flops 1 | bytes 1 | tf_op jit(solution)/shard_map/pallas_call | solution.py:466
  (171 shorter events, 96.9 us)
Async XLA Ops:
  7.2 94.5 %all-gather.3.cloned.1.call-start = ((), (), s32[]{:S(2)}) async-start(), calls=%async_computation.8 | async-start | bytes 7372800 | tf_op jit(solution)/shard_map/all_gather | solution.py:589
  14.7 196.9 %reduce-scatter.7.cloned.1.call-start = ((), (), s32[]{:S(2)}) async-start(), calls=%async_computation.5 | async-start | bytes 1228800 | tf_op jit(solution)/shard_map/reduce_scatter | solution.py:532
  14.8 65.8 %collective-permute-start = (bf16[2816,512]{1,0:T(8,128)(2,1)}, bf16[2816,512]{1,0:T(8,128)(2,1)}, u32[]{:S(2)}, u32[]{:S(2)}) collective-permute-start(bf16[2816,512]{1,0:T(8,128)(2,1)} %shard_map.136), channel_id=1, source_target_pairs={{0,4},{4,0},{8,12},{12,8},{16,20},{20,16},{24,28},{28,24},{1,5},{5... | collective-permute-start | bytes 8650760 | tf_op jit(solution)/shard_map/ppermute | solution.py:494
  90.5 31.0 %collective-permute-start.3 = (bf16[1280,512]{1,0:T(8,128)(2,1)}, bf16[1280,512]{1,0:T(8,128)(2,1)}, u32[]{:S(2)}, u32[]{:S(2)}) collective-permute-start(bf16[1280,512]{1,0:T(8,128)(2,1)} %shard_map.138.refs_0_), channel_id=1, source_target_pairs={{0,4},{4,0},{8,12},{12,8},{16,20},{20,16},{24,28},{28,24},{1,5},{5... | collective-permute-start | bytes 3932168 | tf_op jit(solution)/shard_map/ppermute | solution.py:494
  99.9 32.1 %collective-permute-start.6 = (bf16[2,4,1,96,640]{4,3,2,1,0:T(8,128)(2,1)}, bf16[2,4,1,96,640]{4,3,2,1,0:T(8,128)(2,1)}, u32[]{:S(2)}, u32[]{:S(2)}) collective-permute-start(bf16[2,4,1,96,640]{4,3,2,1,0:T(8,128)(2,1)} %shard_map.143), channel_id=1, source_target_pairs={{0,2},{1,3},{2,0},{3,1},{4,6},{5,7},{6,4},{7,5},{8,10},{9,11},{10,... | collective-permute-start | bytes 2949128 | tf_op jit(solution)/shard_map/ppermute | solution.py:504
  131.5 6.7 %collective-permute-start.4 = (bf16[1280,384]{1,0:T(8,128)(2,1)}, bf16[1280,384]{1,0:T(8,128)(2,1)}, u32[]{:S(2)}, u32[]{:S(2)}) collective-permute-start(bf16[1280,384]{1,0:T(8,128)(2,1)} %get-tuple-element.146), channel_id=1, source_target_pairs={{0,1},{1,0},{2,3},{3,2},{4,5},{5,4},{6,7},{7,6},{8,9},{9,8},{10,11... | collective-permute-start | bytes 2949128 | tf_op jit(solution)/shard_map/ppermute | solution.py:508
  131.5 6.7 %collective-permute-start.5 = (bf16[1280,384]{1,0:T(8,128)(2,1)}, bf16[1280,384]{1,0:T(8,128)(2,1)}, u32[]{:S(2)}, u32[]{:S(2)}) collective-permute-start(bf16[1280,384]{1,0:T(8,128)(2,1)} %get-tuple-element.147), channel_id=1, source_target_pairs={{0,1},{1,0},{2,3},{3,2},{4,5},{5,4},{6,7},{7,6},{8,9},{9,8},{10,11... | collective-permute-start | bytes 2949128 | tf_op jit(solution)/shard_map/ppermute | solution.py:508
  136.3 97.4 %reduce-scatter.5.cloned.1.call-start = ((), (), s32[]{:S(2)}) async-start(), calls=%async_computation.4 | async-start | bytes 1228800 | tf_op jit(solution)/shard_map/reduce_scatter | solution.py:532
  136.3 25.3 %collective-permute-start.8 = (bf16[4,256,512]{2,1,0:T(8,128)(2,1)}, bf16[4,256,512]{2,1,0:T(8,128)(2,1)S(1)}, u32[]{:S(2)}, u32[]{:S(2)}) collective-permute-start(bf16[4,256,512]{2,1,0:T(8,128)(2,1)} %shard_map.141), channel_id=1, source_target_pairs={{0,4},{4,0},{8,12},{12,8},{16,20},{20,16},{24,28},{28,24},{1,5},{5... | collective-permute-start | bytes 3145736 | tf_op jit(solution)/shard_map/ppermute | solution.py:494
  142.7 42.4 %collective-permute-start.7 = (bf16[2,4,2,80,384]{4,3,2,1,0:T(8,128)(2,1)S(1)}, bf16[2,4,2,80,384]{4,3,2,1,0:T(8,128)(2,1)S(1)}, u32[]{:S(2)}, u32[]{:S(2)}) collective-permute-start(bf16[2,4,2,80,384]{4,3,2,1,0:T(8,128)(2,1)S(1)} %shard_map.147), channel_id=1, source_target_pairs={{0,2},{1,3},{2,0},{3,1},{4,6},{5,7},{6,4},{7,5},{8,10},{9,11},{10,... | collective-permute-start | bytes 2949128 | tf_op jit(solution)/shard_map/ppermute | solution.py:504
  175.9 7.2 %collective-permute-start.9 = (bf16[1280,256]{1,0:T(8,128)(2,1)S(1)}, bf16[1280,256]{1,0:T(8,128)(2,1)S(1)}, u32[]{:S(2)}, u32[]{:S(2)}) collective-permute-start(bf16[1280,256]{1,0:T(8,128)(2,1)S(1)} %get-tuple-element.164), channel_id=1, source_target_pairs={{0,1},{1,0},{2,3},{3,2},{4,5},{5,4},{6,7},{7,6},{8,9},{9,8},{10,11... | collective-permute-start | bytes 1966088 | tf_op jit(solution)/shard_map/ppermute | solution.py:508
  175.9 7.1 %collective-permute-start.10 = (bf16[1280,256]{1,0:T(8,128)(2,1)S(1)}, bf16[1280,256]{1,0:T(8,128)(2,1)S(1)}, u32[]{:S(2)}, u32[]{:S(2)}) collective-permute-start(bf16[1280,256]{1,0:T(8,128)(2,1)S(1)} %get-tuple-element.165), channel_id=1, source_target_pairs={{0,1},{1,0},{2,3},{3,2},{4,5},{5,4},{6,7},{7,6},{8,9},{9,8},{10,11... | collective-permute-start | bytes 1966088 | tf_op jit(solution)/shard_map/ppermute | solution.py:508
  189.6 66.0 %reduce-scatter.9.cloned.1.call-start = ((), (), s32[]{:S(2)}) async-start(), calls=%async_computation.6 | async-start | bytes 819200 | tf_op jit(solution)/shard_map/reduce_scatter | solution.py:532
  190.2 17.0 %collective-permute-start.12 = (bf16[2,4,2,80,256]{4,3,2,1,0:T(8,128)(2,1)}, bf16[2,4,2,80,256]{4,3,2,1,0:T(8,128)(2,1)S(1)}, u32[]{:S(2)}, u32[]{:S(2)}) collective-permute-start(bf16[2,4,2,80,256]{4,3,2,1,0:T(8,128)(2,1)} %copy-done.36), channel_id=1, source_target_pairs={{0,2},{1,3},{2,0},{3,1},{4,6},{5,7},{6,4},{7,5},{8,10},{9,11},{10,... | collective-permute-start | bytes 1966088 | tf_op jit(solution)/shard_map/ppermute | solution.py:504
  209.6 62.1 %reduce-scatter.11.cloned.1.call-start = ((), (), s32[]{:S(2)}) async-start(), calls=%async_computation.7 | async-start | bytes 819200 | tf_op jit(solution)/shard_map/reduce_scatter | solution.py:532
  209.8 30.9 %collective-permute-start.17 = (bf16[2,4,1,64,640]{4,3,2,1,0:T(8,128)(2,1)}, bf16[2,4,1,64,640]{4,3,2,1,0:T(8,128)(2,1)}, u32[]{:S(2)}, u32[]{:S(2)}) collective-permute-start(bf16[2,4,1,64,640]{4,3,2,1,0:T(8,128)(2,1)} %copy-done.35), channel_id=1, source_target_pairs={{0,2},{1,3},{2,0},{3,1},{4,6},{5,7},{6,4},{7,5},{8,10},{9,11},{10,... | collective-permute-start | bytes 1966088 | tf_op jit(solution)/shard_map/ppermute | solution.py:504
  211.6 19.7 %collective-permute-start.11 = (bf16[2,96,640]{2,1,0:T(8,128)(2,1)}, bf16[2,96,640]{2,1,0:T(8,128)(2,1)S(1)}, u32[]{:S(2)}, u32[]{:S(2)}) collective-permute-start(bf16[2,96,640]{2,1,0:T(8,128)(2,1)} %bitcast.48), channel_id=1, source_target_pairs={{0,2},{1,3},{2,0},{3,1},{4,6},{5,7},{6,4},{7,5},{8,10},{9,11},{10,... | collective-permute-start | bytes 737288 | tf_op jit(solution)/shard_map/ppermute | solution.py:504
  235.2 4.9 %collective-permute-start.15 = (bf16[2,80,384]{2,1,0:T(8,128)(2,1)S(1)}, bf16[2,80,384]{2,1,0:T(8,128)(2,1)S(1)}, u32[]{:S(2)}, u32[]{:S(2)}) collective-permute-start(bf16[2,80,384]{2,1,0:T(8,128)(2,1)S(1)} %get-tuple-element.191), channel_id=1, source_target_pairs={{0,4},{4,0},{8,12},{12,8},{16,20},{20,16},{24,28},{28,24},{1,5},{5... | collective-permute-start | bytes 368648 | tf_op jit(solution)/shard_map/ppermute | solution.py:494
  248.0 6.3 %collective-permute-start.16 = (bf16[2,2,80,384]{3,2,1,0:T(8,128)(2,1)S(1)}, bf16[2,2,80,384]{3,2,1,0:T(8,128)(2,1)S(1)}, u32[]{:S(2)}, u32[]{:S(2)}) collective-permute-start(bf16[2,2,80,384]{3,2,1,0:T(8,128)(2,1)S(1)} %shard_map.157.refs_0_), channel_id=1, source_target_pairs={{0,2},{1,3},{2,0},{3,1},{4,6},{5,7},{6,4},{7,5},{8,10},{9,11},{10,... | collective-permute-start | bytes 737288 | tf_op jit(solution)/shard_map/ppermute | solution.py:504
  262.2 5.4 %collective-permute-start.19 = (bf16[2,2,80,256]{3,2,1,0:T(8,128)(2,1)S(1)}, bf16[2,2,80,256]{3,2,1,0:T(8,128)(2,1)S(1)}, u32[]{:S(2)}, u32[]{:S(2)}) collective-permute-start(bf16[2,2,80,256]{3,2,1,0:T(8,128)(2,1)S(1)} %shard_map.161.refs_0_), channel_id=1, source_target_pairs={{0,2},{1,3},{2,0},{3,1},{4,6},{5,7},{6,4},{7,5},{8,10},{9,11},{10,... | collective-permute-start | bytes 491528 | tf_op jit(solution)/shard_map/ppermute | solution.py:504
  264.0 9.2 %collective-permute-start.20 = (bf16[2,2,2,80,384]{4,3,2,1,0:T(8,128)(2,1)}, bf16[2,2,2,80,384]{4,3,2,1,0:T(8,128)(2,1)}, u32[]{:S(2)}, u32[]{:S(2)}) collective-permute-start(bf16[2,2,2,80,384]{4,3,2,1,0:T(8,128)(2,1)} %copy-done.32), channel_id=1, source_target_pairs={{0,1},{1,0},{2,3},{3,2},{4,5},{5,4},{6,7},{7,6},{8,9},{9,8},{10,11... | collective-permute-start | bytes 1474568 | tf_op jit(solution)/shard_map/ppermute | solution.py:508
  271.7 15.6 %collective-permute-start.22 = (bf16[2,64,640]{2,1,0:T(8,128)(2,1)}, bf16[2,64,640]{2,1,0:T(8,128)(2,1)S(1)}, u32[]{:S(2)}, u32[]{:S(2)}) collective-permute-start(bf16[2,64,640]{2,1,0:T(8,128)(2,1)} %bitcast.52), channel_id=1, source_target_pairs={{0,2},{1,3},{2,0},{3,1},{4,6},{5,7},{6,4},{7,5},{8,10},{9,11},{10,... | collective-permute-start | bytes 491528 | tf_op jit(solution)/shard_map/ppermute | solution.py:504
  273.2 15.3 %collective-permute-start.23 = (bf16[2,2,96,640]{3,2,1,0:T(8,128)(2,1)}, bf16[2,2,96,640]{3,2,1,0:T(8,128)(2,1)S(1)}, u32[]{:S(2)}, u32[]{:S(2)}) collective-permute-start(bf16[2,2,96,640]{3,2,1,0:T(8,128)(2,1)} %copy-done.30), channel_id=1, source_target_pairs={{0,1},{1,0},{2,3},{3,2},{4,5},{5,4},{6,7},{7,6},{8,9},{9,8},{10,11... | collective-permute-start | bytes 1474568 | tf_op jit(solution)/shard_map/ppermute | solution.py:508
  295.1 5.6 %collective-permute-start.27 = (f32[32,128]{1,0:T(8,128)S(1)}, f32[32,128]{1,0:T(8,128)S(1)}, u32[]{:S(2)}, u32[]{:S(2)}) collective-permute-start(f32[32,128]{1,0:T(8,128)S(1)} %get-tuple-element.227.refs_0_), channel_id=1, source_target_pairs={{0,24},{4,28},{8,16},{12,20},{16,8},{20,12},{24,0},{28,4},{1,25},{... | collective-permute-start | bytes 49160 | tf_op jit(solution)/shard_map/ppermute | solution.py:498
  (53 other events, 339.4 us)
Sparse Core Ops, SparseCore 0:
  14.9 69.6 all-gather.2
  136.4 27.6 reduce-scatter.6
  189.7 27.5 reduce-scatter.4
  220.0 20.7 reduce-scatter.8
  248.1 23.5 reduce-scatter.10

commit v9 on v7

--- a/solution.py
+++ b/solution.py
@@ -14,9 +14,9 @@
 CHIPS_Z = 4
 LANES = 128
 PARTS = 2
-VMEM = 24 * 1024 * 1024
+VMEM = 20 * 1024 * 1024
 WIDE = 56 * 1024 * 1024
-SMALL = 8 * 1024 * 1024
+SMALL = 4 * 1024 * 1024
 
 
 def moments(weight, first, second, grad):
@@ -622,7 +622,7 @@
         crossed = [across(value) for value in [*order.after(*found[: nz // 2]), *found[nz // 2 :]]]
         packs = [own] + packs
 
-        parts = [PARTS for _ in chunks]
+        parts = [2] + [2] * last
         outs = [None for _ in chunks]
         pieces_in = [(0, 0, cuts[0])]
         if last:
@@ -653,7 +653,7 @@
             chunk, block, width = pieces_in[k]
             got = order.after(pres[chunk], *columns)
             *sends, keep = grad_in_chunk(
-                got[0], got[1:], core, scale_in, 1, block, width
+                got[0], got[1:], core, scale_in, (1 if chunk else 1), block, width
             )
             order.did(keep)
             shape = (nz // CORES, nz, nx, ny, rows // ny, width)
@@ -708,17 +708,17 @@
         if last:
             start_pre(1)
             start_in(1)
+            outs[0].send_z()
             start_out(1)
             ins[1].send_y()
             ins[0].send_z()
-            outs[0].send_z()
             outs[1].send_y()
+            ins[1].send_z()
             ins[0].send_z()
+            ins[1].send_z()
             outs[0].finish()
-            ins[1].send_z()
+            outs[1].send_z()
             ins[0].finish()
-            ins[1].send_z()
-            outs[1].send_z()
             outs[0].stack_y(True)
             ins[0].stack_x()
             ins[1].finish()

time: 263 us -> 261 us (level)
  starting transfers between devices: 53.9 us -> 46.3 us
  waiting for transfers between devices: 74.1 us -> 80.2 us
  Pallas kernels: 121 us -> 117 us
  local copies, waits for them, and re-layouts: 11.6 us -> 14.9 us
    ppermute x8, waiting for transfers between devices: 2.24 us -> 13.9 us  [along_y(): return lax.ppermute(value, 'gy', pairs)]
    ppermute x14, waiting for transfers between devices: 43.8 us -> 39.1 us  [along_z(): return lax.ppermute(value, 'gx', pairs)]
    ppermute x14, starting transfers between devices: 28.3 us -> 24.4 us  [along_z(): return lax.ppermute(value, 'gx', pairs)]
    ppermute x8, starting transfers between devices: 12.5 us -> 8.85 us  [along_y(): return lax.ppermute(value, 'gy', pairs)]
    unnamed x94 -> x100, local copies, waits for them, and re-layouts: 11.6 us -> 14.9 us
    pallas_call x16, Pallas kernels: 28.6 us -> 25.7 us  [reduce_step(): pl.pallas_call(body, grid_spec=pltpu.PrefetchScalarGridSpec(num_scalar_pr...]
  transfers between devices with their start and end apart: 44 -> 44, of which waited for: 17 -> 17; matrix products, arithmetic and copies ran while one was open for 0% -> 0% of each run, Pallas kernels for 40% -> 39%
where the time goes in v9:
time: 261 us; the launch traced here: 260 us
  Pallas kernels  117 us (45%)
  waiting for transfers between devices  80.2 us (31%)
  starting transfers between devices  46.3 us (18%)
  local copies, waits for them, and re-layouts  14.9 us (6%)
    ppermute x14, waiting for transfers between devices, along_z(): return lax.ppermute(value, 'gx', pairs)  39.1 us
    pallas_call x16, Pallas kernels, reduce_step(): pl.pallas_call(body, grid_spec=pltpu.PrefetchScalarGridSpec(num_scalar_pr...  25.7 us
    ppermute x14, starting transfers between devices, along_z(): return lax.ppermute(value, 'gx', pairs)  24.4 us
    ppermute x6, waiting for transfers between devices, along_x(): return lax.ppermute(value, 'gx', pairs)  22.8 us
    pallas_call x2, Pallas kernels, grad_pre_chunk(): pl.pallas_call(body, grid_spec=pltpu.PrefetchScalarGridSpec(num_scalar_pr...  18.1 us
    unnamed x100, local copies, waits for them, and re-layouts  14.9 us
    pallas_call x2, Pallas kernels, grad_in_chunk(): pl.pallas_call(body, grid_spec=pltpu.PrefetchScalarGridSpec(num_scalar_pr...  14.6 us
    ppermute x8, waiting for transfers between devices, along_y(): return lax.ppermute(value, 'gy', pairs)  13.9 us
  transfers between devices with their start and end apart: 44, of which 17 were waited for; matrix products, arithmetic and copies ran while one was open for 0% of the time, Pallas kernels for 39%

profile of v9, /device:TPU:0, one launch (start us, length us, event | category | flops | bytes accessed | tf_op | source)
XLA Modules:
  0.0 260.3 jit_solution(3125740494518645954)
XLA Ops:
  0.7 5.2 %shard_map.136 = bf16[2816,512]{1,0:T(8,128)(2,1)} custom-call(s32[1]{0:T(128)} %bitcast.8.at_ref, bf16[512,5120]{1,0:T(8,128)(2,1)} %h_ref.4, bf16[512,1280]{1,0:T(8,128)(2,1)} %cot_ref.2), custom_call_target="tpu_custom_call" | custom-call | flops 1 | bytes 1 | tf_op jit(solution)/shard_map/pallas_call | solution.py:81
  5.8 2.9 %collective-permute-start = (bf16[2816,512]{1,0:T(8,128)(2,1)}, bf16[2816,512]{1,0:T(8,128)(2,1)}, u32[]{:S(2)}, u32[]{:S(2)}) collective-permute-start(bf16[2816,512]{1,0:T(8,128)(2,1)} %shard_map.136), channel_id=1, source_target_pairs={{0,4},{4,0},{8,12},{12,8},{16,20},{20,16},{24,28},{28,24},{1,5},{5... | collective-permute-start | bytes 8650760 | tf_op jit(solution)/shard_map/ppermute | solution.py:506
  17.7 5.1 %shard_map.139.refs_0_ = bf16[2816,512]{1,0:T(8,128)(2,1)} custom-call(s32[1]{0:T(128)} %bitcast.5.at_ref, bf16[512,5120]{1,0:T(8,128)(2,1)} %h_ref.4, bf16[512,1280]{1,0:T(8,128)(2,1)} %cot_ref.2), custom_call_target="tpu_custom_call" | custom-call | flops 1 | bytes 1 | tf_op jit(solution)/shard_map/pallas_call | solution.py:81
  22.9 3.9 %shard_map.140.refs_2_ = bf16[4,256,512]{2,1,0:T(8,128)(2,1)} custom-call(s32[1]{0:T(128)} %bitcast.3.at_ref, bf16[512,5120]{1,0:T(8,128)(2,1)} %h_ref.4), custom_call_target="tpu_custom_call" | custom-call | flops 1 | bytes 1 | tf_op jit(solution)/shard_map/pallas_call | solution.py:109
  26.7 4.0 %shard_map.141 = bf16[4,256,512]{2,1,0:T(8,128)(2,1)} custom-call(s32[1]{0:T(128)} %bitcast.8.at_ref, bf16[512,5120]{1,0:T(8,128)(2,1)} %h_ref.4), custom_call_target="tpu_custom_call" | custom-call | flops 1 | bytes 1 | tf_op jit(solution)/shard_map/pallas_call | solution.py:109
  30.8 17.7 %collective-permute-done.1.refs_3_.refs_5_ = bf16[320,1280]{1,0:T(8,128)(2,1)} collective-permute-done((bf16[320,1280]{1,0:T(8,128)(2,1)}, bf16[320,1280]{1,0:T(8,128)(2,1)}, u32[]{:S(2)}, u32[]{:S(2)}) %collective-permute-start.1) | collective-permute-done | bytes 819232 | tf_op jit(solution)/shard_map/ppermute | solution.py:510
  52.2 20.2 %collective-permute-done.refs_1_ = bf16[2816,512]{1,0:T(8,128)(2,1)} collective-permute-done((bf16[2816,512]{1,0:T(8,128)(2,1)}, bf16[2816,512]{1,0:T(8,128)(2,1)}, u32[]{:S(2)}, u32[]{:S(2)}) %collective-permute-start) | collective-permute-done | bytes 2883616 | tf_op jit(solution)/shard_map/ppermute | solution.py:506
  72.4 8.1 %shard_map.142 = (bf16[4,192,640]{2,1,0:T(8,128)(2,1)}, bf16[4,192,640]{2,1,0:T(8,128)(2,1)}, bf16[2,4,192,640]{3,2,1,0:T(8,128)(2,1)S(1)}) custom-call(s32[1]{0:T(128)} %bitcast.c_ref, bf16[2816,512]{1,0:T(8,128)(2,1)S(1)} %copy-done, bf16[2816,512]{1,0:T(8,128)(2,1)} %collective-permute-done.refs_1_), custom_call_target="tpu_custom_call" | custom-call | flops 1 | bytes 1 | tf_op jit(solution)/shard_map/pallas_call | solution.py:166
  88.3 3.1 %shard_map.143 = bf16[2,4,1,96,640]{4,3,2,1,0:T(8,128)(2,1)S(1)} custom-call(s32[3]{0:T(128)S(1)} %pad_add_fusion.2.at_ref, bf16[2,4,1,2,96,640]{5,4,3,2,1,0:T(8,128)(2,1)S(1)} %bitcast.21, bf16[4,1,2,96,640]{4,3,2,1,0:T(8,128)(2,1)} %bitcast.10.refs_1_, bf16[4,1,2,96,640]{4,3,2,1,0:T(8,128)(2,1)} %bitcast.11.refs_2_), custom_call_target="tpu_custom_call" | custom-call | flops 1 | bytes 1 | tf_op jit(solution)/shard_map/pallas_call | solution.py:401
  93.1 10.3 %shard_map.144.g_ref = bf16[4,384,1024]{2,1,0:T(8,128)(2,1)S(1)} custom-call(s32[2]{0:T(128)S(1)} %pad_add_fusion.3.c_ref, bf16[2816,512]{1,0:T(8,128)(2,1)S(1)} %copy-done, bf16[2816,512]{1,0:T(8,128)(2,1)} %collective-permute-done.refs_1_, bf16[320,1280]{1,0:T(8,128)(2,1)S(1)} %copy-done.30, bf16[320,1280]{1,0:T(8,128)(2,1)} %collective-permute-done.1.refs_3_.refs_5_, ...), custom_call_target="tpu_custom_call" | custom-call | flops 1 | bytes 1 | tf_op jit(solution)/shard_map/pallas_call | solution.py:205
  103.4 8.8 %shard_map.145 = (bf16[1280,384]{1,0:T(8,128)(2,1)S(1)}, bf16[1280,384]{1,0:T(8,128)(2,1)S(1)}, bf16[2,1280,384]{2,1,0:T(8,128)(2,1)S(1)}) custom-call(s32[1]{0:T(128)} %bitcast.c_ref, bf16[4,384,1024]{2,1,0:T(8,128)(2,1)S(1)} %shard_map.144.g_ref, bf16[1280,512]{1,0:T(8,128)(2,1)} %shard_map.138.refs_0_, bf16[1280,512]{1,0:T(8,128)(2,1)} %collective-permute-done.10.refs_1_), custom_call_target="tpu_custom_call" | custom-call | flops 1 | bytes 1 | tf_op jit(solution)/shard_map/pallas_call | solution.py:242
  122.0 7.8 %shard_map.148.g_ref = bf16[4,256,1024]{2,1,0:T(8,128)(2,1)S(1)} custom-call(s32[2]{0:T(128)S(1)} %pad_add_fusion.3.c_ref, bf16[2816,512]{1,0:T(8,128)(2,1)S(1)} %copy-done, bf16[2816,512]{1,0:T(8,128)(2,1)} %collective-permute-done.refs_1_, bf16[4,256,512]{2,1,0:T(8,128)(2,1)S(1)} %copy-done.26, bf16[4,256,512]{2,1,0:T(8,128)(2,1)S(1)} %collective-permute-done.15.refs_3_, ...), custom_call_target="tpu_custom_call" | custom-call | flops 1 | bytes 1 | tf_op jit(solution)/shard_map/pallas_call | solution.py:205
  129.9 5.8 %shard_map.149 = (bf16[1280,256]{1,0:T(8,128)(2,1)S(1)}, bf16[1280,256]{1,0:T(8,128)(2,1)S(1)}, bf16[2,1280,256]{2,1,0:T(8,128)(2,1)S(1)}) custom-call(s32[1]{0:T(128)} %bitcast.c_ref, bf16[4,256,1024]{2,1,0:T(8,128)(2,1)S(1)} %shard_map.148.g_ref, bf16[1280,512]{1,0:T(8,128)(2,1)} %shard_map.138.refs_0_, bf16[1280,512]{1,0:T(8,128)(2,1)} %collective-permute-done.10.refs_1_), custom_call_target="tpu_custom_call" | custom-call | flops 1 | bytes 1 | tf_op jit(solution)/shard_map/pallas_call | solution.py:242
  137.9 5.6 %shard_map.151 = (bf16[4,128,640]{2,1,0:T(8,128)(2,1)S(1)}, bf16[4,128,640]{2,1,0:T(8,128)(2,1)S(1)}, bf16[2,4,128,640]{3,2,1,0:T(8,128)(2,1)S(1)}) custom-call(s32[1]{0:T(128)} %bitcast.c_ref, bf16[2816,512]{1,0:T(8,128)(2,1)S(1)} %copy-done, bf16[2816,512]{1,0:T(8,128)(2,1)} %collective-permute-done.refs_1_, bf16[4,256,512]{2,1,0:T(8,128)(2,1)S(1)} %copy-done.26, ...), custom_call_target="tpu_custom_call" | custom-call | flops 1 | bytes 1 | tf_op jit(solution)/shard_map/pallas_call | solution.py:166
  152.7 10.1 %collective-permute-done.20.refs_3_ = bf16[2,4,2,80,256]{4,3,2,1,0:T(8,128)(2,1)S(1)} collective-permute-done((bf16[2,4,2,80,256]{4,3,2,1,0:T(8,128)(2,1)S(1)}, bf16[2,4,2,80,256]{4,3,2,1,0:T(8,128)(2,1)S(1)}, u32[]{:S(2)}, u32[]{:S(2)}) %collective-permute-start.20) | collective-permute-done | bytes 655392 | tf_op jit(solution)/shard_map/ppermute | solution.py:516
  170.2 8.5 %collective-permute-done.26.refs_4_ = bf16[2,2,2,80,256]{4,3,2,1,0:T(8,128)(2,1)S(1)} collective-permute-done((bf16[2,2,2,80,256]{4,3,2,1,0:T(8,128)(2,1)S(1)}, bf16[2,2,2,80,256]{4,3,2,1,0:T(8,128)(2,1)S(1)}, u32[]{:S(2)}, u32[]{:S(2)}) %collective-permute-start.26) | collective-permute-done | bytes 327712 | tf_op jit(solution)/shard_map/ppermute | solution.py:510
  179.5 5.4 %collective-permute-done.25.refs_5_ = bf16[2,1,1,96,640]{4,3,2,1,0:T(8,128)(2,1)S(1)} collective-permute-done((bf16[2,1,1,96,640]{4,3,2,1,0:T(8,128)(2,1)S(1)}, bf16[2,1,1,96,640]{4,3,2,1,0:T(8,128)(2,1)S(1)}, u32[]{:S(2)}, u32[]{:S(2)}) %collective-permute-start.25) | collective-permute-done | bytes 245792 | tf_op jit(solution)/shard_map/ppermute | solution.py:510
  200.1 3.4 %collective-permute-start.31 = (bf16[2,1,2,80,256]{4,3,2,1,0:T(8,128)(2,1)}, bf16[2,1,2,80,256]{4,3,2,1,0:T(8,128)(2,1)S(1)}, u32[]{:S(2)}, u32[]{:S(2)}) collective-permute-start(bf16[2,1,2,80,256]{4,3,2,1,0:T(8,128)(2,1)} %copy-done.47), channel_id=1, source_target_pairs={{0,16},{4,20},{8,24},{12,28},{16,0},{20,4},{24,8},{28,12},{1,17},{... | collective-permute-start | bytes 491528 | tf_op jit(solution)/shard_map/ppermute | solution.py:510
  215.8 3.0 %collective-permute-start.34 = (bf16[2,1,1,64,640]{4,3,2,1,0:T(8,128)(2,1)S(1)}, bf16[2,1,1,64,640]{4,3,2,1,0:T(8,128)(2,1)S(1)}, u32[]{:S(2)}, u32[]{:S(2)}) collective-permute-start(bf16[2,1,1,64,640]{4,3,2,1,0:T(8,128)(2,1)S(1)} %shard_map.164), channel_id=1, source_target_pairs={{0,16},{4,20},{8,24},{12,28},{16,0},{20,4},{24,8},{28,12},{1,17},{... | collective-permute-start | bytes 491528 | tf_op jit(solution)/shard_map/ppermute | solution.py:510
  227.8 6.2 %shard_map.169 = (f32[160,5120]{1,0:T(8,128)}, f32[160,5120]{1,0:T(8,128)}, f32[160,5120]{1,0:T(8,128)S(1)}, f32[16,128]{1,0:T(8,128)S(1)}) custom-call(s32[1]{0:T(128)} %bitcast.c_ref, f32[160,5120]{1,0:T(8,128)S(1)} %copy-done.15, f32[160,5120]{1,0:T(8,128)S(1)} %copy-done.33, f32[160,5120]{1,0:T(8,128)S(1)} %copy-done.34, ...), custom_call_target="tpu_custom_call" | custom-call | flops 1 | bytes 1 | tf_op jit(solution)/shard_map/pallas_call | solution.py:451
  236.2 5.3 %shard_map.171 = (f32[640,1280]{1,0:T(8,128)}, f32[640,1280]{1,0:T(8,128)}, f32[640,1280]{1,0:T(8,128)S(1)}, f32[32,128]{1,0:T(8,128)S(1)}) custom-call(s32[1]{0:T(128)} %bitcast.c_ref, f32[640,1280]{1,0:T(8,128)S(1)} %copy-done.6, f32[640,1280]{1,0:T(8,128)S(1)} %copy-done.35, f32[640,1280]{1,0:T(8,128)S(1)} %copy-done.36, ...), custom_call_target="tpu_custom_call" | custom-call | flops 1 | bytes 1 | tf_op jit(solution)/shard_map/pallas_call | solution.py:451
  241.5 3.9 %collective-permute-start.42 = (f32[32,128]{1,0:T(8,128)S(1)}, f32[32,128]{1,0:T(8,128)S(1)}, u32[]{:S(2)}, u32[]{:S(2)}) collective-permute-start(f32[32,128]{1,0:T(8,128)S(1)} %get-tuple-element.345.refs_0_), channel_id=1, source_target_pairs={{0,24},{4,28},{8,16},{12,20},{16,8},{20,12},{24,0},{28,4},{1,25},{... | collective-permute-start | bytes 49160 | tf_op jit(solution)/shard_map/ppermute | solution.py:510
  253.9 3.2 %shard_map.173 = f32[160,5120]{1,0:T(8,128)} custom-call(f32[160,5120]{1,0:T(8,128)S(1)} %copy-done.15, f32[160,5120]{1,0:T(8,128)S(1)} %get-tuple-element.350.u_ref, f32[32,128]{1,0:T(8,128)S(1)} %shard_map.172.refs_0_, f32[32,128]{1,0:T(8,128)S(1)} %collective-permute-done.43.refs_1_), custom_call_target="tpu_custom_call" | custom-call | flops 1 | bytes 1 | tf_op jit(solution)/shard_map/pallas_call | solution.py:478
  257.1 3.2 %shard_map.174 = f32[640,1280]{1,0:T(8,128)} custom-call(f32[640,1280]{1,0:T(8,128)S(1)} %copy-done.6, f32[640,1280]{1,0:T(8,128)S(1)} %get-tuple-element.357.u_ref, f32[32,128]{1,0:T(8,128)S(1)} %shard_map.172.refs_0_, f32[32,128]{1,0:T(8,128)S(1)} %collective-permute-done.43.refs_1_), custom_call_target="tpu_custom_call" | custom-call | flops 1 | bytes 1 | tf_op jit(solution)/shard_map/pallas_call | solution.py:478
  (207 shorter events, 98.3 us)
Async XLA Ops:
  5.8 66.6 %collective-permute-start = (bf16[2816,512]{1,0:T(8,128)(2,1)}, bf16[2816,512]{1,0:T(8,128)(2,1)}, u32[]{:S(2)}, u32[]{:S(2)}) collective-permute-start(bf16[2816,512]{1,0:T(8,128)(2,1)} %shard_map.136), channel_id=1, source_target_pairs={{0,4},{4,0},{8,12},{12,8},{16,20},{20,16},{24,28},{28,24},{1,5},{5... | collective-permute-start | bytes 8650760 | tf_op jit(solution)/shard_map/ppermute | solution.py:506
  11.0 37.4 %collective-permute-start.1 = (bf16[320,1280]{1,0:T(8,128)(2,1)}, bf16[320,1280]{1,0:T(8,128)(2,1)}, u32[]{:S(2)}, u32[]{:S(2)}) collective-permute-start(bf16[320,1280]{1,0:T(8,128)(2,1)} %shard_map.137.refs_2_.refs_4_), channel_id=1, source_target_pairs={{0,8},{4,12},{8,0},{12,4},{16,24},{20,28},{24,16},{28,20},{1,9},{5... | collective-permute-start | bytes 2457608 | tf_op jit(solution)/shard_map/ppermute | solution.py:510
  12.6 38.3 %collective-permute-start.2 = (bf16[320,1280]{1,0:T(8,128)(2,1)}, bf16[320,1280]{1,0:T(8,128)(2,1)}, u32[]{:S(2)}, u32[]{:S(2)}) collective-permute-start(bf16[320,1280]{1,0:T(8,128)(2,1)} %shard_map.137.refs_2_.refs_4_), channel_id=1, source_target_pairs={{0,16},{4,20},{8,24},{12,28},{16,0},{20,4},{24,8},{28,12},{1,17},{... | collective-permute-start | bytes 2457608 | tf_op jit(solution)/shard_map/ppermute | solution.py:510
  50.8 31.4 %collective-permute-start.3 = (bf16[320,1280]{1,0:T(8,128)(2,1)}, bf16[320,1280]{1,0:T(8,128)(2,1)}, u32[]{:S(2)}, u32[]{:S(2)}) collective-permute-start(bf16[320,1280]{1,0:T(8,128)(2,1)} %collective-permute-done.2.refs_4_.refs_6_), channel_id=1, source_target_pairs={{0,8},{4,12},{8,0},{12,4},{16,24},{20,28},{24,16},{28,20},{1,9},{5... | collective-permute-start | bytes 2457608 | tf_op jit(solution)/shard_map/ppermute | solution.py:510
  51.3 52.1 %collective-permute-start.10 = (bf16[1280,512]{1,0:T(8,128)(2,1)}, bf16[1280,512]{1,0:T(8,128)(2,1)}, u32[]{:S(2)}, u32[]{:S(2)}) collective-permute-start(bf16[1280,512]{1,0:T(8,128)(2,1)} %shard_map.138.refs_0_), channel_id=1, source_target_pairs={{0,4},{4,0},{8,12},{12,8},{16,20},{20,16},{24,28},{28,24},{1,5},{5... | collective-permute-start | bytes 3932168 | tf_op jit(solution)/shard_map/ppermute | solution.py:506
  82.3 10.8 %collective-permute-start.6 = (bf16[320,1280]{1,0:T(8,128)(2,1)}, bf16[320,1280]{1,0:T(8,128)(2,1)}, u32[]{:S(2)}, u32[]{:S(2)}) collective-permute-start(bf16[320,1280]{1,0:T(8,128)(2,1)} %collective-permute-done.2.refs_4_.refs_6_), channel_id=1, source_target_pairs={{0,1},{1,0},{2,3},{3,2},{4,5},{5,4},{6,7},{7,6},{8,9},{9,8},{10,11... | collective-permute-start | bytes 2457608 | tf_op jit(solution)/shard_map/ppermute | solution.py:520
  82.3 10.8 %collective-permute-start.7 = (bf16[320,1280]{1,0:T(8,128)(2,1)}, bf16[320,1280]{1,0:T(8,128)(2,1)}, u32[]{:S(2)}, u32[]{:S(2)}) collective-permute-start(bf16[320,1280]{1,0:T(8,128)(2,1)} %collective-permute-done.3.refs_5_.refs_7_), channel_id=1, source_target_pairs={{0,1},{1,0},{2,3},{3,2},{4,5},{5,4},{6,7},{7,6},{8,9},{9,8},{10,11... | collective-permute-start | bytes 2457608 | tf_op jit(solution)/shard_map/ppermute | solution.py:520
  84.7 37.3 %collective-permute-start.15 = (bf16[4,256,512]{2,1,0:T(8,128)(2,1)}, bf16[4,256,512]{2,1,0:T(8,128)(2,1)S(1)}, u32[]{:S(2)}, u32[]{:S(2)}) collective-permute-start(bf16[4,256,512]{2,1,0:T(8,128)(2,1)} %shard_map.141), channel_id=1, source_target_pairs={{0,4},{4,0},{8,12},{12,8},{16,20},{20,16},{24,28},{28,24},{1,5},{5... | collective-permute-start | bytes 3145736 | tf_op jit(solution)/shard_map/ppermute | solution.py:506
  91.4 23.6 %collective-permute-start.13 = (bf16[2,4,1,96,640]{4,3,2,1,0:T(8,128)(2,1)S(1)}, bf16[2,4,1,96,640]{4,3,2,1,0:T(8,128)(2,1)S(1)}, u32[]{:S(2)}, u32[]{:S(2)}) collective-permute-start(bf16[2,4,1,96,640]{4,3,2,1,0:T(8,128)(2,1)S(1)} %shard_map.143), channel_id=1, source_target_pairs={{0,2},{1,3},{2,0},{3,1},{4,6},{5,7},{6,4},{7,5},{8,10},{9,11},{10,... | collective-permute-start | bytes 2949128 | tf_op jit(solution)/shard_map/ppermute | solution.py:516
  116.9 19.4 %collective-permute-start.18 = (bf16[2,2,1,96,640]{4,3,2,1,0:T(8,128)(2,1)S(1)}, bf16[2,2,1,96,640]{4,3,2,1,0:T(8,128)(2,1)S(1)}, u32[]{:S(2)}, u32[]{:S(2)}) collective-permute-start(bf16[2,2,1,96,640]{4,3,2,1,0:T(8,128)(2,1)S(1)} %shard_map.146), channel_id=1, source_target_pairs={{0,8},{4,12},{8,0},{12,4},{16,24},{20,28},{24,16},{28,20},{1,9},{5... | collective-permute-start | bytes 1474568 | tf_op jit(solution)/shard_map/ppermute | solution.py:510
  120.1 27.0 %collective-permute-start.14 = (bf16[2,4,2,80,384]{4,3,2,1,0:T(8,128)(2,1)S(1)}, bf16[2,4,2,80,384]{4,3,2,1,0:T(8,128)(2,1)S(1)}, u32[]{:S(2)}, u32[]{:S(2)}) collective-permute-start(bf16[2,4,2,80,384]{4,3,2,1,0:T(8,128)(2,1)S(1)} %shard_map.147), channel_id=1, source_target_pairs={{0,2},{1,3},{2,0},{3,1},{4,6},{5,7},{6,4},{7,5},{8,10},{9,11},{10,... | collective-permute-start | bytes 2949128 | tf_op jit(solution)/shard_map/ppermute | solution.py:516
  135.7 8.4 %collective-permute-start.16 = (bf16[1280,256]{1,0:T(8,128)(2,1)S(1)}, bf16[1280,256]{1,0:T(8,128)(2,1)S(1)}, u32[]{:S(2)}, u32[]{:S(2)}) collective-permute-start(bf16[1280,256]{1,0:T(8,128)(2,1)S(1)} %get-tuple-element.240), channel_id=1, source_target_pairs={{0,1},{1,0},{2,3},{3,2},{4,5},{5,4},{6,7},{7,6},{8,9},{9,8},{10,11... | collective-permute-start | bytes 1966088 | tf_op jit(solution)/shard_map/ppermute | solution.py:520
  135.7 8.4 %collective-permute-start.17 = (bf16[1280,256]{1,0:T(8,128)(2,1)S(1)}, bf16[1280,256]{1,0:T(8,128)(2,1)S(1)}, u32[]{:S(2)}, u32[]{:S(2)}) collective-permute-start(bf16[1280,256]{1,0:T(8,128)(2,1)S(1)} %get-tuple-element.241), channel_id=1, source_target_pairs={{0,1},{1,0},{2,3},{3,2},{4,5},{5,4},{6,7},{7,6},{8,9},{9,8},{10,11... | collective-permute-start | bytes 1966088 | tf_op jit(solution)/shard_map/ppermute | solution.py:520
  145.2 17.6 %collective-permute-start.20 = (bf16[2,4,2,80,256]{4,3,2,1,0:T(8,128)(2,1)S(1)}, bf16[2,4,2,80,256]{4,3,2,1,0:T(8,128)(2,1)S(1)}, u32[]{:S(2)}, u32[]{:S(2)}) collective-permute-start(bf16[2,4,2,80,256]{4,3,2,1,0:T(8,128)(2,1)S(1)} %shard_map.152), channel_id=1, source_target_pairs={{0,2},{1,3},{2,0},{3,1},{4,6},{5,7},{6,4},{7,5},{8,10},{9,11},{10,... | collective-permute-start | bytes 1966088 | tf_op jit(solution)/shard_map/ppermute | solution.py:516
  148.4 19.9 %collective-permute-start.19 = (bf16[2,2,2,80,384]{4,3,2,1,0:T(8,128)(2,1)S(1)}, bf16[2,2,2,80,384]{4,3,2,1,0:T(8,128)(2,1)S(1)}, u32[]{:S(2)}, u32[]{:S(2)}) collective-permute-start(bf16[2,2,2,80,384]{4,3,2,1,0:T(8,128)(2,1)S(1)} %shard_map.153), channel_id=1, source_target_pairs={{0,8},{4,12},{8,0},{12,4},{16,24},{20,28},{24,16},{28,20},{1,9},{5... | collective-permute-start | bytes 1474568 | tf_op jit(solution)/shard_map/ppermute | solution.py:510
  152.2 35.9 %collective-permute-start.24 = (bf16[2,4,1,64,640]{4,3,2,1,0:T(8,128)(2,1)}, bf16[2,4,1,64,640]{4,3,2,1,0:T(8,128)(2,1)}, u32[]{:S(2)}, u32[]{:S(2)}) collective-permute-start(bf16[2,4,1,64,640]{4,3,2,1,0:T(8,128)(2,1)} %shard_map.154), channel_id=1, source_target_pairs={{0,2},{1,3},{2,0},{3,1},{4,6},{5,7},{6,4},{7,5},{8,10},{9,11},{10,... | collective-permute-start | bytes 1966088 | tf_op jit(solution)/shard_map/ppermute | solution.py:516
  163.9 14.8 %collective-permute-start.26 = (bf16[2,2,2,80,256]{4,3,2,1,0:T(8,128)(2,1)S(1)}, bf16[2,2,2,80,256]{4,3,2,1,0:T(8,128)(2,1)S(1)}, u32[]{:S(2)}, u32[]{:S(2)}) collective-permute-start(bf16[2,2,2,80,256]{4,3,2,1,0:T(8,128)(2,1)S(1)} %shard_map.155), channel_id=1, source_target_pairs={{0,8},{4,12},{8,0},{12,4},{16,24},{20,28},{24,16},{28,20},{1,9},{5... | collective-permute-start | bytes 983048 | tf_op jit(solution)/shard_map/ppermute | solution.py:510
  165.8 19.1 %collective-permute-start.25 = (bf16[2,1,1,96,640]{4,3,2,1,0:T(8,128)(2,1)S(1)}, bf16[2,1,1,96,640]{4,3,2,1,0:T(8,128)(2,1)S(1)}, u32[]{:S(2)}, u32[]{:S(2)}) collective-permute-start(bf16[2,1,1,96,640]{4,3,2,1,0:T(8,128)(2,1)S(1)} %shard_map.150), channel_id=1, source_target_pairs={{0,16},{4,20},{8,24},{12,28},{16,0},{20,4},{24,8},{28,12},{1,17},{... | collective-permute-start | bytes 737288 | tf_op jit(solution)/shard_map/ppermute | solution.py:510
  169.9 22.3 %collective-permute-start.23 = (bf16[2,1,2,80,384]{4,3,2,1,0:T(8,128)(2,1)}, bf16[2,1,2,80,384]{4,3,2,1,0:T(8,128)(2,1)}, u32[]{:S(2)}, u32[]{:S(2)}) collective-permute-start(bf16[2,1,2,80,384]{4,3,2,1,0:T(8,128)(2,1)} %shard_map.156), channel_id=1, source_target_pairs={{0,16},{4,20},{8,24},{12,28},{16,0},{20,4},{24,8},{28,12},{1,17},{... | collective-permute-start | bytes 737288 | tf_op jit(solution)/shard_map/ppermute | solution.py:510
  186.6 16.9 %collective-permute-start.28 = (bf16[2,96,640]{2,1,0:T(8,128)(2,1)S(1)}, bf16[2,96,640]{2,1,0:T(8,128)(2,1)}, u32[]{:S(2)}, u32[]{:S(2)}) collective-permute-start(bf16[2,96,640]{2,1,0:T(8,128)(2,1)S(1)} %shard_map.158.refs_0_), channel_id=1, source_target_pairs={{0,2},{1,3},{2,0},{3,1},{4,6},{5,7},{6,4},{7,5},{8,10},{9,11},{10,... | collective-permute-start | bytes 737288 | tf_op jit(solution)/shard_map/ppermute | solution.py:516
  199.4 14.5 %collective-permute-start.30 = (bf16[2,2,1,64,640]{4,3,2,1,0:T(8,128)(2,1)}, bf16[2,2,1,64,640]{4,3,2,1,0:T(8,128)(2,1)S(1)}, u32[]{:S(2)}, u32[]{:S(2)}) collective-permute-start(bf16[2,2,1,64,640]{4,3,2,1,0:T(8,128)(2,1)} %copy-done.46), channel_id=1, source_target_pairs={{0,8},{4,12},{8,0},{12,4},{16,24},{20,28},{24,16},{28,20},{1,9},{5... | collective-permute-start | bytes 983048 | tf_op jit(solution)/shard_map/ppermute | solution.py:510
  206.5 12.4 %collective-permute-start.29 = (bf16[2,2,80,384]{3,2,1,0:T(8,128)(2,1)S(1)}, bf16[2,2,80,384]{3,2,1,0:T(8,128)(2,1)S(1)}, u32[]{:S(2)}, u32[]{:S(2)}) collective-permute-start(bf16[2,2,80,384]{3,2,1,0:T(8,128)(2,1)S(1)} %shard_map.162.refs_0_), channel_id=1, source_target_pairs={{0,2},{1,3},{2,0},{3,1},{4,6},{5,7},{6,4},{7,5},{8,10},{9,11},{10,... | collective-permute-start | bytes 737288 | tf_op jit(solution)/shard_map/ppermute | solution.py:516
  226.1 7.8 %collective-permute-start.37 = (bf16[2,64,640]{2,1,0:T(8,128)(2,1)S(1)}, bf16[2,64,640]{2,1,0:T(8,128)(2,1)S(1)}, u32[]{:S(2)}, u32[]{:S(2)}) collective-permute-start(bf16[2,64,640]{2,1,0:T(8,128)(2,1)S(1)} %shard_map.167.refs_0_), channel_id=1, source_target_pairs={{0,2},{1,3},{2,0},{3,1},{4,6},{5,7},{6,4},{7,5},{8,10},{9,11},{10,... | collective-permute-start | bytes 491528 | tf_op jit(solution)/shard_map/ppermute | solution.py:516
  226.7 8.0 %collective-permute-start.38 = (bf16[2,2,96,640]{3,2,1,0:T(8,128)(2,1)S(1)}, bf16[2,2,96,640]{3,2,1,0:T(8,128)(2,1)S(1)}, u32[]{:S(2)}, u32[]{:S(2)}) collective-permute-start(bf16[2,2,96,640]{3,2,1,0:T(8,128)(2,1)S(1)} %shard_map.161.refs_0_), channel_id=1, source_target_pairs={{0,1},{1,0},{2,3},{3,2},{4,5},{5,4},{6,7},{7,6},{8,9},{9,8},{10,11... | collective-permute-start | bytes 1474568 | tf_op jit(solution)/shard_map/ppermute | solution.py:520
  (70 other events, 757.9 us)

commit v10 on v9

--- a/solution.py
+++ b/solution.py
@@ -711,20 +711,20 @@
             outs[0].send_z()
             start_out(1)
             ins[1].send_y()
+            outs[1].send_y()
             ins[0].send_z()
-            outs[1].send_y()
             ins[1].send_z()
             ins[0].send_z()
+            outs[1].send_z()
             ins[1].send_z()
             outs[0].finish()
+            ins[0].finish()
             outs[1].send_z()
-            ins[0].finish()
+            ins[1].finish()
+            ins[0].stack_x()
+            ins[1].stack_x()
             outs[0].stack_y(True)
-            ins[0].stack_x()
-            ins[1].finish()
-            outs[1].send_z()
             ins[0].stack_y()
-            ins[1].stack_x()
             outs[1].finish()
             ins[1].stack_y()
         else:

time: 261 us -> 256 us (0.981)
  local copies, waits for them, and re-layouts: 14.9 us -> 10.8 us
    ppermute x14, waiting for transfers between devices: 39.1 us -> 29.3 us  [along_z(): return lax.ppermute(value, 'gx', pairs)]
    unnamed x100 -> x86, local copies, waits for them, and re-layouts: 14.9 us -> 10.8 us
    ppermute x8, waiting for transfers between devices: 13.9 us -> 17.7 us  [along_y(): return lax.ppermute(value, 'gy', pairs)]
  transfers between devices with their start and end apart: 44 -> 44, of which waited for: 17 -> 18; matrix products, arithmetic and copies ran while one was open for 0% -> 0% of each run, Pallas kernels for 39% -> 39%
where the time goes in v10:
time: 256 us; the launch traced here: 255 us
  Pallas kernels  118 us (46%)
  waiting for transfers between devices  77.7 us (30%)
  starting transfers between devices  47.3 us (18%)
  local copies, waits for them, and re-layouts  10.8 us (4%)
    ppermute x14, waiting for transfers between devices, along_z(): return lax.ppermute(value, 'gx', pairs)  29.3 us
    ppermute x6, waiting for transfers between devices, along_x(): return lax.ppermute(value, 'gx', pairs)  25.3 us
    pallas_call x16, Pallas kernels, reduce_step(): pl.pallas_call(body, grid_spec=pltpu.PrefetchScalarGridSpec(num_scalar_pr...  24.7 us
    ppermute x14, starting transfers between devices, along_z(): return lax.ppermute(value, 'gx', pairs)  23.6 us
    pallas_call x2, Pallas kernels, grad_pre_chunk(): pl.pallas_call(body, grid_spec=pltpu.PrefetchScalarGridSpec(num_scalar_pr...  18.1 us
    ppermute x8, waiting for transfers between devices, along_y(): return lax.ppermute(value, 'gy', pairs)  17.7 us
    pallas_call x2, Pallas kernels, grad_in_chunk(): pl.pallas_call(body, grid_spec=pltpu.PrefetchScalarGridSpec(num_scalar_pr...  14.7 us
    pallas_call x2, Pallas kernels, grad_out_chunk(): pl.pallas_call(body, grid_spec=pltpu.PrefetchScalarGridSpec(num_scalar_pr...  13.7 us
  transfers between devices with their start and end apart: 44, of which 18 were waited for; matrix products, arithmetic and copies ran while one was open for 0% of the time, Pallas kernels for 39%

profile of v10, /device:TPU:0, one launch (start us, length us, event | category | flops | bytes accessed | tf_op | source)
XLA Modules:
  0.0 254.8 jit_solution(732020624151015608)
XLA Ops:
  0.7 5.2 %shard_map.136 = bf16[2816,512]{1,0:T(8,128)(2,1)} custom-call(s32[1]{0:T(128)} %bitcast.8.at_ref, bf16[512,5120]{1,0:T(8,128)(2,1)} %h_ref.4, bf16[512,1280]{1,0:T(8,128)(2,1)} %cot_ref.2), custom_call_target="tpu_custom_call" | custom-call | flops 1 | bytes 1 | tf_op jit(solution)/shard_map/pallas_call | solution.py:81
  5.8 2.9 %collective-permute-start = (bf16[2816,512]{1,0:T(8,128)(2,1)}, bf16[2816,512]{1,0:T(8,128)(2,1)}, u32[]{:S(2)}, u32[]{:S(2)}) collective-permute-start(bf16[2816,512]{1,0:T(8,128)(2,1)} %shard_map.136), channel_id=1, source_target_pairs={{0,4},{4,0},{8,12},{12,8},{16,20},{20,16},{24,28},{28,24},{1,5},{5... | collective-permute-start | bytes 8650760 | tf_op jit(solution)/shard_map/ppermute | solution.py:506
  12.6 2.6 %collective-permute-start.2 = (bf16[320,1280]{1,0:T(8,128)(2,1)}, bf16[320,1280]{1,0:T(8,128)(2,1)}, u32[]{:S(2)}, u32[]{:S(2)}) collective-permute-start(bf16[320,1280]{1,0:T(8,128)(2,1)} %shard_map.137.refs_2_.refs_4_), channel_id=1, source_target_pairs={{0,16},{4,20},{8,24},{12,28},{16,0},{20,4},{24,8},{28,12},{1,17},{... | collective-permute-start | bytes 2457608 | tf_op jit(solution)/shard_map/ppermute | solution.py:510
  17.7 5.1 %shard_map.139.refs_0_ = bf16[2816,512]{1,0:T(8,128)(2,1)} custom-call(s32[1]{0:T(128)} %bitcast.5.at_ref, bf16[512,5120]{1,0:T(8,128)(2,1)} %h_ref.4, bf16[512,1280]{1,0:T(8,128)(2,1)} %cot_ref.2), custom_call_target="tpu_custom_call" | custom-call | flops 1 | bytes 1 | tf_op jit(solution)/shard_map/pallas_call | solution.py:81
  22.8 3.9 %shard_map.140.refs_2_ = bf16[4,256,512]{2,1,0:T(8,128)(2,1)} custom-call(s32[1]{0:T(128)} %bitcast.3.at_ref, bf16[512,5120]{1,0:T(8,128)(2,1)} %h_ref.4), custom_call_target="tpu_custom_call" | custom-call | flops 1 | bytes 1 | tf_op jit(solution)/shard_map/pallas_call | solution.py:109
  26.7 4.0 %shard_map.141 = bf16[4,256,512]{2,1,0:T(8,128)(2,1)} custom-call(s32[1]{0:T(128)} %bitcast.8.at_ref, bf16[512,5120]{1,0:T(8,128)(2,1)} %h_ref.4), custom_call_target="tpu_custom_call" | custom-call | flops 1 | bytes 1 | tf_op jit(solution)/shard_map/pallas_call | solution.py:109
  30.7 17.7 %collective-permute-done.1.refs_3_.refs_5_ = bf16[320,1280]{1,0:T(8,128)(2,1)} collective-permute-done((bf16[320,1280]{1,0:T(8,128)(2,1)}, bf16[320,1280]{1,0:T(8,128)(2,1)}, u32[]{:S(2)}, u32[]{:S(2)}) %collective-permute-start.1) | collective-permute-done | bytes 819232 | tf_op jit(solution)/shard_map/ppermute | solution.py:510
  52.1 20.2 %collective-permute-done.refs_1_ = bf16[2816,512]{1,0:T(8,128)(2,1)} collective-permute-done((bf16[2816,512]{1,0:T(8,128)(2,1)}, bf16[2816,512]{1,0:T(8,128)(2,1)}, u32[]{:S(2)}, u32[]{:S(2)}) %collective-permute-start) | collective-permute-done | bytes 2883616 | tf_op jit(solution)/shard_map/ppermute | solution.py:506
  72.4 8.1 %shard_map.142 = (bf16[4,192,640]{2,1,0:T(8,128)(2,1)}, bf16[4,192,640]{2,1,0:T(8,128)(2,1)}, bf16[2,4,192,640]{3,2,1,0:T(8,128)(2,1)S(1)}) custom-call(s32[1]{0:T(128)} %bitcast.c_ref, bf16[2816,512]{1,0:T(8,128)(2,1)S(1)} %copy-done, bf16[2816,512]{1,0:T(8,128)(2,1)} %collective-permute-done.refs_1_), custom_call_target="tpu_custom_call" | custom-call | flops 1 | bytes 1 | tf_op jit(solution)/shard_map/pallas_call | solution.py:166
  87.7 3.2 %shard_map.143 = bf16[2,4,1,96,640]{4,3,2,1,0:T(8,128)(2,1)S(1)} custom-call(s32[3]{0:T(128)S(1)} %pad_add_fusion.2.at_ref, bf16[2,4,1,2,96,640]{5,4,3,2,1,0:T(8,128)(2,1)S(1)} %bitcast.21, bf16[4,1,2,96,640]{4,3,2,1,0:T(8,128)(2,1)} %bitcast.10.refs_1_, bf16[4,1,2,96,640]{4,3,2,1,0:T(8,128)(2,1)} %bitcast.11.refs_2_), custom_call_target="tpu_custom_call" | custom-call | flops 1 | bytes 1 | tf_op jit(solution)/shard_map/pallas_call | solution.py:401
  94.7 10.3 %shard_map.144.g_ref = bf16[4,384,1024]{2,1,0:T(8,128)(2,1)S(1)} custom-call(s32[2]{0:T(128)S(1)} %pad_add_fusion.3.c_ref, bf16[2816,512]{1,0:T(8,128)(2,1)S(1)} %copy-done, bf16[2816,512]{1,0:T(8,128)(2,1)} %collective-permute-done.refs_1_, bf16[320,1280]{1,0:T(8,128)(2,1)S(1)} %copy-done.19, bf16[320,1280]{1,0:T(8,128)(2,1)} %collective-permute-done.1.refs_3_.refs_5_, ...), custom_call_target="tpu_custom_call" | custom-call | flops 1 | bytes 1 | tf_op jit(solution)/shard_map/pallas_call | solution.py:205
  105.0 8.9 %shard_map.145 = (bf16[1280,384]{1,0:T(8,128)(2,1)S(1)}, bf16[1280,384]{1,0:T(8,128)(2,1)S(1)}, bf16[2,1280,384]{2,1,0:T(8,128)(2,1)S(1)}) custom-call(s32[1]{0:T(128)} %bitcast.c_ref, bf16[4,384,1024]{2,1,0:T(8,128)(2,1)S(1)} %shard_map.144.g_ref, bf16[1280,512]{1,0:T(8,128)(2,1)} %shard_map.138.refs_0_, bf16[1280,512]{1,0:T(8,128)(2,1)} %collective-permute-done.10.refs_1_), custom_call_target="tpu_custom_call" | custom-call | flops 1 | bytes 1 | tf_op jit(solution)/shard_map/pallas_call | solution.py:242
  122.0 7.9 %shard_map.148.g_ref = bf16[4,256,1024]{2,1,0:T(8,128)(2,1)S(1)} custom-call(s32[2]{0:T(128)S(1)} %pad_add_fusion.3.c_ref, bf16[2816,512]{1,0:T(8,128)(2,1)S(1)} %copy-done, bf16[2816,512]{1,0:T(8,128)(2,1)} %collective-permute-done.refs_1_, bf16[4,256,512]{2,1,0:T(8,128)(2,1)S(1)} %copy-done.17, bf16[4,256,512]{2,1,0:T(8,128)(2,1)S(1)} %collective-permute-done.15.refs_3_, ...), custom_call_target="tpu_custom_call" | custom-call | flops 1 | bytes 1 | tf_op jit(solution)/shard_map/pallas_call | solution.py:205
  129.9 5.8 %shard_map.149 = (bf16[1280,256]{1,0:T(8,128)(2,1)S(1)}, bf16[1280,256]{1,0:T(8,128)(2,1)S(1)}, bf16[2,1280,256]{2,1,0:T(8,128)(2,1)S(1)}) custom-call(s32[1]{0:T(128)} %bitcast.c_ref, bf16[4,256,1024]{2,1,0:T(8,128)(2,1)S(1)} %shard_map.148.g_ref, bf16[1280,512]{1,0:T(8,128)(2,1)} %shard_map.138.refs_0_, bf16[1280,512]{1,0:T(8,128)(2,1)} %collective-permute-done.10.refs_1_), custom_call_target="tpu_custom_call" | custom-call | flops 1 | bytes 1 | tf_op jit(solution)/shard_map/pallas_call | solution.py:242
  137.9 5.6 %shard_map.151 = (bf16[4,128,640]{2,1,0:T(8,128)(2,1)S(1)}, bf16[4,128,640]{2,1,0:T(8,128)(2,1)S(1)}, bf16[2,4,128,640]{3,2,1,0:T(8,128)(2,1)S(1)}) custom-call(s32[1]{0:T(128)} %bitcast.c_ref, bf16[2816,512]{1,0:T(8,128)(2,1)S(1)} %copy-done, bf16[2816,512]{1,0:T(8,128)(2,1)} %collective-permute-done.refs_1_, bf16[4,256,512]{2,1,0:T(8,128)(2,1)S(1)} %copy-done.17, ...), custom_call_target="tpu_custom_call" | custom-call | flops 1 | bytes 1 | tf_op jit(solution)/shard_map/pallas_call | solution.py:166
  152.5 10.5 %collective-permute-done.22.refs_3_ = bf16[2,4,2,80,256]{4,3,2,1,0:T(8,128)(2,1)S(1)} collective-permute-done((bf16[2,4,2,80,256]{4,3,2,1,0:T(8,128)(2,1)S(1)}, bf16[2,4,2,80,256]{4,3,2,1,0:T(8,128)(2,1)S(1)}, u32[]{:S(2)}, u32[]{:S(2)}) %collective-permute-start.22) | collective-permute-done | bytes 655392 | tf_op jit(solution)/shard_map/ppermute | solution.py:516
  169.6 6.5 %collective-permute-done.26.refs_3_ = bf16[2,4,1,64,640]{4,3,2,1,0:T(8,128)(2,1)S(1)} collective-permute-done((bf16[2,4,1,64,640]{4,3,2,1,0:T(8,128)(2,1)S(1)}, bf16[2,4,1,64,640]{4,3,2,1,0:T(8,128)(2,1)S(1)}, u32[]{:S(2)}, u32[]{:S(2)}) %collective-permute-start.26) | collective-permute-done | bytes 655392 | tf_op jit(solution)/shard_map/ppermute | solution.py:516
  185.8 6.0 %collective-permute-done.23.refs_5_ = bf16[2,1,2,80,384]{4,3,2,1,0:T(8,128)(2,1)S(1)} collective-permute-done((bf16[2,1,2,80,384]{4,3,2,1,0:T(8,128)(2,1)S(1)}, bf16[2,1,2,80,384]{4,3,2,1,0:T(8,128)(2,1)S(1)}, u32[]{:S(2)}, u32[]{:S(2)}) %collective-permute-start.23) | collective-permute-done | bytes 245792 | tf_op jit(solution)/shard_map/ppermute | solution.py:510
  223.2 6.2 %shard_map.169 = (f32[160,5120]{1,0:T(8,128)}, f32[160,5120]{1,0:T(8,128)}, f32[160,5120]{1,0:T(8,128)S(1)}, f32[16,128]{1,0:T(8,128)S(1)}) custom-call(s32[1]{0:T(128)} %bitcast.c_ref, f32[160,5120]{1,0:T(8,128)S(1)} %copy-done.9, f32[160,5120]{1,0:T(8,128)S(1)} %copy-done.25, f32[160,5120]{1,0:T(8,128)S(1)} %copy-done.26, ...), custom_call_target="tpu_custom_call" | custom-call | flops 1 | bytes 1 | tf_op jit(solution)/shard_map/pallas_call | solution.py:451
  231.7 5.4 %shard_map.171 = (f32[640,1280]{1,0:T(8,128)}, f32[640,1280]{1,0:T(8,128)}, f32[640,1280]{1,0:T(8,128)S(1)}, f32[32,128]{1,0:T(8,128)S(1)}) custom-call(s32[1]{0:T(128)} %bitcast.c_ref, f32[640,1280]{1,0:T(8,128)S(1)} %copy-done.4, f32[640,1280]{1,0:T(8,128)S(1)} %copy-done.27, f32[640,1280]{1,0:T(8,128)S(1)} %copy-done.28, ...), custom_call_target="tpu_custom_call" | custom-call | flops 1 | bytes 1 | tf_op jit(solution)/shard_map/pallas_call | solution.py:451
  237.1 2.7 %collective-permute-start.42 = (f32[32,128]{1,0:T(8,128)S(1)}, f32[32,128]{1,0:T(8,128)S(1)}, u32[]{:S(2)}, u32[]{:S(2)}) collective-permute-start(f32[32,128]{1,0:T(8,128)S(1)} %get-tuple-element.345.refs_0_), channel_id=1, source_target_pairs={{0,24},{4,28},{8,16},{12,20},{16,8},{20,12},{24,0},{28,4},{1,25},{... | collective-permute-start | bytes 49160 | tf_op jit(solution)/shard_map/ppermute | solution.py:510
  245.6 2.7 %collective-permute-done.43.refs_1_ = f32[32,128]{1,0:T(8,128)S(1)} collective-permute-done((f32[32,128]{1,0:T(8,128)S(1)}, f32[32,128]{1,0:T(8,128)S(1)}, u32[]{:S(2)}, u32[]{:S(2)}) %collective-permute-start.43) | collective-permute-done | bytes 16416 | tf_op jit(solution)/shard_map/ppermute | solution.py:506
  248.3 3.2 %shard_map.173 = f32[160,5120]{1,0:T(8,128)} custom-call(f32[160,5120]{1,0:T(8,128)S(1)} %copy-done.9, f32[160,5120]{1,0:T(8,128)S(1)} %get-tuple-element.350.u_ref, f32[32,128]{1,0:T(8,128)S(1)} %shard_map.172.refs_0_, f32[32,128]{1,0:T(8,128)S(1)} %collective-permute-done.43.refs_1_), custom_call_target="tpu_custom_call" | custom-call | flops 1 | bytes 1 | tf_op jit(solution)/shard_map/pallas_call | solution.py:478
  251.6 3.2 %shard_map.174 = f32[640,1280]{1,0:T(8,128)} custom-call(f32[640,1280]{1,0:T(8,128)S(1)} %copy-done.4, f32[640,1280]{1,0:T(8,128)S(1)} %get-tuple-element.357.u_ref, f32[32,128]{1,0:T(8,128)S(1)} %shard_map.172.refs_0_, f32[32,128]{1,0:T(8,128)S(1)} %collective-permute-done.43.refs_1_), custom_call_target="tpu_custom_call" | custom-call | flops 1 | bytes 1 | tf_op jit(solution)/shard_map/pallas_call | solution.py:478
  (193 shorter events, 95.6 us)
Async XLA Ops:
  5.8 66.6 %collective-permute-start = (bf16[2816,512]{1,0:T(8,128)(2,1)}, bf16[2816,512]{1,0:T(8,128)(2,1)}, u32[]{:S(2)}, u32[]{:S(2)}) collective-permute-start(bf16[2816,512]{1,0:T(8,128)(2,1)} %shard_map.136), channel_id=1, source_target_pairs={{0,4},{4,0},{8,12},{12,8},{16,20},{20,16},{24,28},{28,24},{1,5},{5... | collective-permute-start | bytes 8650760 | tf_op jit(solution)/shard_map/ppermute | solution.py:506
  11.0 37.4 %collective-permute-start.1 = (bf16[320,1280]{1,0:T(8,128)(2,1)}, bf16[320,1280]{1,0:T(8,128)(2,1)}, u32[]{:S(2)}, u32[]{:S(2)}) collective-permute-start(bf16[320,1280]{1,0:T(8,128)(2,1)} %shard_map.137.refs_2_.refs_4_), channel_id=1, source_target_pairs={{0,8},{4,12},{8,0},{12,4},{16,24},{20,28},{24,16},{28,20},{1,9},{5... | collective-permute-start | bytes 2457608 | tf_op jit(solution)/shard_map/ppermute | solution.py:510
  12.6 38.3 %collective-permute-start.2 = (bf16[320,1280]{1,0:T(8,128)(2,1)}, bf16[320,1280]{1,0:T(8,128)(2,1)}, u32[]{:S(2)}, u32[]{:S(2)}) collective-permute-start(bf16[320,1280]{1,0:T(8,128)(2,1)} %shard_map.137.refs_2_.refs_4_), channel_id=1, source_target_pairs={{0,16},{4,20},{8,24},{12,28},{16,0},{20,4},{24,8},{28,12},{1,17},{... | collective-permute-start | bytes 2457608 | tf_op jit(solution)/shard_map/ppermute | solution.py:510
  50.8 31.5 %collective-permute-start.3 = (bf16[320,1280]{1,0:T(8,128)(2,1)}, bf16[320,1280]{1,0:T(8,128)(2,1)}, u32[]{:S(2)}, u32[]{:S(2)}) collective-permute-start(bf16[320,1280]{1,0:T(8,128)(2,1)} %collective-permute-done.2.refs_4_.refs_6_), channel_id=1, source_target_pairs={{0,8},{4,12},{8,0},{12,4},{16,24},{20,28},{24,16},{28,20},{1,9},{5... | collective-permute-start | bytes 2457608 | tf_op jit(solution)/shard_map/ppermute | solution.py:510
  51.2 53.7 %collective-permute-start.10 = (bf16[1280,512]{1,0:T(8,128)(2,1)}, bf16[1280,512]{1,0:T(8,128)(2,1)}, u32[]{:S(2)}, u32[]{:S(2)}) collective-permute-start(bf16[1280,512]{1,0:T(8,128)(2,1)} %shard_map.138.refs_0_), channel_id=1, source_target_pairs={{0,4},{4,0},{8,12},{12,8},{16,20},{20,16},{24,28},{28,24},{1,5},{5... | collective-permute-start | bytes 3932168 | tf_op jit(solution)/shard_map/ppermute | solution.py:506
  82.3 12.4 %collective-permute-start.6 = (bf16[320,1280]{1,0:T(8,128)(2,1)}, bf16[320,1280]{1,0:T(8,128)(2,1)}, u32[]{:S(2)}, u32[]{:S(2)}) collective-permute-start(bf16[320,1280]{1,0:T(8,128)(2,1)} %collective-permute-done.2.refs_4_.refs_6_), channel_id=1, source_target_pairs={{0,1},{1,0},{2,3},{3,2},{4,5},{5,4},{6,7},{7,6},{8,9},{9,8},{10,11... | collective-permute-start | bytes 2457608 | tf_op jit(solution)/shard_map/ppermute | solution.py:520
  82.3 12.3 %collective-permute-start.7 = (bf16[320,1280]{1,0:T(8,128)(2,1)}, bf16[320,1280]{1,0:T(8,128)(2,1)}, u32[]{:S(2)}, u32[]{:S(2)}) collective-permute-start(bf16[320,1280]{1,0:T(8,128)(2,1)} %collective-permute-done.3.refs_5_.refs_7_), channel_id=1, source_target_pairs={{0,1},{1,0},{2,3},{3,2},{4,5},{5,4},{6,7},{7,6},{8,9},{9,8},{10,11... | collective-permute-start | bytes 2457608 | tf_op jit(solution)/shard_map/ppermute | solution.py:520
  90.9 24.2 %collective-permute-start.13 = (bf16[2,4,1,96,640]{4,3,2,1,0:T(8,128)(2,1)S(1)}, bf16[2,4,1,96,640]{4,3,2,1,0:T(8,128)(2,1)S(1)}, u32[]{:S(2)}, u32[]{:S(2)}) collective-permute-start(bf16[2,4,1,96,640]{4,3,2,1,0:T(8,128)(2,1)S(1)} %shard_map.143), channel_id=1, source_target_pairs={{0,2},{1,3},{2,0},{3,1},{4,6},{5,7},{6,4},{7,5},{8,10},{9,11},{10,... | collective-permute-start | bytes 2949128 | tf_op jit(solution)/shard_map/ppermute | solution.py:516
  93.1 28.9 %collective-permute-start.15 = (bf16[4,256,512]{2,1,0:T(8,128)(2,1)S(1)}, bf16[4,256,512]{2,1,0:T(8,128)(2,1)S(1)}, u32[]{:S(2)}, u32[]{:S(2)}) collective-permute-start(bf16[4,256,512]{2,1,0:T(8,128)(2,1)S(1)} %copy-done.42), channel_id=1, source_target_pairs={{0,4},{4,0},{8,12},{12,8},{16,20},{20,16},{24,28},{28,24},{1,5},{5... | collective-permute-start | bytes 3145736 | tf_op jit(solution)/shard_map/ppermute | solution.py:506
  117.0 19.2 %collective-permute-start.16 = (bf16[2,2,1,96,640]{4,3,2,1,0:T(8,128)(2,1)S(1)}, bf16[2,2,1,96,640]{4,3,2,1,0:T(8,128)(2,1)S(1)}, u32[]{:S(2)}, u32[]{:S(2)}) collective-permute-start(bf16[2,2,1,96,640]{4,3,2,1,0:T(8,128)(2,1)S(1)} %shard_map.146), channel_id=1, source_target_pairs={{0,8},{4,12},{8,0},{12,4},{16,24},{20,28},{24,16},{28,20},{1,9},{5... | collective-permute-start | bytes 1474568 | tf_op jit(solution)/shard_map/ppermute | solution.py:510
  120.3 29.4 %collective-permute-start.14 = (bf16[2,4,2,80,384]{4,3,2,1,0:T(8,128)(2,1)S(1)}, bf16[2,4,2,80,384]{4,3,2,1,0:T(8,128)(2,1)S(1)}, u32[]{:S(2)}, u32[]{:S(2)}) collective-permute-start(bf16[2,4,2,80,384]{4,3,2,1,0:T(8,128)(2,1)S(1)} %shard_map.147), channel_id=1, source_target_pairs={{0,2},{1,3},{2,0},{3,1},{4,6},{5,7},{6,4},{7,5},{8,10},{9,11},{10,... | collective-permute-start | bytes 2949128 | tf_op jit(solution)/shard_map/ppermute | solution.py:516
  145.3 17.6 %collective-permute-start.22 = (bf16[2,4,2,80,256]{4,3,2,1,0:T(8,128)(2,1)S(1)}, bf16[2,4,2,80,256]{4,3,2,1,0:T(8,128)(2,1)S(1)}, u32[]{:S(2)}, u32[]{:S(2)}) collective-permute-start(bf16[2,4,2,80,256]{4,3,2,1,0:T(8,128)(2,1)S(1)} %shard_map.152), channel_id=1, source_target_pairs={{0,2},{1,3},{2,0},{3,1},{4,6},{5,7},{6,4},{7,5},{8,10},{9,11},{10,... | collective-permute-start | bytes 1966088 | tf_op jit(solution)/shard_map/ppermute | solution.py:516
  148.3 27.8 %collective-permute-start.26 = (bf16[2,4,1,64,640]{4,3,2,1,0:T(8,128)(2,1)S(1)}, bf16[2,4,1,64,640]{4,3,2,1,0:T(8,128)(2,1)S(1)}, u32[]{:S(2)}, u32[]{:S(2)}) collective-permute-start(bf16[2,4,1,64,640]{4,3,2,1,0:T(8,128)(2,1)S(1)} %shard_map.153), channel_id=1, source_target_pairs={{0,2},{1,3},{2,0},{3,1},{4,6},{5,7},{6,4},{7,5},{8,10},{9,11},{10,... | collective-permute-start | bytes 1966088 | tf_op jit(solution)/shard_map/ppermute | solution.py:516
  150.8 17.6 %collective-permute-start.21 = (bf16[2,2,2,80,384]{4,3,2,1,0:T(8,128)(2,1)S(1)}, bf16[2,2,2,80,384]{4,3,2,1,0:T(8,128)(2,1)S(1)}, u32[]{:S(2)}, u32[]{:S(2)}) collective-permute-start(bf16[2,2,2,80,384]{4,3,2,1,0:T(8,128)(2,1)S(1)} %shard_map.154), channel_id=1, source_target_pairs={{0,8},{4,12},{8,0},{12,4},{16,24},{20,28},{24,16},{28,20},{1,9},{5... | collective-permute-start | bytes 1474568 | tf_op jit(solution)/shard_map/ppermute | solution.py:510
  163.9 15.6 %collective-permute-start.25 = (bf16[2,2,2,80,256]{4,3,2,1,0:T(8,128)(2,1)S(1)}, bf16[2,2,2,80,256]{4,3,2,1,0:T(8,128)(2,1)S(1)}, u32[]{:S(2)}, u32[]{:S(2)}) collective-permute-start(bf16[2,2,2,80,256]{4,3,2,1,0:T(8,128)(2,1)S(1)} %shard_map.155), channel_id=1, source_target_pairs={{0,8},{4,12},{8,0},{12,4},{16,24},{20,28},{24,16},{28,20},{1,9},{5... | collective-permute-start | bytes 983048 | tf_op jit(solution)/shard_map/ppermute | solution.py:510
  165.8 18.3 %collective-permute-start.24 = (bf16[2,1,1,96,640]{4,3,2,1,0:T(8,128)(2,1)S(1)}, bf16[2,1,1,96,640]{4,3,2,1,0:T(8,128)(2,1)S(1)}, u32[]{:S(2)}, u32[]{:S(2)}) collective-permute-start(bf16[2,1,1,96,640]{4,3,2,1,0:T(8,128)(2,1)S(1)} %shard_map.150), channel_id=1, source_target_pairs={{0,16},{4,20},{8,24},{12,28},{16,0},{20,4},{24,8},{28,12},{1,17},{... | collective-permute-start | bytes 737288 | tf_op jit(solution)/shard_map/ppermute | solution.py:510
  169.2 22.7 %collective-permute-start.23 = (bf16[2,1,2,80,384]{4,3,2,1,0:T(8,128)(2,1)S(1)}, bf16[2,1,2,80,384]{4,3,2,1,0:T(8,128)(2,1)S(1)}, u32[]{:S(2)}, u32[]{:S(2)}) collective-permute-start(bf16[2,1,2,80,384]{4,3,2,1,0:T(8,128)(2,1)S(1)} %shard_map.156), channel_id=1, source_target_pairs={{0,16},{4,20},{8,24},{12,28},{16,0},{20,4},{24,8},{28,12},{1,17},{... | collective-permute-start | bytes 737288 | tf_op jit(solution)/shard_map/ppermute | solution.py:510
  177.7 19.4 %collective-permute-start.29 = (bf16[2,2,1,64,640]{4,3,2,1,0:T(8,128)(2,1)}, bf16[2,2,1,64,640]{4,3,2,1,0:T(8,128)(2,1)}, u32[]{:S(2)}, u32[]{:S(2)}) collective-permute-start(bf16[2,2,1,64,640]{4,3,2,1,0:T(8,128)(2,1)} %shard_map.157), channel_id=1, source_target_pairs={{0,8},{4,12},{8,0},{12,4},{16,24},{20,28},{24,16},{28,20},{1,9},{5... | collective-permute-start | bytes 983048 | tf_op jit(solution)/shard_map/ppermute | solution.py:510
  180.8 20.2 %collective-permute-start.28 = (bf16[2,1,2,80,256]{4,3,2,1,0:T(8,128)(2,1)}, bf16[2,1,2,80,256]{4,3,2,1,0:T(8,128)(2,1)}, u32[]{:S(2)}, u32[]{:S(2)}) collective-permute-start(bf16[2,1,2,80,256]{4,3,2,1,0:T(8,128)(2,1)} %shard_map.158), channel_id=1, source_target_pairs={{0,16},{4,20},{8,24},{12,28},{16,0},{20,4},{24,8},{28,12},{1,17},{... | collective-permute-start | bytes 491528 | tf_op jit(solution)/shard_map/ppermute | solution.py:510
  195.6 17.0 %collective-permute-start.31 = (bf16[2,96,640]{2,1,0:T(8,128)(2,1)S(1)}, bf16[2,96,640]{2,1,0:T(8,128)(2,1)}, u32[]{:S(2)}, u32[]{:S(2)}) collective-permute-start(bf16[2,96,640]{2,1,0:T(8,128)(2,1)S(1)} %shard_map.159.refs_0_), channel_id=1, source_target_pairs={{0,2},{1,3},{2,0},{3,1},{4,6},{5,7},{6,4},{7,5},{8,10},{9,11},{10,... | collective-permute-start | bytes 737288 | tf_op jit(solution)/shard_map/ppermute | solution.py:516
  204.3 9.8 %collective-permute-start.30 = (bf16[2,2,80,384]{3,2,1,0:T(8,128)(2,1)S(1)}, bf16[2,2,80,384]{3,2,1,0:T(8,128)(2,1)S(1)}, u32[]{:S(2)}, u32[]{:S(2)}) collective-permute-start(bf16[2,2,80,384]{3,2,1,0:T(8,128)(2,1)S(1)} %shard_map.163.refs_0_), channel_id=1, source_target_pairs={{0,2},{1,3},{2,0},{3,1},{4,6},{5,7},{6,4},{7,5},{8,10},{9,11},{10,... | collective-permute-start | bytes 737288 | tf_op jit(solution)/shard_map/ppermute | solution.py:516
  205.5 9.3 %collective-permute-start.34 = (bf16[2,1,1,64,640]{4,3,2,1,0:T(8,128)(2,1)}, bf16[2,1,1,64,640]{4,3,2,1,0:T(8,128)(2,1)S(1)}, u32[]{:S(2)}, u32[]{:S(2)}) collective-permute-start(bf16[2,1,1,64,640]{4,3,2,1,0:T(8,128)(2,1)} %copy-done.36), channel_id=1, source_target_pairs={{0,16},{4,20},{8,24},{12,28},{16,0},{20,4},{24,8},{28,12},{1,17},{... | collective-permute-start | bytes 491528 | tf_op jit(solution)/shard_map/ppermute | solution.py:510
  220.0 9.4 %collective-permute-start.37 = (bf16[2,64,640]{2,1,0:T(8,128)(2,1)S(1)}, bf16[2,64,640]{2,1,0:T(8,128)(2,1)S(1)}, u32[]{:S(2)}, u32[]{:S(2)}) collective-permute-start(bf16[2,64,640]{2,1,0:T(8,128)(2,1)S(1)} %shard_map.167.refs_0_), channel_id=1, source_target_pairs={{0,2},{1,3},{2,0},{3,1},{4,6},{5,7},{6,4},{7,5},{8,10},{9,11},{10,... | collective-permute-start | bytes 491528 | tf_op jit(solution)/shard_map/ppermute | solution.py:516
  220.6 9.9 %collective-permute-start.38 = (bf16[2,2,96,640]{3,2,1,0:T(8,128)(2,1)S(1)}, bf16[2,2,96,640]{3,2,1,0:T(8,128)(2,1)S(1)}, u32[]{:S(2)}, u32[]{:S(2)}) collective-permute-start(bf16[2,2,96,640]{3,2,1,0:T(8,128)(2,1)S(1)} %shard_map.165.refs_0_), channel_id=1, source_target_pairs={{0,1},{1,0},{2,3},{3,2},{4,5},{5,4},{6,7},{7,6},{8,9},{9,8},{10,11... | collective-permute-start | bytes 1474568 | tf_op jit(solution)/shard_map/ppermute | solution.py:520
  (63 other events, 566.7 us)

commit v11 on v10

--- a/solution.py
+++ b/solution.py
@@ -146,16 +146,22 @@
     half = model // CORES
     high = width // parts
     count = len(tokens.arrays)
+    long = tokens.arrays[0].shape[1]
 
     def body(c_ref, *refs):
-        ins, outs = refs[:count], refs[count:]
+        ins, outs, right_ref = refs[:count], refs[count:-1], refs[-1]
+
+        @pl.when(pl.program_id(0) == 0)
+        def _():
+            for n in range(tokens.count):
+                right_ref[:, n * long : (n + 1) * long] = tokens.cot(ins, n)[...]
+
         acts = jnp.concatenate(
             [gelu(tokens.hidden(ins, n)).astype(BF16) for n in range(tokens.count)], axis=1
         )
         for which in range(2):
             cols = pl.ds(pl.multiple_of((c_ref[0] + 1 + which) % CORES * half, 16), half)
-            right = jnp.concatenate([tokens.cot(ins, n)[cols, :] for n in range(tokens.count)], axis=1)
-            total = (dot(acts, right, ((1,), (1,))) * scale).astype(BF16)
+            total = (dot(acts, right_ref[cols, :], ((1,), (1,))) * scale).astype(BF16)
             for p in range(parts):
                 value = total[p * high : (p + 1) * high]
                 if which:
@@ -171,6 +177,7 @@
             in_specs=tokens.specs,
             out_specs=[pl.BlockSpec((1, high, half), lambda z, c: (z, 0, 0))] * parts
             + [pl.BlockSpec((parts, 1, high, half), lambda z, c: (0, z, 0, 0))],
+            scratch_shapes=[pltpu.VMEM((model, tokens.count * long), BF16)],
         ),
         out_shape=[jax.ShapeDtypeStruct((nz, high, half), BF16)] * parts
         + [jax.ShapeDtypeStruct((parts, nz, high, half), BF16)],
@@ -224,10 +231,15 @@
     high = model // cut
 
     def body(c_ref, g_ref, *refs):
-        in_refs, outs = refs[:count], refs[count:]
-        left = jnp.concatenate([i[...] for i in in_refs], axis=1)
-        total = (dot(left, g_ref[0], ((1,), (1,))) * scale).astype(BF16)
+        in_refs, outs, left_ref = refs[:count], refs[count:-1], refs[-1]
         step = pl.program_id(0)
+
+        @pl.when(step == 0)
+        def _():
+            for n, in_ref in enumerate(in_refs):
+                left_ref[:, n * tokens : (n + 1) * tokens] = in_ref[...]
+
+        total = (dot(left_ref[...], g_ref[0], ((1,), (1,))) * scale).astype(BF16)
         for n in range(half):
 
             @pl.when(step == n)
@@ -253,6 +265,7 @@
             + [pl.BlockSpec((model, tokens), lambda z, c: (0, 0))] * count,
             out_specs=[pl.BlockSpec((high, width), lambda z, c: (0, 0))] * (half * cut)
             + [pl.BlockSpec((1, model, width), lambda z, c: (jnp.maximum(z - half, 0), 0, 0))],
+            scratch_shapes=[pltpu.VMEM((model, count * tokens), BF16)],
         ),
         out_shape=[jax.ShapeDtypeStruct((high, width), BF16)] * (half * cut)
         + [jax.ShapeDtypeStruct((half, model, width), BF16)],
@@ -714,16 +727,16 @@
             outs[1].send_y()
             ins[0].send_z()
             ins[1].send_z()
+            outs[0].finish()
             ins[0].send_z()
             outs[1].send_z()
             ins[1].send_z()
-            outs[0].finish()
             ins[0].finish()
+            outs[0].stack_y(True)
             outs[1].send_z()
             ins[1].finish()
+            ins[1].stack_x()
             ins[0].stack_x()
-            ins[1].stack_x()
-            outs[0].stack_y(True)
             ins[0].stack_y()
             outs[1].finish()
             ins[1].stack_y()

time: 256 us -> 258 us (level)
  waiting for transfers between devices: 77.7 us -> 70.8 us
  local copies, waits for them, and re-layouts: 10.8 us -> 15.8 us
  starting transfers between devices: 47.3 us -> 49.9 us
    unnamed x86 -> x102, local copies, waits for them, and re-layouts: 10.8 us -> 15.8 us
    ppermute x8, waiting for transfers between devices: 17.7 us -> 13.1 us  [along_y(): return lax.ppermute(value, 'gy', pairs)]
    ppermute x14, waiting for transfers between devices: 29.3 us -> 26.6 us  [along_z(): return lax.ppermute(value, 'gx', pairs)]
  transfers between devices with their start and end apart: 44 -> 44, of which waited for: 18 -> 19; matrix products, arithmetic and copies ran while one was open for 0% -> 0% of each run, Pallas kernels for 39% -> 39%
where the time goes in v11:
time: 258 us; the launch traced here: 257 us
  Pallas kernels  119 us (46%)
  waiting for transfers between devices  70.8 us (27%)
  starting transfers between devices  49.9 us (19%)
  local copies, waits for them, and re-layouts  15.8 us (6%)
    ppermute x14, waiting for transfers between devices, along_z(): return lax.ppermute(value, 'gx', pairs)  26.6 us
    ppermute x6, waiting for transfers between devices, along_x(): return lax.ppermute(value, 'gx', pairs)  26.4 us
    pallas_call x16, Pallas kernels, reduce_step(): pl.pallas_call(body, grid_spec=pltpu.PrefetchScalarGridSpec(num_scalar_pr...  26.3 us
    ppermute x14, starting transfers between devices, along_z(): return lax.ppermute(value, 'gx', pairs)  24.7 us
    pallas_call x2, Pallas kernels, grad_pre_chunk(): pl.pallas_call(body, grid_spec=pltpu.PrefetchScalarGridSpec(num_scalar_pr...  18.1 us
    unnamed x102, local copies, waits for them, and re-layouts  15.8 us
    pallas_call x2, Pallas kernels, grad_in_chunk(): pl.pallas_call(body, grid_spec=pltpu.PrefetchScalarGridSpec(num_scalar_pr...  15.1 us
    pallas_call x2, Pallas kernels, grad_out_chunk(): pl.pallas_call(body, grid_spec=pltpu.PrefetchScalarGridSpec(num_scalar_pr...  14.3 us
  transfers between devices with their start and end apart: 44, of which 19 were waited for; matrix products, arithmetic and copies ran while one was open for 0% of the time, Pallas kernels for 39%

profile of v11, /device:TPU:0, one launch (start us, length us, event | category | flops | bytes accessed | tf_op | source)
XLA Modules:
  0.0 257.2 jit_solution(5851997645870856295)
XLA Ops:
  0.7 5.2 %shard_map.136 = bf16[2816,512]{1,0:T(8,128)(2,1)} custom-call(s32[1]{0:T(128)} %bitcast.8.at_ref, bf16[512,5120]{1,0:T(8,128)(2,1)} %h_ref.4, bf16[512,1280]{1,0:T(8,128)(2,1)} %cot_ref.2), custom_call_target="tpu_custom_call" | custom-call | flops 1 | bytes 1 | tf_op jit(solution)/shard_map/pallas_call | solution.py:81
  5.8 2.9 %collective-permute-start = (bf16[2816,512]{1,0:T(8,128)(2,1)}, bf16[2816,512]{1,0:T(8,128)(2,1)}, u32[]{:S(2)}, u32[]{:S(2)}) collective-permute-start(bf16[2816,512]{1,0:T(8,128)(2,1)} %shard_map.136), channel_id=1, source_target_pairs={{0,4},{4,0},{8,12},{12,8},{16,20},{20,16},{24,28},{28,24},{1,5},{5... | collective-permute-start | bytes 8650760 | tf_op jit(solution)/shard_map/ppermute | solution.py:519
  17.7 5.1 %shard_map.139.refs_0_ = bf16[2816,512]{1,0:T(8,128)(2,1)} custom-call(s32[1]{0:T(128)} %bitcast.5.at_ref, bf16[512,5120]{1,0:T(8,128)(2,1)} %h_ref.4, bf16[512,1280]{1,0:T(8,128)(2,1)} %cot_ref.2), custom_call_target="tpu_custom_call" | custom-call | flops 1 | bytes 1 | tf_op jit(solution)/shard_map/pallas_call | solution.py:81
  22.8 3.9 %shard_map.140.refs_2_ = bf16[4,256,512]{2,1,0:T(8,128)(2,1)} custom-call(s32[1]{0:T(128)} %bitcast.3.at_ref, bf16[512,5120]{1,0:T(8,128)(2,1)} %h_ref.4), custom_call_target="tpu_custom_call" | custom-call | flops 1 | bytes 1 | tf_op jit(solution)/shard_map/pallas_call | solution.py:109
  26.7 4.0 %shard_map.141 = bf16[4,256,512]{2,1,0:T(8,128)(2,1)} custom-call(s32[1]{0:T(128)} %bitcast.8.at_ref, bf16[512,5120]{1,0:T(8,128)(2,1)} %h_ref.4), custom_call_target="tpu_custom_call" | custom-call | flops 1 | bytes 1 | tf_op jit(solution)/shard_map/pallas_call | solution.py:109
  30.7 17.7 %collective-permute-done.1.refs_3_.refs_5_ = bf16[320,1280]{1,0:T(8,128)(2,1)} collective-permute-done((bf16[320,1280]{1,0:T(8,128)(2,1)}, bf16[320,1280]{1,0:T(8,128)(2,1)}, u32[]{:S(2)}, u32[]{:S(2)}) %collective-permute-start.1) | collective-permute-done | bytes 819232 | tf_op jit(solution)/shard_map/ppermute | solution.py:523
  52.1 20.2 %collective-permute-done.refs_1_ = bf16[2816,512]{1,0:T(8,128)(2,1)} collective-permute-done((bf16[2816,512]{1,0:T(8,128)(2,1)}, bf16[2816,512]{1,0:T(8,128)(2,1)}, u32[]{:S(2)}, u32[]{:S(2)}) %collective-permute-start) | collective-permute-done | bytes 2883616 | tf_op jit(solution)/shard_map/ppermute | solution.py:519
  72.4 8.3 %shard_map.142 = (bf16[4,192,640]{2,1,0:T(8,128)(2,1)}, bf16[4,192,640]{2,1,0:T(8,128)(2,1)}, bf16[2,4,192,640]{3,2,1,0:T(8,128)(2,1)S(1)}) custom-call(s32[1]{0:T(128)} %bitcast.c_ref, bf16[2816,512]{1,0:T(8,128)(2,1)S(1)} %copy-done, bf16[2816,512]{1,0:T(8,128)(2,1)} %collective-permute-done.refs_1_), custom_call_target="tpu_custom_call" | custom-call | flops 1 | bytes 1 | tf_op jit(solution)/shard_map/pallas_call | solution.py:172
  87.8 3.2 %shard_map.143 = bf16[2,4,1,96,640]{4,3,2,1,0:T(8,128)(2,1)S(1)} custom-call(s32[3]{0:T(128)S(1)} %pad_add_fusion.2.at_ref, bf16[2,4,1,2,96,640]{5,4,3,2,1,0:T(8,128)(2,1)S(1)} %bitcast.21, bf16[4,1,2,96,640]{4,3,2,1,0:T(8,128)(2,1)} %bitcast.10.refs_1_, bf16[4,1,2,96,640]{4,3,2,1,0:T(8,128)(2,1)} %bitcast.11.refs_2_), custom_call_target="tpu_custom_call" | custom-call | flops 1 | bytes 1 | tf_op jit(solution)/shard_map/pallas_call | solution.py:414
  94.8 10.3 %shard_map.144.g_ref = bf16[4,384,1024]{2,1,0:T(8,128)(2,1)S(1)} custom-call(s32[2]{0:T(128)S(1)} %pad_add_fusion.3.c_ref, bf16[2816,512]{1,0:T(8,128)(2,1)S(1)} %copy-done, bf16[2816,512]{1,0:T(8,128)(2,1)} %collective-permute-done.refs_1_, bf16[320,1280]{1,0:T(8,128)(2,1)S(1)} %copy-done.29, bf16[320,1280]{1,0:T(8,128)(2,1)} %collective-permute-done.1.refs_3_.refs_5_, ...), custom_call_target="tpu_custom_call" | custom-call | flops 1 | bytes 1 | tf_op jit(solution)/shard_map/pallas_call | solution.py:212
  105.1 9.1 %shard_map.145 = (bf16[1280,384]{1,0:T(8,128)(2,1)S(1)}, bf16[1280,384]{1,0:T(8,128)(2,1)S(1)}, bf16[2,1280,384]{2,1,0:T(8,128)(2,1)S(1)}) custom-call(s32[1]{0:T(128)} %bitcast.c_ref, bf16[4,384,1024]{2,1,0:T(8,128)(2,1)S(1)} %shard_map.144.g_ref, bf16[1280,512]{1,0:T(8,128)(2,1)} %shard_map.138.refs_0_, bf16[1280,512]{1,0:T(8,128)(2,1)} %collective-permute-done.10.refs_1_), custom_call_target="tpu_custom_call" | custom-call | flops 1 | bytes 1 | tf_op jit(solution)/shard_map/pallas_call | solution.py:254
  122.0 7.9 %shard_map.148.g_ref = bf16[4,256,1024]{2,1,0:T(8,128)(2,1)S(1)} custom-call(s32[2]{0:T(128)S(1)} %pad_add_fusion.3.c_ref, bf16[2816,512]{1,0:T(8,128)(2,1)S(1)} %copy-done, bf16[2816,512]{1,0:T(8,128)(2,1)} %collective-permute-done.refs_1_, bf16[4,256,512]{2,1,0:T(8,128)(2,1)S(1)} %copy-done.25, bf16[4,256,512]{2,1,0:T(8,128)(2,1)S(1)} %collective-permute-done.15.refs_3_, ...), custom_call_target="tpu_custom_call" | custom-call | flops 1 | bytes 1 | tf_op jit(solution)/shard_map/pallas_call | solution.py:212
  129.9 6.0 %shard_map.149 = (bf16[1280,256]{1,0:T(8,128)(2,1)S(1)}, bf16[1280,256]{1,0:T(8,128)(2,1)S(1)}, bf16[2,1280,256]{2,1,0:T(8,128)(2,1)S(1)}) custom-call(s32[1]{0:T(128)} %bitcast.c_ref, bf16[4,256,1024]{2,1,0:T(8,128)(2,1)S(1)} %shard_map.148.g_ref, bf16[1280,512]{1,0:T(8,128)(2,1)} %shard_map.138.refs_0_, bf16[1280,512]{1,0:T(8,128)(2,1)} %collective-permute-done.10.refs_1_), custom_call_target="tpu_custom_call" | custom-call | flops 1 | bytes 1 | tf_op jit(solution)/shard_map/pallas_call | solution.py:254
  138.1 6.0 %shard_map.151 = (bf16[4,128,640]{2,1,0:T(8,128)(2,1)S(1)}, bf16[4,128,640]{2,1,0:T(8,128)(2,1)S(1)}, bf16[2,4,128,640]{3,2,1,0:T(8,128)(2,1)S(1)}) custom-call(s32[1]{0:T(128)} %bitcast.c_ref, bf16[2816,512]{1,0:T(8,128)(2,1)S(1)} %copy-done, bf16[2816,512]{1,0:T(8,128)(2,1)} %collective-permute-done.refs_1_, bf16[4,256,512]{2,1,0:T(8,128)(2,1)S(1)} %copy-done.25, ...), custom_call_target="tpu_custom_call" | custom-call | flops 1 | bytes 1 | tf_op jit(solution)/shard_map/pallas_call | solution.py:172
  155.5 8.1 %collective-permute-done.23.refs_3_ = bf16[2,4,2,80,256]{4,3,2,1,0:T(8,128)(2,1)S(1)} collective-permute-done((bf16[2,4,2,80,256]{4,3,2,1,0:T(8,128)(2,1)S(1)}, bf16[2,4,2,80,256]{4,3,2,1,0:T(8,128)(2,1)S(1)}, u32[]{:S(2)}, u32[]{:S(2)}) %collective-permute-start.23) | collective-permute-done | bytes 655392 | tf_op jit(solution)/shard_map/ppermute | solution.py:529
  166.4 3.4 %collective-permute-done.22.refs_5_ = bf16[2,1,1,96,640]{4,3,2,1,0:T(8,128)(2,1)S(1)} collective-permute-done((bf16[2,1,1,96,640]{4,3,2,1,0:T(8,128)(2,1)S(1)}, bf16[2,1,1,96,640]{4,3,2,1,0:T(8,128)(2,1)S(1)}, u32[]{:S(2)}, u32[]{:S(2)}) %collective-permute-start.22) | collective-permute-done | bytes 245792 | tf_op jit(solution)/shard_map/ppermute | solution.py:523
  173.1 3.4 %collective-permute-start.24 = (bf16[2,1,2,80,384]{4,3,2,1,0:T(8,128)(2,1)}, bf16[2,1,2,80,384]{4,3,2,1,0:T(8,128)(2,1)}, u32[]{:S(2)}, u32[]{:S(2)}) collective-permute-start(bf16[2,1,2,80,384]{4,3,2,1,0:T(8,128)(2,1)} %shard_map.157), channel_id=1, source_target_pairs={{0,16},{4,20},{8,24},{12,28},{16,0},{20,4},{24,8},{28,12},{1,17},{... | collective-permute-start | bytes 737288 | tf_op jit(solution)/shard_map/ppermute | solution.py:523
  209.6 3.8 %collective-permute-done.31.refs_1_ = bf16[2,80,256]{2,1,0:T(8,128)(2,1)S(1)} collective-permute-done((bf16[2,80,256]{2,1,0:T(8,128)(2,1)S(1)}, bf16[2,80,256]{2,1,0:T(8,128)(2,1)S(1)}, u32[]{:S(2)}, u32[]{:S(2)}) %collective-permute-start.31) | collective-permute-done | bytes 81952 | tf_op jit(solution)/shard_map/ppermute | solution.py:519
  216.6 4.2 %collective-permute-done.32.refs_1_ = bf16[2,2,80,384]{3,2,1,0:T(8,128)(2,1)S(1)} collective-permute-done((bf16[2,2,80,384]{3,2,1,0:T(8,128)(2,1)S(1)}, bf16[2,2,80,384]{3,2,1,0:T(8,128)(2,1)S(1)}, u32[]{:S(2)}, u32[]{:S(2)}) %collective-permute-start.32) | collective-permute-done | bytes 245792 | tf_op jit(solution)/shard_map/ppermute | solution.py:529
  226.8 6.2 %shard_map.169 = (f32[160,5120]{1,0:T(8,128)}, f32[160,5120]{1,0:T(8,128)}, f32[160,5120]{1,0:T(8,128)S(1)}, f32[16,128]{1,0:T(8,128)S(1)}) custom-call(s32[1]{0:T(128)} %bitcast.c_ref, f32[160,5120]{1,0:T(8,128)S(1)} %copy-done.15, f32[160,5120]{1,0:T(8,128)S(1)} %copy-done.35, f32[160,5120]{1,0:T(8,128)S(1)} %copy-done.36, ...), custom_call_target="tpu_custom_call" | custom-call | flops 1 | bytes 1 | tf_op jit(solution)/shard_map/pallas_call | solution.py:464
  235.3 5.4 %shard_map.171 = (f32[640,1280]{1,0:T(8,128)}, f32[640,1280]{1,0:T(8,128)}, f32[640,1280]{1,0:T(8,128)S(1)}, f32[32,128]{1,0:T(8,128)S(1)}) custom-call(s32[1]{0:T(128)} %bitcast.c_ref, f32[640,1280]{1,0:T(8,128)S(1)} %copy-done.6, f32[640,1280]{1,0:T(8,128)S(1)} %copy-done.37, f32[640,1280]{1,0:T(8,128)S(1)} %copy-done.38, ...), custom_call_target="tpu_custom_call" | custom-call | flops 1 | bytes 1 | tf_op jit(solution)/shard_map/pallas_call | solution.py:464
  242.2 2.9 %collective-permute-start.40 = (f32[32,128]{1,0:T(8,128)S(1)}, f32[32,128]{1,0:T(8,128)S(1)}, u32[]{:S(2)}, u32[]{:S(2)}) collective-permute-start(f32[32,128]{1,0:T(8,128)S(1)} %get-tuple-element.345.refs_0_), channel_id=1, source_target_pairs={{0,8},{4,12},{8,0},{12,4},{16,24},{20,28},{24,16},{28,20},{1,9},{5... | collective-permute-start | bytes 49160 | tf_op jit(solution)/shard_map/ppermute | solution.py:523
  250.7 3.2 %shard_map.173 = f32[160,5120]{1,0:T(8,128)} custom-call(f32[160,5120]{1,0:T(8,128)S(1)} %copy-done.15, f32[160,5120]{1,0:T(8,128)S(1)} %get-tuple-element.350.u_ref, f32[32,128]{1,0:T(8,128)S(1)} %shard_map.172.refs_0_, f32[32,128]{1,0:T(8,128)S(1)} %collective-permute-done.43.refs_1_), custom_call_target="tpu_custom_call" | custom-call | flops 1 | bytes 1 | tf_op jit(solution)/shard_map/pallas_call | solution.py:491
  254.0 3.2 %shard_map.174 = f32[640,1280]{1,0:T(8,128)} custom-call(f32[640,1280]{1,0:T(8,128)S(1)} %copy-done.6, f32[640,1280]{1,0:T(8,128)S(1)} %get-tuple-element.357.u_ref, f32[32,128]{1,0:T(8,128)S(1)} %shard_map.172.refs_0_, f32[32,128]{1,0:T(8,128)S(1)} %collective-permute-done.43.refs_1_), custom_call_target="tpu_custom_call" | custom-call | flops 1 | bytes 1 | tf_op jit(solution)/shard_map/pallas_call | solution.py:491
  (209 shorter events, 102.4 us)
Async XLA Ops:
  5.8 66.6 %collective-permute-start = (bf16[2816,512]{1,0:T(8,128)(2,1)}, bf16[2816,512]{1,0:T(8,128)(2,1)}, u32[]{:S(2)}, u32[]{:S(2)}) collective-permute-start(bf16[2816,512]{1,0:T(8,128)(2,1)} %shard_map.136), channel_id=1, source_target_pairs={{0,4},{4,0},{8,12},{12,8},{16,20},{20,16},{24,28},{28,24},{1,5},{5... | collective-permute-start | bytes 8650760 | tf_op jit(solution)/shard_map/ppermute | solution.py:519
  11.0 37.4 %collective-permute-start.1 = (bf16[320,1280]{1,0:T(8,128)(2,1)}, bf16[320,1280]{1,0:T(8,128)(2,1)}, u32[]{:S(2)}, u32[]{:S(2)}) collective-permute-start(bf16[320,1280]{1,0:T(8,128)(2,1)} %shard_map.137.refs_2_.refs_4_), channel_id=1, source_target_pairs={{0,8},{4,12},{8,0},{12,4},{16,24},{20,28},{24,16},{28,20},{1,9},{5... | collective-permute-start | bytes 2457608 | tf_op jit(solution)/shard_map/ppermute | solution.py:523
  12.6 38.3 %collective-permute-start.2 = (bf16[320,1280]{1,0:T(8,128)(2,1)}, bf16[320,1280]{1,0:T(8,128)(2,1)}, u32[]{:S(2)}, u32[]{:S(2)}) collective-permute-start(bf16[320,1280]{1,0:T(8,128)(2,1)} %shard_map.137.refs_2_.refs_4_), channel_id=1, source_target_pairs={{0,16},{4,20},{8,24},{12,28},{16,0},{20,4},{24,8},{28,12},{1,17},{... | collective-permute-start | bytes 2457608 | tf_op jit(solution)/shard_map/ppermute | solution.py:523
  50.8 31.6 %collective-permute-start.3 = (bf16[320,1280]{1,0:T(8,128)(2,1)}, bf16[320,1280]{1,0:T(8,128)(2,1)}, u32[]{:S(2)}, u32[]{:S(2)}) collective-permute-start(bf16[320,1280]{1,0:T(8,128)(2,1)} %collective-permute-done.2.refs_4_.refs_6_), channel_id=1, source_target_pairs={{0,8},{4,12},{8,0},{12,4},{16,24},{20,28},{24,16},{28,20},{1,9},{5... | collective-permute-start | bytes 2457608 | tf_op jit(solution)/shard_map/ppermute | solution.py:523
  51.2 53.9 %collective-permute-start.10 = (bf16[1280,512]{1,0:T(8,128)(2,1)}, bf16[1280,512]{1,0:T(8,128)(2,1)}, u32[]{:S(2)}, u32[]{:S(2)}) collective-permute-start(bf16[1280,512]{1,0:T(8,128)(2,1)} %shard_map.138.refs_0_), channel_id=1, source_target_pairs={{0,4},{4,0},{8,12},{12,8},{16,20},{20,16},{24,28},{28,24},{1,5},{5... | collective-permute-start | bytes 3932168 | tf_op jit(solution)/shard_map/ppermute | solution.py:519
  82.4 12.3 %collective-permute-start.6 = (bf16[320,1280]{1,0:T(8,128)(2,1)}, bf16[320,1280]{1,0:T(8,128)(2,1)}, u32[]{:S(2)}, u32[]{:S(2)}) collective-permute-start(bf16[320,1280]{1,0:T(8,128)(2,1)} %collective-permute-done.2.refs_4_.refs_6_), channel_id=1, source_target_pairs={{0,1},{1,0},{2,3},{3,2},{4,5},{5,4},{6,7},{7,6},{8,9},{9,8},{10,11... | collective-permute-start | bytes 2457608 | tf_op jit(solution)/shard_map/ppermute | solution.py:533
  82.4 12.3 %collective-permute-start.7 = (bf16[320,1280]{1,0:T(8,128)(2,1)}, bf16[320,1280]{1,0:T(8,128)(2,1)}, u32[]{:S(2)}, u32[]{:S(2)}) collective-permute-start(bf16[320,1280]{1,0:T(8,128)(2,1)} %collective-permute-done.3.refs_5_.refs_7_), channel_id=1, source_target_pairs={{0,1},{1,0},{2,3},{3,2},{4,5},{5,4},{6,7},{7,6},{8,9},{9,8},{10,11... | collective-permute-start | bytes 2457608 | tf_op jit(solution)/shard_map/ppermute | solution.py:533
  91.0 24.2 %collective-permute-start.13 = (bf16[2,4,1,96,640]{4,3,2,1,0:T(8,128)(2,1)S(1)}, bf16[2,4,1,96,640]{4,3,2,1,0:T(8,128)(2,1)S(1)}, u32[]{:S(2)}, u32[]{:S(2)}) collective-permute-start(bf16[2,4,1,96,640]{4,3,2,1,0:T(8,128)(2,1)S(1)} %shard_map.143), channel_id=1, source_target_pairs={{0,2},{1,3},{2,0},{3,1},{4,6},{5,7},{6,4},{7,5},{8,10},{9,11},{10,... | collective-permute-start | bytes 2949128 | tf_op jit(solution)/shard_map/ppermute | solution.py:529
  93.2 28.8 %collective-permute-start.15 = (bf16[4,256,512]{2,1,0:T(8,128)(2,1)S(1)}, bf16[4,256,512]{2,1,0:T(8,128)(2,1)S(1)}, u32[]{:S(2)}, u32[]{:S(2)}) collective-permute-start(bf16[4,256,512]{2,1,0:T(8,128)(2,1)S(1)} %copy-done.50), channel_id=1, source_target_pairs={{0,4},{4,0},{8,12},{12,8},{16,20},{20,16},{24,28},{28,24},{1,5},{5... | collective-permute-start | bytes 3145736 | tf_op jit(solution)/shard_map/ppermute | solution.py:519
  117.2 19.3 %collective-permute-start.16 = (bf16[2,2,1,96,640]{4,3,2,1,0:T(8,128)(2,1)S(1)}, bf16[2,2,1,96,640]{4,3,2,1,0:T(8,128)(2,1)S(1)}, u32[]{:S(2)}, u32[]{:S(2)}) collective-permute-start(bf16[2,2,1,96,640]{4,3,2,1,0:T(8,128)(2,1)S(1)} %shard_map.146), channel_id=1, source_target_pairs={{0,8},{4,12},{8,0},{12,4},{16,24},{20,28},{24,16},{28,20},{1,9},{5... | collective-permute-start | bytes 1474568 | tf_op jit(solution)/shard_map/ppermute | solution.py:523
  120.4 29.7 %collective-permute-start.14 = (bf16[2,4,2,80,384]{4,3,2,1,0:T(8,128)(2,1)S(1)}, bf16[2,4,2,80,384]{4,3,2,1,0:T(8,128)(2,1)S(1)}, u32[]{:S(2)}, u32[]{:S(2)}) collective-permute-start(bf16[2,4,2,80,384]{4,3,2,1,0:T(8,128)(2,1)S(1)} %shard_map.147), channel_id=1, source_target_pairs={{0,2},{1,3},{2,0},{3,1},{4,6},{5,7},{6,4},{7,5},{8,10},{9,11},{10,... | collective-permute-start | bytes 2949128 | tf_op jit(solution)/shard_map/ppermute | solution.py:529
  135.9 8.9 %collective-permute-start.19 = (bf16[1280,256]{1,0:T(8,128)(2,1)S(1)}, bf16[1280,256]{1,0:T(8,128)(2,1)S(1)}, u32[]{:S(2)}, u32[]{:S(2)}) collective-permute-start(bf16[1280,256]{1,0:T(8,128)(2,1)S(1)} %get-tuple-element.252), channel_id=1, source_target_pairs={{0,1},{1,0},{2,3},{3,2},{4,5},{5,4},{6,7},{7,6},{8,9},{9,8},{10,11... | collective-permute-start | bytes 1966088 | tf_op jit(solution)/shard_map/ppermute | solution.py:533
  136.0 8.8 %collective-permute-start.20 = (bf16[1280,256]{1,0:T(8,128)(2,1)S(1)}, bf16[1280,256]{1,0:T(8,128)(2,1)S(1)}, u32[]{:S(2)}, u32[]{:S(2)}) collective-permute-start(bf16[1280,256]{1,0:T(8,128)(2,1)S(1)} %get-tuple-element.253), channel_id=1, source_target_pairs={{0,1},{1,0},{2,3},{3,2},{4,5},{5,4},{6,7},{7,6},{8,9},{9,8},{10,11... | collective-permute-start | bytes 1966088 | tf_op jit(solution)/shard_map/ppermute | solution.py:533
  145.9 17.6 %collective-permute-start.23 = (bf16[2,4,2,80,256]{4,3,2,1,0:T(8,128)(2,1)S(1)}, bf16[2,4,2,80,256]{4,3,2,1,0:T(8,128)(2,1)S(1)}, u32[]{:S(2)}, u32[]{:S(2)}) collective-permute-start(bf16[2,4,2,80,256]{4,3,2,1,0:T(8,128)(2,1)S(1)} %shard_map.152), channel_id=1, source_target_pairs={{0,2},{1,3},{2,0},{3,1},{4,6},{5,7},{6,4},{7,5},{8,10},{9,11},{10,... | collective-permute-start | bytes 1966088 | tf_op jit(solution)/shard_map/ppermute | solution.py:529
  148.8 28.0 %collective-permute-start.26 = (bf16[2,4,1,64,640]{4,3,2,1,0:T(8,128)(2,1)S(1)}, bf16[2,4,1,64,640]{4,3,2,1,0:T(8,128)(2,1)S(1)}, u32[]{:S(2)}, u32[]{:S(2)}) collective-permute-start(bf16[2,4,1,64,640]{4,3,2,1,0:T(8,128)(2,1)S(1)} %shard_map.153), channel_id=1, source_target_pairs={{0,2},{1,3},{2,0},{3,1},{4,6},{5,7},{6,4},{7,5},{8,10},{9,11},{10,... | collective-permute-start | bytes 1966088 | tf_op jit(solution)/shard_map/ppermute | solution.py:529
  151.3 20.2 %collective-permute-start.21 = (bf16[2,2,2,80,384]{4,3,2,1,0:T(8,128)(2,1)S(1)}, bf16[2,2,2,80,384]{4,3,2,1,0:T(8,128)(2,1)S(1)}, u32[]{:S(2)}, u32[]{:S(2)}) collective-permute-start(bf16[2,2,2,80,384]{4,3,2,1,0:T(8,128)(2,1)S(1)} %shard_map.154), channel_id=1, source_target_pairs={{0,8},{4,12},{8,0},{12,4},{16,24},{20,28},{24,16},{28,20},{1,9},{5... | collective-permute-start | bytes 1474568 | tf_op jit(solution)/shard_map/ppermute | solution.py:523
  152.9 16.9 %collective-permute-start.22 = (bf16[2,1,1,96,640]{4,3,2,1,0:T(8,128)(2,1)S(1)}, bf16[2,1,1,96,640]{4,3,2,1,0:T(8,128)(2,1)S(1)}, u32[]{:S(2)}, u32[]{:S(2)}) collective-permute-start(bf16[2,1,1,96,640]{4,3,2,1,0:T(8,128)(2,1)S(1)} %shard_map.150), channel_id=1, source_target_pairs={{0,16},{4,20},{8,24},{12,28},{16,0},{20,4},{24,8},{28,12},{1,17},{... | collective-permute-start | bytes 737288 | tf_op jit(solution)/shard_map/ppermute | solution.py:523
  164.6 17.1 %collective-permute-start.25 = (bf16[2,2,2,80,256]{4,3,2,1,0:T(8,128)(2,1)S(1)}, bf16[2,2,2,80,256]{4,3,2,1,0:T(8,128)(2,1)S(1)}, u32[]{:S(2)}, u32[]{:S(2)}) collective-permute-start(bf16[2,2,2,80,256]{4,3,2,1,0:T(8,128)(2,1)S(1)} %shard_map.155), channel_id=1, source_target_pairs={{0,8},{4,12},{8,0},{12,4},{16,24},{20,28},{24,16},{28,20},{1,9},{5... | collective-permute-start | bytes 983048 | tf_op jit(solution)/shard_map/ppermute | solution.py:523
  173.1 13.5 %collective-permute-start.24 = (bf16[2,1,2,80,384]{4,3,2,1,0:T(8,128)(2,1)}, bf16[2,1,2,80,384]{4,3,2,1,0:T(8,128)(2,1)}, u32[]{:S(2)}, u32[]{:S(2)}) collective-permute-start(bf16[2,1,2,80,384]{4,3,2,1,0:T(8,128)(2,1)} %shard_map.157), channel_id=1, source_target_pairs={{0,16},{4,20},{8,24},{12,28},{16,0},{20,4},{24,8},{28,12},{1,17},{... | collective-permute-start | bytes 737288 | tf_op jit(solution)/shard_map/ppermute | solution.py:523
  178.4 19.1 %collective-permute-start.29 = (bf16[2,2,1,64,640]{4,3,2,1,0:T(8,128)(2,1)}, bf16[2,2,1,64,640]{4,3,2,1,0:T(8,128)(2,1)}, u32[]{:S(2)}, u32[]{:S(2)}) collective-permute-start(bf16[2,2,1,64,640]{4,3,2,1,0:T(8,128)(2,1)} %shard_map.158), channel_id=1, source_target_pairs={{0,8},{4,12},{8,0},{12,4},{16,24},{20,28},{24,16},{28,20},{1,9},{5... | collective-permute-start | bytes 983048 | tf_op jit(solution)/shard_map/ppermute | solution.py:523
  180.2 15.7 %collective-permute-start.30 = (bf16[2,96,640]{2,1,0:T(8,128)(2,1)S(1)}, bf16[2,96,640]{2,1,0:T(8,128)(2,1)}, u32[]{:S(2)}, u32[]{:S(2)}) collective-permute-start(bf16[2,96,640]{2,1,0:T(8,128)(2,1)S(1)} %shard_map.156.refs_0_), channel_id=1, source_target_pairs={{0,2},{1,3},{2,0},{3,1},{4,6},{5,7},{6,4},{7,5},{8,10},{9,11},{10,... | collective-permute-start | bytes 737288 | tf_op jit(solution)/shard_map/ppermute | solution.py:529
  183.0 19.7 %collective-permute-start.28 = (bf16[2,1,2,80,256]{4,3,2,1,0:T(8,128)(2,1)}, bf16[2,1,2,80,256]{4,3,2,1,0:T(8,128)(2,1)}, u32[]{:S(2)}, u32[]{:S(2)}) collective-permute-start(bf16[2,1,2,80,256]{4,3,2,1,0:T(8,128)(2,1)} %shard_map.159), channel_id=1, source_target_pairs={{0,16},{4,20},{8,24},{12,28},{16,0},{20,4},{24,8},{28,12},{1,17},{... | collective-permute-start | bytes 491528 | tf_op jit(solution)/shard_map/ppermute | solution.py:523
  194.3 19.6 %collective-permute-start.27 = (bf16[2,80,384]{2,1,0:T(8,128)(2,1)}, bf16[2,80,384]{2,1,0:T(8,128)(2,1)S(1)}, u32[]{:S(2)}, u32[]{:S(2)}) collective-permute-start(bf16[2,80,384]{2,1,0:T(8,128)(2,1)} %get-tuple-element.295), channel_id=1, source_target_pairs={{0,4},{4,0},{8,12},{12,8},{16,20},{20,16},{24,28},{28,24},{1,5},{5... | collective-permute-start | bytes 368648 | tf_op jit(solution)/shard_map/ppermute | solution.py:519
  214.9 9.0 %collective-permute-start.33 = (bf16[2,2,80,256]{3,2,1,0:T(8,128)(2,1)S(1)}, bf16[2,2,80,256]{3,2,1,0:T(8,128)(2,1)S(1)}, u32[]{:S(2)}, u32[]{:S(2)}) collective-permute-start(bf16[2,2,80,256]{3,2,1,0:T(8,128)(2,1)S(1)} %shard_map.164.refs_0_), channel_id=1, source_target_pairs={{0,2},{1,3},{2,0},{3,1},{4,6},{5,7},{6,4},{7,5},{8,10},{9,11},{10,... | collective-permute-start | bytes 491528 | tf_op jit(solution)/shard_map/ppermute | solution.py:529
  (71 other events, 889.8 us)

commit v12 on v10

--- a/solution.py
+++ b/solution.py
@@ -14,9 +14,10 @@
 CHIPS_Z = 4
 LANES = 128
 PARTS = 2
-VMEM = 20 * 1024 * 1024
+VMEM = 16 * 1024 * 1024
 WIDE = 56 * 1024 * 1024
 SMALL = 4 * 1024 * 1024
+STATE = 8 * 1024 * 1024
 
 
 def moments(weight, first, second, grad):
@@ -119,16 +120,20 @@
     )(jnp.reshape(at, (1,)).astype(jnp.int32), hidden)
 
 
+def once(shape, index_map):
+    return pl.BlockSpec(shape, index_map, pipeline_mode=pl.Buffered(1))
+
+
 class Tokens:
     def __init__(self, packs, hiddens, model, nz, width):
         tokens = packs[0].shape[1]
         self.model, self.width, self.count = model, width, len(packs)
         if hiddens is None:
             self.arrays = list(packs)
-            self.specs = [pl.BlockSpec(packs[0].shape, lambda z, c: (0, 0))] * len(packs)
+            self.specs = [once(packs[0].shape, lambda z, c: (0, 0))] * len(packs)
         else:
             self.arrays = [*packs, *hiddens]
-            self.specs = [pl.BlockSpec((model, tokens), lambda z, c: (0, 0))] * len(packs)
+            self.specs = [once((model, tokens), lambda z, c: (0, 0))] * len(packs)
             self.specs += [pl.BlockSpec((1, width, tokens), lambda z, c: (z, 0, 0))] * len(packs)
 
     def cot(self, refs, n):
@@ -201,7 +206,7 @@
                 grad_act * gelu_slope(tokens.hidden(ins, n))
             ).astype(BF16)
 
-    w_specs = [pl.BlockSpec((part, model), lambda z, c: (0, 0))] * nz
+    w_specs = [once((part, model), lambda z, c: (0, 0))] * nz
     return pl.pallas_call(
         body,
         grid_spec=pltpu.PrefetchScalarGridSpec(
@@ -250,7 +255,7 @@
                     lambda z, c: ((c[0] + 1 + z // half) % CORES * half + z % half, block, 0),
                 )
             ]
-            + [pl.BlockSpec((model, tokens), lambda z, c: (0, 0))] * count,
+            + [once((model, tokens), lambda z, c: (0, 0))] * count,
             out_specs=[pl.BlockSpec((high, width), lambda z, c: (0, 0))] * (half * cut)
             + [pl.BlockSpec((1, model, width), lambda z, c: (jnp.maximum(z - half, 0), 0, 0))],
         ),
@@ -459,7 +464,7 @@
             out_specs=[state_spec] * 3 + [pl.BlockSpec((long, LANES), lambda n, c: (0, 0))],
         ),
         out_shape=[state] * 3 + [jax.ShapeDtypeStruct((long, LANES), F32)],
-        **params(),
+        **params(STATE),
     )(core, weight, first, second, *mine, *other, *tiles)
 
 
@@ -481,7 +486,7 @@
         in_specs=[spec] * 2 + [tile] * count,
         out_specs=spec,
         out_shape=jax.ShapeDtypeStruct(weight.shape, F32),
-        **params(),
+        **params(STATE),
     )(weight, update, *tiles)
 
 
@@ -686,13 +691,13 @@
                 *got[:3],
                 got[4 : 5 + last],
                 got[5 + last :],
-                (CORES,),
-                pl.BlockSpec((shard, half), lambda n, c: (0, n)),
+                (model // LANES,),
+                pl.BlockSpec((shard, LANES), lambda n, c: (0, n)),
                 [
-                    pl.BlockSpec((p, ny, w // p // ny, half), lambda n, c: (0, 0, 0, 0))
+                    pl.BlockSpec((p, ny, w // p // ny, LANES), lambda n, c: (0, 0, 0, n % (half // LANES)))
                     for w, p in zip(cuts, parts)
                 ],
-                lambda n: n,
+                lambda n: n // (half // LANES),
                 0,
                 [got[3]],
             )

time: 256 us -> 257 us (level)
  no operation moved by 1% of the time
where the time goes in v12:
time: 257 us; the launch traced here: 256 us
  Pallas kernels  119 us (46%)
  waiting for transfers between devices  77.7 us (30%)
  starting transfers between devices  47.3 us (18%)
  local copies, waits for them, and re-layouts  10.8 us (4%)
    ppermute x14, waiting for transfers between devices, along_z(): return lax.ppermute(value, 'gx', pairs)  29.3 us
    ppermute x6, waiting for transfers between devices, along_x(): return lax.ppermute(value, 'gx', pairs)  25.3 us
    pallas_call x16, Pallas kernels, reduce_step(): pl.pallas_call(body, grid_spec=pltpu.PrefetchScalarGridSpec(num_scalar_pr...  24.7 us
    ppermute x14, starting transfers between devices, along_z(): return lax.ppermute(value, 'gx', pairs)  23.6 us
    pallas_call x2, Pallas kernels, grad_pre_chunk(): pl.pallas_call(body, grid_spec=pltpu.PrefetchScalarGridSpec(num_scalar_pr...  18.1 us
    ppermute x8, waiting for transfers between devices, along_y(): return lax.ppermute(value, 'gy', pairs)  17.7 us
    pallas_call x2, Pallas kernels, grad_in_chunk(): pl.pallas_call(body, grid_spec=pltpu.PrefetchScalarGridSpec(num_scalar_pr...  14.7 us
    pallas_call x2, Pallas kernels, grad_out_chunk(): pl.pallas_call(body, grid_spec=pltpu.PrefetchScalarGridSpec(num_scalar_pr...  13.7 us
  transfers between devices with their start and end apart: 44, of which 18 were waited for; matrix products, arithmetic and copies ran while one was open for 0% of the time, Pallas kernels for 39%

profile of v12, /device:TPU:0, one launch (start us, length us, event | category | flops | bytes accessed | tf_op | source)
XLA Modules:
  0.0 256.3 jit_solution(15935798755653236995)
XLA Ops:
  0.7 5.2 %shard_map.136 = bf16[2816,512]{1,0:T(8,128)(2,1)} custom-call(s32[1]{0:T(128)} %bitcast.8.at_ref, bf16[512,5120]{1,0:T(8,128)(2,1)} %h_ref.4, bf16[512,1280]{1,0:T(8,128)(2,1)} %cot_ref.2), custom_call_target="tpu_custom_call" | custom-call | flops 1 | bytes 1 | tf_op jit(solution)/shard_map/pallas_call | solution.py:82
  5.8 2.9 %collective-permute-start = (bf16[2816,512]{1,0:T(8,128)(2,1)}, bf16[2816,512]{1,0:T(8,128)(2,1)}, u32[]{:S(2)}, u32[]{:S(2)}) collective-permute-start(bf16[2816,512]{1,0:T(8,128)(2,1)} %shard_map.136), channel_id=1, source_target_pairs={{0,4},{4,0},{8,12},{12,8},{16,20},{20,16},{24,28},{28,24},{1,5},{5... | collective-permute-start | bytes 8650760 | tf_op jit(solution)/shard_map/ppermute | solution.py:511
  12.6 2.6 %collective-permute-start.2 = (bf16[320,1280]{1,0:T(8,128)(2,1)}, bf16[320,1280]{1,0:T(8,128)(2,1)}, u32[]{:S(2)}, u32[]{:S(2)}) collective-permute-start(bf16[320,1280]{1,0:T(8,128)(2,1)} %shard_map.137.refs_2_.refs_4_), channel_id=1, source_target_pairs={{0,16},{4,20},{8,24},{12,28},{16,0},{20,4},{24,8},{28,12},{1,17},{... | collective-permute-start | bytes 2457608 | tf_op jit(solution)/shard_map/ppermute | solution.py:515
  17.7 5.1 %shard_map.139.refs_0_ = bf16[2816,512]{1,0:T(8,128)(2,1)} custom-call(s32[1]{0:T(128)} %bitcast.5.at_ref, bf16[512,5120]{1,0:T(8,128)(2,1)} %h_ref.4, bf16[512,1280]{1,0:T(8,128)(2,1)} %cot_ref.2), custom_call_target="tpu_custom_call" | custom-call | flops 1 | bytes 1 | tf_op jit(solution)/shard_map/pallas_call | solution.py:82
  22.8 3.9 %shard_map.140.refs_2_ = bf16[4,256,512]{2,1,0:T(8,128)(2,1)} custom-call(s32[1]{0:T(128)} %bitcast.3.at_ref, bf16[512,5120]{1,0:T(8,128)(2,1)} %h_ref.4), custom_call_target="tpu_custom_call" | custom-call | flops 1 | bytes 1 | tf_op jit(solution)/shard_map/pallas_call | solution.py:110
  26.7 4.0 %shard_map.141 = bf16[4,256,512]{2,1,0:T(8,128)(2,1)} custom-call(s32[1]{0:T(128)} %bitcast.8.at_ref, bf16[512,5120]{1,0:T(8,128)(2,1)} %h_ref.4), custom_call_target="tpu_custom_call" | custom-call | flops 1 | bytes 1 | tf_op jit(solution)/shard_map/pallas_call | solution.py:110
  30.7 17.7 %collective-permute-done.1.refs_3_.refs_5_ = bf16[320,1280]{1,0:T(8,128)(2,1)} collective-permute-done((bf16[320,1280]{1,0:T(8,128)(2,1)}, bf16[320,1280]{1,0:T(8,128)(2,1)}, u32[]{:S(2)}, u32[]{:S(2)}) %collective-permute-start.1) | collective-permute-done | bytes 819232 | tf_op jit(solution)/shard_map/ppermute | solution.py:515
  52.1 20.2 %collective-permute-done.refs_1_ = bf16[2816,512]{1,0:T(8,128)(2,1)} collective-permute-done((bf16[2816,512]{1,0:T(8,128)(2,1)}, bf16[2816,512]{1,0:T(8,128)(2,1)}, u32[]{:S(2)}, u32[]{:S(2)}) %collective-permute-start) | collective-permute-done | bytes 2883616 | tf_op jit(solution)/shard_map/ppermute | solution.py:511
  72.4 8.1 %shard_map.142 = (bf16[4,192,640]{2,1,0:T(8,128)(2,1)}, bf16[4,192,640]{2,1,0:T(8,128)(2,1)}, bf16[2,4,192,640]{3,2,1,0:T(8,128)(2,1)S(1)}) custom-call(s32[1]{0:T(128)} %bitcast.c_ref, bf16[2816,512]{1,0:T(8,128)(2,1)S(1)} %copy-done, bf16[2816,512]{1,0:T(8,128)(2,1)} %collective-permute-done.refs_1_), custom_call_target="tpu_custom_call" | custom-call | flops 1 | bytes 1 | tf_op jit(solution)/shard_map/pallas_call | solution.py:171
  87.7 3.2 %shard_map.143 = bf16[2,4,1,96,640]{4,3,2,1,0:T(8,128)(2,1)S(1)} custom-call(s32[3]{0:T(128)S(1)} %pad_add_fusion.2.at_ref, bf16[2,4,1,2,96,640]{5,4,3,2,1,0:T(8,128)(2,1)S(1)} %bitcast.21, bf16[4,1,2,96,640]{4,3,2,1,0:T(8,128)(2,1)} %bitcast.10.refs_1_, bf16[4,1,2,96,640]{4,3,2,1,0:T(8,128)(2,1)} %bitcast.11.refs_2_), custom_call_target="tpu_custom_call" | custom-call | flops 1 | bytes 1 | tf_op jit(solution)/shard_map/pallas_call | solution.py:406
  94.7 10.3 %shard_map.144.g_ref = bf16[4,384,1024]{2,1,0:T(8,128)(2,1)S(1)} custom-call(s32[2]{0:T(128)S(1)} %pad_add_fusion.3.c_ref, bf16[2816,512]{1,0:T(8,128)(2,1)S(1)} %copy-done, bf16[2816,512]{1,0:T(8,128)(2,1)} %collective-permute-done.refs_1_, bf16[320,1280]{1,0:T(8,128)(2,1)S(1)} %copy-done.19, bf16[320,1280]{1,0:T(8,128)(2,1)} %collective-permute-done.1.refs_3_.refs_5_, ...), custom_call_target="tpu_custom_call" | custom-call | flops 1 | bytes 1 | tf_op jit(solution)/shard_map/pallas_call | solution.py:210
  105.0 8.9 %shard_map.145 = (bf16[1280,384]{1,0:T(8,128)(2,1)S(1)}, bf16[1280,384]{1,0:T(8,128)(2,1)S(1)}, bf16[2,1280,384]{2,1,0:T(8,128)(2,1)S(1)}) custom-call(s32[1]{0:T(128)} %bitcast.c_ref, bf16[4,384,1024]{2,1,0:T(8,128)(2,1)S(1)} %shard_map.144.g_ref, bf16[1280,512]{1,0:T(8,128)(2,1)} %shard_map.138.refs_0_, bf16[1280,512]{1,0:T(8,128)(2,1)} %collective-permute-done.10.refs_1_), custom_call_target="tpu_custom_call" | custom-call | flops 1 | bytes 1 | tf_op jit(solution)/shard_map/pallas_call | solution.py:247
  122.0 7.9 %shard_map.148.g_ref = bf16[4,256,1024]{2,1,0:T(8,128)(2,1)S(1)} custom-call(s32[2]{0:T(128)S(1)} %pad_add_fusion.3.c_ref, bf16[2816,512]{1,0:T(8,128)(2,1)S(1)} %copy-done, bf16[2816,512]{1,0:T(8,128)(2,1)} %collective-permute-done.refs_1_, bf16[4,256,512]{2,1,0:T(8,128)(2,1)S(1)} %copy-done.17, bf16[4,256,512]{2,1,0:T(8,128)(2,1)S(1)} %collective-permute-done.15.refs_3_, ...), custom_call_target="tpu_custom_call" | custom-call | flops 1 | bytes 1 | tf_op jit(solution)/shard_map/pallas_call | solution.py:210
  129.9 5.8 %shard_map.149 = (bf16[1280,256]{1,0:T(8,128)(2,1)S(1)}, bf16[1280,256]{1,0:T(8,128)(2,1)S(1)}, bf16[2,1280,256]{2,1,0:T(8,128)(2,1)S(1)}) custom-call(s32[1]{0:T(128)} %bitcast.c_ref, bf16[4,256,1024]{2,1,0:T(8,128)(2,1)S(1)} %shard_map.148.g_ref, bf16[1280,512]{1,0:T(8,128)(2,1)} %shard_map.138.refs_0_, bf16[1280,512]{1,0:T(8,128)(2,1)} %collective-permute-done.10.refs_1_), custom_call_target="tpu_custom_call" | custom-call | flops 1 | bytes 1 | tf_op jit(solution)/shard_map/pallas_call | solution.py:247
  137.9 5.6 %shard_map.151 = (bf16[4,128,640]{2,1,0:T(8,128)(2,1)S(1)}, bf16[4,128,640]{2,1,0:T(8,128)(2,1)S(1)}, bf16[2,4,128,640]{3,2,1,0:T(8,128)(2,1)S(1)}) custom-call(s32[1]{0:T(128)} %bitcast.c_ref, bf16[2816,512]{1,0:T(8,128)(2,1)S(1)} %copy-done, bf16[2816,512]{1,0:T(8,128)(2,1)} %collective-permute-done.refs_1_, bf16[4,256,512]{2,1,0:T(8,128)(2,1)S(1)} %copy-done.17, ...), custom_call_target="tpu_custom_call" | custom-call | flops 1 | bytes 1 | tf_op jit(solution)/shard_map/pallas_call | solution.py:171
  152.5 10.5 %collective-permute-done.22.refs_3_ = bf16[2,4,2,80,256]{4,3,2,1,0:T(8,128)(2,1)S(1)} collective-permute-done((bf16[2,4,2,80,256]{4,3,2,1,0:T(8,128)(2,1)S(1)}, bf16[2,4,2,80,256]{4,3,2,1,0:T(8,128)(2,1)S(1)}, u32[]{:S(2)}, u32[]{:S(2)}) %collective-permute-start.22) | collective-permute-done | bytes 655392 | tf_op jit(solution)/shard_map/ppermute | solution.py:521
  169.6 6.5 %collective-permute-done.26.refs_3_ = bf16[2,4,1,64,640]{4,3,2,1,0:T(8,128)(2,1)S(1)} collective-permute-done((bf16[2,4,1,64,640]{4,3,2,1,0:T(8,128)(2,1)S(1)}, bf16[2,4,1,64,640]{4,3,2,1,0:T(8,128)(2,1)S(1)}, u32[]{:S(2)}, u32[]{:S(2)}) %collective-permute-start.26) | collective-permute-done | bytes 655392 | tf_op jit(solution)/shard_map/ppermute | solution.py:521
  185.8 6.0 %collective-permute-done.23.refs_5_ = bf16[2,1,2,80,384]{4,3,2,1,0:T(8,128)(2,1)S(1)} collective-permute-done((bf16[2,1,2,80,384]{4,3,2,1,0:T(8,128)(2,1)S(1)}, bf16[2,1,2,80,384]{4,3,2,1,0:T(8,128)(2,1)S(1)}, u32[]{:S(2)}, u32[]{:S(2)}) %collective-permute-start.23) | collective-permute-done | bytes 245792 | tf_op jit(solution)/shard_map/ppermute | solution.py:515
  223.2 6.2 %shard_map.169 = (f32[160,5120]{1,0:T(8,128)}, f32[160,5120]{1,0:T(8,128)}, f32[160,5120]{1,0:T(8,128)S(1)}, f32[16,128]{1,0:T(8,128)S(1)}) custom-call(s32[1]{0:T(128)} %bitcast.c_ref, f32[160,5120]{1,0:T(8,128)S(1)} %copy-done.9, f32[160,5120]{1,0:T(8,128)S(1)} %copy-done.25, f32[160,5120]{1,0:T(8,128)S(1)} %copy-done.26, ...), custom_call_target="tpu_custom_call" | custom-call | flops 1 | bytes 1 | tf_op jit(solution)/shard_map/pallas_call | solution.py:456
  231.7 6.9 %shard_map.171 = (f32[640,1280]{1,0:T(8,128)}, f32[640,1280]{1,0:T(8,128)}, f32[640,1280]{1,0:T(8,128)S(1)}, f32[32,128]{1,0:T(8,128)S(1)}) custom-call(s32[1]{0:T(128)} %bitcast.c_ref, f32[640,1280]{1,0:T(8,128)S(1)} %copy-done.4, f32[640,1280]{1,0:T(8,128)S(1)} %copy-done.27, f32[640,1280]{1,0:T(8,128)S(1)} %copy-done.28, ...), custom_call_target="tpu_custom_call" | custom-call | flops 1 | bytes 1 | tf_op jit(solution)/shard_map/pallas_call | solution.py:456
  238.6 2.7 %collective-permute-start.42 = (f32[32,128]{1,0:T(8,128)S(1)}, f32[32,128]{1,0:T(8,128)S(1)}, u32[]{:S(2)}, u32[]{:S(2)}) collective-permute-start(f32[32,128]{1,0:T(8,128)S(1)} %get-tuple-element.345.refs_0_), channel_id=1, source_target_pairs={{0,24},{4,28},{8,16},{12,20},{16,8},{20,12},{24,0},{28,4},{1,25},{... | collective-permute-start | bytes 49160 | tf_op jit(solution)/shard_map/ppermute | solution.py:515
  247.1 2.7 %collective-permute-done.43.refs_1_ = f32[32,128]{1,0:T(8,128)S(1)} collective-permute-done((f32[32,128]{1,0:T(8,128)S(1)}, f32[32,128]{1,0:T(8,128)S(1)}, u32[]{:S(2)}, u32[]{:S(2)}) %collective-permute-start.43) | collective-permute-done | bytes 16416 | tf_op jit(solution)/shard_map/ppermute | solution.py:511
  249.8 3.2 %shard_map.173 = f32[160,5120]{1,0:T(8,128)} custom-call(f32[160,5120]{1,0:T(8,128)S(1)} %copy-done.9, f32[160,5120]{1,0:T(8,128)S(1)} %get-tuple-element.350.u_ref, f32[32,128]{1,0:T(8,128)S(1)} %shard_map.172.refs_0_, f32[32,128]{1,0:T(8,128)S(1)} %collective-permute-done.43.refs_1_), custom_call_target="tpu_custom_call" | custom-call | flops 1 | bytes 1 | tf_op jit(solution)/shard_map/pallas_call | solution.py:483
  253.1 3.2 %shard_map.174 = f32[640,1280]{1,0:T(8,128)} custom-call(f32[640,1280]{1,0:T(8,128)S(1)} %copy-done.4, f32[640,1280]{1,0:T(8,128)S(1)} %get-tuple-element.357.u_ref, f32[32,128]{1,0:T(8,128)S(1)} %shard_map.172.refs_0_, f32[32,128]{1,0:T(8,128)S(1)} %collective-permute-done.43.refs_1_), custom_call_target="tpu_custom_call" | custom-call | flops 1 | bytes 1 | tf_op jit(solution)/shard_map/pallas_call | solution.py:483
  (193 shorter events, 95.6 us)
Async XLA Ops:
  5.8 66.6 %collective-permute-start = (bf16[2816,512]{1,0:T(8,128)(2,1)}, bf16[2816,512]{1,0:T(8,128)(2,1)}, u32[]{:S(2)}, u32[]{:S(2)}) collective-permute-start(bf16[2816,512]{1,0:T(8,128)(2,1)} %shard_map.136), channel_id=1, source_target_pairs={{0,4},{4,0},{8,12},{12,8},{16,20},{20,16},{24,28},{28,24},{1,5},{5... | collective-permute-start | bytes 8650760 | tf_op jit(solution)/shard_map/ppermute | solution.py:511
  11.0 37.4 %collective-permute-start.1 = (bf16[320,1280]{1,0:T(8,128)(2,1)}, bf16[320,1280]{1,0:T(8,128)(2,1)}, u32[]{:S(2)}, u32[]{:S(2)}) collective-permute-start(bf16[320,1280]{1,0:T(8,128)(2,1)} %shard_map.137.refs_2_.refs_4_), channel_id=1, source_target_pairs={{0,8},{4,12},{8,0},{12,4},{16,24},{20,28},{24,16},{28,20},{1,9},{5... | collective-permute-start | bytes 2457608 | tf_op jit(solution)/shard_map/ppermute | solution.py:515
  12.6 38.3 %collective-permute-start.2 = (bf16[320,1280]{1,0:T(8,128)(2,1)}, bf16[320,1280]{1,0:T(8,128)(2,1)}, u32[]{:S(2)}, u32[]{:S(2)}) collective-permute-start(bf16[320,1280]{1,0:T(8,128)(2,1)} %shard_map.137.refs_2_.refs_4_), channel_id=1, source_target_pairs={{0,16},{4,20},{8,24},{12,28},{16,0},{20,4},{24,8},{28,12},{1,17},{... | collective-permute-start | bytes 2457608 | tf_op jit(solution)/shard_map/ppermute | solution.py:515
  50.8 31.5 %collective-permute-start.3 = (bf16[320,1280]{1,0:T(8,128)(2,1)}, bf16[320,1280]{1,0:T(8,128)(2,1)}, u32[]{:S(2)}, u32[]{:S(2)}) collective-permute-start(bf16[320,1280]{1,0:T(8,128)(2,1)} %collective-permute-done.2.refs_4_.refs_6_), channel_id=1, source_target_pairs={{0,8},{4,12},{8,0},{12,4},{16,24},{20,28},{24,16},{28,20},{1,9},{5... | collective-permute-start | bytes 2457608 | tf_op jit(solution)/shard_map/ppermute | solution.py:515
  51.2 53.7 %collective-permute-start.10 = (bf16[1280,512]{1,0:T(8,128)(2,1)}, bf16[1280,512]{1,0:T(8,128)(2,1)}, u32[]{:S(2)}, u32[]{:S(2)}) collective-permute-start(bf16[1280,512]{1,0:T(8,128)(2,1)} %shard_map.138.refs_0_), channel_id=1, source_target_pairs={{0,4},{4,0},{8,12},{12,8},{16,20},{20,16},{24,28},{28,24},{1,5},{5... | collective-permute-start | bytes 3932168 | tf_op jit(solution)/shard_map/ppermute | solution.py:511
  82.3 12.4 %collective-permute-start.6 = (bf16[320,1280]{1,0:T(8,128)(2,1)}, bf16[320,1280]{1,0:T(8,128)(2,1)}, u32[]{:S(2)}, u32[]{:S(2)}) collective-permute-start(bf16[320,1280]{1,0:T(8,128)(2,1)} %collective-permute-done.2.refs_4_.refs_6_), channel_id=1, source_target_pairs={{0,1},{1,0},{2,3},{3,2},{4,5},{5,4},{6,7},{7,6},{8,9},{9,8},{10,11... | collective-permute-start | bytes 2457608 | tf_op jit(solution)/shard_map/ppermute | solution.py:525
  82.3 12.3 %collective-permute-start.7 = (bf16[320,1280]{1,0:T(8,128)(2,1)}, bf16[320,1280]{1,0:T(8,128)(2,1)}, u32[]{:S(2)}, u32[]{:S(2)}) collective-permute-start(bf16[320,1280]{1,0:T(8,128)(2,1)} %collective-permute-done.3.refs_5_.refs_7_), channel_id=1, source_target_pairs={{0,1},{1,0},{2,3},{3,2},{4,5},{5,4},{6,7},{7,6},{8,9},{9,8},{10,11... | collective-permute-start | bytes 2457608 | tf_op jit(solution)/shard_map/ppermute | solution.py:525
  90.9 24.2 %collective-permute-start.13 = (bf16[2,4,1,96,640]{4,3,2,1,0:T(8,128)(2,1)S(1)}, bf16[2,4,1,96,640]{4,3,2,1,0:T(8,128)(2,1)S(1)}, u32[]{:S(2)}, u32[]{:S(2)}) collective-permute-start(bf16[2,4,1,96,640]{4,3,2,1,0:T(8,128)(2,1)S(1)} %shard_map.143), channel_id=1, source_target_pairs={{0,2},{1,3},{2,0},{3,1},{4,6},{5,7},{6,4},{7,5},{8,10},{9,11},{10,... | collective-permute-start | bytes 2949128 | tf_op jit(solution)/shard_map/ppermute | solution.py:521
  93.1 28.9 %collective-permute-start.15 = (bf16[4,256,512]{2,1,0:T(8,128)(2,1)S(1)}, bf16[4,256,512]{2,1,0:T(8,128)(2,1)S(1)}, u32[]{:S(2)}, u32[]{:S(2)}) collective-permute-start(bf16[4,256,512]{2,1,0:T(8,128)(2,1)S(1)} %copy-done.42), channel_id=1, source_target_pairs={{0,4},{4,0},{8,12},{12,8},{16,20},{20,16},{24,28},{28,24},{1,5},{5... | collective-permute-start | bytes 3145736 | tf_op jit(solution)/shard_map/ppermute | solution.py:511
  117.0 19.2 %collective-permute-start.16 = (bf16[2,2,1,96,640]{4,3,2,1,0:T(8,128)(2,1)S(1)}, bf16[2,2,1,96,640]{4,3,2,1,0:T(8,128)(2,1)S(1)}, u32[]{:S(2)}, u32[]{:S(2)}) collective-permute-start(bf16[2,2,1,96,640]{4,3,2,1,0:T(8,128)(2,1)S(1)} %shard_map.146), channel_id=1, source_target_pairs={{0,8},{4,12},{8,0},{12,4},{16,24},{20,28},{24,16},{28,20},{1,9},{5... | collective-permute-start | bytes 1474568 | tf_op jit(solution)/shard_map/ppermute | solution.py:515
  120.3 29.4 %collective-permute-start.14 = (bf16[2,4,2,80,384]{4,3,2,1,0:T(8,128)(2,1)S(1)}, bf16[2,4,2,80,384]{4,3,2,1,0:T(8,128)(2,1)S(1)}, u32[]{:S(2)}, u32[]{:S(2)}) collective-permute-start(bf16[2,4,2,80,384]{4,3,2,1,0:T(8,128)(2,1)S(1)} %shard_map.147), channel_id=1, source_target_pairs={{0,2},{1,3},{2,0},{3,1},{4,6},{5,7},{6,4},{7,5},{8,10},{9,11},{10,... | collective-permute-start | bytes 2949128 | tf_op jit(solution)/shard_map/ppermute | solution.py:521
  145.3 17.6 %collective-permute-start.22 = (bf16[2,4,2,80,256]{4,3,2,1,0:T(8,128)(2,1)S(1)}, bf16[2,4,2,80,256]{4,3,2,1,0:T(8,128)(2,1)S(1)}, u32[]{:S(2)}, u32[]{:S(2)}) collective-permute-start(bf16[2,4,2,80,256]{4,3,2,1,0:T(8,128)(2,1)S(1)} %shard_map.152), channel_id=1, source_target_pairs={{0,2},{1,3},{2,0},{3,1},{4,6},{5,7},{6,4},{7,5},{8,10},{9,11},{10,... | collective-permute-start | bytes 1966088 | tf_op jit(solution)/shard_map/ppermute | solution.py:521
  148.3 27.8 %collective-permute-start.26 = (bf16[2,4,1,64,640]{4,3,2,1,0:T(8,128)(2,1)S(1)}, bf16[2,4,1,64,640]{4,3,2,1,0:T(8,128)(2,1)S(1)}, u32[]{:S(2)}, u32[]{:S(2)}) collective-permute-start(bf16[2,4,1,64,640]{4,3,2,1,0:T(8,128)(2,1)S(1)} %shard_map.153), channel_id=1, source_target_pairs={{0,2},{1,3},{2,0},{3,1},{4,6},{5,7},{6,4},{7,5},{8,10},{9,11},{10,... | collective-permute-start | bytes 1966088 | tf_op jit(solution)/shard_map/ppermute | solution.py:521
  150.8 17.6 %collective-permute-start.21 = (bf16[2,2,2,80,384]{4,3,2,1,0:T(8,128)(2,1)S(1)}, bf16[2,2,2,80,384]{4,3,2,1,0:T(8,128)(2,1)S(1)}, u32[]{:S(2)}, u32[]{:S(2)}) collective-permute-start(bf16[2,2,2,80,384]{4,3,2,1,0:T(8,128)(2,1)S(1)} %shard_map.154), channel_id=1, source_target_pairs={{0,8},{4,12},{8,0},{12,4},{16,24},{20,28},{24,16},{28,20},{1,9},{5... | collective-permute-start | bytes 1474568 | tf_op jit(solution)/shard_map/ppermute | solution.py:515
  163.9 15.6 %collective-permute-start.25 = (bf16[2,2,2,80,256]{4,3,2,1,0:T(8,128)(2,1)S(1)}, bf16[2,2,2,80,256]{4,3,2,1,0:T(8,128)(2,1)S(1)}, u32[]{:S(2)}, u32[]{:S(2)}) collective-permute-start(bf16[2,2,2,80,256]{4,3,2,1,0:T(8,128)(2,1)S(1)} %shard_map.155), channel_id=1, source_target_pairs={{0,8},{4,12},{8,0},{12,4},{16,24},{20,28},{24,16},{28,20},{1,9},{5... | collective-permute-start | bytes 983048 | tf_op jit(solution)/shard_map/ppermute | solution.py:515
  165.8 18.3 %collective-permute-start.24 = (bf16[2,1,1,96,640]{4,3,2,1,0:T(8,128)(2,1)S(1)}, bf16[2,1,1,96,640]{4,3,2,1,0:T(8,128)(2,1)S(1)}, u32[]{:S(2)}, u32[]{:S(2)}) collective-permute-start(bf16[2,1,1,96,640]{4,3,2,1,0:T(8,128)(2,1)S(1)} %shard_map.150), channel_id=1, source_target_pairs={{0,16},{4,20},{8,24},{12,28},{16,0},{20,4},{24,8},{28,12},{1,17},{... | collective-permute-start | bytes 737288 | tf_op jit(solution)/shard_map/ppermute | solution.py:515
  169.2 22.7 %collective-permute-start.23 = (bf16[2,1,2,80,384]{4,3,2,1,0:T(8,128)(2,1)S(1)}, bf16[2,1,2,80,384]{4,3,2,1,0:T(8,128)(2,1)S(1)}, u32[]{:S(2)}, u32[]{:S(2)}) collective-permute-start(bf16[2,1,2,80,384]{4,3,2,1,0:T(8,128)(2,1)S(1)} %shard_map.156), channel_id=1, source_target_pairs={{0,16},{4,20},{8,24},{12,28},{16,0},{20,4},{24,8},{28,12},{1,17},{... | collective-permute-start | bytes 737288 | tf_op jit(solution)/shard_map/ppermute | solution.py:515
  177.7 19.4 %collective-permute-start.29 = (bf16[2,2,1,64,640]{4,3,2,1,0:T(8,128)(2,1)}, bf16[2,2,1,64,640]{4,3,2,1,0:T(8,128)(2,1)}, u32[]{:S(2)}, u32[]{:S(2)}) collective-permute-start(bf16[2,2,1,64,640]{4,3,2,1,0:T(8,128)(2,1)} %shard_map.157), channel_id=1, source_target_pairs={{0,8},{4,12},{8,0},{12,4},{16,24},{20,28},{24,16},{28,20},{1,9},{5... | collective-permute-start | bytes 983048 | tf_op jit(solution)/shard_map/ppermute | solution.py:515
  180.8 20.2 %collective-permute-start.28 = (bf16[2,1,2,80,256]{4,3,2,1,0:T(8,128)(2,1)}, bf16[2,1,2,80,256]{4,3,2,1,0:T(8,128)(2,1)}, u32[]{:S(2)}, u32[]{:S(2)}) collective-permute-start(bf16[2,1,2,80,256]{4,3,2,1,0:T(8,128)(2,1)} %shard_map.158), channel_id=1, source_target_pairs={{0,16},{4,20},{8,24},{12,28},{16,0},{20,4},{24,8},{28,12},{1,17},{... | collective-permute-start | bytes 491528 | tf_op jit(solution)/shard_map/ppermute | solution.py:515
  195.6 17.0 %collective-permute-start.31 = (bf16[2,96,640]{2,1,0:T(8,128)(2,1)S(1)}, bf16[2,96,640]{2,1,0:T(8,128)(2,1)}, u32[]{:S(2)}, u32[]{:S(2)}) collective-permute-start(bf16[2,96,640]{2,1,0:T(8,128)(2,1)S(1)} %shard_map.159.refs_0_), channel_id=1, source_target_pairs={{0,2},{1,3},{2,0},{3,1},{4,6},{5,7},{6,4},{7,5},{8,10},{9,11},{10,... | collective-permute-start | bytes 737288 | tf_op jit(solution)/shard_map/ppermute | solution.py:521
  204.3 9.8 %collective-permute-start.30 = (bf16[2,2,80,384]{3,2,1,0:T(8,128)(2,1)S(1)}, bf16[2,2,80,384]{3,2,1,0:T(8,128)(2,1)S(1)}, u32[]{:S(2)}, u32[]{:S(2)}) collective-permute-start(bf16[2,2,80,384]{3,2,1,0:T(8,128)(2,1)S(1)} %shard_map.163.refs_0_), channel_id=1, source_target_pairs={{0,2},{1,3},{2,0},{3,1},{4,6},{5,7},{6,4},{7,5},{8,10},{9,11},{10,... | collective-permute-start | bytes 737288 | tf_op jit(solution)/shard_map/ppermute | solution.py:521
  205.5 9.3 %collective-permute-start.34 = (bf16[2,1,1,64,640]{4,3,2,1,0:T(8,128)(2,1)}, bf16[2,1,1,64,640]{4,3,2,1,0:T(8,128)(2,1)S(1)}, u32[]{:S(2)}, u32[]{:S(2)}) collective-permute-start(bf16[2,1,1,64,640]{4,3,2,1,0:T(8,128)(2,1)} %copy-done.36), channel_id=1, source_target_pairs={{0,16},{4,20},{8,24},{12,28},{16,0},{20,4},{24,8},{28,12},{1,17},{... | collective-permute-start | bytes 491528 | tf_op jit(solution)/shard_map/ppermute | solution.py:515
  220.0 9.4 %collective-permute-start.37 = (bf16[2,64,640]{2,1,0:T(8,128)(2,1)S(1)}, bf16[2,64,640]{2,1,0:T(8,128)(2,1)S(1)}, u32[]{:S(2)}, u32[]{:S(2)}) collective-permute-start(bf16[2,64,640]{2,1,0:T(8,128)(2,1)S(1)} %shard_map.167.refs_0_), channel_id=1, source_target_pairs={{0,2},{1,3},{2,0},{3,1},{4,6},{5,7},{6,4},{7,5},{8,10},{9,11},{10,... | collective-permute-start | bytes 491528 | tf_op jit(solution)/shard_map/ppermute | solution.py:521
  220.6 9.9 %collective-permute-start.38 = (bf16[2,2,96,640]{3,2,1,0:T(8,128)(2,1)S(1)}, bf16[2,2,96,640]{3,2,1,0:T(8,128)(2,1)S(1)}, u32[]{:S(2)}, u32[]{:S(2)}) collective-permute-start(bf16[2,2,96,640]{3,2,1,0:T(8,128)(2,1)S(1)} %shard_map.165.refs_0_), channel_id=1, source_target_pairs={{0,1},{1,0},{2,3},{3,2},{4,5},{5,4},{6,7},{7,6},{8,9},{9,8},{10,11... | collective-permute-start | bytes 1474568 | tf_op jit(solution)/shard_map/ppermute | solution.py:525
  (63 other events, 566.7 us)

commit v13 on v10

--- a/solution.py
+++ b/solution.py
@@ -717,15 +717,15 @@
             ins[0].send_z()
             outs[1].send_z()
             ins[1].send_z()
-            outs[0].finish()
             ins[0].finish()
             outs[1].send_z()
             ins[1].finish()
             ins[0].stack_x()
             ins[1].stack_x()
-            outs[0].stack_y(True)
+            outs[0].finish()
             ins[0].stack_y()
             outs[1].finish()
+            outs[0].stack_y(True)
             ins[1].stack_y()
         else:
             outs[0].send_z()

time: 256 us -> 264 us (1.031)
  local copies, waits for them, and re-layouts: 10.8 us -> 17.7 us
    unnamed x86 -> x106, local copies, waits for them, and re-layouts: 10.8 us -> 17.7 us
    ppermute x8, waiting for transfers between devices: 17.7 us -> 21.3 us  [along_y(): return lax.ppermute(value, 'gy', pairs)]
  transfers between devices with their start and end apart: 44 -> 44, of which waited for: 18 -> 19; matrix products, arithmetic and copies ran while one was open for 0% -> 0% of each run, Pallas kernels for 39% -> 38%
where the time goes in v13:
time: 264 us; the launch traced here: 263 us
  Pallas kernels  117 us (44%)
  waiting for transfers between devices  78.6 us (30%)
  starting transfers between devices  47.7 us (18%)
  local copies, waits for them, and re-layouts  17.7 us (7%)
    ppermute x14, waiting for transfers between devices, along_z(): return lax.ppermute(value, 'gx', pairs)  26.9 us
    ppermute x6, waiting for transfers between devices, along_x(): return lax.ppermute(value, 'gx', pairs)  24.6 us
    pallas_call x16, Pallas kernels, reduce_step(): pl.pallas_call(body, grid_spec=pltpu.PrefetchScalarGridSpec(num_scalar_pr...  23.5 us
    ppermute x14, starting transfers between devices, along_z(): return lax.ppermute(value, 'gx', pairs)  22.7 us
    ppermute x8, waiting for transfers between devices, along_y(): return lax.ppermute(value, 'gy', pairs)  21.3 us
    pallas_call x2, Pallas kernels, grad_pre_chunk(): pl.pallas_call(body, grid_spec=pltpu.PrefetchScalarGridSpec(num_scalar_pr...  18.1 us
    unnamed x106, local copies, waits for them, and re-layouts  17.7 us
    pallas_call x2, Pallas kernels, grad_in_chunk(): pl.pallas_call(body, grid_spec=pltpu.PrefetchScalarGridSpec(num_scalar_pr...  14.7 us
  transfers between devices with their start and end apart: 44, of which 19 were waited for; matrix products, arithmetic and copies ran while one was open for 0% of the time, Pallas kernels for 38%

profile of v13, /device:TPU:0, one launch (start us, length us, event | category | flops | bytes accessed | tf_op | source)
XLA Modules:
  0.0 262.7 jit_solution(14073209757631263986)
XLA Ops:
  0.7 5.2 %shard_map.136 = bf16[2816,512]{1,0:T(8,128)(2,1)} custom-call(s32[1]{0:T(128)} %bitcast.8.at_ref, bf16[512,5120]{1,0:T(8,128)(2,1)} %h_ref.4, bf16[512,1280]{1,0:T(8,128)(2,1)} %cot_ref.2), custom_call_target="tpu_custom_call" | custom-call | flops 1 | bytes 1 | tf_op jit(solution)/shard_map/pallas_call | solution.py:81
  5.8 2.9 %collective-permute-start = (bf16[2816,512]{1,0:T(8,128)(2,1)}, bf16[2816,512]{1,0:T(8,128)(2,1)}, u32[]{:S(2)}, u32[]{:S(2)}) collective-permute-start(bf16[2816,512]{1,0:T(8,128)(2,1)} %shard_map.136), channel_id=1, source_target_pairs={{0,4},{4,0},{8,12},{12,8},{16,20},{20,16},{24,28},{28,24},{1,5},{5... | collective-permute-start | bytes 8650760 | tf_op jit(solution)/shard_map/ppermute | solution.py:506
  17.7 5.1 %shard_map.139.refs_0_ = bf16[2816,512]{1,0:T(8,128)(2,1)} custom-call(s32[1]{0:T(128)} %bitcast.5.at_ref, bf16[512,5120]{1,0:T(8,128)(2,1)} %h_ref.4, bf16[512,1280]{1,0:T(8,128)(2,1)} %cot_ref.2), custom_call_target="tpu_custom_call" | custom-call | flops 1 | bytes 1 | tf_op jit(solution)/shard_map/pallas_call | solution.py:81
  22.8 3.9 %shard_map.140.refs_2_ = bf16[4,256,512]{2,1,0:T(8,128)(2,1)} custom-call(s32[1]{0:T(128)} %bitcast.3.at_ref, bf16[512,5120]{1,0:T(8,128)(2,1)} %h_ref.4), custom_call_target="tpu_custom_call" | custom-call | flops 1 | bytes 1 | tf_op jit(solution)/shard_map/pallas_call | solution.py:109
  26.7 4.0 %shard_map.141 = bf16[4,256,512]{2,1,0:T(8,128)(2,1)} custom-call(s32[1]{0:T(128)} %bitcast.8.at_ref, bf16[512,5120]{1,0:T(8,128)(2,1)} %h_ref.4), custom_call_target="tpu_custom_call" | custom-call | flops 1 | bytes 1 | tf_op jit(solution)/shard_map/pallas_call | solution.py:109
  30.7 17.7 %collective-permute-done.1.refs_3_.refs_5_ = bf16[320,1280]{1,0:T(8,128)(2,1)} collective-permute-done((bf16[320,1280]{1,0:T(8,128)(2,1)}, bf16[320,1280]{1,0:T(8,128)(2,1)}, u32[]{:S(2)}, u32[]{:S(2)}) %collective-permute-start.1) | collective-permute-done | bytes 819232 | tf_op jit(solution)/shard_map/ppermute | solution.py:510
  52.1 20.3 %collective-permute-done.refs_1_ = bf16[2816,512]{1,0:T(8,128)(2,1)} collective-permute-done((bf16[2816,512]{1,0:T(8,128)(2,1)}, bf16[2816,512]{1,0:T(8,128)(2,1)}, u32[]{:S(2)}, u32[]{:S(2)}) %collective-permute-start) | collective-permute-done | bytes 2883616 | tf_op jit(solution)/shard_map/ppermute | solution.py:506
  72.4 8.1 %shard_map.142 = (bf16[4,192,640]{2,1,0:T(8,128)(2,1)}, bf16[4,192,640]{2,1,0:T(8,128)(2,1)}, bf16[2,4,192,640]{3,2,1,0:T(8,128)(2,1)S(1)}) custom-call(s32[1]{0:T(128)} %bitcast.c_ref, bf16[2816,512]{1,0:T(8,128)(2,1)S(1)} %copy-done, bf16[2816,512]{1,0:T(8,128)(2,1)} %collective-permute-done.refs_1_), custom_call_target="tpu_custom_call" | custom-call | flops 1 | bytes 1 | tf_op jit(solution)/shard_map/pallas_call | solution.py:166
  87.7 3.2 %shard_map.143 = bf16[2,4,1,96,640]{4,3,2,1,0:T(8,128)(2,1)S(1)} custom-call(s32[3]{0:T(128)S(1)} %pad_add_fusion.2.at_ref, bf16[2,4,1,2,96,640]{5,4,3,2,1,0:T(8,128)(2,1)S(1)} %bitcast.21, bf16[4,1,2,96,640]{4,3,2,1,0:T(8,128)(2,1)} %bitcast.10.refs_1_, bf16[4,1,2,96,640]{4,3,2,1,0:T(8,128)(2,1)} %bitcast.11.refs_2_), custom_call_target="tpu_custom_call" | custom-call | flops 1 | bytes 1 | tf_op jit(solution)/shard_map/pallas_call | solution.py:401
  94.7 10.3 %shard_map.144.g_ref = bf16[4,384,1024]{2,1,0:T(8,128)(2,1)S(1)} custom-call(s32[2]{0:T(128)S(1)} %pad_add_fusion.3.c_ref, bf16[2816,512]{1,0:T(8,128)(2,1)S(1)} %copy-done, bf16[2816,512]{1,0:T(8,128)(2,1)} %collective-permute-done.refs_1_, bf16[320,1280]{1,0:T(8,128)(2,1)S(1)} %copy-done.25, bf16[320,1280]{1,0:T(8,128)(2,1)} %collective-permute-done.1.refs_3_.refs_5_, ...), custom_call_target="tpu_custom_call" | custom-call | flops 1 | bytes 1 | tf_op jit(solution)/shard_map/pallas_call | solution.py:205
  105.0 8.9 %shard_map.145 = (bf16[1280,384]{1,0:T(8,128)(2,1)S(1)}, bf16[1280,384]{1,0:T(8,128)(2,1)S(1)}, bf16[2,1280,384]{2,1,0:T(8,128)(2,1)S(1)}) custom-call(s32[1]{0:T(128)} %bitcast.c_ref, bf16[4,384,1024]{2,1,0:T(8,128)(2,1)S(1)} %shard_map.144.g_ref, bf16[1280,512]{1,0:T(8,128)(2,1)} %shard_map.138.refs_0_, bf16[1280,512]{1,0:T(8,128)(2,1)} %collective-permute-done.10.refs_1_), custom_call_target="tpu_custom_call" | custom-call | flops 1 | bytes 1 | tf_op jit(solution)/shard_map/pallas_call | solution.py:242
  122.0 7.9 %shard_map.148.g_ref = bf16[4,256,1024]{2,1,0:T(8,128)(2,1)S(1)} custom-call(s32[2]{0:T(128)S(1)} %pad_add_fusion.3.c_ref, bf16[2816,512]{1,0:T(8,128)(2,1)S(1)} %copy-done, bf16[2816,512]{1,0:T(8,128)(2,1)} %collective-permute-done.refs_1_, bf16[4,256,512]{2,1,0:T(8,128)(2,1)S(1)} %copy-done.21, bf16[4,256,512]{2,1,0:T(8,128)(2,1)S(1)} %collective-permute-done.15.refs_3_, ...), custom_call_target="tpu_custom_call" | custom-call | flops 1 | bytes 1 | tf_op jit(solution)/shard_map/pallas_call | solution.py:205
  129.9 5.8 %shard_map.149 = (bf16[1280,256]{1,0:T(8,128)(2,1)S(1)}, bf16[1280,256]{1,0:T(8,128)(2,1)S(1)}, bf16[2,1280,256]{2,1,0:T(8,128)(2,1)S(1)}) custom-call(s32[1]{0:T(128)} %bitcast.c_ref, bf16[4,256,1024]{2,1,0:T(8,128)(2,1)S(1)} %shard_map.148.g_ref, bf16[1280,512]{1,0:T(8,128)(2,1)} %shard_map.138.refs_0_, bf16[1280,512]{1,0:T(8,128)(2,1)} %collective-permute-done.10.refs_1_), custom_call_target="tpu_custom_call" | custom-call | flops 1 | bytes 1 | tf_op jit(solution)/shard_map/pallas_call | solution.py:242
  138.6 5.6 %shard_map.151 = (bf16[4,128,640]{2,1,0:T(8,128)(2,1)S(1)}, bf16[4,128,640]{2,1,0:T(8,128)(2,1)S(1)}, bf16[2,4,128,640]{3,2,1,0:T(8,128)(2,1)S(1)}) custom-call(s32[1]{0:T(128)} %bitcast.c_ref, bf16[2816,512]{1,0:T(8,128)(2,1)S(1)} %copy-done, bf16[2816,512]{1,0:T(8,128)(2,1)} %collective-permute-done.refs_1_, bf16[4,256,512]{2,1,0:T(8,128)(2,1)S(1)} %copy-done.21, ...), custom_call_target="tpu_custom_call" | custom-call | flops 1 | bytes 1 | tf_op jit(solution)/shard_map/pallas_call | solution.py:166
  153.0 10.8 %collective-permute-done.22.refs_3_ = bf16[2,4,2,80,256]{4,3,2,1,0:T(8,128)(2,1)S(1)} collective-permute-done((bf16[2,4,2,80,256]{4,3,2,1,0:T(8,128)(2,1)S(1)}, bf16[2,4,2,80,256]{4,3,2,1,0:T(8,128)(2,1)S(1)}, u32[]{:S(2)}, u32[]{:S(2)}) %collective-permute-start.22) | collective-permute-done | bytes 655392 | tf_op jit(solution)/shard_map/ppermute | solution.py:516
  167.5 2.6 %collective-permute-start.23 = (bf16[2,1,2,80,384]{4,3,2,1,0:T(8,128)(2,1)S(1)}, bf16[2,1,2,80,384]{4,3,2,1,0:T(8,128)(2,1)S(1)}, u32[]{:S(2)}, u32[]{:S(2)}) collective-permute-start(bf16[2,1,2,80,384]{4,3,2,1,0:T(8,128)(2,1)S(1)} %shard_map.156), channel_id=1, source_target_pairs={{0,16},{4,20},{8,24},{12,28},{16,0},{20,4},{24,8},{28,12},{1,17},{... | collective-permute-start | bytes 737288 | tf_op jit(solution)/shard_map/ppermute | solution.py:510
  170.1 6.9 %collective-permute-done.25.refs_3_ = bf16[2,4,1,64,640]{4,3,2,1,0:T(8,128)(2,1)S(1)} collective-permute-done((bf16[2,4,1,64,640]{4,3,2,1,0:T(8,128)(2,1)S(1)}, bf16[2,4,1,64,640]{4,3,2,1,0:T(8,128)(2,1)S(1)}, u32[]{:S(2)}, u32[]{:S(2)}) %collective-permute-start.25) | collective-permute-done | bytes 655392 | tf_op jit(solution)/shard_map/ppermute | solution.py:516
  187.8 3.4 %collective-permute-done.28.refs_4_ = bf16[2,2,1,64,640]{4,3,2,1,0:T(8,128)(2,1)S(1)} collective-permute-done((bf16[2,2,1,64,640]{4,3,2,1,0:T(8,128)(2,1)S(1)}, bf16[2,2,1,64,640]{4,3,2,1,0:T(8,128)(2,1)S(1)}, u32[]{:S(2)}, u32[]{:S(2)}) %collective-permute-start.28) | collective-permute-done | bytes 327712 | tf_op jit(solution)/shard_map/ppermute | solution.py:510
  230.2 6.2 %shard_map.169 = (f32[160,5120]{1,0:T(8,128)}, f32[160,5120]{1,0:T(8,128)}, f32[160,5120]{1,0:T(8,128)S(1)}, f32[16,128]{1,0:T(8,128)S(1)}) custom-call(s32[1]{0:T(128)} %bitcast.c_ref, f32[160,5120]{1,0:T(8,128)S(1)} %copy-done.10, f32[160,5120]{1,0:T(8,128)S(1)} %copy-done.31, f32[160,5120]{1,0:T(8,128)S(1)} %copy-done.32, ...), custom_call_target="tpu_custom_call" | custom-call | flops 1 | bytes 1 | tf_op jit(solution)/shard_map/pallas_call | solution.py:451
  238.6 5.4 %shard_map.171 = (f32[640,1280]{1,0:T(8,128)}, f32[640,1280]{1,0:T(8,128)}, f32[640,1280]{1,0:T(8,128)S(1)}, f32[32,128]{1,0:T(8,128)S(1)}) custom-call(s32[1]{0:T(128)} %bitcast.c_ref, f32[640,1280]{1,0:T(8,128)S(1)} %copy-done.5, f32[640,1280]{1,0:T(8,128)S(1)} %copy-done.33, f32[640,1280]{1,0:T(8,128)S(1)} %copy-done.34, ...), custom_call_target="tpu_custom_call" | custom-call | flops 1 | bytes 1 | tf_op jit(solution)/shard_map/pallas_call | solution.py:451
  244.1 3.7 %collective-permute-start.42 = (f32[32,128]{1,0:T(8,128)S(1)}, f32[32,128]{1,0:T(8,128)S(1)}, u32[]{:S(2)}, u32[]{:S(2)}) collective-permute-start(f32[32,128]{1,0:T(8,128)S(1)} %get-tuple-element.345.refs_0_), channel_id=1, source_target_pairs={{0,24},{4,28},{8,16},{12,20},{16,8},{20,12},{24,0},{28,4},{1,25},{... | collective-permute-start | bytes 49160 | tf_op jit(solution)/shard_map/ppermute | solution.py:510
  249.6 2.8 %collective-permute-done.41.refs_2_ = f32[32,128]{1,0:T(8,128)S(1)} collective-permute-done((f32[32,128]{1,0:T(8,128)S(1)}, f32[32,128]{1,0:T(8,128)S(1)}, u32[]{:S(2)}, u32[]{:S(2)}) %collective-permute-start.41) | collective-permute-done | bytes 16416 | tf_op jit(solution)/shard_map/ppermute | solution.py:510
  256.2 3.2 %shard_map.173 = f32[160,5120]{1,0:T(8,128)} custom-call(f32[160,5120]{1,0:T(8,128)S(1)} %copy-done.10, f32[160,5120]{1,0:T(8,128)S(1)} %get-tuple-element.350.u_ref, f32[32,128]{1,0:T(8,128)S(1)} %shard_map.172.refs_0_, f32[32,128]{1,0:T(8,128)S(1)} %collective-permute-done.43.refs_1_), custom_call_target="tpu_custom_call" | custom-call | flops 1 | bytes 1 | tf_op jit(solution)/shard_map/pallas_call | solution.py:478
  259.5 3.2 %shard_map.174 = f32[640,1280]{1,0:T(8,128)} custom-call(f32[640,1280]{1,0:T(8,128)S(1)} %copy-done.5, f32[640,1280]{1,0:T(8,128)S(1)} %get-tuple-element.357.u_ref, f32[32,128]{1,0:T(8,128)S(1)} %shard_map.172.refs_0_, f32[32,128]{1,0:T(8,128)S(1)} %collective-permute-done.43.refs_1_), custom_call_target="tpu_custom_call" | custom-call | flops 1 | bytes 1 | tf_op jit(solution)/shard_map/pallas_call | solution.py:478
  (213 shorter events, 104.3 us)
Async XLA Ops:
  5.8 66.6 %collective-permute-start = (bf16[2816,512]{1,0:T(8,128)(2,1)}, bf16[2816,512]{1,0:T(8,128)(2,1)}, u32[]{:S(2)}, u32[]{:S(2)}) collective-permute-start(bf16[2816,512]{1,0:T(8,128)(2,1)} %shard_map.136), channel_id=1, source_target_pairs={{0,4},{4,0},{8,12},{12,8},{16,20},{20,16},{24,28},{28,24},{1,5},{5... | collective-permute-start | bytes 8650760 | tf_op jit(solution)/shard_map/ppermute | solution.py:506
  11.0 37.4 %collective-permute-start.1 = (bf16[320,1280]{1,0:T(8,128)(2,1)}, bf16[320,1280]{1,0:T(8,128)(2,1)}, u32[]{:S(2)}, u32[]{:S(2)}) collective-permute-start(bf16[320,1280]{1,0:T(8,128)(2,1)} %shard_map.137.refs_2_.refs_4_), channel_id=1, source_target_pairs={{0,8},{4,12},{8,0},{12,4},{16,24},{20,28},{24,16},{28,20},{1,9},{5... | collective-permute-start | bytes 2457608 | tf_op jit(solution)/shard_map/ppermute | solution.py:510
  12.5 38.3 %collective-permute-start.2 = (bf16[320,1280]{1,0:T(8,128)(2,1)}, bf16[320,1280]{1,0:T(8,128)(2,1)}, u32[]{:S(2)}, u32[]{:S(2)}) collective-permute-start(bf16[320,1280]{1,0:T(8,128)(2,1)} %shard_map.137.refs_2_.refs_4_), channel_id=1, source_target_pairs={{0,16},{4,20},{8,24},{12,28},{16,0},{20,4},{24,8},{28,12},{1,17},{... | collective-permute-start | bytes 2457608 | tf_op jit(solution)/shard_map/ppermute | solution.py:510
  50.8 31.5 %collective-permute-start.3 = (bf16[320,1280]{1,0:T(8,128)(2,1)}, bf16[320,1280]{1,0:T(8,128)(2,1)}, u32[]{:S(2)}, u32[]{:S(2)}) collective-permute-start(bf16[320,1280]{1,0:T(8,128)(2,1)} %collective-permute-done.2.refs_4_.refs_6_), channel_id=1, source_target_pairs={{0,8},{4,12},{8,0},{12,4},{16,24},{20,28},{24,16},{28,20},{1,9},{5... | collective-permute-start | bytes 2457608 | tf_op jit(solution)/shard_map/ppermute | solution.py:510
  51.2 53.8 %collective-permute-start.10 = (bf16[1280,512]{1,0:T(8,128)(2,1)}, bf16[1280,512]{1,0:T(8,128)(2,1)}, u32[]{:S(2)}, u32[]{:S(2)}) collective-permute-start(bf16[1280,512]{1,0:T(8,128)(2,1)} %shard_map.138.refs_0_), channel_id=1, source_target_pairs={{0,4},{4,0},{8,12},{12,8},{16,20},{20,16},{24,28},{28,24},{1,5},{5... | collective-permute-start | bytes 3932168 | tf_op jit(solution)/shard_map/ppermute | solution.py:506
  82.3 12.4 %collective-permute-start.6 = (bf16[320,1280]{1,0:T(8,128)(2,1)}, bf16[320,1280]{1,0:T(8,128)(2,1)}, u32[]{:S(2)}, u32[]{:S(2)}) collective-permute-start(bf16[320,1280]{1,0:T(8,128)(2,1)} %collective-permute-done.2.refs_4_.refs_6_), channel_id=1, source_target_pairs={{0,1},{1,0},{2,3},{3,2},{4,5},{5,4},{6,7},{7,6},{8,9},{9,8},{10,11... | collective-permute-start | bytes 2457608 | tf_op jit(solution)/shard_map/ppermute | solution.py:520
  82.3 12.3 %collective-permute-start.7 = (bf16[320,1280]{1,0:T(8,128)(2,1)}, bf16[320,1280]{1,0:T(8,128)(2,1)}, u32[]{:S(2)}, u32[]{:S(2)}) collective-permute-start(bf16[320,1280]{1,0:T(8,128)(2,1)} %collective-permute-done.3.refs_5_.refs_7_), channel_id=1, source_target_pairs={{0,1},{1,0},{2,3},{3,2},{4,5},{5,4},{6,7},{7,6},{8,9},{9,8},{10,11... | collective-permute-start | bytes 2457608 | tf_op jit(solution)/shard_map/ppermute | solution.py:520
  90.9 24.2 %collective-permute-start.13 = (bf16[2,4,1,96,640]{4,3,2,1,0:T(8,128)(2,1)S(1)}, bf16[2,4,1,96,640]{4,3,2,1,0:T(8,128)(2,1)S(1)}, u32[]{:S(2)}, u32[]{:S(2)}) collective-permute-start(bf16[2,4,1,96,640]{4,3,2,1,0:T(8,128)(2,1)S(1)} %shard_map.143), channel_id=1, source_target_pairs={{0,2},{1,3},{2,0},{3,1},{4,6},{5,7},{6,4},{7,5},{8,10},{9,11},{10,... | collective-permute-start | bytes 2949128 | tf_op jit(solution)/shard_map/ppermute | solution.py:516
  93.1 28.9 %collective-permute-start.15 = (bf16[4,256,512]{2,1,0:T(8,128)(2,1)S(1)}, bf16[4,256,512]{2,1,0:T(8,128)(2,1)S(1)}, u32[]{:S(2)}, u32[]{:S(2)}) collective-permute-start(bf16[4,256,512]{2,1,0:T(8,128)(2,1)S(1)} %copy-done.52), channel_id=1, source_target_pairs={{0,4},{4,0},{8,12},{12,8},{16,20},{20,16},{24,28},{28,24},{1,5},{5... | collective-permute-start | bytes 3145736 | tf_op jit(solution)/shard_map/ppermute | solution.py:506
  117.0 19.2 %collective-permute-start.16 = (bf16[2,2,1,96,640]{4,3,2,1,0:T(8,128)(2,1)S(1)}, bf16[2,2,1,96,640]{4,3,2,1,0:T(8,128)(2,1)S(1)}, u32[]{:S(2)}, u32[]{:S(2)}) collective-permute-start(bf16[2,2,1,96,640]{4,3,2,1,0:T(8,128)(2,1)S(1)} %shard_map.146), channel_id=1, source_target_pairs={{0,8},{4,12},{8,0},{12,4},{16,24},{20,28},{24,16},{28,20},{1,9},{5... | collective-permute-start | bytes 1474568 | tf_op jit(solution)/shard_map/ppermute | solution.py:510
  120.3 29.9 %collective-permute-start.14 = (bf16[2,4,2,80,384]{4,3,2,1,0:T(8,128)(2,1)S(1)}, bf16[2,4,2,80,384]{4,3,2,1,0:T(8,128)(2,1)S(1)}, u32[]{:S(2)}, u32[]{:S(2)}) collective-permute-start(bf16[2,4,2,80,384]{4,3,2,1,0:T(8,128)(2,1)S(1)} %shard_map.147), channel_id=1, source_target_pairs={{0,2},{1,3},{2,0},{3,1},{4,6},{5,7},{6,4},{7,5},{8,10},{9,11},{10,... | collective-permute-start | bytes 2949128 | tf_op jit(solution)/shard_map/ppermute | solution.py:516
  135.7 9.1 %collective-permute-start.19 = (bf16[1280,256]{1,0:T(8,128)(2,1)S(1)}, bf16[1280,256]{1,0:T(8,128)(2,1)S(1)}, u32[]{:S(2)}, u32[]{:S(2)}) collective-permute-start(bf16[1280,256]{1,0:T(8,128)(2,1)S(1)} %get-tuple-element.252), channel_id=1, source_target_pairs={{0,1},{1,0},{2,3},{3,2},{4,5},{5,4},{6,7},{7,6},{8,9},{9,8},{10,11... | collective-permute-start | bytes 1966088 | tf_op jit(solution)/shard_map/ppermute | solution.py:520
  135.8 9.1 %collective-permute-start.20 = (bf16[1280,256]{1,0:T(8,128)(2,1)S(1)}, bf16[1280,256]{1,0:T(8,128)(2,1)S(1)}, u32[]{:S(2)}, u32[]{:S(2)}) collective-permute-start(bf16[1280,256]{1,0:T(8,128)(2,1)S(1)} %get-tuple-element.253), channel_id=1, source_target_pairs={{0,1},{1,0},{2,3},{3,2},{4,5},{5,4},{6,7},{7,6},{8,9},{9,8},{10,11... | collective-permute-start | bytes 1966088 | tf_op jit(solution)/shard_map/ppermute | solution.py:520
  146.1 17.6 %collective-permute-start.22 = (bf16[2,4,2,80,256]{4,3,2,1,0:T(8,128)(2,1)S(1)}, bf16[2,4,2,80,256]{4,3,2,1,0:T(8,128)(2,1)S(1)}, u32[]{:S(2)}, u32[]{:S(2)}) collective-permute-start(bf16[2,4,2,80,256]{4,3,2,1,0:T(8,128)(2,1)S(1)} %shard_map.152), channel_id=1, source_target_pairs={{0,2},{1,3},{2,0},{3,1},{4,6},{5,7},{6,4},{7,5},{8,10},{9,11},{10,... | collective-permute-start | bytes 1966088 | tf_op jit(solution)/shard_map/ppermute | solution.py:516
  149.0 28.0 %collective-permute-start.25 = (bf16[2,4,1,64,640]{4,3,2,1,0:T(8,128)(2,1)S(1)}, bf16[2,4,1,64,640]{4,3,2,1,0:T(8,128)(2,1)S(1)}, u32[]{:S(2)}, u32[]{:S(2)}) collective-permute-start(bf16[2,4,1,64,640]{4,3,2,1,0:T(8,128)(2,1)S(1)} %shard_map.153), channel_id=1, source_target_pairs={{0,2},{1,3},{2,0},{3,1},{4,6},{5,7},{6,4},{7,5},{8,10},{9,11},{10,... | collective-permute-start | bytes 1966088 | tf_op jit(solution)/shard_map/ppermute | solution.py:516
  151.3 15.3 %collective-permute-start.21 = (bf16[2,2,2,80,384]{4,3,2,1,0:T(8,128)(2,1)S(1)}, bf16[2,2,2,80,384]{4,3,2,1,0:T(8,128)(2,1)S(1)}, u32[]{:S(2)}, u32[]{:S(2)}) collective-permute-start(bf16[2,2,2,80,384]{4,3,2,1,0:T(8,128)(2,1)S(1)} %shard_map.154), channel_id=1, source_target_pairs={{0,8},{4,12},{8,0},{12,4},{16,24},{20,28},{24,16},{28,20},{1,9},{5... | collective-permute-start | bytes 1474568 | tf_op jit(solution)/shard_map/ppermute | solution.py:510
  164.8 15.0 %collective-permute-start.24 = (bf16[2,2,2,80,256]{4,3,2,1,0:T(8,128)(2,1)S(1)}, bf16[2,2,2,80,256]{4,3,2,1,0:T(8,128)(2,1)S(1)}, u32[]{:S(2)}, u32[]{:S(2)}) collective-permute-start(bf16[2,2,2,80,256]{4,3,2,1,0:T(8,128)(2,1)S(1)} %shard_map.155), channel_id=1, source_target_pairs={{0,8},{4,12},{8,0},{12,4},{16,24},{20,28},{24,16},{28,20},{1,9},{5... | collective-permute-start | bytes 983048 | tf_op jit(solution)/shard_map/ppermute | solution.py:510
  167.5 16.3 %collective-permute-start.23 = (bf16[2,1,2,80,384]{4,3,2,1,0:T(8,128)(2,1)S(1)}, bf16[2,1,2,80,384]{4,3,2,1,0:T(8,128)(2,1)S(1)}, u32[]{:S(2)}, u32[]{:S(2)}) collective-permute-start(bf16[2,1,2,80,384]{4,3,2,1,0:T(8,128)(2,1)S(1)} %shard_map.156), channel_id=1, source_target_pairs={{0,16},{4,20},{8,24},{12,28},{16,0},{20,4},{24,8},{28,12},{1,17},{... | collective-permute-start | bytes 737288 | tf_op jit(solution)/shard_map/ppermute | solution.py:510
  177.9 13.3 %collective-permute-start.28 = (bf16[2,2,1,64,640]{4,3,2,1,0:T(8,128)(2,1)S(1)}, bf16[2,2,1,64,640]{4,3,2,1,0:T(8,128)(2,1)S(1)}, u32[]{:S(2)}, u32[]{:S(2)}) collective-permute-start(bf16[2,2,1,64,640]{4,3,2,1,0:T(8,128)(2,1)S(1)} %shard_map.157), channel_id=1, source_target_pairs={{0,8},{4,12},{8,0},{12,4},{16,24},{20,28},{24,16},{28,20},{1,9},{5... | collective-permute-start | bytes 983048 | tf_op jit(solution)/shard_map/ppermute | solution.py:510
  181.1 16.4 %collective-permute-start.27 = (bf16[2,1,2,80,256]{4,3,2,1,0:T(8,128)(2,1)}, bf16[2,1,2,80,256]{4,3,2,1,0:T(8,128)(2,1)}, u32[]{:S(2)}, u32[]{:S(2)}) collective-permute-start(bf16[2,1,2,80,256]{4,3,2,1,0:T(8,128)(2,1)} %shard_map.158), channel_id=1, source_target_pairs={{0,16},{4,20},{8,24},{12,28},{16,0},{20,4},{24,8},{28,12},{1,17},{... | collective-permute-start | bytes 491528 | tf_op jit(solution)/shard_map/ppermute | solution.py:510
  185.9 19.2 %collective-permute-start.26 = (bf16[2,80,384]{2,1,0:T(8,128)(2,1)}, bf16[2,80,384]{2,1,0:T(8,128)(2,1)}, u32[]{:S(2)}, u32[]{:S(2)}) collective-permute-start(bf16[2,80,384]{2,1,0:T(8,128)(2,1)} %get-tuple-element.289), channel_id=1, source_target_pairs={{0,4},{4,0},{8,12},{12,8},{16,20},{20,16},{24,28},{28,24},{1,5},{5... | collective-permute-start | bytes 368648 | tf_op jit(solution)/shard_map/ppermute | solution.py:506
  187.4 28.0 %collective-permute-start.30 = (bf16[2,1,1,96,640]{4,3,2,1,0:T(8,128)(2,1)}, bf16[2,1,1,96,640]{4,3,2,1,0:T(8,128)(2,1)}, u32[]{:S(2)}, u32[]{:S(2)}) collective-permute-start(bf16[2,1,1,96,640]{4,3,2,1,0:T(8,128)(2,1)} %shard_map.150), channel_id=1, source_target_pairs={{0,16},{4,20},{8,24},{12,28},{16,0},{20,4},{24,8},{28,12},{1,17},{... | collective-permute-start | bytes 737288 | tf_op jit(solution)/shard_map/ppermute | solution.py:510
  206.6 15.5 %collective-permute-start.29 = (bf16[2,2,80,384]{3,2,1,0:T(8,128)(2,1)S(1)}, bf16[2,2,80,384]{3,2,1,0:T(8,128)(2,1)}, u32[]{:S(2)}, u32[]{:S(2)}) collective-permute-start(bf16[2,2,80,384]{3,2,1,0:T(8,128)(2,1)S(1)} %shard_map.162.refs_0_), channel_id=1, source_target_pairs={{0,2},{1,3},{2,0},{3,1},{4,6},{5,7},{6,4},{7,5},{8,10},{9,11},{10,... | collective-permute-start | bytes 737288 | tf_op jit(solution)/shard_map/ppermute | solution.py:516
  210.3 13.3 %collective-permute-start.34 = (bf16[2,1,1,64,640]{4,3,2,1,0:T(8,128)(2,1)}, bf16[2,1,1,64,640]{4,3,2,1,0:T(8,128)(2,1)S(1)}, u32[]{:S(2)}, u32[]{:S(2)}) collective-permute-start(bf16[2,1,1,64,640]{4,3,2,1,0:T(8,128)(2,1)} %copy-done.47), channel_id=1, source_target_pairs={{0,16},{4,20},{8,24},{12,28},{16,0},{20,4},{24,8},{28,12},{1,17},{... | collective-permute-start | bytes 491528 | tf_op jit(solution)/shard_map/ppermute | solution.py:510
  (73 other events, 679.4 us)

commit v14 on v10

--- a/solution.py
+++ b/solution.py
@@ -714,10 +714,10 @@
             outs[1].send_y()
             ins[0].send_z()
             ins[1].send_z()
+            outs[0].finish()
             ins[0].send_z()
             outs[1].send_z()
             ins[1].send_z()
-            outs[0].finish()
             ins[0].finish()
             outs[1].send_z()
             ins[1].finish()

time: 256 us -> 253 us (0.988)
  waiting for transfers between devices: 77.7 us -> 74 us
    ppermute x8, waiting for transfers between devices: 17.7 us -> 9.39 us  [along_y(): return lax.ppermute(value, 'gy', pairs)]
    ppermute x14, waiting for transfers between devices: 29.3 us -> 34.4 us  [along_z(): return lax.ppermute(value, 'gx', pairs)]
  transfers between devices with their start and end apart: 44 -> 44, of which waited for: 18 -> 21; matrix products, arithmetic and copies ran while one was open for 0% -> 0% of each run, Pallas kernels for 39% -> 40%
where the time goes in v14:
time: 253 us; the launch traced here: 252 us
  Pallas kernels  118 us (47%)
  waiting for transfers between devices  74 us (29%)
  starting transfers between devices  48.5 us (19%)
  local copies, waits for them, and re-layouts  10.8 us (4%)
    ppermute x14, waiting for transfers between devices, along_z(): return lax.ppermute(value, 'gx', pairs)  34.4 us
    ppermute x14, starting transfers between devices, along_z(): return lax.ppermute(value, 'gx', pairs)  25.9 us
    pallas_call x16, Pallas kernels, reduce_step(): pl.pallas_call(body, grid_spec=pltpu.PrefetchScalarGridSpec(num_scalar_pr...  24.7 us
    ppermute x6, waiting for transfers between devices, along_x(): return lax.ppermute(value, 'gx', pairs)  24.3 us
    pallas_call x2, Pallas kernels, grad_pre_chunk(): pl.pallas_call(body, grid_spec=pltpu.PrefetchScalarGridSpec(num_scalar_pr...  18.1 us
    pallas_call x2, Pallas kernels, grad_in_chunk(): pl.pallas_call(body, grid_spec=pltpu.PrefetchScalarGridSpec(num_scalar_pr...  14.7 us
    pallas_call x2, Pallas kernels, grad_out_chunk(): pl.pallas_call(body, grid_spec=pltpu.PrefetchScalarGridSpec(num_scalar_pr...  13.7 us
    pallas_call x2, Pallas kernels, moments_kernel(): pl.pallas_call(body, grid_spec=pltpu.PrefetchScalarGridSpec(num_scalar_pr...  11.6 us
  transfers between devices with their start and end apart: 44, of which 21 were waited for; matrix products, arithmetic and copies ran while one was open for 0% of the time, Pallas kernels for 40%

profile of v14, /device:TPU:0, one launch (start us, length us, event | category | flops | bytes accessed | tf_op | source)
XLA Modules:
  0.0 252.3 jit_solution(16487471037229735727)
XLA Ops:
  0.7 5.2 %shard_map.136 = bf16[2816,512]{1,0:T(8,128)(2,1)} custom-call(s32[1]{0:T(128)} %bitcast.8.at_ref, bf16[512,5120]{1,0:T(8,128)(2,1)} %h_ref.4, bf16[512,1280]{1,0:T(8,128)(2,1)} %cot_ref.2), custom_call_target="tpu_custom_call" | custom-call | flops 1 | bytes 1 | tf_op jit(solution)/shard_map/pallas_call | solution.py:81
  5.8 2.9 %collective-permute-start = (bf16[2816,512]{1,0:T(8,128)(2,1)}, bf16[2816,512]{1,0:T(8,128)(2,1)}, u32[]{:S(2)}, u32[]{:S(2)}) collective-permute-start(bf16[2816,512]{1,0:T(8,128)(2,1)} %shard_map.136), channel_id=1, source_target_pairs={{0,4},{4,0},{8,12},{12,8},{16,20},{20,16},{24,28},{28,24},{1,5},{5... | collective-permute-start | bytes 8650760 | tf_op jit(solution)/shard_map/ppermute | solution.py:506
  17.7 5.1 %shard_map.139.refs_0_ = bf16[2816,512]{1,0:T(8,128)(2,1)} custom-call(s32[1]{0:T(128)} %bitcast.5.at_ref, bf16[512,5120]{1,0:T(8,128)(2,1)} %h_ref.4, bf16[512,1280]{1,0:T(8,128)(2,1)} %cot_ref.2), custom_call_target="tpu_custom_call" | custom-call | flops 1 | bytes 1 | tf_op jit(solution)/shard_map/pallas_call | solution.py:81
  22.8 3.9 %shard_map.140.refs_2_ = bf16[4,256,512]{2,1,0:T(8,128)(2,1)} custom-call(s32[1]{0:T(128)} %bitcast.3.at_ref, bf16[512,5120]{1,0:T(8,128)(2,1)} %h_ref.4), custom_call_target="tpu_custom_call" | custom-call | flops 1 | bytes 1 | tf_op jit(solution)/shard_map/pallas_call | solution.py:109
  26.7 4.0 %shard_map.141 = bf16[4,256,512]{2,1,0:T(8,128)(2,1)} custom-call(s32[1]{0:T(128)} %bitcast.8.at_ref, bf16[512,5120]{1,0:T(8,128)(2,1)} %h_ref.4), custom_call_target="tpu_custom_call" | custom-call | flops 1 | bytes 1 | tf_op jit(solution)/shard_map/pallas_call | solution.py:109
  30.7 17.7 %collective-permute-done.1.refs_3_.refs_5_ = bf16[320,1280]{1,0:T(8,128)(2,1)} collective-permute-done((bf16[320,1280]{1,0:T(8,128)(2,1)}, bf16[320,1280]{1,0:T(8,128)(2,1)}, u32[]{:S(2)}, u32[]{:S(2)}) %collective-permute-start.1) | collective-permute-done | bytes 819232 | tf_op jit(solution)/shard_map/ppermute | solution.py:510
  52.1 20.2 %collective-permute-done.refs_1_ = bf16[2816,512]{1,0:T(8,128)(2,1)} collective-permute-done((bf16[2816,512]{1,0:T(8,128)(2,1)}, bf16[2816,512]{1,0:T(8,128)(2,1)}, u32[]{:S(2)}, u32[]{:S(2)}) %collective-permute-start) | collective-permute-done | bytes 2883616 | tf_op jit(solution)/shard_map/ppermute | solution.py:506
  72.4 8.1 %shard_map.142 = (bf16[4,192,640]{2,1,0:T(8,128)(2,1)}, bf16[4,192,640]{2,1,0:T(8,128)(2,1)}, bf16[2,4,192,640]{3,2,1,0:T(8,128)(2,1)S(1)}) custom-call(s32[1]{0:T(128)} %bitcast.c_ref, bf16[2816,512]{1,0:T(8,128)(2,1)S(1)} %copy-done, bf16[2816,512]{1,0:T(8,128)(2,1)} %collective-permute-done.refs_1_), custom_call_target="tpu_custom_call" | custom-call | flops 1 | bytes 1 | tf_op jit(solution)/shard_map/pallas_call | solution.py:166
  87.7 3.2 %shard_map.143 = bf16[2,4,1,96,640]{4,3,2,1,0:T(8,128)(2,1)S(1)} custom-call(s32[3]{0:T(128)S(1)} %pad_add_fusion.2.at_ref, bf16[2,4,1,2,96,640]{5,4,3,2,1,0:T(8,128)(2,1)S(1)} %bitcast.21, bf16[4,1,2,96,640]{4,3,2,1,0:T(8,128)(2,1)} %bitcast.10.refs_1_, bf16[4,1,2,96,640]{4,3,2,1,0:T(8,128)(2,1)} %bitcast.11.refs_2_), custom_call_target="tpu_custom_call" | custom-call | flops 1 | bytes 1 | tf_op jit(solution)/shard_map/pallas_call | solution.py:401
  94.7 10.3 %shard_map.144.g_ref = bf16[4,384,1024]{2,1,0:T(8,128)(2,1)S(1)} custom-call(s32[2]{0:T(128)S(1)} %pad_add_fusion.3.c_ref, bf16[2816,512]{1,0:T(8,128)(2,1)S(1)} %copy-done, bf16[2816,512]{1,0:T(8,128)(2,1)} %collective-permute-done.refs_1_, bf16[320,1280]{1,0:T(8,128)(2,1)S(1)} %copy-done.19, bf16[320,1280]{1,0:T(8,128)(2,1)} %collective-permute-done.1.refs_3_.refs_5_, ...), custom_call_target="tpu_custom_call" | custom-call | flops 1 | bytes 1 | tf_op jit(solution)/shard_map/pallas_call | solution.py:205
  105.0 8.9 %shard_map.145 = (bf16[1280,384]{1,0:T(8,128)(2,1)S(1)}, bf16[1280,384]{1,0:T(8,128)(2,1)S(1)}, bf16[2,1280,384]{2,1,0:T(8,128)(2,1)S(1)}) custom-call(s32[1]{0:T(128)} %bitcast.c_ref, bf16[4,384,1024]{2,1,0:T(8,128)(2,1)S(1)} %shard_map.144.g_ref, bf16[1280,512]{1,0:T(8,128)(2,1)} %shard_map.138.refs_0_, bf16[1280,512]{1,0:T(8,128)(2,1)} %collective-permute-done.10.refs_1_), custom_call_target="tpu_custom_call" | custom-call | flops 1 | bytes 1 | tf_op jit(solution)/shard_map/pallas_call | solution.py:242
  122.0 7.9 %shard_map.148.g_ref = bf16[4,256,1024]{2,1,0:T(8,128)(2,1)S(1)} custom-call(s32[2]{0:T(128)S(1)} %pad_add_fusion.3.c_ref, bf16[2816,512]{1,0:T(8,128)(2,1)S(1)} %copy-done, bf16[2816,512]{1,0:T(8,128)(2,1)} %collective-permute-done.refs_1_, bf16[4,256,512]{2,1,0:T(8,128)(2,1)S(1)} %copy-done.17, bf16[4,256,512]{2,1,0:T(8,128)(2,1)S(1)} %collective-permute-done.15.refs_3_, ...), custom_call_target="tpu_custom_call" | custom-call | flops 1 | bytes 1 | tf_op jit(solution)/shard_map/pallas_call | solution.py:205
  129.9 5.8 %shard_map.149 = (bf16[1280,256]{1,0:T(8,128)(2,1)S(1)}, bf16[1280,256]{1,0:T(8,128)(2,1)S(1)}, bf16[2,1280,256]{2,1,0:T(8,128)(2,1)S(1)}) custom-call(s32[1]{0:T(128)} %bitcast.c_ref, bf16[4,256,1024]{2,1,0:T(8,128)(2,1)S(1)} %shard_map.148.g_ref, bf16[1280,512]{1,0:T(8,128)(2,1)} %shard_map.138.refs_0_, bf16[1280,512]{1,0:T(8,128)(2,1)} %collective-permute-done.10.refs_1_), custom_call_target="tpu_custom_call" | custom-call | flops 1 | bytes 1 | tf_op jit(solution)/shard_map/pallas_call | solution.py:242
  137.9 5.6 %shard_map.151 = (bf16[4,128,640]{2,1,0:T(8,128)(2,1)S(1)}, bf16[4,128,640]{2,1,0:T(8,128)(2,1)S(1)}, bf16[2,4,128,640]{3,2,1,0:T(8,128)(2,1)S(1)}) custom-call(s32[1]{0:T(128)} %bitcast.c_ref, bf16[2816,512]{1,0:T(8,128)(2,1)S(1)} %copy-done, bf16[2816,512]{1,0:T(8,128)(2,1)} %collective-permute-done.refs_1_, bf16[4,256,512]{2,1,0:T(8,128)(2,1)S(1)} %copy-done.17, ...), custom_call_target="tpu_custom_call" | custom-call | flops 1 | bytes 1 | tf_op jit(solution)/shard_map/pallas_call | solution.py:166
  155.0 7.9 %collective-permute-done.23.refs_3_ = bf16[2,4,2,80,256]{4,3,2,1,0:T(8,128)(2,1)S(1)} collective-permute-done((bf16[2,4,2,80,256]{4,3,2,1,0:T(8,128)(2,1)S(1)}, bf16[2,4,2,80,256]{4,3,2,1,0:T(8,128)(2,1)S(1)}, u32[]{:S(2)}, u32[]{:S(2)}) %collective-permute-start.23) | collective-permute-done | bytes 655392 | tf_op jit(solution)/shard_map/ppermute | solution.py:516
  165.8 3.6 %collective-permute-done.22.refs_5_ = bf16[2,1,1,96,640]{4,3,2,1,0:T(8,128)(2,1)S(1)} collective-permute-done((bf16[2,1,1,96,640]{4,3,2,1,0:T(8,128)(2,1)S(1)}, bf16[2,1,1,96,640]{4,3,2,1,0:T(8,128)(2,1)S(1)}, u32[]{:S(2)}, u32[]{:S(2)}) %collective-permute-start.22) | collective-permute-done | bytes 245792 | tf_op jit(solution)/shard_map/ppermute | solution.py:510
  171.9 3.4 %collective-permute-start.24 = (bf16[2,1,2,80,384]{4,3,2,1,0:T(8,128)(2,1)S(1)}, bf16[2,1,2,80,384]{4,3,2,1,0:T(8,128)(2,1)S(1)}, u32[]{:S(2)}, u32[]{:S(2)}) collective-permute-start(bf16[2,1,2,80,384]{4,3,2,1,0:T(8,128)(2,1)S(1)} %shard_map.157), channel_id=1, source_target_pairs={{0,16},{4,20},{8,24},{12,28},{16,0},{20,4},{24,8},{28,12},{1,17},{... | collective-permute-start | bytes 737288 | tf_op jit(solution)/shard_map/ppermute | solution.py:510
  189.5 2.6 %collective-permute-done.29.refs_4_ = bf16[2,2,1,64,640]{4,3,2,1,0:T(8,128)(2,1)} collective-permute-done((bf16[2,2,1,64,640]{4,3,2,1,0:T(8,128)(2,1)}, bf16[2,2,1,64,640]{4,3,2,1,0:T(8,128)(2,1)}, u32[]{:S(2)}, u32[]{:S(2)}) %collective-permute-start.29) | collective-permute-done | bytes 327712 | tf_op jit(solution)/shard_map/ppermute | solution.py:510
  220.1 6.2 %shard_map.169 = (f32[160,5120]{1,0:T(8,128)}, f32[160,5120]{1,0:T(8,128)}, f32[160,5120]{1,0:T(8,128)S(1)}, f32[16,128]{1,0:T(8,128)S(1)}) custom-call(s32[1]{0:T(128)} %bitcast.c_ref, f32[160,5120]{1,0:T(8,128)S(1)} %copy-done.9, f32[160,5120]{1,0:T(8,128)S(1)} %copy-done.25, f32[160,5120]{1,0:T(8,128)S(1)} %copy-done.26, ...), custom_call_target="tpu_custom_call" | custom-call | flops 1 | bytes 1 | tf_op jit(solution)/shard_map/pallas_call | solution.py:451
  228.6 5.4 %shard_map.171 = (f32[640,1280]{1,0:T(8,128)}, f32[640,1280]{1,0:T(8,128)}, f32[640,1280]{1,0:T(8,128)S(1)}, f32[32,128]{1,0:T(8,128)S(1)}) custom-call(s32[1]{0:T(128)} %bitcast.c_ref, f32[640,1280]{1,0:T(8,128)S(1)} %copy-done.4, f32[640,1280]{1,0:T(8,128)S(1)} %copy-done.27, f32[640,1280]{1,0:T(8,128)S(1)} %copy-done.28, ...), custom_call_target="tpu_custom_call" | custom-call | flops 1 | bytes 1 | tf_op jit(solution)/shard_map/pallas_call | solution.py:451
  234.0 3.4 %collective-permute-start.42 = (f32[32,128]{1,0:T(8,128)S(1)}, f32[32,128]{1,0:T(8,128)S(1)}, u32[]{:S(2)}, u32[]{:S(2)}) collective-permute-start(f32[32,128]{1,0:T(8,128)S(1)} %get-tuple-element.345.refs_0_), channel_id=1, source_target_pairs={{0,24},{4,28},{8,16},{12,20},{16,8},{20,12},{24,0},{28,4},{1,25},{... | collective-permute-start | bytes 49160 | tf_op jit(solution)/shard_map/ppermute | solution.py:510
  242.7 3.1 %collective-permute-done.43.refs_1_ = f32[32,128]{1,0:T(8,128)S(1)} collective-permute-done((f32[32,128]{1,0:T(8,128)S(1)}, f32[32,128]{1,0:T(8,128)S(1)}, u32[]{:S(2)}, u32[]{:S(2)}) %collective-permute-start.43) | collective-permute-done | bytes 16416 | tf_op jit(solution)/shard_map/ppermute | solution.py:506
  245.8 3.2 %shard_map.173 = f32[160,5120]{1,0:T(8,128)} custom-call(f32[160,5120]{1,0:T(8,128)S(1)} %copy-done.9, f32[160,5120]{1,0:T(8,128)S(1)} %get-tuple-element.350.u_ref, f32[32,128]{1,0:T(8,128)S(1)} %shard_map.172.refs_0_, f32[32,128]{1,0:T(8,128)S(1)} %collective-permute-done.43.refs_1_), custom_call_target="tpu_custom_call" | custom-call | flops 1 | bytes 1 | tf_op jit(solution)/shard_map/pallas_call | solution.py:478
  249.1 3.2 %shard_map.174 = f32[640,1280]{1,0:T(8,128)} custom-call(f32[640,1280]{1,0:T(8,128)S(1)} %copy-done.4, f32[640,1280]{1,0:T(8,128)S(1)} %get-tuple-element.357.u_ref, f32[32,128]{1,0:T(8,128)S(1)} %shard_map.172.refs_0_, f32[32,128]{1,0:T(8,128)S(1)} %collective-permute-done.43.refs_1_), custom_call_target="tpu_custom_call" | custom-call | flops 1 | bytes 1 | tf_op jit(solution)/shard_map/pallas_call | solution.py:478
  (193 shorter events, 100.2 us)
Async XLA Ops:
  5.8 66.6 %collective-permute-start = (bf16[2816,512]{1,0:T(8,128)(2,1)}, bf16[2816,512]{1,0:T(8,128)(2,1)}, u32[]{:S(2)}, u32[]{:S(2)}) collective-permute-start(bf16[2816,512]{1,0:T(8,128)(2,1)} %shard_map.136), channel_id=1, source_target_pairs={{0,4},{4,0},{8,12},{12,8},{16,20},{20,16},{24,28},{28,24},{1,5},{5... | collective-permute-start | bytes 8650760 | tf_op jit(solution)/shard_map/ppermute | solution.py:506
  11.0 37.4 %collective-permute-start.1 = (bf16[320,1280]{1,0:T(8,128)(2,1)}, bf16[320,1280]{1,0:T(8,128)(2,1)}, u32[]{:S(2)}, u32[]{:S(2)}) collective-permute-start(bf16[320,1280]{1,0:T(8,128)(2,1)} %shard_map.137.refs_2_.refs_4_), channel_id=1, source_target_pairs={{0,8},{4,12},{8,0},{12,4},{16,24},{20,28},{24,16},{28,20},{1,9},{5... | collective-permute-start | bytes 2457608 | tf_op jit(solution)/shard_map/ppermute | solution.py:510
  12.6 38.3 %collective-permute-start.2 = (bf16[320,1280]{1,0:T(8,128)(2,1)}, bf16[320,1280]{1,0:T(8,128)(2,1)}, u32[]{:S(2)}, u32[]{:S(2)}) collective-permute-start(bf16[320,1280]{1,0:T(8,128)(2,1)} %shard_map.137.refs_2_.refs_4_), channel_id=1, source_target_pairs={{0,16},{4,20},{8,24},{12,28},{16,0},{20,4},{24,8},{28,12},{1,17},{... | collective-permute-start | bytes 2457608 | tf_op jit(solution)/shard_map/ppermute | solution.py:510
  50.8 31.5 %collective-permute-start.3 = (bf16[320,1280]{1,0:T(8,128)(2,1)}, bf16[320,1280]{1,0:T(8,128)(2,1)}, u32[]{:S(2)}, u32[]{:S(2)}) collective-permute-start(bf16[320,1280]{1,0:T(8,128)(2,1)} %collective-permute-done.2.refs_4_.refs_6_), channel_id=1, source_target_pairs={{0,8},{4,12},{8,0},{12,4},{16,24},{20,28},{24,16},{28,20},{1,9},{5... | collective-permute-start | bytes 2457608 | tf_op jit(solution)/shard_map/ppermute | solution.py:510
  51.2 53.7 %collective-permute-start.10 = (bf16[1280,512]{1,0:T(8,128)(2,1)}, bf16[1280,512]{1,0:T(8,128)(2,1)}, u32[]{:S(2)}, u32[]{:S(2)}) collective-permute-start(bf16[1280,512]{1,0:T(8,128)(2,1)} %shard_map.138.refs_0_), channel_id=1, source_target_pairs={{0,4},{4,0},{8,12},{12,8},{16,20},{20,16},{24,28},{28,24},{1,5},{5... | collective-permute-start | bytes 3932168 | tf_op jit(solution)/shard_map/ppermute | solution.py:506
  82.3 12.4 %collective-permute-start.6 = (bf16[320,1280]{1,0:T(8,128)(2,1)}, bf16[320,1280]{1,0:T(8,128)(2,1)}, u32[]{:S(2)}, u32[]{:S(2)}) collective-permute-start(bf16[320,1280]{1,0:T(8,128)(2,1)} %collective-permute-done.2.refs_4_.refs_6_), channel_id=1, source_target_pairs={{0,1},{1,0},{2,3},{3,2},{4,5},{5,4},{6,7},{7,6},{8,9},{9,8},{10,11... | collective-permute-start | bytes 2457608 | tf_op jit(solution)/shard_map/ppermute | solution.py:520
  82.3 12.3 %collective-permute-start.7 = (bf16[320,1280]{1,0:T(8,128)(2,1)}, bf16[320,1280]{1,0:T(8,128)(2,1)}, u32[]{:S(2)}, u32[]{:S(2)}) collective-permute-start(bf16[320,1280]{1,0:T(8,128)(2,1)} %collective-permute-done.3.refs_5_.refs_7_), channel_id=1, source_target_pairs={{0,1},{1,0},{2,3},{3,2},{4,5},{5,4},{6,7},{7,6},{8,9},{9,8},{10,11... | collective-permute-start | bytes 2457608 | tf_op jit(solution)/shard_map/ppermute | solution.py:520
  90.9 24.2 %collective-permute-start.13 = (bf16[2,4,1,96,640]{4,3,2,1,0:T(8,128)(2,1)S(1)}, bf16[2,4,1,96,640]{4,3,2,1,0:T(8,128)(2,1)S(1)}, u32[]{:S(2)}, u32[]{:S(2)}) collective-permute-start(bf16[2,4,1,96,640]{4,3,2,1,0:T(8,128)(2,1)S(1)} %shard_map.143), channel_id=1, source_target_pairs={{0,2},{1,3},{2,0},{3,1},{4,6},{5,7},{6,4},{7,5},{8,10},{9,11},{10,... | collective-permute-start | bytes 2949128 | tf_op jit(solution)/shard_map/ppermute | solution.py:516
  93.1 28.9 %collective-permute-start.15 = (bf16[4,256,512]{2,1,0:T(8,128)(2,1)S(1)}, bf16[4,256,512]{2,1,0:T(8,128)(2,1)S(1)}, u32[]{:S(2)}, u32[]{:S(2)}) collective-permute-start(bf16[4,256,512]{2,1,0:T(8,128)(2,1)S(1)} %copy-done.42), channel_id=1, source_target_pairs={{0,4},{4,0},{8,12},{12,8},{16,20},{20,16},{24,28},{28,24},{1,5},{5... | collective-permute-start | bytes 3145736 | tf_op jit(solution)/shard_map/ppermute | solution.py:506
  117.0 19.2 %collective-permute-start.16 = (bf16[2,2,1,96,640]{4,3,2,1,0:T(8,128)(2,1)S(1)}, bf16[2,2,1,96,640]{4,3,2,1,0:T(8,128)(2,1)S(1)}, u32[]{:S(2)}, u32[]{:S(2)}) collective-permute-start(bf16[2,2,1,96,640]{4,3,2,1,0:T(8,128)(2,1)S(1)} %shard_map.146), channel_id=1, source_target_pairs={{0,8},{4,12},{8,0},{12,4},{16,24},{20,28},{24,16},{28,20},{1,9},{5... | collective-permute-start | bytes 1474568 | tf_op jit(solution)/shard_map/ppermute | solution.py:510
  120.3 29.4 %collective-permute-start.14 = (bf16[2,4,2,80,384]{4,3,2,1,0:T(8,128)(2,1)S(1)}, bf16[2,4,2,80,384]{4,3,2,1,0:T(8,128)(2,1)S(1)}, u32[]{:S(2)}, u32[]{:S(2)}) collective-permute-start(bf16[2,4,2,80,384]{4,3,2,1,0:T(8,128)(2,1)S(1)} %shard_map.147), channel_id=1, source_target_pairs={{0,2},{1,3},{2,0},{3,1},{4,6},{5,7},{6,4},{7,5},{8,10},{9,11},{10,... | collective-permute-start | bytes 2949128 | tf_op jit(solution)/shard_map/ppermute | solution.py:516
  145.3 17.6 %collective-permute-start.23 = (bf16[2,4,2,80,256]{4,3,2,1,0:T(8,128)(2,1)S(1)}, bf16[2,4,2,80,256]{4,3,2,1,0:T(8,128)(2,1)S(1)}, u32[]{:S(2)}, u32[]{:S(2)}) collective-permute-start(bf16[2,4,2,80,256]{4,3,2,1,0:T(8,128)(2,1)S(1)} %shard_map.152), channel_id=1, source_target_pairs={{0,2},{1,3},{2,0},{3,1},{4,6},{5,7},{6,4},{7,5},{8,10},{9,11},{10,... | collective-permute-start | bytes 1966088 | tf_op jit(solution)/shard_map/ppermute | solution.py:516
  148.3 27.8 %collective-permute-start.26 = (bf16[2,4,1,64,640]{4,3,2,1,0:T(8,128)(2,1)S(1)}, bf16[2,4,1,64,640]{4,3,2,1,0:T(8,128)(2,1)S(1)}, u32[]{:S(2)}, u32[]{:S(2)}) collective-permute-start(bf16[2,4,1,64,640]{4,3,2,1,0:T(8,128)(2,1)S(1)} %shard_map.153), channel_id=1, source_target_pairs={{0,2},{1,3},{2,0},{3,1},{4,6},{5,7},{6,4},{7,5},{8,10},{9,11},{10,... | collective-permute-start | bytes 1966088 | tf_op jit(solution)/shard_map/ppermute | solution.py:516
  150.8 20.2 %collective-permute-start.21 = (bf16[2,2,2,80,384]{4,3,2,1,0:T(8,128)(2,1)S(1)}, bf16[2,2,2,80,384]{4,3,2,1,0:T(8,128)(2,1)S(1)}, u32[]{:S(2)}, u32[]{:S(2)}) collective-permute-start(bf16[2,2,2,80,384]{4,3,2,1,0:T(8,128)(2,1)S(1)} %shard_map.154), channel_id=1, source_target_pairs={{0,8},{4,12},{8,0},{12,4},{16,24},{20,28},{24,16},{28,20},{1,9},{5... | collective-permute-start | bytes 1474568 | tf_op jit(solution)/shard_map/ppermute | solution.py:510
  152.5 16.9 %collective-permute-start.22 = (bf16[2,1,1,96,640]{4,3,2,1,0:T(8,128)(2,1)S(1)}, bf16[2,1,1,96,640]{4,3,2,1,0:T(8,128)(2,1)S(1)}, u32[]{:S(2)}, u32[]{:S(2)}) collective-permute-start(bf16[2,1,1,96,640]{4,3,2,1,0:T(8,128)(2,1)S(1)} %shard_map.150), channel_id=1, source_target_pairs={{0,16},{4,20},{8,24},{12,28},{16,0},{20,4},{24,8},{28,12},{1,17},{... | collective-permute-start | bytes 737288 | tf_op jit(solution)/shard_map/ppermute | solution.py:510
  163.9 16.7 %collective-permute-start.25 = (bf16[2,2,2,80,256]{4,3,2,1,0:T(8,128)(2,1)S(1)}, bf16[2,2,2,80,256]{4,3,2,1,0:T(8,128)(2,1)S(1)}, u32[]{:S(2)}, u32[]{:S(2)}) collective-permute-start(bf16[2,2,2,80,256]{4,3,2,1,0:T(8,128)(2,1)S(1)} %shard_map.155), channel_id=1, source_target_pairs={{0,8},{4,12},{8,0},{12,4},{16,24},{20,28},{24,16},{28,20},{1,9},{5... | collective-permute-start | bytes 983048 | tf_op jit(solution)/shard_map/ppermute | solution.py:510
  171.9 13.4 %collective-permute-start.24 = (bf16[2,1,2,80,384]{4,3,2,1,0:T(8,128)(2,1)S(1)}, bf16[2,1,2,80,384]{4,3,2,1,0:T(8,128)(2,1)S(1)}, u32[]{:S(2)}, u32[]{:S(2)}) collective-permute-start(bf16[2,1,2,80,384]{4,3,2,1,0:T(8,128)(2,1)S(1)} %shard_map.157), channel_id=1, source_target_pairs={{0,16},{4,20},{8,24},{12,28},{16,0},{20,4},{24,8},{28,12},{1,17},{... | collective-permute-start | bytes 737288 | tf_op jit(solution)/shard_map/ppermute | solution.py:510
  177.7 14.4 %collective-permute-start.29 = (bf16[2,2,1,64,640]{4,3,2,1,0:T(8,128)(2,1)}, bf16[2,2,1,64,640]{4,3,2,1,0:T(8,128)(2,1)}, u32[]{:S(2)}, u32[]{:S(2)}) collective-permute-start(bf16[2,2,1,64,640]{4,3,2,1,0:T(8,128)(2,1)} %shard_map.158), channel_id=1, source_target_pairs={{0,8},{4,12},{8,0},{12,4},{16,24},{20,28},{24,16},{28,20},{1,9},{5... | collective-permute-start | bytes 983048 | tf_op jit(solution)/shard_map/ppermute | solution.py:510
  181.9 14.1 %collective-permute-start.28 = (bf16[2,1,2,80,256]{4,3,2,1,0:T(8,128)(2,1)}, bf16[2,1,2,80,256]{4,3,2,1,0:T(8,128)(2,1)}, u32[]{:S(2)}, u32[]{:S(2)}) collective-permute-start(bf16[2,1,2,80,256]{4,3,2,1,0:T(8,128)(2,1)} %shard_map.159), channel_id=1, source_target_pairs={{0,16},{4,20},{8,24},{12,28},{16,0},{20,4},{24,8},{28,12},{1,17},{... | collective-permute-start | bytes 491528 | tf_op jit(solution)/shard_map/ppermute | solution.py:510
  187.5 10.3 %collective-permute-start.27 = (bf16[2,80,384]{2,1,0:T(8,128)(2,1)}, bf16[2,80,384]{2,1,0:T(8,128)(2,1)}, u32[]{:S(2)}, u32[]{:S(2)}) collective-permute-start(bf16[2,80,384]{2,1,0:T(8,128)(2,1)} %get-tuple-element.295), channel_id=1, source_target_pairs={{0,4},{4,0},{8,12},{12,8},{16,20},{20,16},{24,28},{28,24},{1,5},{5... | collective-permute-start | bytes 368648 | tf_op jit(solution)/shard_map/ppermute | solution.py:506
  189.0 18.6 %collective-permute-start.31 = (bf16[2,96,640]{2,1,0:T(8,128)(2,1)S(1)}, bf16[2,96,640]{2,1,0:T(8,128)(2,1)}, u32[]{:S(2)}, u32[]{:S(2)}) collective-permute-start(bf16[2,96,640]{2,1,0:T(8,128)(2,1)S(1)} %shard_map.156.refs_0_), channel_id=1, source_target_pairs={{0,2},{1,3},{2,0},{3,1},{4,6},{5,7},{6,4},{7,5},{8,10},{9,11},{10,... | collective-permute-start | bytes 737288 | tf_op jit(solution)/shard_map/ppermute | solution.py:516
  199.3 9.8 %collective-permute-start.30 = (bf16[2,2,80,384]{3,2,1,0:T(8,128)(2,1)S(1)}, bf16[2,2,80,384]{3,2,1,0:T(8,128)(2,1)S(1)}, u32[]{:S(2)}, u32[]{:S(2)}) collective-permute-start(bf16[2,2,80,384]{3,2,1,0:T(8,128)(2,1)S(1)} %shard_map.163.refs_0_), channel_id=1, source_target_pairs={{0,2},{1,3},{2,0},{3,1},{4,6},{5,7},{6,4},{7,5},{8,10},{9,11},{10,... | collective-permute-start | bytes 737288 | tf_op jit(solution)/shard_map/ppermute | solution.py:516
  216.6 9.7 %collective-permute-start.37 = (bf16[2,64,640]{2,1,0:T(8,128)(2,1)S(1)}, bf16[2,64,640]{2,1,0:T(8,128)(2,1)S(1)}, u32[]{:S(2)}, u32[]{:S(2)}) collective-permute-start(bf16[2,64,640]{2,1,0:T(8,128)(2,1)S(1)} %shard_map.167.refs_0_), channel_id=1, source_target_pairs={{0,2},{1,3},{2,0},{3,1},{4,6},{5,7},{6,4},{7,5},{8,10},{9,11},{10,... | collective-permute-start | bytes 491528 | tf_op jit(solution)/shard_map/ppermute | solution.py:516
  217.0 10.0 %collective-permute-start.38 = (bf16[2,2,96,640]{3,2,1,0:T(8,128)(2,1)S(1)}, bf16[2,2,96,640]{3,2,1,0:T(8,128)(2,1)S(1)}, u32[]{:S(2)}, u32[]{:S(2)}) collective-permute-start(bf16[2,2,96,640]{3,2,1,0:T(8,128)(2,1)S(1)} %shard_map.165.refs_0_), channel_id=1, source_target_pairs={{0,1},{1,0},{2,3},{3,2},{4,5},{5,4},{6,7},{7,6},{8,9},{9,8},{10,11... | collective-permute-start | bytes 1474568 | tf_op jit(solution)/shard_map/ppermute | solution.py:520
  (63 other events, 576.9 us)
